TPU v7x, 32 devices: a whole 2x2x4 slice. The times are simulated.
32 devices in a mesh: dp: 8 (over y, x, core), tm: 4 (over z).
Axes of the slice: x: 2, y: 2, z: 4, core: 2. Of those that a mesh axis runs over, the one named last changes fastest.
Arguments:
- frames: bfloat16 [4096, 1024], P(('dp', 'tm')), may hold values from -40 to 40
- out_grad: bfloat16 [4096, 1024], P(('dp', 'tm')), may hold values from -0.25 to 0.25
- norm1_gain: float32 [1024], replicated, may hold values from 0.25 to 1.75
- w_query: bfloat16 [1024, 512], replicated, may hold values from -0.1875 to 0.1875
- w_kv: bfloat16 [1024, 1024], replicated, may hold values from -0.1875 to 0.1875
- w_out: bfloat16 [512, 1024], replicated, may hold values from -0.25 to 0.25
- norm2_gain: float32 [1024], replicated, may hold values from 0.25 to 1.75
- conv_kernel: float32 [31, 1024], replicated, may hold values from -1 to 1
- conv_bias: float32 [1024], replicated, may hold values from -3 to 3
- utt_blocks: int32 [8, 2], P('dp'), may hold values from 1 to 6, 8 in all within a row
- block_slot: int32 [8, 8], P('dp'), may hold values from 0 to 7, each once within a row
- left_count: int32 [8, 8], P('dp'), may hold values from 0 to 2
Outputs:
- layer_out: bfloat16 [4096, 1024], P(('dp', 'tm'))
- kv_grad: float32 [1024, 1024], P('dp', 'tm')
Inputs may be any that keep to these rules, and one draw needn't show every extreme that they name: `utt_blocks`: the 2 lengths of a group add up to 8. `block_slot`: each group's row names every slot once; slot s lies on index s // 2 of tm.
All inputs are finite; a program needn't handle non-finite values.
Results may differ from a plain program's by a relative error of at most 0.018.
Values may be sent and summed in bfloat16 or wider, within the bound.
No kernel may reach another device: no remote copies, remote signals or barrier semaphores. Data moves between devices by JAX's collectives and lax.ppermute only.
A program may use at most 64 MiB of HBM per device.

v0:
```python
import math

import jax
import jax.numpy as jnp
from jax import lax
from jax.sharding import PartitionSpec as P

HEADS = 8
KERNEL = 31
BLOCK = 64
LC = 2


EPSILON = 1e-05
SOFT_CAP = 4.0


def norm_parts(values):
    row_mean = jnp.mean(values, axis=-1, keepdims=True)
    centred = values - row_mean
    scale_inv = lax.rsqrt(jnp.mean(centred * centred, axis=-1, keepdims=True) + EPSILON)
    return (centred * scale_inv, scale_inv)


def norm_back(grad_in, unit_rows, scale_inv, gain_row):
    scaled = grad_in * gain_row
    first_mean = jnp.mean(scaled, axis=-1, keepdims=True)
    second_mean = jnp.mean(scaled * unit_rows, axis=-1, keepdims=True)
    return scale_inv * (scaled - first_mean - unit_rows * second_mean)


def block_layout(lengths, counts, block_total):
    utter_ends = jnp.cumsum(lengths)
    utter_starts = utter_ends - lengths
    block_index = jnp.arange(block_total, dtype=jnp.int32)
    past_end = block_index[:, None] >= utter_ends[None, :]
    utterance = jnp.sum(past_end.astype(jnp.int32), axis=1)
    matches = utterance[:, None] == jnp.arange(lengths.shape[0], dtype=jnp.int32)[None, :]
    first_block = jnp.sum(jnp.where(matches, utter_starts[None, :], 0), axis=1)
    position = block_index - first_block
    return (position, jnp.minimum(counts, position))


def pick(int_table, positions):
    matches = positions[..., None] == jnp.arange(int_table.shape[0], dtype=jnp.int32)
    return jnp.sum(jnp.where(matches, int_table, 0), axis=-1)


def attend(queries, keys_values, allowed):
    block_count, row_count, query_width = queries.shape
    head_size = query_width // HEADS
    query_heads = queries.reshape(block_count, row_count, HEADS, head_size)
    key_heads = keys_values[..., :query_width].reshape(block_count, -1, HEADS, head_size)
    value_heads = keys_values[..., query_width:].reshape(block_count, -1, HEADS, head_size)
    raw_scores = jnp.einsum(
        "nrhd,nkhd->nhrk", query_heads, key_heads, preferred_element_type=jnp.float32
    )
    capped = SOFT_CAP * jnp.tanh(raw_scores / (SOFT_CAP * math.sqrt(head_size)))
    exped = jnp.where(allowed[:, None], jnp.exp(capped), 0.0)
    attn_probs = exped / jnp.sum(exped, axis=-1, keepdims=True)
    context = jnp.einsum(
        "nhrk,nkhd->nrhd",
        attn_probs.astype(jnp.bfloat16),
        value_heads,
        preferred_element_type=jnp.float32,
    )
    return (
        context.astype(jnp.bfloat16).reshape(block_count, row_count, query_width),
        attn_probs,
        capped,
    )


def attend_back(queries, keys_values, context, attn_probs, capped, grad_context):
    block_count, row_count, query_width = queries.shape
    head_size = query_width // HEADS
    query_heads = queries.reshape(block_count, row_count, HEADS, head_size)
    value_heads = keys_values[..., query_width:].reshape(block_count, -1, HEADS, head_size)
    grad_heads = grad_context.reshape(block_count, row_count, HEADS, head_size)
    context_heads = context.reshape(block_count, row_count, HEADS, head_size)
    grad_probs = jnp.einsum(
        "nrhd,nkhd->nhrk", grad_heads, value_heads, preferred_element_type=jnp.float32
    )
    delta_rows = jnp.sum(
        grad_heads.astype(jnp.float32) * context_heads.astype(jnp.float32), axis=-1
    )
    delta_rows = jnp.transpose(delta_rows, (0, 2, 1))[..., None]
    grad_raw = (
        attn_probs
        * (grad_probs - delta_rows)
        * (1.0 - (capped / SOFT_CAP) ** 2)
        / math.sqrt(head_size)
    )
    key_part = jnp.einsum(
        "nhrk,nrhd->nkhd",
        grad_raw.astype(jnp.bfloat16),
        query_heads,
        preferred_element_type=jnp.float32,
    )
    value_part = jnp.einsum(
        "nhrk,nrhd->nkhd",
        attn_probs.astype(jnp.bfloat16),
        grad_heads,
        preferred_element_type=jnp.float32,
    )
    key_rows = key_part.shape[1]
    joined = jnp.concatenate(
        [
            key_part.reshape(block_count, key_rows, query_width),
            value_part.reshape(block_count, key_rows, query_width),
        ],
        axis=-1,
    )
    return joined.astype(jnp.bfloat16)


def project_back(grad_rows, w_out):
    product = lax.dot_general(
        grad_rows.astype(jnp.bfloat16),
        w_out,
        (((2,), (1,)), ((), ())),
        preferred_element_type=jnp.float32,
    )
    return product.astype(jnp.bfloat16)


def conv_pass(cache_rows, conv_in, hidden, out_grad_f, conv_kernel, conv_bias):
    row_count = conv_in.shape[1]
    tail_rows = cache_rows.shape[1]
    extended = jnp.concatenate([cache_rows, conv_in], axis=1).astype(jnp.float32)
    mixed_conv = conv_bias + conv_kernel[0] * extended[:, :row_count]
    for tap_index in range(1, conv_kernel.shape[0]):
        mixed_conv = (
            mixed_conv + conv_kernel[tap_index] * extended[:, tap_index : tap_index + row_count]
        )
    gate_value = jax.nn.sigmoid(mixed_conv)
    layer_out = (hidden + mixed_conv * gate_value).astype(jnp.bfloat16)
    grad_mixed = out_grad_f * gate_value * (1.0 + mixed_conv * (1.0 - gate_value))
    padded = jnp.pad(grad_mixed, ((0, 0), (tail_rows, tail_rows), (0, 0)))
    grad_ext = conv_kernel[0] * padded[:, tail_rows : tail_rows + row_count + tail_rows]
    for tap_index in range(1, conv_kernel.shape[0]):
        grad_ext = (
            grad_ext
            + conv_kernel[tap_index]
            * padded[:, tail_rows - tap_index : tail_rows - tap_index + row_count + tail_rows]
        )
    return (layer_out, grad_ext)


def on_device(
    frames,
    out_grad,
    norm1_gain,
    w_query,
    w_kv,
    w_out,
    norm2_gain,
    conv_kernel,
    conv_bias,
    utt_blocks,
    block_slot,
    left_count,
):
    time_devices = lax.axis_size("tm")
    data_devices = lax.axis_size("dp")
    model_width = frames.shape[1]
    kv_width = w_kv.shape[1]
    tail_rows = KERNEL - 1
    local_count = frames.shape[0] // BLOCK
    block_total = local_count * time_devices
    slot_table = block_slot[0]
    position, reach = block_layout(utt_blocks[0], left_count[0], block_total)
    block_index = jnp.arange(block_total, dtype=jnp.int32)
    slot_matches = slot_table[None, :] == block_index[:, None]
    block_of_slot = jnp.sum(jnp.where(slot_matches, block_index[None, :], 0), axis=1)
    my_slots = lax.axis_index("tm") * local_count + jnp.arange(local_count, dtype=jnp.int32)
    my_blocks = pick(block_of_slot, my_slots)
    my_reach = pick(reach, my_blocks)
    my_prev = jnp.maximum(my_blocks - 1, 0)
    has_prev = pick(position, my_blocks) >= 1
    own_rows = frames.reshape(local_count, BLOCK, model_width).astype(jnp.float32)
    out_grad_f = out_grad.reshape(local_count, BLOCK, model_width).astype(jnp.float32)
    gathered = lax.all_gather(frames, "tm", axis=0, tiled=True)
    all_blocks = gathered.reshape(block_total, BLOCK, model_width)
    span_blocks = LC + 1
    window = jnp.maximum(
        my_blocks[:, None] - (span_blocks - 1) + jnp.arange(span_blocks, dtype=jnp.int32)[None, :],
        0,
    )
    window_slots = pick(slot_table, window)
    window_rows = jnp.take(all_blocks, window_slots.reshape(-1), axis=0).reshape(
        local_count, span_blocks, BLOCK, model_width
    )
    unit_first, unused_inv = norm_parts(window_rows.astype(jnp.float32))
    normed = (unit_first * norm1_gain).astype(jnp.bfloat16)
    flat_normed = normed.reshape(local_count, span_blocks * BLOCK, model_width)
    keys_values = jnp.dot(flat_normed, w_kv, preferred_element_type=jnp.float32).astype(
        jnp.bfloat16
    )
    own_queries = jnp.dot(
        normed[:, span_blocks - 1], w_query, preferred_element_type=jnp.float32
    ).astype(jnp.bfloat16)
    window_lane = jnp.arange(span_blocks, dtype=jnp.int32)[None, :]
    own_ok = window_lane >= span_blocks - 1 - my_reach[:, None]
    key_total = span_blocks * BLOCK
    own_mask = jnp.broadcast_to(
        jnp.repeat(own_ok, BLOCK, axis=1)[:, None, :], (local_count, BLOCK, key_total)
    )
    context, attn_probs, capped = attend(own_queries, keys_values, own_mask)
    hidden = own_rows + jnp.dot(context, w_out, preferred_element_type=jnp.float32)
    unit_second, inv_second = norm_parts(hidden)
    conv_in = (unit_second * norm2_gain).astype(jnp.bfloat16)
    tail_pieces = lax.all_gather(conv_in[:, BLOCK - tail_rows :], "tm", axis=0, tiled=True)
    cache_rows = jnp.take(tail_pieces, pick(slot_table, my_prev), axis=0)
    cache_rows = jnp.where(has_prev[:, None, None], cache_rows, jnp.zeros((), jnp.bfloat16))
    layer_out, grad_ext = conv_pass(cache_rows, conv_in, hidden, out_grad_f, conv_kernel, conv_bias)
    carried = jnp.where(has_prev[:, None, None], grad_ext[:, :tail_rows], 0.0)
    grad_hidden = out_grad_f + norm_back(
        grad_ext[:, tail_rows:], unit_second, inv_second, norm2_gain
    )
    returned = lax.all_gather(carried.astype(jnp.bfloat16), "tm", axis=0, tiled=True).astype(
        carried.dtype
    )
    next_block = my_blocks + 1
    next_ok = next_block < block_total
    next_slot = pick(slot_table, jnp.minimum(next_block, block_total - 1))
    incoming = jnp.where(next_ok[:, None, None], jnp.take(returned, next_slot, axis=0), 0.0)
    grad_carried = norm_back(
        incoming,
        unit_second[:, BLOCK - tail_rows :],
        inv_second[:, BLOCK - tail_rows :],
        norm2_gain,
    )
    grad_context = project_back(jnp.concatenate([grad_hidden, grad_carried], axis=1), w_out)
    term_own = attend_back(
        own_queries, keys_values, context, attn_probs, capped, grad_context[:, :BLOCK]
    )
    term_carried = attend_back(
        own_queries[:, BLOCK - tail_rows :],
        keys_values,
        context[:, BLOCK - tail_rows :],
        attn_probs[:, :, BLOCK - tail_rows :],
        capped[:, :, BLOCK - tail_rows :],
        grad_context[:, BLOCK:],
    )
    grad_pairs = ((flat_normed, term_own), (flat_normed, term_carried))
    share_width = kv_width // time_devices
    share_rows = model_width // data_devices
    running = jnp.zeros((share_rows * lax.axis_size("dp"), kv_width), jnp.float32)
    for normed_part, term_part in grad_pairs:
        running = running + jnp.einsum(
            "nkd,nke->de", normed_part, term_part, preferred_element_type=jnp.float32
        )
    grad_part = lax.psum_scatter(running, "dp", scatter_dimension=0, tiled=True)
    grad_whole = lax.psum(grad_part.astype(jnp.bfloat16), "tm").astype(jnp.float32)
    kv_grad = lax.dynamic_slice_in_dim(
        grad_whole, lax.axis_index("tm") * share_width, share_width, 1
    )
    return (layer_out.reshape(local_count * BLOCK, model_width), kv_grad)


def solution(mesh):
    return jax.shard_map(
        on_device,
        mesh=mesh,
        in_specs=(
            P(("dp", "tm"), None),
            P(("dp", "tm"), None),
            P(),
            P(),
            P(),
            P(),
            P(),
            P(),
            P(),
            P("dp", None),
            P("dp", None),
            P("dp", None),
        ),
        out_specs=(P(("dp", "tm"), None), P("dp", "tm")),
        check_vma=False,
    )
```

profile of v0, /device:TPU:0, one launch (start us, length us, event | category | flops | bytes accessed | tf_op | source)
XLA Modules:
  0.0 228.1 jit_solution(9259792076600674154)
XLA Ops:
  7.2 0.7 all-gather.2.cloned.1.call-update
  8.0 0.8 select_reduce_fusion
  9.0 0.9 fusion.154
  10.2 0.8 reduce-window.4
  11.0 0.7 fusion.163
  11.9 0.7 bitcast_minimum_fusion
  13.0 0.9 fusion.159
  14.0 0.6 pad_clamp_fusion.1
  14.6 0.6 pad_clamp_fusion
  15.2 0.6 compare_and_fusion
  15.8 0.6 compare_and_fusion.1
  16.4 1.7 fusion.180
  18.1 2.0 fusion.179
  20.1 20.2 %all-gather.2.cloned.1.call-done = bf16[512,1024]{1,0:T(8,128)(2,1)} async-done(((bf16[128,1024]{1,0:T(8,128)(2,1)}), bf16[512,1024]{1,0:T(8,128)(2,1)}) %all-gather.2.cloned.1.call-update) | async-done | bytes 1048592 | tf_op jit(solution)/shard_map/all_gather | solution.py:183
  40.2 1.8 gather_fusion
  42.1 0.3 convert_reduce_fusion
  42.5 0.4 fusion.3
  43.0 1.6 convolution_convert_fusion.6
  44.6 0.6 slice.509
  45.2 0.8 copy.123
  46.1 0.4 multiply_convert_fusion
  46.5 1.0 fusion.4
  47.5 0.2 copy.100
  48.0 2.6 %broadcast_multiply_fusion = (f32[2,8,64,192]{3,2,1,0:T(8,128)}, f32[2,8,64]{2,1,0:T(8,128)S(1)}, f32[2,8,64,192]{3,2,1,0:T(8,128)S(1)}) fusion(pred[2,192]{1,0:T(4,128)(4,1)S(1)} %broadcast_in_dim_reshape.3, bf16[2,64,8,64]{1,3,2,0:T(8,128)(2,1)} %bitcast.145, bf16[2,192,8,64]{1,3,2,0:T(8,128)(2,1)S(1)} %bitcast.138), kind=kOutput, calls=%fused_computation.220 | convolution fusion | flops 25951232 | bytes 2101632 | tf_op jit(solution)/shard_map/nrhd,nkhd->nhrk/dot_general | solution.py:55
  50.6 0.4 convolution_convert_fusion.4
  51.0 0.5 copy-done.2
  51.6 0.9 slice_convert_fusion.2
  52.5 0.4 fusion.181
  53.0 0.2 multiply_reduce_fusion.2
  53.2 0.6 slice_bitcast_fusion
  54.0 15.7 %all_gather.10 = bf16[8,30,1024]{2,1,0:T(8,128)(2,1)} all-gather(bf16[2,30,1024]{2,1,0:T(8,128)(2,1)S(1)} %slice.473), channel_id=1, replica_groups=mesh['dp'=8,'tm'=4] {'tm'}, dimensions={0}, use_global_device_ids=true | all-gather | bytes 614400 | tf_op jit(solution)/shard_map/all_gather | solution.py:213
  69.8 1.7 gather_fusion.1
  71.5 0.8 select_select_fusion
  72.7 4.0 %fusion.91 = (f32[2,64,1024]{2,1,0:T(8,128)S(1)}, f32[2,64,1024]{2,1,0:T(8,128)}) fusion(bf16[2,64,1024]{2,1,0:T(8,128)(2,1)S(1)} %bitcast.141, f32[2,94,1024]{2,1,0:T(8,128)S(1)} %maximum_convert_fusion, f32[1024]{0:T(1024)} %bitcast.172, f32[1024]{0:T(1024)} %bitcast.174, f32[1024]{0:T(1024)} %bitcast.178, f32[1024]{0:T(1024)} %bitcast.180, ...), kind=kLoop, calls=%fused_computation.143 | loop fusion | flops 9306112 | bytes 17694720 | tf_op jit(solution)/shard_map/mul | solution.py:138
  77.0 2.6 %fusion.77 = f32[2,94,1024]{2,1,0:T(8,128)S(1)} fusion(f32[2,64,1024]{2,1,0:T(8,128)S(1)} %get-tuple-element.10, f32[1024]{0:T(1024)S(1)} %bitcast.173, f32[1024]{0:T(1024)S(1)} %bitcast.175, f32[1024]{0:T(1024)S(1)} %bitcast.179, f32[1024]{0:T(1024)S(1)} %bitcast.181, f32[1024]{0:T(1024)S(1)} %bitcast.183, f32[1024]{0:T(1024)S(1)} %bitcast.185, ...), kind=kLoop, calls=%fused_computation.125 | loop fusion | flops 11743232 | bytes 1421312 | tf_op jit(solution)/shard_map/add | solution.py:143
  79.7 0.8 copy-done.1
  80.7 15.3 %all_gather.11 = bf16[8,30,1024]{2,1,0:T(8,128)(2,1)S(1)} all-gather(bf16[2,30,1024]{2,1,0:T(8,128)(2,1)S(1)} %fusion.137), channel_id=1, replica_groups=mesh['dp'=8,'tm'=4] {'tm'}, dimensions={0}, use_global_device_ids=true | all-gather | bytes 614400 | tf_op jit(solution)/shard_map/all_gather | solution.py:221
  96.1 1.1 convert_element_type.119
  97.2 1.9 gather_fusion.2
  99.1 0.2 fusion.148
  99.4 1.4 fusion.92
  101.0 0.5 convolution_convert_fusion.5
  101.5 0.7 slice.508
  102.2 1.2 fusion.21
  103.4 0.8 reshape.377
  104.2 0.9 copy.137
  105.3 1.1 multiply_reduce_fusion.4
  106.5 1.1 copy.104
  107.6 0.7 multiply_reduce_fusion
  108.3 2.5 %convolution_convert_fusion = bf16[2,8,64,192]{3,2,1,0:T(8,128)(2,1)} fusion(bf16[2,64,8,64]{1,3,2,0:T(8,128)(2,1)S(1)} %bitcast.142, f32[2,8,64]{2,1,0:T(8,128)S(1)} %copy-done.49, pred[2,192]{1,0:T(4,128)(4,1)S(1)} %copy-done.51, f32[2,8,64,192]{3,2,1,0:T(8,128)} %copy-done.2), kind=kOutput, calls=%fused_computation.50 | convolution fusion | flops 26148864 | bytes 1315200 | tf_op jit(solution)/shard_map/nhrk,nrhd->nkhd/dot_general | solution.py:100
  110.8 2.8 %convolution_convert_fusion.1 = bf16[2,8,64,192]{3,2,1,0:T(8,128)(2,1)} fusion(bf16[2,64,8,64]{1,3,2,0:T(8,128)(2,1)} %bitcast.146, bf16[2,64,8,64]{1,3,2,0:T(8,128)(2,1)S(1)} %bitcast.143, bf16[2,192,8,64]{1,3,2,0:T(8,128)(2,1)S(1)} %bitcast.137, f32[2,8,64,192]{3,2,1,0:T(8,128)} %copy-done.2, f32[2,8,64]{2,1,0:T(8,128)} %bitcast.214, ...), kind=kOutput, calls=%fused_computation.51 | convolution fusion | flops 52494336 | bytes 1843584 | tf_op jit(solution)/shard_map/nhrk,nrhd->nkhd/dot_general | solution.py:94
  113.6 2.0 copy.107
  115.6 1.4 convolution_convert_fusion.2
  117.0 0.9 copy.116
  117.9 2.8 %convolution_convert_fusion.3 = bf16[2,8,64,192]{3,2,1,0:T(8,128)(2,1)} fusion(bf16[2,192,8,64]{1,3,2,0:T(8,128)(2,1)} %bitcast.136, f32[2,8,64,192]{3,2,1,0:T(8,128)} %get-tuple-element.14, f32[2,8,64,192]{3,2,1,0:T(8,128)} %fusion.21, f32[2,8,30]{2,1,0:T(8,128)S(1)} %copy.112, bf16[2,30,8,64]{3,2,1,0:T(8,128)(2,1)} %reshape.377, ...), kind=kOutput, calls=%fused_computation.53 | convolution fusion | flops 24526848 | bytes 2152320 | tf_op jit(solution)/shard_map/nhrk,nrhd->nkhd/dot_general | solution.py:94
  120.8 2.0 copy.115
  122.8 2.0 copy.108
  124.8 2.5 %fusion.84 = f32[1024,1024,1]{1,0,2:T(8,128)S(1)} fusion(bf16[2,192,1024]{2,1,0:T(8,128)(2,1)S(1)} %copy-done.5, bf16[2,192,512]{2,1,0:T(8,128)(2,1)} %copy.108, bf16[2,192,512]{2,1,0:T(8,128)(2,1)} %copy.107), kind=kOutput, calls=%fused_computation.132 | convolution fusion | flops 806879232 | bytes 5767168 | tf_op jit(solution)/shard_map/nkd,nke->de/dot_general | solution.py:251
  127.3 3.3 %bitcast_add_fusion = f32[1024,1024]{1,0:T(8,128)} fusion(f32[1024,1024,1]{1,0,2:T(8,128)S(1)} %fusion.84, bf16[2,192,1024]{2,1,0:T(8,128)(2,1)S(1)} %copy-done.5, bf16[2,192,512]{2,1,0:T(8,128)(2,1)S(1)} %copy-done.12, bf16[2,192,512]{2,1,0:T(8,128)(2,1)S(1)} %copy-done.13), kind=kOutput, calls=%fused_computation.34 | convolution fusion | flops 807927808 | bytes 9961472 | tf_op jit(solution)/shard_map/nkd,nke->de/dot_general | solution.py:251
  130.6 51.6 %reduce-scatter.2.cloned.1.call-done = f32[128,1024]{1,0:T(8,128)} async-done(((f32[1024,1024]{1,0:T(8,128)}), f32[128,1024]{1,0:T(8,128)}) %reduce-scatter.2.cloned.1.call-update) | async-done | bytes 524304 | tf_op jit(solution)/shard_map/reduce_scatter | solution.py:254
  182.2 1.8 convert_element_type.129
  184.0 0.9 add_convert_fusion
  184.9 35.1 %all-reduce.3.cloned.1.call-done = bf16[128,1024]{1,0:T(8,128)(2,1)} async-done(((bf16[128,1024]{1,0:T(8,128)(2,1)}), bf16[128,1024]{1,0:T(8,128)(2,1)}) %all-reduce.3.cloned.1.call-update) | async-done | bytes 262160 | tf_op jit(solution)/shard_map/psum | solution.py:255
  220.0 1.5 dynamic-slice_convert_fusion
  (173 shorter events, 3.3 us)
Async XLA Ops:
  7.2 39.3 %copy-start = (bf16[1024,1024]{1,0:T(8,128)(2,1)S(1)}, bf16[1024,1024]{1,0:T(8,128)(2,1)}, u32[]{:S(2)}) copy-start(bf16[1024,1024]{1,0:T(8,128)(2,1)} %param.16) | copy-start | bytes 6291460
  7.2 33.1 %all-gather.2.cloned.1.call-start = ((), (), s32[]{:S(2)}) async-start(), calls=%async_computation.1 | async-start | bytes 1310720 | tf_op jit(solution)/shard_map/all_gather | solution.py:183
  7.9 174.3 %reduce-scatter.2.cloned.1.call-start = ((), (), s32[]{:S(2)}) async-start(), calls=%async_computation.2 | async-start | bytes 4718592 | tf_op jit(solution)/shard_map/reduce_scatter | solution.py:254
  13.0 37.6 %copy-start.50 = (pred[2,192]{1,0:T(4,128)(4,1)}, pred[2,192]{1,0:T(4,128)(4,1)S(1)}, u32[]{:S(2)}) copy-start(pred[2,192]{1,0:T(4,128)(4,1)S(1)} %broadcast_in_dim_reshape.3) | copy-start | bytes 1156
  40.2 2.8 %copy-start.57 = (f32[1024]{0:T(1024)S(1)}, f32[1024]{0:T(1024)}, u32[]{:S(2)}) copy-start(f32[1024]{0:T(1024)} %param.14) | copy-start | bytes 12292
  46.5 1.0 copy-start.4
  48.0 3.1 %copy-start.10 = (bf16[2,192,512]{1,2,0:T(8,128)(2,1)}, bf16[2,192,512]{1,2,0:T(8,128)(2,1)S(1)}, u32[]{:S(2)}) copy-start(bf16[2,192,512]{1,2,0:T(8,128)(2,1)S(1)} %copy.96) | copy-start | bytes 1179652
  50.6 1.0 copy-start.2
  50.6 1.0 copy-start.48
  50.6 1.9 copy-start.15
  50.6 1.9 copy-start.17
  51.6 1.6 copy-start.6
  51.6 2.2 copy-start.19
  53.2 0.8 copy-start.52
  71.5 1.0 copy-start.14
  72.4 4.3 %copy-start.20 = (f32[1,1024]{1,0:T(1,128)S(1)}, f32[1,1024]{1,0:T(1,128)}, u32[]{:S(2)}) copy-start(f32[1,1024]{1,0:T(1,128)} %get-tuple-element.40) | copy-start | bytes 12292
  72.4 4.3 %copy-start.21 = (f32[1,1024]{1,0:T(1,128)S(1)}, f32[1,1024]{1,0:T(1,128)}, u32[]{:S(2)}) copy-start(f32[1,1024]{1,0:T(1,128)} %get-tuple-element.41) | copy-start | bytes 12292
  72.5 4.3 %copy-start.22 = (f32[1,1024]{1,0:T(1,128)S(1)}, f32[1,1024]{1,0:T(1,128)}, u32[]{:S(2)}) copy-start(f32[1,1024]{1,0:T(1,128)} %get-tuple-element.42) | copy-start | bytes 12292
  72.5 4.3 %copy-start.23 = (f32[1,1024]{1,0:T(1,128)S(1)}, f32[1,1024]{1,0:T(1,128)}, u32[]{:S(2)}) copy-start(f32[1,1024]{1,0:T(1,128)} %get-tuple-element.43) | copy-start | bytes 12292
  72.5 4.3 %copy-start.24 = (f32[1,1024]{1,0:T(1,128)S(1)}, f32[1,1024]{1,0:T(1,128)}, u32[]{:S(2)}) copy-start(f32[1,1024]{1,0:T(1,128)} %get-tuple-element.44) | copy-start | bytes 12292
  72.5 4.3 %copy-start.25 = (f32[1,1024]{1,0:T(1,128)S(1)}, f32[1,1024]{1,0:T(1,128)}, u32[]{:S(2)}) copy-start(f32[1,1024]{1,0:T(1,128)} %get-tuple-element.45) | copy-start | bytes 12292
  72.5 4.3 %copy-start.26 = (f32[1,1024]{1,0:T(1,128)S(1)}, f32[1,1024]{1,0:T(1,128)}, u32[]{:S(2)}) copy-start(f32[1,1024]{1,0:T(1,128)} %get-tuple-element.46) | copy-start | bytes 12292
  72.5 4.3 %copy-start.27 = (f32[1,1024]{1,0:T(1,128)S(1)}, f32[1,1024]{1,0:T(1,128)}, u32[]{:S(2)}) copy-start(f32[1,1024]{1,0:T(1,128)} %get-tuple-element.47) | copy-start | bytes 12292
  72.5 4.3 %copy-start.28 = (f32[1,1024]{1,0:T(1,128)S(1)}, f32[1,1024]{1,0:T(1,128)}, u32[]{:S(2)}) copy-start(f32[1,1024]{1,0:T(1,128)} %get-tuple-element.48) | copy-start | bytes 12292
  72.5 4.3 %copy-start.29 = (f32[1,1024]{1,0:T(1,128)S(1)}, f32[1,1024]{1,0:T(1,128)}, u32[]{:S(2)}) copy-start(f32[1,1024]{1,0:T(1,128)} %get-tuple-element.18) | copy-start | bytes 12292
  72.5 4.3 %copy-start.30 = (f32[1,1024]{1,0:T(1,128)S(1)}, f32[1,1024]{1,0:T(1,128)}, u32[]{:S(2)}) copy-start(f32[1,1024]{1,0:T(1,128)} %get-tuple-element.19) | copy-start | bytes 12292
  72.5 4.3 %copy-start.31 = (f32[1,1024]{1,0:T(1,128)S(1)}, f32[1,1024]{1,0:T(1,128)}, u32[]{:S(2)}) copy-start(f32[1,1024]{1,0:T(1,128)} %get-tuple-element.20) | copy-start | bytes 12292
  72.5 4.3 %copy-start.32 = (f32[1,1024]{1,0:T(1,128)S(1)}, f32[1,1024]{1,0:T(1,128)}, u32[]{:S(2)}) copy-start(f32[1,1024]{1,0:T(1,128)} %get-tuple-element.21) | copy-start | bytes 12292
  72.5 4.3 %copy-start.33 = (f32[1,1024]{1,0:T(1,128)S(1)}, f32[1,1024]{1,0:T(1,128)}, u32[]{:S(2)}) copy-start(f32[1,1024]{1,0:T(1,128)} %get-tuple-element.22) | copy-start | bytes 12292
  72.6 4.3 %copy-start.34 = (f32[1,1024]{1,0:T(1,128)S(1)}, f32[1,1024]{1,0:T(1,128)}, u32[]{:S(2)}) copy-start(f32[1,1024]{1,0:T(1,128)} %get-tuple-element.23) | copy-start | bytes 12292
  72.6 4.3 %copy-start.35 = (f32[1,1024]{1,0:T(1,128)S(1)}, f32[1,1024]{1,0:T(1,128)}, u32[]{:S(2)}) copy-start(f32[1,1024]{1,0:T(1,128)} %get-tuple-element.24) | copy-start | bytes 12292
  72.6 4.3 %copy-start.36 = (f32[1,1024]{1,0:T(1,128)S(1)}, f32[1,1024]{1,0:T(1,128)}, u32[]{:S(2)}) copy-start(f32[1,1024]{1,0:T(1,128)} %get-tuple-element.25) | copy-start | bytes 12292
  72.6 4.3 %copy-start.37 = (f32[1,1024]{1,0:T(1,128)S(1)}, f32[1,1024]{1,0:T(1,128)}, u32[]{:S(2)}) copy-start(f32[1,1024]{1,0:T(1,128)} %get-tuple-element.26) | copy-start | bytes 12292
  72.6 4.3 %copy-start.38 = (f32[1,1024]{1,0:T(1,128)S(1)}, f32[1,1024]{1,0:T(1,128)}, u32[]{:S(2)}) copy-start(f32[1,1024]{1,0:T(1,128)} %get-tuple-element.27) | copy-start | bytes 12292
  72.6 4.3 %copy-start.39 = (f32[1,1024]{1,0:T(1,128)S(1)}, f32[1,1024]{1,0:T(1,128)}, u32[]{:S(2)}) copy-start(f32[1,1024]{1,0:T(1,128)} %get-tuple-element.28) | copy-start | bytes 12292
  72.6 4.3 %copy-start.40 = (f32[1,1024]{1,0:T(1,128)S(1)}, f32[1,1024]{1,0:T(1,128)}, u32[]{:S(2)}) copy-start(f32[1,1024]{1,0:T(1,128)} %get-tuple-element.29) | copy-start | bytes 12292
  72.6 4.3 %copy-start.41 = (f32[1,1024]{1,0:T(1,128)S(1)}, f32[1,1024]{1,0:T(1,128)}, u32[]{:S(2)}) copy-start(f32[1,1024]{1,0:T(1,128)} %get-tuple-element.30) | copy-start | bytes 12292
  72.6 4.3 %copy-start.42 = (f32[1,1024]{1,0:T(1,128)S(1)}, f32[1,1024]{1,0:T(1,128)}, u32[]{:S(2)}) copy-start(f32[1,1024]{1,0:T(1,128)} %get-tuple-element.31) | copy-start | bytes 12292
  72.6 4.3 %copy-start.43 = (f32[1,1024]{1,0:T(1,128)S(1)}, f32[1,1024]{1,0:T(1,128)}, u32[]{:S(2)}) copy-start(f32[1,1024]{1,0:T(1,128)} %get-tuple-element.32) | copy-start | bytes 12292
  72.7 4.3 %copy-start.44 = (f32[1,1024]{1,0:T(1,128)S(1)}, f32[1,1024]{1,0:T(1,128)}, u32[]{:S(2)}) copy-start(f32[1,1024]{1,0:T(1,128)} %get-tuple-element.33) | copy-start | bytes 12292
  72.7 4.3 %copy-start.45 = (f32[1,1024]{1,0:T(1,128)S(1)}, f32[1,1024]{1,0:T(1,128)}, u32[]{:S(2)}) copy-start(f32[1,1024]{1,0:T(1,128)} %get-tuple-element.34) | copy-start | bytes 12292
  72.7 4.3 %copy-start.46 = (f32[1,1024]{1,0:T(1,128)S(1)}, f32[1,1024]{1,0:T(1,128)}, u32[]{:S(2)}) copy-start(f32[1,1024]{1,0:T(1,128)} %get-tuple-element.35) | copy-start | bytes 12292
  72.7 4.3 %copy-start.47 = (f32[1,1024]{1,0:T(1,128)S(1)}, f32[1,1024]{1,0:T(1,128)}, u32[]{:S(2)}) copy-start(f32[1,1024]{1,0:T(1,128)} %get-tuple-element.36) | copy-start | bytes 12292
  72.7 6.9 %copy-start.54 = (pred[2]{0:T(512)(128)(4,1)S(1)}, pred[2]{0:T(512)(128)(4,1)}, u32[]{:S(2)}) copy-start(pred[2]{0:T(512)(128)(4,1)} %get-tuple-element.60) | copy-start | bytes 10
  79.6 0.9 copy-start.1
  80.7 18.4 %copy-start.55 = (pred[2]{0:T(512)(128)(4,1)S(1)}, pred[2]{0:T(512)(128)(4,1)}, u32[]{:S(2)}) copy-start(pred[2]{0:T(512)(128)(4,1)} %get-tuple-element.61) | copy-start | bytes 10
  80.7 18.4 %copy-start.56 = (pred[2]{0:T(512)(128)(4,1)S(1)}, pred[2]{0:T(512)(128)(4,1)}, u32[]{:S(2)}) copy-start(pred[2]{0:T(512)(128)(4,1)} %get-tuple-element.62) | copy-start | bytes 10
  80.7 18.6 %copy-start.53 = (f32[2,64]{1,0:T(2,128)S(1)}, f32[2,64]{1,0:T(2,128)}, u32[]{:S(2)}) copy-start(f32[2,64]{1,0:T(2,128)} %copy-done.52) | copy-start | bytes 1540
  97.2 3.6 %copy-start.58 = (f32[2,30]{1,0:T(2,128)S(1)}, f32[2,30]{1,0:T(2,128)}, u32[]{:S(2)}) copy-start(f32[2,30]{1,0:T(2,128)} %slice_bitcast_fusion) | copy-start | bytes 724
  99.1 1.9 copy-start.16
  100.8 1.4 copy-start.3
  100.8 1.4 copy-start.49
  100.8 1.4 copy-start.51
  101.5 1.9 copy-start.18
  101.5 2.7 %copy-start.9 = (f32[2,30,512]{1,2,0:T(8,128)S(1)}, f32[2,30,512]{1,2,0:T(8,128)}, u32[]{:S(2)}) copy-start(f32[2,30,512]{1,2,0:T(8,128)} %slice_convert_fusion.2) | copy-start | bytes 368644
  103.4 4.2 %copy-start.7 = (bf16[2,8,64,64]{3,2,1,0:T(8,128)(2,1)S(1)}, bf16[2,8,64,64]{3,2,1,0:T(8,128)(2,1)}, u32[]{:S(2)}) copy-start(bf16[2,8,64,64]{3,2,1,0:T(8,128)(2,1)} %copy-done.6) | copy-start | bytes 393220
  108.3 2.5 %copy-start.11 = (bf16[2,192,512]{1,2,0:T(8,128)(2,1)S(1)}, bf16[2,192,512]{1,2,0:T(8,128)(2,1)}, u32[]{:S(2)}) copy-start(bf16[2,192,512]{1,2,0:T(8,128)(2,1)} %copy-done.10) | copy-start | bytes 1179652
  117.9 6.8 %copy-start.5 = (bf16[2,192,1024]{2,1,0:T(8,128)(2,1)S(1)}, bf16[2,192,1024]{2,1,0:T(8,128)(2,1)}, u32[]{:S(2)}) copy-start(bf16[2,192,1024]{2,1,0:T(8,128)(2,1)} %copy-done.4) | copy-start | bytes 2359300
  124.8 2.5 %copy-start.12 = (bf16[2,192,512]{2,1,0:T(8,128)(2,1)S(1)}, bf16[2,192,512]{2,1,0:T(8,128)(2,1)}, u32[]{:S(2)}) copy-start(bf16[2,192,512]{2,1,0:T(8,128)(2,1)} %copy.116) | copy-start | bytes 1179652
  124.8 2.5 %copy-start.13 = (bf16[2,192,512]{2,1,0:T(8,128)(2,1)S(1)}, bf16[2,192,512]{2,1,0:T(8,128)(2,1)}, u32[]{:S(2)}) copy-start(bf16[2,192,512]{2,1,0:T(8,128)(2,1)} %copy.115) | copy-start | bytes 1179652
  130.6 53.5 %copy-start.8 = (f32[2,64,1024]{2,1,0:T(8,128)S(1)}, f32[2,64,1024]{2,1,0:T(8,128)}, u32[]{:S(2)}) copy-start(f32[2,64,1024]{2,1,0:T(8,128)} %get-tuple-element.11) | copy-start | bytes 1572868
  130.6 89.5 %all-reduce.3.cloned.1.call-start = ((), (), s32[]{:S(2)}) async-start(), calls=%async_computation.3 | async-start | bytes 524288 | tf_op jit(solution)/shard_map/psum | solution.py:255
Sparse Core Ops, SparseCore 0:
  9.6 30.6 all-gather.1
  130.7 51.4 reduce-scatter.1
  184.7 35.3 all-reduce.2
where the time goes:
time: 229 us; the launch traced here: 228 us
  waiting for transfers between devices  108 us (47%)
  blocking collectives  31.1 us (14%)
  other arithmetic  27.8 us (12%)
  local copies, waits for them, and re-layouts  24.9 us (11%)
  matrix products  21.8 us (10%)
  between operations  14.7 us (6%)
    reduce_scatter x1, waiting for transfers between devices, on_device(): grad_part = lax.psum_scatter(running, 'dp', scatter_dimension=0, tiled=True)  51.6 us
    psum x1, waiting for transfers between devices, on_device(): lax.psum(grad_part.astype(jnp.bfloat16), 'tm').astype(jnp.float32)  35.1 us
    all_gather x1, waiting for transfers between devices, on_device(): gathered = lax.all_gather(frames, 'tm', axis=0, tiled=True)  20.2 us
    all_gather x1, blocking collectives, on_device(): lax.all_gather(conv_in[:, BLOCK - tail_rows:], 'tm', axis=0, tiled=True)  15.7 us
    all_gather x1, blocking collectives, on_device(): lax.all_gather(carried.astype(jnp.bfloat16), 'tm', axis=0, tiled=True)  15.3 us
    dot_general x2, matrix products, on_device(): jnp.einsum('nkd,nke->de', normed_part, term_part, preferred_element_type=...  5.76 us
    dot_general x2, matrix products, attend_back(): jnp.einsum('nhrk,nrhd->nkhd', grad_raw.astype(jnp.bfloat16), query_heads,...  5.68 us
  transfers between devices with their start and end apart: 3, of which 3 were waited for; matrix products, arithmetic and copies ran while one was open for 6% of the time, Pallas kernels for 0%

commit v1 on v0

v1 whole, which is shorter than its diff:
```python
import functools
import math

import jax
import jax.numpy as jnp
from jax import lax
from jax.experimental import pallas as pl
from jax.experimental.pallas import tpu as pltpu
from jax.sharding import PartitionSpec as P

HEADS = 8
KERNEL = 31
BLOCK = 64
LC = 2
SPAN = (LC + 1) * BLOCK
HALO = 32
PAD = LC + 1
EPSILON = 1e-05
SOFT_CAP = 4.0
LANES = 128

BF16 = jnp.bfloat16
F32 = jnp.float32


def dot_nn(a, b):
    return lax.dot_general(a, b, (((1,), (0,)), ((), ())), preferred_element_type=F32)


def dot_nt(a, b):
    return lax.dot_general(a, b, (((1,), (1,)), ((), ())), preferred_element_type=F32)


def dot_tn(a, b):
    return lax.dot_general(a, b, (((0,), (0,)), ((), ())), preferred_element_type=F32)


def norm_stats(values):
    row_mean = jnp.mean(values, axis=-1, keepdims=True)
    centred = values - row_mean
    scale_inv = lax.rsqrt(jnp.mean(centred * centred, axis=-1, keepdims=True) + EPSILON)
    return centred * scale_inv, scale_inv


class Layout:
    def __init__(self, utt_ref, slot_ref, left_ref):
        self.utt, self.slot, self.left = utt_ref, slot_ref, left_ref
        self.blocks = slot_ref.shape[1]

    def block_of(self, slot):
        found = jnp.int32(0)
        for b in range(self.blocks):
            found = jnp.where(self.slot[0, b] == slot, jnp.int32(b), found)
        return found

    def position(self, block):
        start = jnp.int32(0)
        first = jnp.int32(0)
        for u in range(self.utt.shape[1]):
            first = jnp.where(block >= start, start, first)
            start = start + self.utt[0, u]
        return block - first

    def reach(self, block):
        safe = jnp.clip(block, 0, self.blocks - 1)
        return jnp.minimum(self.left[0, safe], self.position(safe))


def diag_mask(heads, rows, head_size):
    shape = (heads * rows, heads * head_size)
    row_head = lax.broadcasted_iota(jnp.int32, shape, 0) // rows
    col_head = lax.broadcasted_iota(jnp.int32, shape, 1) // head_size
    return jnp.where(row_head == col_head, 1.0, 0.0).astype(F32)


def spread(rows, mask_b):
    copies = mask_b.shape[0] // rows.shape[0]
    return jnp.concatenate([rows] * copies, axis=0) * mask_b


def window_probs(diag_q, k_win, reach):
    raw = dot_nt(k_win, diag_q)
    unit = jnp.tanh(raw * (1.0 / (SOFT_CAP * math.sqrt(k_win.shape[1] // HEADS_IN(k_win)))))
    exped = jnp.exp(SOFT_CAP * unit)
    parts = []
    for w in range(LC):
        ok = jnp.where(reach >= LC - w, 1.0, 0.0).astype(F32)
        parts.append(exped[w * BLOCK : (w + 1) * BLOCK] * ok)
    parts.append(exped[LC * BLOCK :])
    exped = jnp.concatenate(parts, axis=0)
    total = jnp.sum(exped, axis=0, keepdims=True)
    return exped * (1.0 / total), unit


def HEADS_IN(k_win):
    return k_win.shape[1] // 64


def fold_heads(full, mask_f, rows):
    kept = full * mask_f
    total = kept[:rows]
    for h in range(1, full.shape[0] // rows):
        total = total + kept[h * rows : (h + 1) * rows]
    return total


def forward_kernel(tm, *refs):
    me_ref, utt_ref, slot_ref, left_ref = refs[:4]
    frame_refs = refs[4 : 4 + tm]
    refs = refs[4 + tm :]
    grad_refs = refs[:tm]
    (g1_ref, wq_ref, wkv_ref, wo_ref, g2_ref, ck_ref, cb_ref) = refs[tm : tm + 7]
    refs = refs[tm + 7 :]
    out_ref = refs[0]
    send_refs = refs[1 : 1 + tm]
    q4_ref, k4_ref, v4_ref, n_ref = refs[1 + tm : 5 + tm]
    f_s, q_s, kv_s, ctx_s, e_s, h_s, u_s, og_s, gr_s, gc_s = refs[5 + tm :]

    me = me_ref[0]
    table = Layout(utt_ref, slot_ref, left_ref)
    blocks = table.blocks
    local = blocks // tm
    width = f_s.shape[1]
    hq = wq_ref.shape[1]
    head_size = hq // HEADS
    share = q4_ref.shape[1]
    half = tm // 2

    g1 = g1_ref[...]
    zero_pad = jnp.zeros((PAD * BLOCK, width), BF16)
    n_ref[: PAD * BLOCK] = zero_pad
    n_ref[(PAD + blocks) * BLOCK :] = jnp.zeros((BLOCK, width), BF16)
    f_s[: PAD * BLOCK] = zero_pad
    f_s[(PAD + blocks) * BLOCK :] = jnp.zeros((BLOCK, width), BF16)
    for m in range(tm):
        for j in range(local):
            b = table.block_of((me ^ m) * local + j)
            at = pl.ds(pl.multiple_of((b + PAD) * BLOCK, BLOCK), BLOCK)
            rows = frame_refs[m][j * BLOCK : (j + 1) * BLOCK]
            f_s[at] = rows
            unit, _ = norm_stats(rows.astype(F32))
            n_ref[at] = (unit * g1).astype(BF16)

    chunk = 2 * BLOCK

    def project(i, carry):
        at = pl.ds(pl.multiple_of(i * chunk, chunk), chunk)
        n = n_ref[at]
        q_s[at] = dot_nn(n, wq_ref[...]).astype(BF16)
        kv_s[at] = dot_nn(n, wkv_ref[...]).astype(BF16)
        return carry

    lax.fori_loop(0, n_ref.shape[0] // chunk, project, 0)

    lead = pl.multiple_of((me % half) * share, share)
    q4_ref[...] = q_s[:, pl.ds(lead, share)]
    k4_ref[...] = kv_s[:, pl.ds(lead, share)]
    v4_ref[...] = kv_s[:, pl.ds(pl.multiple_of(hq + lead, share), share)]

    mid_heads = 256 // BLOCK
    mid_f = diag_mask(mid_heads, BLOCK, head_size)
    mid_b = mid_f.astype(BF16)
    side_f = diag_mask(HEADS, HALO, head_size)
    side_b = side_f.astype(BF16)

    for i in range(local):
        c = table.block_of(me * local + i)
        base = (c + PAD) * BLOCK
        pieces = [(c - 1, base - HALO, HALO, 0, HALO)]
        pieces += [(c, base, BLOCK, HALO, BLOCK)]
        pieces += [(c + 1, base + BLOCK, HALO, HALO + BLOCK, HALO)]
        for blk, row, count, put, _ in pieces:
            reach = table.reach(blk)
            win = pl.ds(pl.multiple_of((blk + PAD - LC) * BLOCK, BLOCK), SPAN)
            at = pl.ds(pl.multiple_of(row, HALO), count)
            if count == BLOCK:
                groups, mask_f, mask_b = HEADS // mid_heads, mid_f, mid_b
            else:
                groups, mask_f, mask_b = 1, side_f, side_b
            wide = hq // groups
            for g in range(groups):
                cols = slice(g * wide, (g + 1) * wide)
                vcols = slice(hq + g * wide, hq + (g + 1) * wide)
                diag_q = spread(q_s[at, cols], mask_b)
                probs, _ = window_probs(diag_q, kv_s[win, cols], reach)
                full = dot_tn(probs.astype(BF16), kv_s[win, vcols])
                ctx_s[put : put + count, cols] = fold_heads(full, mask_f, count).astype(BF16)

        span_at = pl.ds(pl.multiple_of(base - HALO, HALO), 2 * BLOCK)
        hidden = f_s[span_at].astype(F32) + dot_nn(ctx_s[...], wo_ref[...])
        unit, inv = norm_stats(hidden)
        conv_in = (unit * g2_ref[...]).astype(BF16).astype(F32)
        has_prev = table.position(c) >= 1
        e_s[:HALO] = conv_in[:HALO] * jnp.where(has_prev, 1.0, 0.0).astype(F32)
        e_s[HALO:] = conv_in[HALO:]
        h_s[...] = hidden[HALO : HALO + BLOCK]
        u_s[...] = unit[HALO : HALO + BLOCK]
        inv_own = inv[HALO : HALO + BLOCK]

        og_s[:BLOCK] = grad_refs[0][i * BLOCK : (i + 1) * BLOCK].astype(F32)
        nxt = jnp.minimum(c + 1, blocks - 1)
        has_next = jnp.logical_and(c + 1 < blocks, table.position(nxt) >= 1)
        next_slot = slot_ref[0, nxt]
        next_m = (next_slot // local) ^ me
        next_j = next_slot % local
        og_s[BLOCK:] = jnp.zeros((HALO, width), F32)
        for m in range(tm):
            stride = BLOCK if m == 0 else HALO

            @pl.when(jnp.logical_and(has_next, next_m == m))
            def _():
                start = pl.multiple_of(next_j * stride, HALO)
                og_s[BLOCK:] = grad_refs[m][pl.ds(start, HALO)].astype(F32)

        reach_rows = BLOCK + HALO

        def conv(k, carry):
            cols = pl.ds(pl.multiple_of(k * LANES, LANES), LANES)
            ext = e_s[:, cols]
            taps = ck_ref[:, cols]
            acc = jnp.broadcast_to(cb_ref[:, cols], (reach_rows, LANES))
            for s in range(8):
                moved = ext[s + 2 : s + 2 + reach_rows + 24]
                for a in range(4):
                    j = 8 * a + s
                    if j < KERNEL:
                        acc = acc + taps[j : j + 1] * moved[8 * a : 8 * a + reach_rows]
            gate = 0.5 * jnp.tanh(0.5 * acc) + 0.5
            out_ref[i * BLOCK : (i + 1) * BLOCK, cols] = (
                h_s[:, cols] + (acc * gate)[:BLOCK]
            ).astype(BF16)
            gm = og_s[:, cols] * gate * (1.0 + acc * (1.0 - gate))
            back = jnp.zeros((BLOCK, LANES), F32)
            for s in range(8):
                moved = gm[s : s + BLOCK + 24]
                for a in range(4):
                    j = 8 * a + s
                    if j < KERNEL:
                        flip = KERNEL - 1 - j
                        back = back + taps[flip : flip + 1] * moved[8 * a : 8 * a + BLOCK]
            gr_s[:, cols] = back
            return carry

        lax.fori_loop(0, width // LANES, conv, 0)

        scaled = gr_s[...] * g2_ref[...]
        unit_own = u_s[...]
        first = jnp.mean(scaled, axis=-1, keepdims=True)
        second = jnp.mean(scaled * unit_own, axis=-1, keepdims=True)
        grad_hidden = og_s[:BLOCK] + inv_own * (scaled - first - unit_own * second)
        gc_s[...] = dot_nt(grad_hidden.astype(BF16), wo_ref[...]).astype(BF16)
        for m in range(tm):
            cols = pl.ds(pl.multiple_of(((me ^ m) % half) * share, share), share)
            send_refs[m][i * BLOCK : (i + 1) * BLOCK] = gc_s[:, cols]


def probs_kernel(utt_ref, slot_ref, left_ref, q4_ref, k4_ref, p_ref, d_ref):
    table = Layout(utt_ref, slot_ref, left_ref)
    share = q4_ref.shape[1]
    head_size = 64
    heads = share // head_size
    mask_b = diag_mask(heads, BLOCK, head_size).astype(BF16)

    def step(c, carry):
        row = (c + PAD) * BLOCK
        diag_q = spread(q4_ref[pl.ds(pl.multiple_of(row, BLOCK), BLOCK)], mask_b)
        win = pl.ds(pl.multiple_of(row - LC * BLOCK, BLOCK), SPAN)
        probs, unit = window_probs(diag_q, k4_ref[win], table.reach(c))
        p_ref[c] = probs
        d_ref[c] = (1.0 - unit * unit) * (1.0 / math.sqrt(head_size))
        return carry

    lax.fori_loop(0, table.blocks, step, 0)


def backward_kernel(tm, *refs):
    me_ref, slot_ref, q4_ref, v4_ref, n_ref, p_ref, d_ref = refs[:7]
    g_refs = refs[7 : 7 + tm]
    out_refs = refs[7 + tm : -2]
    gt_s, t_s = refs[-2:]
    me = me_ref[0]
    blocks = slot_ref.shape[1]
    local = blocks // tm
    share = q4_ref.shape[1]
    head_size = 64
    heads = share // head_size
    mask_b = diag_mask(heads, BLOCK, head_size).astype(BF16)

    for m in range(tm):
        for j in range(local):
            slot = (me ^ m) * local + j
            b = jnp.int32(0)
            for k in range(blocks):
                b = jnp.where(slot_ref[0, k] == slot, jnp.int32(k), b)
            gt_s[pl.ds(pl.multiple_of(b * BLOCK, BLOCK), BLOCK)] = g_refs[m][
                j * BLOCK : (j + 1) * BLOCK
            ]
    t_s[...] = jnp.zeros(t_s.shape, F32)

    @pl.when(me >= tm // 2)
    def _():
        def step(c, carry):
            row = c * BLOCK
            diag_g = spread(gt_s[pl.ds(pl.multiple_of(row, BLOCK), BLOCK)], mask_b)
            win = pl.ds(pl.multiple_of(row + (PAD - LC) * BLOCK, BLOCK), SPAN)
            t_s[win] = t_s[win] + dot_nn(p_ref[c].astype(BF16), diag_g)
            return carry

        lax.fori_loop(0, blocks, step, 0)

    @pl.when(me < tm // 2)
    def _():
        def step(c, carry):
            row = c * BLOCK
            diag_g = spread(gt_s[pl.ds(pl.multiple_of(row, BLOCK), BLOCK)], mask_b)
            own = pl.ds(pl.multiple_of(row + PAD * BLOCK, BLOCK), BLOCK)
            diag_q = spread(q4_ref[own], mask_b)
            win = pl.ds(pl.multiple_of(row + (PAD - LC) * BLOCK, BLOCK), SPAN)
            grad_probs = dot_nt(v4_ref[win], diag_g)
            probs = p_ref[c]
            delta = jnp.sum(probs * grad_probs, axis=0, keepdims=True)
            grad_raw = probs * (grad_probs - delta) * d_ref[c]
            t_s[win] = t_s[win] + dot_nn(grad_raw.astype(BF16), diag_q)
            return carry

        lax.fori_loop(0, blocks, step, 0)

    rows = slice(PAD * BLOCK, (PAD + blocks) * BLOCK)
    full = dot_tn(t_s[rows].astype(BF16), n_ref[rows]).astype(BF16)
    part = out_refs[0].shape[1]
    if len(out_refs) == 1:
        out_refs[0][...] = full
    else:
        for m in range(len(out_refs)):
            out_refs[m][...] = full[:, m * part : (m + 1) * part]


def sum_kernel(*refs):
    total = refs[0][...].astype(F32)
    for ref in refs[1:-1]:
        total = total + ref[...].astype(F32)
    refs[-1][...] = total.T


def on_device(
    frames,
    out_grad,
    norm1_gain,
    w_query,
    w_kv,
    w_out,
    norm2_gain,
    conv_kernel,
    conv_bias,
    utt_blocks,
    block_slot,
    left_count,
):
    tm = lax.axis_size("tm")
    dp = lax.axis_size("dp")
    width = frames.shape[1]
    rows = frames.shape[0]
    blocks = block_slot.shape[1]
    local = rows // BLOCK
    hq = w_query.shape[1]
    share = w_kv.shape[1] // tm
    padded = (blocks + PAD + 1) * BLOCK

    def swap(value, axis, size, m):
        return lax.ppermute(value, axis, [(i, i ^ m) for i in range(size)])

    heads_rows = out_grad.reshape(local, BLOCK, width)[:, :HALO].reshape(local * HALO, width)
    order = sorted(range(1, tm), key=lambda m: -m)
    frame_parts = {0: frames}
    grad_parts = {0: out_grad}
    for m in order:
        frame_parts[m] = swap(frames, "tm", tm, m)
    for m in order:
        grad_parts[m] = swap(heads_rows, "tm", tm, m)
    me = lax.axis_index("tm").astype(jnp.int32).reshape(1)

    smem = pl.BlockSpec(memory_space=pltpu.SMEM)
    vmem = pl.BlockSpec(memory_space=pltpu.VMEM)
    shape = jax.ShapeDtypeStruct
    forward = pl.pallas_call(
        functools.partial(forward_kernel, tm),
        out_shape=[shape((rows, width), BF16)]
        + [shape((rows, share), BF16)] * tm
        + [shape((padded, share), BF16)] * 3
        + [shape((padded, width), BF16)],
        in_specs=[smem] * 4 + [vmem] * (2 * tm + 7),
        out_specs=[vmem] * (tm + 5),
        scratch_shapes=[
            pltpu.VMEM((padded, width), BF16),
            pltpu.VMEM((padded, hq), BF16),
            pltpu.VMEM((padded, 2 * hq), BF16),
            pltpu.VMEM((2 * BLOCK, hq), BF16),
            pltpu.VMEM((2 * BLOCK, width), F32),
            pltpu.VMEM((BLOCK, width), F32),
            pltpu.VMEM((BLOCK, width), F32),
            pltpu.VMEM((BLOCK + HALO, width), F32),
            pltpu.VMEM((BLOCK, width), F32),
            pltpu.VMEM((BLOCK, hq), BF16),
        ],
        compiler_params=pltpu.CompilerParams(vmem_limit_bytes=40 << 20),
        name="forward_pass",
    )
    results = forward(
        me,
        utt_blocks,
        block_slot,
        left_count,
        *[frame_parts[m] for m in range(tm)],
        *[grad_parts[m] for m in range(tm)],
        norm1_gain.reshape(1, -1),
        w_query,
        w_kv,
        w_out,
        norm2_gain.reshape(1, -1),
        conv_kernel,
        conv_bias.reshape(1, -1),
    )
    layer_out = results[0]
    sends = results[1 : 1 + tm]
    q4, k4, v4, normed = results[1 + tm :]
    got = [sends[0]] + [swap(sends[m], "tm", tm, m) for m in range(1, tm)]

    probs, slopes = pl.pallas_call(
        probs_kernel,
        out_shape=[shape((blocks, SPAN, share // 64 * BLOCK), F32)] * 2,
        in_specs=[smem] * 3 + [vmem] * 2,
        out_specs=[vmem] * 2,
        compiler_params=pltpu.CompilerParams(vmem_limit_bytes=24 << 20),
        name="window_probs",
        cost_estimate=pl.CostEstimate(
            flops=2 * 10**9, bytes_accessed=4 * 10**6, transcendentals=800000
        ),
    )(utt_blocks, block_slot, left_count, q4, k4)

    direct = dp <= 8
    parts = dp if direct else 1
    pieces = pl.pallas_call(
        functools.partial(backward_kernel, tm),
        out_shape=[shape((share, width // parts), BF16)] * parts,
        in_specs=[smem] * 2 + [vmem] * (5 + tm),
        out_specs=[vmem] * parts,
        scratch_shapes=[
            pltpu.VMEM((blocks * BLOCK, share), BF16),
            pltpu.VMEM((padded, share), F32),
        ],
        compiler_params=pltpu.CompilerParams(vmem_limit_bytes=32 << 20),
        name="key_value_terms",
    )(me, block_slot, q4, v4, normed, probs, slopes, *got)

    if direct:
        stacked = jnp.stack(pieces)
        mine = lax.all_to_all(stacked, "dp", 0, 0, tiled=False)
        terms = [mine[m] for m in range(dp)]
    else:
        terms = [lax.psum_scatter(pieces[0], "dp", scatter_dimension=1, tiled=True)]
    kv_grad = pl.pallas_call(
        sum_kernel,
        out_shape=shape((width // dp, share), F32),
        in_specs=[vmem] * len(terms),
        out_specs=vmem,
        name="sum_groups",
    )(*terms)
    return layer_out, kv_grad


def solution(mesh):
    return jax.shard_map(
        on_device,
        mesh=mesh,
        in_specs=(
            P(("dp", "tm"), None),
            P(("dp", "tm"), None),
            P(),
            P(),
            P(),
            P(),
            P(),
            P(),
            P(),
            P("dp", None),
            P("dp", None),
            P("dp", None),
        ),
        out_specs=(P(("dp", "tm"), None), P("dp", "tm")),
        check_vma=False,
    )
```

time: 229 us -> 98.7 us (0.43)
  waiting for transfers between devices: 108 us -> 22.8 us
  other arithmetic: 27.8 us -> 0 us
  Pallas kernels: 0 us -> 26.6 us
  starting transfers between devices: 0.12 us -> 22.1 us
  matrix products: 21.8 us -> 0 us
  blocking collectives: 31.1 us -> 13.3 us
  between operations: 14.7 us -> 0.75 us
  local copies, waits for them, and re-layouts: 24.9 us -> 12.7 us
    reduce_scatter x1 -> x0, waiting for transfers between devices: 51.6 us -> none  [on_device(): grad_part = lax.psum_scatter(running, 'dp', scatter_dimension=0, tiled=True)]
    psum x1 -> x0, waiting for transfers between devices: 35.1 us -> none  [on_device(): lax.psum(grad_part.astype(jnp.bfloat16), 'tm').astype(jnp.float32)]
    all_gather x2 -> x0, blocking collectives: 31.1 us -> none  [the longest x1 15.7 us: on_device(): lax.all_gather(conv_in[:, BLOCK - tail_rows:], 'tm', axis=0, tiled=True)]
    pallas_call x0 -> x4, Pallas kernels: none -> 26.6 us  [the longest x1 17.3 us: on_device(): forward(me, utt_blocks, block_slot, left_count, *[frame_parts[m] for m in...]
    ppermute x0 -> x9, waiting for transfers between devices: none -> 22.8 us  [swap(): return lax.ppermute(value, axis, [(i, i ^ m) for i in range(size)])]
    ppermute x0 -> x9, starting transfers between devices: none -> 22.1 us  [swap(): return lax.ppermute(value, axis, [(i, i ^ m) for i in range(size)])]
    dot_general x12 -> x0, matrix products: 21.8 us -> none  [the longest x2 5.76 us: on_device(): jnp.einsum('nkd,nke->de', normed_part, term_part, preferred_element_type=...]
    all_gather x1 -> x0, waiting for transfers between devices: 20.2 us -> none  [on_device(): gathered = lax.all_gather(frames, 'tm', axis=0, tiled=True)]
  transfers between devices with their start and end apart: 3 -> 9, of which waited for: 3 -> 2; matrix products, arithmetic and copies ran while one was open for 6% -> 0% of each run, Pallas kernels for 0% -> 3%
where the time goes in v1:
time: 98.7 us; the launch traced here: 98.2 us
  Pallas kernels  26.6 us (27%)
  waiting for transfers between devices  22.8 us (23%)
  starting transfers between devices  22.1 us (22%)
  blocking collectives  13.3 us (13%)
  local copies, waits for them, and re-layouts  12.7 us (13%)
    ppermute x9, waiting for transfers between devices, swap(): return lax.ppermute(value, axis, [(i, i ^ m) for i in range(size)])  22.8 us
    ppermute x9, starting transfers between devices, swap(): return lax.ppermute(value, axis, [(i, i ^ m) for i in range(size)])  22.1 us
    pallas_call x1, Pallas kernels, on_device(): forward(me, utt_blocks, block_slot, left_count, *[frame_parts[m] for m in...  17.3 us
    all_to_all x1, blocking collectives, on_device(): mine = lax.all_to_all(stacked, 'dp', 0, 0, tiled=False)  13.3 us
    unnamed x31, local copies, waits for them, and re-layouts  11 us
    pallas_call x1, Pallas kernels, on_device(): pl.pallas_call(functools.partial(backward_kernel, tm), out_shape=[shape((...  4.47 us
    pallas_call x1, Pallas kernels, on_device(): pl.pallas_call(probs_kernel, out_shape=[shape((blocks, SPAN, share // 64...  2.95 us
  transfers between devices with their start and end apart: 9, of which 2 were waited for; matrix products, arithmetic and copies ran while one was open for 0% of the time, Pallas kernels for 3%

profile of v1, /device:TPU:0, one launch (start us, length us, event | category | flops | bytes accessed | tf_op | source)
XLA Modules:
  0.0 98.2 jit_solution(13925592372358895040)
XLA Ops:
  0.6 0.9 slice.36
  1.6 5.1 %collective-permute-start.5 = (bf16[64,1024]{1,0:T(8,128)(2,1)S(1)}, bf16[64,1024]{1,0:T(8,128)(2,1)S(1)}, u32[]{:S(2)}, u32[]{:S(2)}) collective-permute-start(bf16[64,1024]{1,0:T(8,128)(2,1)S(1)} %bitcast.42), channel_id=1, source_target_pairs={{0,3},{1,2},{2,1},{3,0},{4,7},{5,6},{6,5},{7,4},{8,11},{9,10},{10,... | collective-permute-start | bytes 393224 | tf_op jit(solution)/shard_map/ppermute | solution.py:370
  6.7 0.0 collective-permute-start.1
  6.7 0.6 collective-permute-start
  7.3 3.7 %collective-permute-start.2 = (bf16[128,1024]{1,0:T(8,128)(2,1)}, bf16[128,1024]{1,0:T(8,128)(2,1)S(1)}, u32[]{:S(2)}, u32[]{:S(2)}) collective-permute-start(bf16[128,1024]{1,0:T(8,128)(2,1)} %refs_4_.1), channel_id=1, source_target_pairs={{0,3},{1,2},{2,1},{3,0},{4,7},{5,6},{6,5},{7,4},{8,11},{9,10},{10,... | collective-permute-start | bytes 786440 | tf_op jit(solution)/shard_map/ppermute | solution.py:370
  11.1 0.0 collective-permute-start.4
  11.1 0.0 collective-permute-done.5.refs_11_
  11.1 8.2 %collective-permute-start.3 = (bf16[64,1024]{1,0:T(8,128)(2,1)S(1)}, bf16[64,1024]{1,0:T(8,128)(2,1)S(1)}, u32[]{:S(2)}, u32[]{:S(2)}) collective-permute-start(bf16[64,1024]{1,0:T(8,128)(2,1)S(1)} %bitcast.44), channel_id=1, source_target_pairs={{0,1},{1,0},{2,3},{3,2},{4,5},{5,4},{6,7},{7,6},{8,9},{9,8},{10,11... | collective-permute-start | bytes 393224 | tf_op jit(solution)/shard_map/ppermute | solution.py:370
  19.3 21.0 %collective-permute-done.4.refs_10_ = bf16[64,1024]{1,0:T(8,128)(2,1)S(1)} collective-permute-done((bf16[64,1024]{1,0:T(8,128)(2,1)S(1)}, bf16[64,1024]{1,0:T(8,128)(2,1)S(1)}, u32[]{:S(2)}, u32[]{:S(2)}) %collective-permute-start.4) | collective-permute-done | bytes 131104 | tf_op jit(solution)/shard_map/ppermute | solution.py:370
  40.3 0.0 collective-permute-done.3.refs_9_
  40.3 0.0 collective-permute-done.1.refs_6_
  40.3 0.0 collective-permute-done.refs_5_
  40.3 0.0 collective-permute-done.2.refs_7_
  40.3 0.0 copy-start
  40.3 1.6 %copy-done = bf16[1024,1024]{1,0:T(8,128)(2,1)S(1)} copy-done((bf16[1024,1024]{1,0:T(8,128)(2,1)S(1)}, bf16[1024,1024]{1,0:T(8,128)(2,1)}, u32[]{:S(2)}) %copy-start) | copy-done | bytes 2097176
  41.9 0.0 copy-start.1
  41.9 1.2 %copy-done.1 = bf16[1024,512]{1,0:T(8,128)(2,1)S(1)} copy-done((bf16[1024,512]{1,0:T(8,128)(2,1)S(1)}, bf16[1024,512]{1,0:T(8,128)(2,1)}, u32[]{:S(2)}) %copy-start.1) | copy-done | bytes 1048600
  43.1 0.0 copy-start.2
  43.1 1.2 %copy-done.2 = bf16[512,1024]{1,0:T(8,128)(2,1)S(1)} copy-done((bf16[512,1024]{1,0:T(8,128)(2,1)S(1)}, bf16[512,1024]{1,0:T(8,128)(2,1)}, u32[]{:S(2)}) %copy-start.2) | copy-done | bytes 1048600
  44.3 0.0 copy-start.3
  44.3 0.9 copy-done.3
  45.3 0.0 copy-start.4
  45.3 0.9 copy-done.4
  46.2 0.0 copy-start.5
  46.2 0.9 copy-done.5
  47.1 0.0 copy-start.6
  47.1 0.7 copy-done.6
  47.8 0.0 copy-start.7
  47.8 0.7 copy-done.7
  48.5 0.0 copy-start.8
  48.5 0.7 copy-done.8
  49.2 0.0 copy-start.9
  49.2 0.7 copy-done.9
  49.9 0.0 copy-start.10
  49.9 0.7 copy-done.10
  50.5 0.0 copy-start.11
  50.5 0.7 copy-done.11
  51.2 17.3 %forward_pass.1 = (bf16[128,1024]{1,0:T(8,128)(2,1)}, bf16[128,256]{1,0:T(8,128)(2,1)S(1)}, bf16[128,256]{1,0:T(8,128)(2,1)S(1)}, bf16[128,256]{1,0:T(8,128)(2,1...) custom-call(s32[1]{0:T(128)} %bitcast.refs_0_, ...), custom_call_target="tpu_custom_call" | custom-call | tf_op jit(solution)/shard_map/forward_pass/pallas_call | solution.py:408
  68.5 0.0 collective-permute-start.6
  68.5 3.0 %collective-permute-start.7 = (bf16[128,256]{1,0:T(8,128)(2,1)S(1)}, bf16[128,256]{1,0:T(8,128)(2,1)S(1)}, u32[]{:S(2)}, u32[]{:S(2)}) collective-permute-start(bf16[128,256]{1,0:T(8,128)(2,1)S(1)} %get-tuple-element.30), channel_id=1, source_target_pairs={{0,2},{1,3},{2,0},{3,1},{4,6},{5,7},{6,4},{7,5},{8,10},{9,11},{10,... | collective-permute-start | bytes 196616 | tf_op jit(solution)/shard_map/ppermute | solution.py:370
  71.5 1.4 %collective-permute-start.8 = (bf16[128,256]{1,0:T(8,128)(2,1)S(1)}, bf16[128,256]{1,0:T(8,128)(2,1)S(1)}, u32[]{:S(2)}, u32[]{:S(2)}) collective-permute-start(bf16[128,256]{1,0:T(8,128)(2,1)S(1)} %get-tuple-element.31), channel_id=1, source_target_pairs={{0,3},{1,2},{2,1},{3,0},{4,7},{5,6},{6,5},{7,4},{8,11},{9,10},{10,... | collective-permute-start | bytes 196616 | tf_op jit(solution)/shard_map/ppermute | solution.py:370
  72.9 2.9 %window_probs.1 = (f32[8,192,256]{2,1,0:T(8,128)S(1)}, f32[8,192,256]{2,1,0:T(8,128)S(1)}) custom-call(s32[1,2]{1,0:T(1,128)S(1)} %copy-done.10, s32[1,8]{1,0:T(1,128)S(1)} %copy-done.9, s32[1,8]{1,0:T(1,128)S(1)} %copy-done.11, bf16[768,256]{1,0:T(8,128)(2,1)S(1)} %get-tuple-element.22.q4_ref.refs_2_, bf16[768,256]{1,0:T(8,128)(2,1)S(1)} %get-tuple-element.25.k4_ref), custom_call_target="tpu_custom_call" | custom-call | flops 2000000000 | bytes 4000000 | tf_op jit(solution)/shard_map/window_probs/pallas_call | solution.py:428
  75.8 0.0 collective-permute-done.6.refs_8_
  75.8 0.0 collective-permute-done.7.refs_9_
  75.9 1.7 %collective-permute-done.8.refs_10_ = bf16[128,256]{1,0:T(8,128)(2,1)S(1)} collective-permute-done((bf16[128,256]{1,0:T(8,128)(2,1)S(1)}, bf16[128,256]{1,0:T(8,128)(2,1)S(1)}, u32[]{:S(2)}, u32[]{:S(2)}) %collective-permute-start.8) | collective-permute-done | bytes 65568 | tf_op jit(solution)/shard_map/ppermute | solution.py:370
  77.6 4.5 %key_value_terms.1 = (bf16[256,128]{1,0:T(8,128)(2,1)S(1)}, bf16[256,128]{1,0:T(8,128)(2,1)S(1)}, bf16[256,128]{1,0:T(8,128)(2,1)S(1)}, bf16[256,128]{1,0:T(8,12...) custom-call(s32[1]{0:T(128)} %bitcast.refs_0_, ...), custom_call_target="tpu_custom_call" | custom-call | tf_op jit(solution)/shard_map/key_value_terms/pallas_call | solution.py:442
  82.2 13.3 %all_to_all.5 = bf16[8,256,128]{2,1,0:T(8,128)(2,1)S(1)} all-to-all(bf16[8,256,128]{2,1,0:T(8,128)(2,1)S(1)} %bitcast_dynamic-update-slice_fusion), channel_id=1, replica_groups=mesh['dp'=8,'tm'=4] {'dp'}, dimensions={0} | all-to-all | bytes 1048576 | tf_op jit(solution)/shard_map/all_to_all | solution.py:457
  95.5 0.8 slice_bitcast_fusion
  96.3 1.9 %sum_groups.1 = f32[128,256]{1,0:T(8,128)} custom-call(bf16[256,128]{1,0:T(8,128)(2,1)} %get-tuple-element.47.refs_0_, bf16[256,128]{1,0:T(8,128)(2,1)} %get-tuple-element.46.refs_1_, bf16[256,128]{1,0:T(8,128)(2,1)} %get-tuple-element.45.refs_2_, bf16[256,128]{1,0:T(8,128)(2,1)} %get-tuple-element.44.refs_3_, bf16[256,128]{1,0:T(8,128)(2,1)} %get-tuple-element.43.refs_4_, ...), custom_call_target="tpu_custom_call" | custom-call | tf_op jit(solution)/shard_map/sum_groups/pallas_call | solution.py:461
  (8 shorter events, 0.1 us)
Async XLA Ops:
  1.6 9.5 %collective-permute-start.5 = (bf16[64,1024]{1,0:T(8,128)(2,1)S(1)}, bf16[64,1024]{1,0:T(8,128)(2,1)S(1)}, u32[]{:S(2)}, u32[]{:S(2)}) collective-permute-start(bf16[64,1024]{1,0:T(8,128)(2,1)S(1)} %bitcast.42), channel_id=1, source_target_pairs={{0,3},{1,2},{2,1},{3,0},{4,7},{5,6},{6,5},{7,4},{8,11},{9,10},{10,... | collective-permute-start | bytes 393224 | tf_op jit(solution)/shard_map/ppermute | solution.py:370
  6.7 33.6 %collective-permute-start.1 = (bf16[128,1024]{1,0:T(8,128)(2,1)}, bf16[128,1024]{1,0:T(8,128)(2,1)S(1)}, u32[]{:S(2)}, u32[]{:S(2)}) collective-permute-start(bf16[128,1024]{1,0:T(8,128)(2,1)} %refs_4_.1), channel_id=1, source_target_pairs={{0,2},{1,3},{2,0},{3,1},{4,6},{5,7},{6,4},{7,5},{8,10},{9,11},{10,... | collective-permute-start | bytes 786440 | tf_op jit(solution)/shard_map/ppermute | solution.py:370
  6.7 33.6 %collective-permute-start = (bf16[128,1024]{1,0:T(8,128)(2,1)}, bf16[128,1024]{1,0:T(8,128)(2,1)S(1)}, u32[]{:S(2)}, u32[]{:S(2)}) collective-permute-start(bf16[128,1024]{1,0:T(8,128)(2,1)} %refs_4_.1), channel_id=1, source_target_pairs={{0,1},{1,0},{2,3},{3,2},{4,5},{5,4},{6,7},{7,6},{8,9},{9,8},{10,11... | collective-permute-start | bytes 786440 | tf_op jit(solution)/shard_map/ppermute | solution.py:370
  7.3 33.0 %collective-permute-start.2 = (bf16[128,1024]{1,0:T(8,128)(2,1)}, bf16[128,1024]{1,0:T(8,128)(2,1)S(1)}, u32[]{:S(2)}, u32[]{:S(2)}) collective-permute-start(bf16[128,1024]{1,0:T(8,128)(2,1)} %refs_4_.1), channel_id=1, source_target_pairs={{0,3},{1,2},{2,1},{3,0},{4,7},{5,6},{6,5},{7,4},{8,11},{9,10},{10,... | collective-permute-start | bytes 786440 | tf_op jit(solution)/shard_map/ppermute | solution.py:370
  11.1 29.2 %collective-permute-start.4 = (bf16[64,1024]{1,0:T(8,128)(2,1)S(1)}, bf16[64,1024]{1,0:T(8,128)(2,1)S(1)}, u32[]{:S(2)}, u32[]{:S(2)}) collective-permute-start(bf16[64,1024]{1,0:T(8,128)(2,1)S(1)} %bitcast.43), channel_id=1, source_target_pairs={{0,2},{1,3},{2,0},{3,1},{4,6},{5,7},{6,4},{7,5},{8,10},{9,11},{10,... | collective-permute-start | bytes 393224 | tf_op jit(solution)/shard_map/ppermute | solution.py:370
  11.1 29.2 %collective-permute-start.3 = (bf16[64,1024]{1,0:T(8,128)(2,1)S(1)}, bf16[64,1024]{1,0:T(8,128)(2,1)S(1)}, u32[]{:S(2)}, u32[]{:S(2)}) collective-permute-start(bf16[64,1024]{1,0:T(8,128)(2,1)S(1)} %bitcast.44), channel_id=1, source_target_pairs={{0,1},{1,0},{2,3},{3,2},{4,5},{5,4},{6,7},{7,6},{8,9},{9,8},{10,11... | collective-permute-start | bytes 393224 | tf_op jit(solution)/shard_map/ppermute | solution.py:370
  40.3 1.6 %copy-start = (bf16[1024,1024]{1,0:T(8,128)(2,1)S(1)}, bf16[1024,1024]{1,0:T(8,128)(2,1)}, u32[]{:S(2)}) copy-start(bf16[1024,1024]{1,0:T(8,128)(2,1)} %refs_14_.1) | copy-start | bytes 6291460
  41.9 1.2 %copy-start.1 = (bf16[1024,512]{1,0:T(8,128)(2,1)S(1)}, bf16[1024,512]{1,0:T(8,128)(2,1)}, u32[]{:S(2)}) copy-start(bf16[1024,512]{1,0:T(8,128)(2,1)} %refs_13_.1) | copy-start | bytes 3145732
  43.1 1.2 %copy-start.2 = (bf16[512,1024]{1,0:T(8,128)(2,1)S(1)}, bf16[512,1024]{1,0:T(8,128)(2,1)}, u32[]{:S(2)}) copy-start(bf16[512,1024]{1,0:T(8,128)(2,1)} %refs_15_.1) | copy-start | bytes 3145732
  44.3 0.9 copy-start.3
  45.3 0.9 copy-start.4
  46.2 0.9 copy-start.5
  47.1 0.7 copy-start.6
  47.8 0.7 copy-start.7
  48.5 0.7 copy-start.8
  49.2 0.7 copy-start.9
  49.9 0.7 copy-start.10
  50.5 0.7 copy-start.11
  68.5 7.3 %collective-permute-start.6 = (bf16[128,256]{1,0:T(8,128)(2,1)S(1)}, bf16[128,256]{1,0:T(8,128)(2,1)S(1)}, u32[]{:S(2)}, u32[]{:S(2)}) collective-permute-start(bf16[128,256]{1,0:T(8,128)(2,1)S(1)} %get-tuple-element.29), channel_id=1, source_target_pairs={{0,1},{1,0},{2,3},{3,2},{4,5},{5,4},{6,7},{7,6},{8,9},{9,8},{10,11... | collective-permute-start | bytes 196616 | tf_op jit(solution)/shard_map/ppermute | solution.py:370
  68.5 7.4 %collective-permute-start.7 = (bf16[128,256]{1,0:T(8,128)(2,1)S(1)}, bf16[128,256]{1,0:T(8,128)(2,1)S(1)}, u32[]{:S(2)}, u32[]{:S(2)}) collective-permute-start(bf16[128,256]{1,0:T(8,128)(2,1)S(1)} %get-tuple-element.30), channel_id=1, source_target_pairs={{0,2},{1,3},{2,0},{3,1},{4,6},{5,7},{6,4},{7,5},{8,10},{9,11},{10,... | collective-permute-start | bytes 196616 | tf_op jit(solution)/shard_map/ppermute | solution.py:370
  71.5 6.1 %collective-permute-start.8 = (bf16[128,256]{1,0:T(8,128)(2,1)S(1)}, bf16[128,256]{1,0:T(8,128)(2,1)S(1)}, u32[]{:S(2)}, u32[]{:S(2)}) collective-permute-start(bf16[128,256]{1,0:T(8,128)(2,1)S(1)} %get-tuple-element.31), channel_id=1, source_target_pairs={{0,3},{1,2},{2,1},{3,0},{4,7},{5,6},{6,5},{7,4},{8,11},{9,10},{10,... | collective-permute-start | bytes 196616 | tf_op jit(solution)/shard_map/ppermute | solution.py:370

commit v2 on v1

v2 whole, which is shorter than its diff:
```python
import functools
import math

import jax
import jax.numpy as jnp
from jax import lax
from jax.experimental import pallas as pl
from jax.experimental.pallas import tpu as pltpu
from jax.sharding import PartitionSpec as P

HEADS = 8
KERNEL = 31
BLOCK = 64
LC = 2
SPAN = (LC + 1) * BLOCK
HALO = 32
ROWS = HALO + BLOCK
PAD = LC + 1
EPSILON = 1e-05
SOFT_CAP = 4.0
LANES = 128
SUB = 8

BF16 = jnp.bfloat16
F32 = jnp.float32


def dot_nn(a, b):
    return lax.dot_general(a, b, (((1,), (0,)), ((), ())), preferred_element_type=F32)


def dot_nt(a, b):
    return lax.dot_general(a, b, (((1,), (1,)), ((), ())), preferred_element_type=F32)


def dot_tn(a, b):
    return lax.dot_general(a, b, (((0,), (0,)), ((), ())), preferred_element_type=F32)


def norm_stats(values):
    row_mean = jnp.mean(values, axis=-1, keepdims=True)
    centred = values - row_mean
    scale_inv = lax.rsqrt(jnp.mean(centred * centred, axis=-1, keepdims=True) + EPSILON)
    return centred * scale_inv, scale_inv


class Layout:
    def __init__(self, meta_ref, utts, blocks):
        self.ref, self.utts, self.blocks = meta_ref, utts, blocks

    def me(self):
        return self.ref[0, 0]

    def dp(self):
        return self.ref[0, 1]

    def block_of(self, slot):
        found = jnp.int32(0)
        for b in range(self.blocks):
            found = jnp.where(self.ref[0, 2 + self.utts + b] == slot, jnp.int32(b), found)
        return found

    def position(self, block):
        start = jnp.int32(0)
        first = jnp.int32(0)
        for u in range(self.utts):
            first = jnp.where(block >= start, start, first)
            start = start + self.ref[0, 2 + u]
        return block - first

    def reach(self, block):
        safe = jnp.maximum(block, 0)
        left = self.ref[0, 2 + self.utts + self.blocks + safe]
        return jnp.minimum(left, self.position(safe))


def row_at(block, count=BLOCK, shift=0):
    return pl.ds(pl.multiple_of((block + PAD) * BLOCK + shift, math.gcd(BLOCK, shift)), count)


def diag_mask(heads, rows, head_size):
    shape = (heads * rows, heads * head_size)
    row_head = lax.broadcasted_iota(jnp.int32, shape, 0) // rows
    col_head = lax.broadcasted_iota(jnp.int32, shape, 1) // head_size
    return jnp.where(row_head == col_head, 1.0, 0.0).astype(F32)


def spread(rows, mask_b):
    copies = mask_b.shape[0] // rows.shape[0]
    return jnp.concatenate([rows] * copies, axis=0) * mask_b


def fold_heads(full, mask_f, rows):
    kept = full * mask_f
    total = kept[:rows]
    for h in range(1, full.shape[0] // rows):
        total = total + kept[h * rows : (h + 1) * rows]
    return total


def window_probs(diag_q, k_win, reach, head_size):
    raw = dot_nt(k_win, diag_q)
    unit = jnp.tanh(raw * (1.0 / (SOFT_CAP * math.sqrt(head_size))))
    exped = jnp.exp(SOFT_CAP * unit)
    parts = []
    for w in range(LC):
        ok = jnp.where(reach >= LC - w, 1.0, 0.0).astype(F32)
        parts.append(exped[w * BLOCK : (w + 1) * BLOCK] * ok)
    parts.append(exped[LC * BLOCK :])
    exped = jnp.concatenate(parts, axis=0)
    total = jnp.sum(exped, axis=0, keepdims=True)
    return exped * (1.0 / total), unit


def project_kernel(crossed_at, *refs):
    meta_ref, g1_ref, wq_ref, wkv_ref = refs[:4]
    if crossed_at:
        crossed_ref, handed_ref, n_ref, q_ref, kv_ref, x_ref = refs[4:]
        me = meta_ref[0, 0]
        middle = functools.reduce(jnp.logical_or, [me == t for t in crossed_at])
        rows = jnp.where(middle, crossed_ref[...], handed_ref[...])
        x_ref[...] = rows
    else:
        x_ref, n_ref, q_ref, kv_ref = refs[4:]
        rows = x_ref[...]
    unit, _ = norm_stats(rows.astype(F32))
    normed = (unit * g1_ref[...]).astype(BF16)
    n_ref[...] = normed
    q_ref[...] = dot_nn(normed, wq_ref[...]).astype(BF16)
    kv_ref[...] = dot_nn(normed, wkv_ref[...]).astype(BF16)


def forward_kernel(sizes, tm, head_size, *refs):
    meta_ref, grad_ref, wo_ref, small_ref = refs[:4]
    x_refs, q_refs, kv_refs = (refs[4 + k * tm : 4 + (k + 1) * tm] for k in range(3))
    refs = refs[4 + 3 * tm :]
    out_ref = refs[0]
    send_refs = refs[1 : 1 + tm]
    q4_ref, k4_ref, v4_ref = refs[1 + tm : 4 + tm]
    q_ref, kv_ref, tail_s, ctx_s, e_s, h_s, u_s, gr_s, gc_s, taps_s = refs[4 + tm :]

    table = Layout(meta_ref, *sizes)
    me = table.me()
    local = table.blocks // tm
    width = out_ref.shape[1]
    hq = q_ref.shape[1]
    share = q4_ref.shape[1]
    half = tm // 2

    for ref in (q_ref, kv_ref):
        ref[: PAD * BLOCK] = jnp.zeros((PAD * BLOCK, ref.shape[1]), BF16)
    tail_s[:HALO] = jnp.zeros((HALO, width), BF16)
    for m in range(tm):
        for j in range(local):
            b = table.block_of((me ^ m) * local + j)
            here = slice(j * BLOCK, (j + 1) * BLOCK)
            q_ref[row_at(b)] = q_refs[m][here]
            kv_ref[row_at(b)] = kv_refs[m][here]
            after = pl.ds(pl.multiple_of((b + 1) * HALO, HALO), HALO)
            tail_s[after] = x_refs[m][(j + 1) * BLOCK - HALO : (j + 1) * BLOCK]

    lead = pl.multiple_of((me % half) * share, share)
    q4_ref[...] = q_ref[:, pl.ds(lead, share)]
    k4_ref[...] = kv_ref[:, pl.ds(lead, share)]
    v4_ref[...] = kv_ref[:, pl.ds(pl.multiple_of(hq + lead, share), share)]
    for j in range(KERNEL):
        taps_s[j * SUB : (j + 1) * SUB] = jnp.broadcast_to(small_ref[j : j + 1], (SUB, width))

    mid_heads = 256 // BLOCK
    mid_f = diag_mask(mid_heads, BLOCK, head_size)
    mid_b = mid_f.astype(BF16)
    side_f = diag_mask(HEADS, HALO, head_size)
    side_b = side_f.astype(BF16)

    own = [table.block_of(me * local + i) for i in range(local)]
    keep = [jnp.where(table.position(c) >= 1, 1.0, 0.0).astype(F32) for c in own]
    for i, c in enumerate(own):
        for blk, shift, count, put in ((c - 1, HALO, HALO, 0), (c, 0, BLOCK, HALO)):
            reach = table.reach(blk)
            win = row_at(blk - LC, SPAN)
            at = row_at(blk, count, shift)
            if count == BLOCK:
                groups, mask_f, mask_b = HEADS // mid_heads, mid_f, mid_b
            else:
                groups, mask_f, mask_b = 1, side_f, side_b
            wide = hq // groups
            for g in range(groups):
                cols = slice(g * wide, (g + 1) * wide)
                vcols = slice(hq + g * wide, hq + (g + 1) * wide)
                probs, _ = window_probs(
                    spread(q_ref[at, cols], mask_b), kv_ref[win, cols], reach, head_size
                )
                full = dot_tn(probs.astype(BF16), kv_ref[win, vcols])
                ctx_s[i * ROWS + put : i * ROWS + put + count, cols] = fold_heads(
                    full, mask_f, count
                ).astype(BF16)

    gain = small_ref[KERNEL + 1 : KERNEL + 2]
    product = dot_nn(ctx_s[...], wo_ref[...])
    scales = []
    for i, c in enumerate(own):
        here = slice(i * ROWS, (i + 1) * ROWS)
        tail = tail_s[pl.ds(pl.multiple_of(c * HALO, HALO), HALO)]
        rows = jnp.concatenate([tail, x_refs[0][i * BLOCK : (i + 1) * BLOCK]], axis=0)
        hidden = rows.astype(F32) + product[here]
        unit, inv = norm_stats(hidden)
        conv_in = (unit * gain).astype(BF16).astype(F32)
        e_s[i * ROWS : i * ROWS + HALO] = conv_in[:HALO] * keep[i]
        e_s[i * ROWS + HALO : (i + 1) * ROWS] = conv_in[HALO:]
        h_s[i * BLOCK : (i + 1) * BLOCK] = hidden[HALO:]
        u_s[here] = unit
        scales.append(inv)

    groups = BLOCK // SUB

    def conv(k, carry):
        cols = pl.ds(pl.multiple_of(k * LANES, LANES), LANES)
        bias = jnp.broadcast_to(small_ref[KERNEL : KERNEL + 1, cols], (SUB, LANES))
        taps = lambda j: taps_s[j * SUB : (j + 1) * SUB, cols]
        for i in range(local):
            ext = e_s[i * ROWS : (i + 1) * ROWS, cols]
            acc = [bias] * groups
            for s in range(SUB):
                reps = (KERNEL - s + SUB - 1) // SUB
                moved = ext[s + 2 : s + 2 + BLOCK + SUB * (reps - 1)]
                for a in range(reps):
                    tap = taps(SUB * a + s)
                    for r in range(groups):
                        piece = moved[(a + r) * SUB : (a + r + 1) * SUB]
                        acc[r] = acc[r] + tap * piece
            mixed = jnp.concatenate(acc, axis=0)
            gate = 0.5 * jnp.tanh(0.5 * mixed) + 0.5
            rows = slice(i * BLOCK, (i + 1) * BLOCK)
            out_ref[rows, cols] = (h_s[rows, cols] + mixed * gate).astype(BF16)
            slope = gate * (1.0 + mixed * (1.0 - gate))
            gm = grad_ref[rows, cols].astype(F32) * slope
            zeros = jnp.zeros((HALO, LANES), F32)
            padded = jnp.concatenate([zeros, gm, zeros], axis=0)
            back = [None] * (ROWS // SUB)
            low = HALO // SUB - 1
            for s in range(SUB):
                reps = (KERNEL - s + SUB - 1) // SUB
                start = low if s else low + 1
                moved = padded[start * SUB + s : ROWS + s]
                for a in range(reps):
                    tap = taps(KERNEL - 1 - SUB * a - s)
                    for g in range(start, ROWS // SUB):
                        r = g - a
                        piece = tap * moved[(g - start) * SUB : (g - start + 1) * SUB]
                        back[r] = piece if back[r] is None else back[r] + piece
            for r in range(ROWS // SUB):
                scale = keep[i] if r < HALO // SUB else 1.0
                gr_s[i * ROWS + r * SUB : i * ROWS + (r + 1) * SUB, cols] = back[r] * scale
        return carry

    lax.fori_loop(0, width // LANES, conv, 0)

    for i in range(local):
        here = slice(i * ROWS, (i + 1) * ROWS)
        scaled = gr_s[here] * gain
        unit = u_s[here]
        first = jnp.mean(scaled, axis=-1, keepdims=True)
        second = jnp.mean(scaled * unit, axis=-1, keepdims=True)
        back = scales[i] * (scaled - first - unit * second)
        own_grad = grad_ref[i * BLOCK : (i + 1) * BLOCK].astype(F32) + back[HALO:]
        gc_s[i * ROWS : i * ROWS + HALO] = back[:HALO].astype(BF16)
        gc_s[i * ROWS + HALO : (i + 1) * ROWS] = own_grad.astype(BF16)
    for m in range(tm):
        at = pl.ds(pl.multiple_of(((me ^ m) % half) * share, share), share)
        send_refs[m][...] = dot_nt(gc_s[...], wo_ref[at]).astype(BF16)


def probs_kernel(sizes, head_size, meta_ref, q4_ref, k4_ref, p_ref, d_ref):
    table = Layout(meta_ref, *sizes)
    heads = q4_ref.shape[1] // head_size
    mask_b = diag_mask(heads, BLOCK, head_size).astype(BF16)
    for c in range(table.blocks):
        own = slice((c + PAD) * BLOCK, (c + PAD + 1) * BLOCK)
        win = slice((c + PAD - LC) * BLOCK, (c + PAD + 1) * BLOCK)
        diag_q = spread(q4_ref[own], mask_b)
        probs, unit = window_probs(diag_q, k4_ref[win], table.reach(c), head_size)
        p_ref[c] = probs
        d_ref[c] = (1.0 - unit * unit) * (1.0 / math.sqrt(head_size))


def backward_kernel(sizes, tm, part, head_size, *refs):
    meta_ref, q4_ref, v4_ref, p_ref, d_ref = refs[:5]
    n_refs = refs[5 : 5 + tm]
    g_refs = refs[5 + tm : 5 + 2 * tm]
    out_refs = refs[5 + 2 * tm : -3]
    gt_s, t_s, full_s = refs[-3:]
    table = Layout(meta_ref, *sizes)
    me = table.me()
    blocks = table.blocks
    local = blocks // tm
    share = q4_ref.shape[1]
    mask_b = diag_mask(share // head_size, BLOCK, head_size).astype(BF16)

    places = [(m, j, table.block_of((me ^ m) * local + j)) for m in range(tm) for j in range(local)]
    for m, j, b in places:
        gt_s[row_at(b)] = g_refs[m][j * ROWS + HALO : (j + 1) * ROWS].astype(F32)
    gt_s[(PAD - 1) * BLOCK : PAD * BLOCK] = jnp.zeros((BLOCK, share), F32)
    for m, j, b in places:
        at = row_at(b, HALO, -HALO)
        gt_s[at] = gt_s[at] + g_refs[m][j * ROWS : j * ROWS + HALO].astype(F32)
    t_s[...] = jnp.zeros(t_s.shape, F32)

    def spans(c):
        own = slice((c + PAD) * BLOCK, (c + PAD + 1) * BLOCK)
        win = slice((c + PAD - LC) * BLOCK, (c + PAD + 1) * BLOCK)
        return own, win, spread(gt_s[own].astype(BF16), mask_b)

    @pl.when(me >= tm // 2)
    def _():
        for c in range(blocks):
            own, win, diag_g = spans(c)
            t_s[win] = t_s[win] + dot_nn(p_ref[c].astype(BF16), diag_g)

    @pl.when(me < tm // 2)
    def _():
        for c in range(blocks):
            own, win, diag_g = spans(c)
            grad_probs = dot_nt(v4_ref[win], diag_g)
            probs = p_ref[c]
            delta = jnp.sum(probs * grad_probs, axis=0, keepdims=True)
            grad_raw = probs * (grad_probs - delta) * d_ref[c]
            t_s[win] = t_s[win] + dot_nn(grad_raw.astype(BF16), spread(q4_ref[own], mask_b))

    terms = jnp.concatenate([t_s[row_at(b)].astype(BF16) for _, _, b in places], axis=0)
    full = dot_tn(terms, jnp.concatenate([ref[...] for ref in n_refs], axis=0))
    if len(out_refs) == 1:
        out_refs[0][...] = full.astype(BF16)
        return
    full_s[...] = full
    chip, core = table.dp() // 2, table.dp() % 2
    for q in range(out_refs[0].shape[1] // part):
        for ref, side in zip(out_refs, (core, 1 - core)):
            at = pl.ds(pl.multiple_of(((chip ^ q) * 2 + side) * part, part), part)
            ref[:, q * part : (q + 1) * part] = full_s[:, at].astype(ref.dtype)


def pair_kernel(kept_ref, got_ref, *out_refs):
    part = out_refs[0].shape[1]
    for q, ref in enumerate(out_refs):
        cols = slice(q * part, (q + 1) * part)
        ref[...] = (kept_ref[:, cols] + got_ref[:, cols].astype(F32)).astype(ref.dtype)


def sum_kernel(*refs):
    total = refs[0][...].astype(F32)
    for ref in refs[1:-1]:
        total = total + ref[...].astype(F32)
    refs[-1][...] = total.T


def on_device(
    frames,
    out_grad,
    norm1_gain,
    w_query,
    w_kv,
    w_out,
    norm2_gain,
    conv_kernel,
    conv_bias,
    utt_blocks,
    block_slot,
    left_count,
):
    tm = lax.axis_size("tm")
    dp = lax.axis_size("dp")
    rows, width = frames.shape
    blocks = block_slot.shape[1]
    utts = utt_blocks.shape[1]
    sizes = (utts, blocks)
    local = rows // BLOCK
    hq = w_query.shape[1]
    head_size = hq // HEADS
    kv_width = w_kv.shape[1]
    share = kv_width // tm
    padded = (blocks + PAD) * BLOCK

    def swap(value, axis, size, m):
        return lax.ppermute(value, axis, [(i, i ^ m) for i in range(size)])

    meta = jnp.concatenate(
        [
            lax.axis_index("tm").astype(jnp.int32).reshape(1, 1),
            lax.axis_index("dp").astype(jnp.int32).reshape(1, 1),
            utt_blocks,
            block_slot,
            left_count,
        ],
        axis=1,
    )
    small = jnp.concatenate(
        [conv_kernel, conv_bias.reshape(1, -1), norm2_gain.reshape(1, -1)], axis=0
    )

    smem = pl.BlockSpec(memory_space=pltpu.SMEM)
    vmem = pl.BlockSpec(memory_space=pltpu.VMEM)
    shape = jax.ShapeDtypeStruct

    x, normed, queries, keys_values = {}, {}, {}, {}
    made = [shape((rows, w), BF16) for w in (width, hq, kv_width, width)]

    def project(m, parts):
        two = len(parts) == 2
        outs = pl.pallas_call(
            functools.partial(project_kernel, (1, 2) if two else ()),
            out_shape=made if two else made[:3],
            in_specs=[smem] + [vmem] * (3 + len(parts)),
            out_specs=[vmem] * (4 if two else 3),
            compiler_params=pltpu.CompilerParams(vmem_limit_bytes=32 << 20),
            cost_estimate=pl.CostEstimate(
                flops=2 * rows * width * (hq + kv_width), bytes_accessed=4 << 20, transcendentals=0
            ),
            name=f"project_rows_{m}",
        )(meta, norm1_gain.reshape(1, -1), w_query, w_kv, *parts)
        normed[m], queries[m], keys_values[m] = outs[:3]
        x[m] = outs[3] if two else parts[0]

    project(0, (frames,))
    if tm == 4:
        facing = swap(frames, "tm", tm, 2)
        beside = swap(frames, "tm", tm, 1)
        later, passed, normed[0] = lax.optimization_barrier((frames, facing, normed[0]))
        crossed = lax.ppermute(later, "tm", [(1, 2), (2, 1)])
        handed = lax.ppermute(passed, "tm", [(1, 0), (2, 3)])
        project(2, (passed,))
        project(1, (beside,))
        project(3, (crossed, handed))
    else:
        for m in range(1, tm):
            project(m, (swap(frames, "tm", tm, m),))

    def by_m(arrays):
        return [arrays[m] for m in range(tm)]

    own_rows = local * ROWS
    results = pl.pallas_call(
        functools.partial(forward_kernel, sizes, tm, head_size),
        out_shape=[shape((rows, width), BF16)]
        + [shape((own_rows, share), BF16)] * tm
        + [shape((padded, share), BF16)] * 3,
        in_specs=[smem] + [vmem] * (3 + 3 * tm),
        out_specs=[vmem] * (tm + 4),
        scratch_shapes=[
            pltpu.VMEM((padded, hq), BF16),
            pltpu.VMEM((padded, kv_width), BF16),
            pltpu.VMEM(((blocks + 1) * HALO, width), BF16),
            pltpu.VMEM((own_rows, hq), BF16),
            pltpu.VMEM((own_rows, width), F32),
            pltpu.VMEM((rows, width), F32),
            pltpu.VMEM((own_rows, width), F32),
            pltpu.VMEM((own_rows, width), F32),
            pltpu.VMEM((own_rows, width), BF16),
            pltpu.VMEM((KERNEL * SUB, width), F32),
        ],
        compiler_params=pltpu.CompilerParams(vmem_limit_bytes=32 << 20),
        name="forward_pass",
    )(meta, out_grad, w_out, small, *by_m(x), *by_m(queries), *by_m(keys_values))
    layer_out = results[0]
    sends = results[1 : 1 + tm]
    q4, k4, v4 = results[1 + tm :]
    got = [sends[0]] + [swap(sends[m], "tm", tm, m) for m in range(1, tm)]

    pair_width = share // head_size * BLOCK
    probs, slopes = pl.pallas_call(
        functools.partial(probs_kernel, sizes, head_size),
        out_shape=[shape((blocks, SPAN, pair_width), F32)] * 2,
        in_specs=[smem] + [vmem] * 2,
        out_specs=[vmem] * 2,
        compiler_params=pltpu.CompilerParams(vmem_limit_bytes=24 << 20),
        name="window_probs",
        cost_estimate=pl.CostEstimate(
            flops=2 * 10**9, bytes_accessed=4 * 10**6, transcendentals=800000
        ),
    )(meta, q4, k4)

    direct = dp <= 8
    half_width = width // 2
    if direct:
        piece_shapes = [shape((share, half_width), F32), shape((share, half_width), BF16)]
    else:
        piece_shapes = [shape((share, width), BF16)]
    pieces = pl.pallas_call(
        functools.partial(backward_kernel, sizes, tm, width // dp, head_size),
        out_shape=piece_shapes,
        in_specs=[smem] + [vmem] * (4 + 2 * tm),
        out_specs=[vmem] * len(piece_shapes),
        scratch_shapes=[
            pltpu.VMEM((padded, share), F32),
            pltpu.VMEM((padded, share), F32),
            pltpu.VMEM((share, width), F32),
        ],
        compiler_params=pltpu.CompilerParams(vmem_limit_bytes=32 << 20),
        name="key_value_terms",
    )(meta, q4, v4, probs, slopes, *by_m(normed), *got)

    if direct:
        kept, away = pieces
        arrived = swap(away, "dp", dp, 1)
        chips = dp // 2
        part = width // dp
        summed = pl.pallas_call(
            pair_kernel,
            out_shape=[shape((share, part), BF16)] * chips,
            in_specs=[vmem] * 2,
            out_specs=[vmem] * chips,
            name="sum_pair",
        )(kept, arrived)
        terms = [summed[0]] + [swap(summed[q], "dp", dp, 2 * q) for q in range(1, chips)]
    else:
        terms = [lax.psum_scatter(pieces[0], "dp", scatter_dimension=1, tiled=True)]
    kv_grad = pl.pallas_call(
        sum_kernel,
        out_shape=shape((width // dp, share), F32),
        in_specs=[vmem] * len(terms),
        out_specs=vmem,
        name="sum_groups",
    )(*terms)
    return layer_out, kv_grad


def solution(mesh):
    return jax.shard_map(
        on_device,
        mesh=mesh,
        in_specs=(
            P(("dp", "tm"), None),
            P(("dp", "tm"), None),
            P(),
            P(),
            P(),
            P(),
            P(),
            P(),
            P(),
            P("dp", None),
            P("dp", None),
            P("dp", None),
        ),
        out_specs=(P(("dp", "tm"), None), P("dp", "tm")),
        check_vma=False,
    )
```

time: 98.7 us -> 66.8 us (0.68)
  blocking collectives: 13.3 us -> 0 us
  starting transfers between devices: 22.1 us -> 15.5 us
  local copies, waits for them, and re-layouts: 12.7 us -> 6.45 us
  Pallas kernels: 26.6 us -> 21.2 us
    all_to_all x1 -> x0, blocking collectives: 13.3 us -> none  [on_device(): mine = lax.all_to_all(stacked, 'dp', 0, 0, tiled=False)]
    ppermute x9, starting transfers between devices: 22.1 us -> 13.6 us  [swap(): return lax.ppermute(value, axis, [(i, i ^ m) for i in range(size)])]
    ppermute x9, waiting for transfers between devices: 22.8 us -> 16.7 us  [swap(): return lax.ppermute(value, axis, [(i, i ^ m) for i in range(size)])]
    ppermute x0 -> x2, waiting for transfers between devices: none -> 5.69 us  [the longest x1 5.69 us: on_device(): handed = lax.ppermute(passed, 'tm', [(1, 0), (2, 3)])]
    unnamed x31 -> x26, local copies, waits for them, and re-layouts: 11 us -> 5.67 us
    pallas_call x3 -> x8, Pallas kernels: 24.7 us -> 19.6 us  [the longest x1 8.16 us: on_device(): pl.pallas_call(functools.partial(forward_kernel, sizes, tm, head_size), o...]
    ppermute x0 -> x2, starting transfers between devices: none -> 1.96 us  [the longest x1 1.29 us: on_device(): handed = lax.ppermute(passed, 'tm', [(1, 0), (2, 3)])]
  transfers between devices with their start and end apart: 9 -> 11, of which waited for: 2 -> 7; matrix products, arithmetic and copies ran while one was open for 0% -> 1% of each run, Pallas kernels for 3% -> 9%
where the time goes in v2:
time: 66.8 us; the launch traced here: 66.4 us
  waiting for transfers between devices  22.3 us (33%)
  Pallas kernels  21.2 us (32%)
  starting transfers between devices  15.5 us (23%)
  local copies, waits for them, and re-layouts  6.45 us (10%)
  between operations  0.81 us (1%)
    ppermute x9, waiting for transfers between devices, swap(): return lax.ppermute(value, axis, [(i, i ^ m) for i in range(size)])  16.7 us
    ppermute x9, starting transfers between devices, swap(): return lax.ppermute(value, axis, [(i, i ^ m) for i in range(size)])  13.6 us
    pallas_call x1, Pallas kernels, on_device(): pl.pallas_call(functools.partial(forward_kernel, sizes, tm, head_size), o...  8.16 us
    ppermute x1, waiting for transfers between devices, on_device(): handed = lax.ppermute(passed, 'tm', [(1, 0), (2, 3)])  5.69 us
    pallas_call x4, Pallas kernels, project(): pl.pallas_call(functools.partial(project_kernel, (1, 2) if two else ()),...  5.68 us
    unnamed x26, local copies, waits for them, and re-layouts  5.67 us
    pallas_call x1, Pallas kernels, on_device(): pl.pallas_call(functools.partial(backward_kernel, sizes, tm, width // dp,...  2.43 us
    pallas_call x1, Pallas kernels, on_device(): pl.pallas_call(pair_kernel, out_shape=[shape((share, part), BF16)] * chip...  1.81 us
  transfers between devices with their start and end apart: 11, of which 7 were waited for; matrix products, arithmetic and copies ran while one was open for 1% of the time, Pallas kernels for 9%

profile of v2, /device:TPU:0, one launch (start us, length us, event | category | flops | bytes accessed | tf_op | source)
XLA Modules:
  0.0 66.4 jit_solution(599140806501319986)
XLA Ops:
  0.6 4.1 %collective-permute-start.1 = (bf16[128,1024]{1,0:T(8,128)(2,1)}, bf16[128,1024]{1,0:T(8,128)(2,1)S(1)}, u32[]{:S(2)}, u32[]{:S(2)}) collective-permute-start(bf16[128,1024]{1,0:T(8,128)(2,1)} %refs_4_.3), channel_id=1, source_target_pairs={{0,2},{1,3},{2,0},{3,1},{4,6},{5,7},{6,4},{7,5},{8,10},{9,11},{10,... | collective-permute-start | bytes 786440 | tf_op jit(solution)/shard_map/ppermute | solution.py:384
  4.7 1.6 %collective-permute-start = (bf16[128,1024]{1,0:T(8,128)(2,1)}, bf16[128,1024]{1,0:T(8,128)(2,1)S(1)}, u32[]{:S(2)}, u32[]{:S(2)}) collective-permute-start(bf16[128,1024]{1,0:T(8,128)(2,1)} %refs_4_.3), channel_id=1, source_target_pairs={{0,1},{1,0},{2,3},{3,2},{4,5},{5,4},{6,7},{7,6},{8,9},{9,8},{10,11... | collective-permute-start | bytes 786440 | tf_op jit(solution)/shard_map/ppermute | solution.py:384
  6.3 0.8 %concatenate.6.refs_0_.meta_ref = s32[1,20]{1,0:T(1,128)S(1)} concatenate(s32[1,1]{1,0:T(1,128)} %bitcast, s32[1,1]{1,0:T(1,128)} %bitcast.1, s32[1,2]{1,0:T(1,128)} %param.21, s32[1,8]{1,0:T(1,128)} %param.22, s32[1,8]{1,0:T(1,128)} %param.23), dimensions={1} | concatenate | bytes 160 | tf_op jit(solution)/shard_map/concatenate | solution.py:386
  7.1 0.0 copy-start
  7.1 1.6 %copy-done = bf16[1024,1024]{1,0:T(8,128)(2,1)S(1)} copy-done((bf16[1024,1024]{1,0:T(8,128)(2,1)S(1)}, bf16[1024,1024]{1,0:T(8,128)(2,1)}, u32[]{:S(2)}) %copy-start) | copy-done | bytes 2097176
  8.7 0.0 copy-start.1
  8.7 1.2 %copy-done.1 = bf16[1024,512]{1,0:T(8,128)(2,1)S(1)} copy-done((bf16[1024,512]{1,0:T(8,128)(2,1)S(1)}, bf16[1024,512]{1,0:T(8,128)(2,1)}, u32[]{:S(2)}) %copy-start.1) | copy-done | bytes 1048600
  9.9 0.0 copy-start.5
  9.9 0.7 %copy-done.5 = f32[1024]{0:T(1024)S(1)} copy-done((f32[1024]{0:T(1024)S(1)}, f32[1024]{0:T(1024)}, u32[]{:S(2)}) %copy-start.5) | copy-done | bytes 4120
  10.6 0.0 copy-start.7
  10.6 0.0 copy-start.11
  10.6 0.0 copy-start.12
  10.6 1.8 %project_rows_0.1 = (bf16[128,1024]{1,0:T(8,128)(2,1)S(1)}, bf16[128,512]{1,0:T(8,128)(2,1)S(1)}, bf16[128,1024]{1,0:T(8,128)(2,1)S(1)}) custom-call(s32[1,20]{1,0:T(1,128)S(1)} %concatenate.6.refs_0_.meta_ref, f32[1,1024]{1,0:T(1,128)S(1)} %bitcast.5, bf16[1024,512]{1,0:T(8,128)(2,1)S(1)} %copy-done.1, bf16[1024,1024]{1,0:T(8,128)(2,1)S(1)} %copy-done, ...), custom_call_target="tpu_custom_call" | custom-call | flops 402653184 | bytes 4194304 | tf_op jit(solution)/shard_map/project_rows_0/pallas_call | solution.py:409
  12.4 4.6 %collective-permute-done.1.refs_4_.refs_6_ = bf16[128,1024]{1,0:T(8,128)(2,1)S(1)} collective-permute-done((bf16[128,1024]{1,0:T(8,128)(2,1)}, bf16[128,1024]{1,0:T(8,128)(2,1)S(1)}, u32[]{:S(2)}, u32[]{:S(2)}) %collective-permute-start.1) | collective-permute-done | bytes 262176 | tf_op jit(solution)/shard_map/ppermute | solution.py:384
  17.0 0.7 %collective-permute-start.2 = (bf16[128,1024]{1,0:T(8,128)(2,1)}, bf16[128,1024]{1,0:T(8,128)(2,1)S(1)}, u32[]{:S(2)}, u32[]{:S(2)}) collective-permute-start(bf16[128,1024]{1,0:T(8,128)(2,1)} %refs_4_.3), channel_id=1, source_target_pairs={{1,2},{2,1},{5,6},{6,5},{9,10},{10,9},{13,14},{14,13},{17,18},{18,... | collective-permute-start | bytes 786440 | tf_op jit(solution)/shard_map/ppermute | solution.py:428
  17.7 1.3 %collective-permute-start.3 = (bf16[128,1024]{1,0:T(8,128)(2,1)S(1)}, bf16[128,1024]{1,0:T(8,128)(2,1)S(1)}, u32[]{:S(2)}, u32[]{:S(2)}) collective-permute-start(bf16[128,1024]{1,0:T(8,128)(2,1)S(1)} %collective-permute-done.1.refs_4_.refs_6_), channel_id=1, source_target_pairs={{1,0},{2,3},{5,4},{6,7},{9,8},{10,11},{13,12},{14,15},{17,16},{18,... | collective-permute-start | bytes 786440 | tf_op jit(solution)/shard_map/ppermute | solution.py:429
  19.0 0.0 copy-done.7
  19.0 0.0 copy-done.11
  19.0 0.0 copy-done.12
  19.0 1.3 %project_rows_2.1 = (bf16[128,1024]{1,0:T(8,128)(2,1)S(1)}, bf16[128,512]{1,0:T(8,128)(2,1)S(1)}, bf16[128,1024]{1,0:T(8,128)(2,1)S(1)}) custom-call(s32[1,20]{1,0:T(1,128)S(1)} %concatenate.6.refs_0_.meta_ref, f32[1,1024]{1,0:T(1,128)S(1)} %bitcast.6, bf16[1024,512]{1,0:T(8,128)(2,1)S(1)} %copy-done.1, bf16[1024,1024]{1,0:T(8,128)(2,1)S(1)} %copy-done, ...), custom_call_target="tpu_custom_call" | custom-call | flops 402653184 | bytes 4194304 | tf_op jit(solution)/shard_map/project_rows_2/pallas_call | solution.py:409
  20.3 0.0 collective-permute-done.refs_4_.refs_5_
  20.3 1.3 %project_rows_1.1 = (bf16[128,1024]{1,0:T(8,128)(2,1)S(1)}, bf16[128,512]{1,0:T(8,128)(2,1)S(1)}, bf16[128,1024]{1,0:T(8,128)(2,1)S(1)}) custom-call(s32[1,20]{1,0:T(1,128)S(1)} %concatenate.6.refs_0_.meta_ref, f32[1,1024]{1,0:T(1,128)S(1)} %bitcast.7, bf16[1024,512]{1,0:T(8,128)(2,1)S(1)} %copy-done.1, bf16[1024,1024]{1,0:T(8,128)(2,1)S(1)} %copy-done, ...), custom_call_target="tpu_custom_call" | custom-call | flops 402653184 | bytes 4194304 | tf_op jit(solution)/shard_map/project_rows_1/pallas_call | solution.py:409
  21.7 0.0 copy-start.2
  21.7 0.0 copy-start.4
  21.7 0.0 collective-permute-done.2.refs_4_
  21.7 5.7 %collective-permute-done.3.refs_5_ = bf16[128,1024]{1,0:T(8,128)(2,1)S(1)} collective-permute-done((bf16[128,1024]{1,0:T(8,128)(2,1)S(1)}, bf16[128,1024]{1,0:T(8,128)(2,1)S(1)}, u32[]{:S(2)}, u32[]{:S(2)}) %collective-permute-start.3) | collective-permute-done | bytes 262176 | tf_op jit(solution)/shard_map/ppermute | solution.py:429
  27.4 1.3 %project_rows_3.1 = (bf16[128,1024]{1,0:T(8,128)(2,1)S(1)}, bf16[128,512]{1,0:T(8,128)(2,1)S(1)}, bf16[128,1024]{1,0:T(8,128)(2,1)S(1)}, bf16[128,1024]{1,0:T(8,128)(2,1)S(1)}) custom-call(s32[1,20]{1,0:T(1,128)S(1)} %concatenate.6.refs_0_.meta_ref, f32[1,1024]{1,0:T(1,128)S(1)} %bitcast.8, bf16[1024,512]{1,0:T(8,128)(2,1)S(1)} %copy-done.1, ...), custom_call_target="tpu_custom_call" | custom-call | flops 402653184 | bytes 4194304 | tf_op jit(solution)/shard_map/project_rows_3/pallas_call | solution.py:409
  28.7 0.0 copy-done.2
  28.7 0.0 copy-done.4
  28.7 8.2 %forward_pass.1 = (bf16[128,1024]{1,0:T(8,128)(2,1)}, bf16[192,256]{1,0:T(8,128)(2,1)S(1)}, bf16[192,256]{1,0:T(8,128)(2,1)S(1)}, bf16[192,256]{1,0:T(8,128)(2,1...) custom-call(s32[1,20]{1,0:T(1,128)S(1)} %concatenate.6.refs_0_.meta_, ...), custom_call_target="tpu_custom_call" | custom-call | tf_op jit(solution)/shard_map/forward_pass/pallas_call | solution.py:441
  36.9 0.7 %collective-permute-start.4 = (bf16[192,256]{1,0:T(8,128)(2,1)S(1)}, bf16[192,256]{1,0:T(8,128)(2,1)S(1)}, u32[]{:S(2)}, u32[]{:S(2)}) collective-permute-start(bf16[192,256]{1,0:T(8,128)(2,1)S(1)} %get-tuple-element.57), channel_id=1, source_target_pairs={{0,1},{1,0},{2,3},{3,2},{4,5},{5,4},{6,7},{7,6},{8,9},{9,8},{10,11... | collective-permute-start | bytes 294920 | tf_op jit(solution)/shard_map/ppermute | solution.py:384
  37.5 3.7 %collective-permute-start.5 = (bf16[192,256]{1,0:T(8,128)(2,1)S(1)}, bf16[192,256]{1,0:T(8,128)(2,1)S(1)}, u32[]{:S(2)}, u32[]{:S(2)}) collective-permute-start(bf16[192,256]{1,0:T(8,128)(2,1)S(1)} %get-tuple-element.58), channel_id=1, source_target_pairs={{0,2},{1,3},{2,0},{3,1},{4,6},{5,7},{6,4},{7,5},{8,10},{9,11},{10,... | collective-permute-start | bytes 294920 | tf_op jit(solution)/shard_map/ppermute | solution.py:384
  41.3 0.0 collective-permute-start.6
  41.3 1.5 %window_probs.1 = (f32[8,192,256]{2,1,0:T(8,128)S(1)}, f32[8,192,256]{2,1,0:T(8,128)S(1)}) custom-call(s32[1,20]{1,0:T(1,128)S(1)} %concatenate.6.refs_0_.meta_ref, bf16[704,256]{1,0:T(8,128)(2,1)S(1)} %get-tuple-element.47.q4_ref.refs_1_, bf16[704,256]{1,0:T(8,128)(2,1)S(1)} %get-tuple-element.49.k4_ref), custom_call_target="tpu_custom_call" | custom-call | flops 2000000000 | bytes 4000000 | tf_op jit(solution)/shard_map/window_probs/pallas_call | solution.py:469
  42.8 0.0 collective-permute-done.4.refs_10_
  42.8 5.6 %collective-permute-done.5.refs_11_ = bf16[192,256]{1,0:T(8,128)(2,1)S(1)} collective-permute-done((bf16[192,256]{1,0:T(8,128)(2,1)S(1)}, bf16[192,256]{1,0:T(8,128)(2,1)S(1)}, u32[]{:S(2)}, u32[]{:S(2)}) %collective-permute-start.5) | collective-permute-done | bytes 98336 | tf_op jit(solution)/shard_map/ppermute | solution.py:384
  48.4 0.0 collective-permute-done.6.refs_12_
  48.4 2.4 %key_value_terms.1 = (f32[256,512]{1,0:T(8,128)S(1)}, bf16[256,512]{1,0:T(8,128)(2,1)S(1)}) custom-call(s32[1,20]{1,0:T(1,128)S(1)} %concatenate.6.refs_0_.meta_ref, bf16[704,256]{1,0:T(8,128)(2,1)S(1)} %get-tuple-element.47.q4_ref.refs_1_, bf16[704,256]{1,0:T(8,128)(2,1)S(1)} %get-tuple-element.48.refs_2_, f32[8,192,256]{2,1,0:T(8,128)S(1)} %get-tuple-element.50.refs_3_, ...), custom_call_target="tpu_custom_call" | custom-call | tf_op jit(solution)/shard_map/key_value_terms/pallas_call | solution.py:487
  50.8 0.0 copy-start.3
  50.8 0.8 %copy-done.3 = f32[256,512]{1,0:T(8,128)} copy-done((f32[256,512]{1,0:T(8,128)}, f32[256,512]{1,0:T(8,128)S(1)}, u32[]{:S(2)}) %copy-start.3) | copy-done | bytes 524312
  51.6 0.0 collective-permute-start.7
  51.6 1.5 %collective-permute-done.7.got_ref = bf16[256,512]{1,0:T(8,128)(2,1)S(1)} collective-permute-done((bf16[256,512]{1,0:T(8,128)(2,1)S(1)}, bf16[256,512]{1,0:T(8,128)(2,1)S(1)}, u32[]{:S(2)}, u32[]{:S(2)}) %collective-permute-start.7) | collective-permute-done | bytes 262176 | tf_op jit(solution)/shard_map/ppermute | solution.py:384
  53.2 0.0 copy-start.6
  53.2 0.7 %copy-done.6 = bf16[256,512]{1,0:T(8,128)(2,1)} copy-done((bf16[256,512]{1,0:T(8,128)(2,1)}, bf16[256,512]{1,0:T(8,128)(2,1)S(1)}, u32[]{:S(2)}) %copy-start.6) | copy-done | bytes 262168
  53.9 1.8 %sum_pair.1 = (bf16[256,128]{1,0:T(8,128)(2,1)}, bf16[256,128]{1,0:T(8,128)(2,1)}, bf16[256,128]{1,0:T(8,128)(2,1)}, bf16[256,128]{1,0:T(8,128)(2,1)}) custom-call(f32[256,512]{1,0:T(8,128)} %copy-done.3, bf16[256,512]{1,0:T(8,128)(2,1)} %copy-done.6), custom_call_target="tpu_custom_call" | custom-call | tf_op jit(solution)/shard_map/sum_pair/pallas_call | solution.py:506
  55.7 1.5 %collective-permute-start.8 = (bf16[256,128]{1,0:T(8,128)(2,1)}, bf16[256,128]{1,0:T(8,128)(2,1)S(1)}, u32[]{:S(2)}, u32[]{:S(2)}) collective-permute-start(bf16[256,128]{1,0:T(8,128)(2,1)} %get-tuple-element.63), channel_id=1, source_target_pairs={{0,8},{4,12},{8,0},{12,4},{16,24},{20,28},{24,16},{28,20},{1,9},{5... | collective-permute-start | bytes 196616 | tf_op jit(solution)/shard_map/ppermute | solution.py:384
  57.2 1.5 %collective-permute-start.9 = (bf16[256,128]{1,0:T(8,128)(2,1)}, bf16[256,128]{1,0:T(8,128)(2,1)S(1)}, u32[]{:S(2)}, u32[]{:S(2)}) collective-permute-start(bf16[256,128]{1,0:T(8,128)(2,1)} %get-tuple-element.64), channel_id=1, source_target_pairs={{0,16},{4,20},{8,24},{12,28},{16,0},{20,4},{24,8},{28,12},{1,17},{... | collective-permute-start | bytes 196616 | tf_op jit(solution)/shard_map/ppermute | solution.py:384
  58.7 0.5 collective-permute-start.10
  59.2 1.0 %collective-permute-done.8.refs_1_ = bf16[256,128]{1,0:T(8,128)(2,1)S(1)} collective-permute-done((bf16[256,128]{1,0:T(8,128)(2,1)}, bf16[256,128]{1,0:T(8,128)(2,1)S(1)}, u32[]{:S(2)}, u32[]{:S(2)}) %collective-permute-start.8) | collective-permute-done | bytes 65568 | tf_op jit(solution)/shard_map/ppermute | solution.py:384
  60.2 0.0 copy-start.8
  60.2 1.5 %collective-permute-done.9.refs_2_ = bf16[256,128]{1,0:T(8,128)(2,1)S(1)} collective-permute-done((bf16[256,128]{1,0:T(8,128)(2,1)}, bf16[256,128]{1,0:T(8,128)(2,1)S(1)}, u32[]{:S(2)}, u32[]{:S(2)}) %collective-permute-start.9) | collective-permute-done | bytes 65568 | tf_op jit(solution)/shard_map/ppermute | solution.py:384
  61.7 0.0 copy-start.9
  61.7 2.4 %collective-permute-done.10.refs_3_ = bf16[256,128]{1,0:T(8,128)(2,1)S(1)} collective-permute-done((bf16[256,128]{1,0:T(8,128)(2,1)}, bf16[256,128]{1,0:T(8,128)(2,1)S(1)}, u32[]{:S(2)}, u32[]{:S(2)}) %collective-permute-start.10) | collective-permute-done | bytes 65568 | tf_op jit(solution)/shard_map/ppermute | solution.py:384
  64.1 0.0 copy-start.10
  64.1 0.0 copy-done.8
  64.1 0.0 copy-done.9
  64.1 0.6 copy-done.10
  64.7 1.7 %sum_groups.1 = f32[128,256]{1,0:T(8,128)} custom-call(bf16[256,128]{1,0:T(8,128)(2,1)} %get-tuple-element.62.refs_0_, bf16[256,128]{1,0:T(8,128)(2,1)} %copy-done.8, bf16[256,128]{1,0:T(8,128)(2,1)} %copy-done.9, bf16[256,128]{1,0:T(8,128)(2,1)} %copy-done.10), custom_call_target="tpu_custom_call" | custom-call | tf_op jit(solution)/shard_map/sum_groups/pallas_call | solution.py:516
  (1 shorter events, 0.0 us)
Async XLA Ops:
  0.6 16.3 %collective-permute-start.1 = (bf16[128,1024]{1,0:T(8,128)(2,1)}, bf16[128,1024]{1,0:T(8,128)(2,1)S(1)}, u32[]{:S(2)}, u32[]{:S(2)}) collective-permute-start(bf16[128,1024]{1,0:T(8,128)(2,1)} %refs_4_.3), channel_id=1, source_target_pairs={{0,2},{1,3},{2,0},{3,1},{4,6},{5,7},{6,4},{7,5},{8,10},{9,11},{10,... | collective-permute-start | bytes 786440 | tf_op jit(solution)/shard_map/ppermute | solution.py:384
  4.7 15.6 %collective-permute-start = (bf16[128,1024]{1,0:T(8,128)(2,1)}, bf16[128,1024]{1,0:T(8,128)(2,1)S(1)}, u32[]{:S(2)}, u32[]{:S(2)}) collective-permute-start(bf16[128,1024]{1,0:T(8,128)(2,1)} %refs_4_.3), channel_id=1, source_target_pairs={{0,1},{1,0},{2,3},{3,2},{4,5},{5,4},{6,7},{7,6},{8,9},{9,8},{10,11... | collective-permute-start | bytes 786440 | tf_op jit(solution)/shard_map/ppermute | solution.py:384
  7.1 1.6 %copy-start = (bf16[1024,1024]{1,0:T(8,128)(2,1)S(1)}, bf16[1024,1024]{1,0:T(8,128)(2,1)}, u32[]{:S(2)}) copy-start(bf16[1024,1024]{1,0:T(8,128)(2,1)} %refs_3_.7) | copy-start | bytes 6291460
  8.7 1.2 %copy-start.1 = (bf16[1024,512]{1,0:T(8,128)(2,1)S(1)}, bf16[1024,512]{1,0:T(8,128)(2,1)}, u32[]{:S(2)}) copy-start(bf16[1024,512]{1,0:T(8,128)(2,1)} %refs_2_.8) | copy-start | bytes 3145732
  9.9 0.7 %copy-start.5 = (f32[1024]{0:T(1024)S(1)}, f32[1024]{0:T(1024)}, u32[]{:S(2)}) copy-start(f32[1024]{0:T(1024)} %param.14) | copy-start | bytes 12292
  10.6 8.4 %copy-start.7 = (f32[31,1024]{1,0:T(8,128)S(1)}, f32[31,1024]{1,0:T(8,128)}, u32[]{:S(2)}) copy-start(f32[31,1024]{1,0:T(8,128)} %param.19) | copy-start | bytes 380932
  10.6 8.4 %copy-start.11 = (f32[1024]{0:T(1024)S(1)}, f32[1024]{0:T(1024)}, u32[]{:S(2)}) copy-start(f32[1024]{0:T(1024)} %param.18) | copy-start | bytes 12292
  10.6 8.4 %copy-start.12 = (f32[1024]{0:T(1024)S(1)}, f32[1024]{0:T(1024)}, u32[]{:S(2)}) copy-start(f32[1024]{0:T(1024)} %param.20) | copy-start | bytes 12292
  17.0 4.7 %collective-permute-start.2 = (bf16[128,1024]{1,0:T(8,128)(2,1)}, bf16[128,1024]{1,0:T(8,128)(2,1)S(1)}, u32[]{:S(2)}, u32[]{:S(2)}) collective-permute-start(bf16[128,1024]{1,0:T(8,128)(2,1)} %refs_4_.3), channel_id=1, source_target_pairs={{1,2},{2,1},{5,6},{6,5},{9,10},{10,9},{13,14},{14,13},{17,18},{18,... | collective-permute-start | bytes 786440 | tf_op jit(solution)/shard_map/ppermute | solution.py:428
  17.7 9.7 %collective-permute-start.3 = (bf16[128,1024]{1,0:T(8,128)(2,1)S(1)}, bf16[128,1024]{1,0:T(8,128)(2,1)S(1)}, u32[]{:S(2)}, u32[]{:S(2)}) collective-permute-start(bf16[128,1024]{1,0:T(8,128)(2,1)S(1)} %collective-permute-done.1.refs_4_.refs_6_), channel_id=1, source_target_pairs={{1,0},{2,3},{5,4},{6,7},{9,8},{10,11},{13,12},{14,15},{17,16},{18,... | collective-permute-start | bytes 786440 | tf_op jit(solution)/shard_map/ppermute | solution.py:429
  21.7 7.0 %copy-start.2 = (bf16[512,1024]{1,0:T(8,128)(2,1)S(1)}, bf16[512,1024]{1,0:T(8,128)(2,1)}, u32[]{:S(2)}) copy-start(bf16[512,1024]{1,0:T(8,128)(2,1)} %refs_2_.9) | copy-start | bytes 3145732
  21.7 7.0 %copy-start.4 = (bf16[128,1024]{1,0:T(8,128)(2,1)S(1)}, bf16[128,1024]{1,0:T(8,128)(2,1)}, u32[]{:S(2)}) copy-start(bf16[128,1024]{1,0:T(8,128)(2,1)} %refs_1_.1) | copy-start | bytes 786436
  36.9 5.9 %collective-permute-start.4 = (bf16[192,256]{1,0:T(8,128)(2,1)S(1)}, bf16[192,256]{1,0:T(8,128)(2,1)S(1)}, u32[]{:S(2)}, u32[]{:S(2)}) collective-permute-start(bf16[192,256]{1,0:T(8,128)(2,1)S(1)} %get-tuple-element.57), channel_id=1, source_target_pairs={{0,1},{1,0},{2,3},{3,2},{4,5},{5,4},{6,7},{7,6},{8,9},{9,8},{10,11... | collective-permute-start | bytes 294920 | tf_op jit(solution)/shard_map/ppermute | solution.py:384
  37.5 10.8 %collective-permute-start.5 = (bf16[192,256]{1,0:T(8,128)(2,1)S(1)}, bf16[192,256]{1,0:T(8,128)(2,1)S(1)}, u32[]{:S(2)}, u32[]{:S(2)}) collective-permute-start(bf16[192,256]{1,0:T(8,128)(2,1)S(1)} %get-tuple-element.58), channel_id=1, source_target_pairs={{0,2},{1,3},{2,0},{3,1},{4,6},{5,7},{6,4},{7,5},{8,10},{9,11},{10,... | collective-permute-start | bytes 294920 | tf_op jit(solution)/shard_map/ppermute | solution.py:384
  41.3 7.1 %collective-permute-start.6 = (bf16[192,256]{1,0:T(8,128)(2,1)S(1)}, bf16[192,256]{1,0:T(8,128)(2,1)S(1)}, u32[]{:S(2)}, u32[]{:S(2)}) collective-permute-start(bf16[192,256]{1,0:T(8,128)(2,1)S(1)} %get-tuple-element.59), channel_id=1, source_target_pairs={{0,3},{1,2},{2,1},{3,0},{4,7},{5,6},{6,5},{7,4},{8,11},{9,10},{10,... | collective-permute-start | bytes 294920 | tf_op jit(solution)/shard_map/ppermute | solution.py:384
  50.8 0.8 %copy-start.3 = (f32[256,512]{1,0:T(8,128)}, f32[256,512]{1,0:T(8,128)S(1)}, u32[]{:S(2)}) copy-start(f32[256,512]{1,0:T(8,128)S(1)} %get-tuple-element.60.kept_ref) | copy-start | bytes 1572868
  51.6 1.5 %collective-permute-start.7 = (bf16[256,512]{1,0:T(8,128)(2,1)S(1)}, bf16[256,512]{1,0:T(8,128)(2,1)S(1)}, u32[]{:S(2)}, u32[]{:S(2)}) collective-permute-start(bf16[256,512]{1,0:T(8,128)(2,1)S(1)} %get-tuple-element.61), channel_id=1, source_target_pairs={{0,4},{4,0},{8,12},{12,8},{16,20},{20,16},{24,28},{28,24},{1,5},{5... | collective-permute-start | bytes 786440 | tf_op jit(solution)/shard_map/ppermute | solution.py:384
  53.2 0.7 %copy-start.6 = (bf16[256,512]{1,0:T(8,128)(2,1)}, bf16[256,512]{1,0:T(8,128)(2,1)S(1)}, u32[]{:S(2)}) copy-start(bf16[256,512]{1,0:T(8,128)(2,1)S(1)} %collective-permute-done.7.got_ref) | copy-start | bytes 786436
  55.7 4.5 %collective-permute-start.8 = (bf16[256,128]{1,0:T(8,128)(2,1)}, bf16[256,128]{1,0:T(8,128)(2,1)S(1)}, u32[]{:S(2)}, u32[]{:S(2)}) collective-permute-start(bf16[256,128]{1,0:T(8,128)(2,1)} %get-tuple-element.63), channel_id=1, source_target_pairs={{0,8},{4,12},{8,0},{12,4},{16,24},{20,28},{24,16},{28,20},{1,9},{5... | collective-permute-start | bytes 196616 | tf_op jit(solution)/shard_map/ppermute | solution.py:384
  57.2 4.5 %collective-permute-start.9 = (bf16[256,128]{1,0:T(8,128)(2,1)}, bf16[256,128]{1,0:T(8,128)(2,1)S(1)}, u32[]{:S(2)}, u32[]{:S(2)}) collective-permute-start(bf16[256,128]{1,0:T(8,128)(2,1)} %get-tuple-element.64), channel_id=1, source_target_pairs={{0,16},{4,20},{8,24},{12,28},{16,0},{20,4},{24,8},{28,12},{1,17},{... | collective-permute-start | bytes 196616 | tf_op jit(solution)/shard_map/ppermute | solution.py:384
  58.7 5.4 %collective-permute-start.10 = (bf16[256,128]{1,0:T(8,128)(2,1)}, bf16[256,128]{1,0:T(8,128)(2,1)S(1)}, u32[]{:S(2)}, u32[]{:S(2)}) collective-permute-start(bf16[256,128]{1,0:T(8,128)(2,1)} %get-tuple-element.65), channel_id=1, source_target_pairs={{0,24},{4,28},{8,16},{12,20},{16,8},{20,12},{24,0},{28,4},{1,25},{... | collective-permute-start | bytes 196616 | tf_op jit(solution)/shard_map/ppermute | solution.py:384
  60.2 3.9 %copy-start.8 = (bf16[256,128]{1,0:T(8,128)(2,1)}, bf16[256,128]{1,0:T(8,128)(2,1)S(1)}, u32[]{:S(2)}) copy-start(bf16[256,128]{1,0:T(8,128)(2,1)S(1)} %collective-permute-done.8.refs_1_) | copy-start | bytes 196612
  61.7 2.4 %copy-start.9 = (bf16[256,128]{1,0:T(8,128)(2,1)}, bf16[256,128]{1,0:T(8,128)(2,1)S(1)}, u32[]{:S(2)}) copy-start(bf16[256,128]{1,0:T(8,128)(2,1)S(1)} %collective-permute-done.9.refs_2_) | copy-start | bytes 196612
  64.1 0.6 copy-start.10

commit v3 on v2

--- a/solution.py
+++ b/solution.py
@@ -110,6 +110,12 @@
     exped = jnp.concatenate(parts, axis=0)
     total = jnp.sum(exped, axis=0, keepdims=True)
     return exped * (1.0 / total), unit
+
+
+def taps_kernel(small_ref, taps_ref):
+    for j in range(KERNEL):
+        rows = jnp.broadcast_to(small_ref[j : j + 1], (SUB, small_ref.shape[1]))
+        taps_ref[j * SUB : (j + 1) * SUB] = rows
 
 
 def project_kernel(crossed_at, *refs):
@@ -131,20 +137,19 @@
 
 
 def forward_kernel(sizes, tm, head_size, *refs):
-    meta_ref, grad_ref, wo_ref, small_ref = refs[:4]
-    x_refs, q_refs, kv_refs = (refs[4 + k * tm : 4 + (k + 1) * tm] for k in range(3))
-    refs = refs[4 + 3 * tm :]
+    meta_ref, grad_ref, wo_ref, small_ref, taps_ref = refs[:5]
+    x_refs, q_refs, kv_refs = (refs[5 + k * tm : 5 + (k + 1) * tm] for k in range(3))
+    refs = refs[5 + 3 * tm :]
     out_ref = refs[0]
     send_refs = refs[1 : 1 + tm]
-    q4_ref, k4_ref, v4_ref = refs[1 + tm : 4 + tm]
-    q_ref, kv_ref, tail_s, ctx_s, e_s, h_s, u_s, gr_s, gc_s, taps_s = refs[4 + tm :]
+    q_ref, kv_ref, tail_s, ctx_s, e_s, h_s, u_s, gr_s, gc_s = refs[1 + tm :]
 
     table = Layout(meta_ref, *sizes)
     me = table.me()
     local = table.blocks // tm
     width = out_ref.shape[1]
     hq = q_ref.shape[1]
-    share = q4_ref.shape[1]
+    share = send_refs[0].shape[1]
     half = tm // 2
 
     for ref in (q_ref, kv_ref):
@@ -158,13 +163,6 @@
             kv_ref[row_at(b)] = kv_refs[m][here]
             after = pl.ds(pl.multiple_of((b + 1) * HALO, HALO), HALO)
             tail_s[after] = x_refs[m][(j + 1) * BLOCK - HALO : (j + 1) * BLOCK]
-
-    lead = pl.multiple_of((me % half) * share, share)
-    q4_ref[...] = q_ref[:, pl.ds(lead, share)]
-    k4_ref[...] = kv_ref[:, pl.ds(lead, share)]
-    v4_ref[...] = kv_ref[:, pl.ds(pl.multiple_of(hq + lead, share), share)]
-    for j in range(KERNEL):
-        taps_s[j * SUB : (j + 1) * SUB] = jnp.broadcast_to(small_ref[j : j + 1], (SUB, width))
 
     mid_heads = 256 // BLOCK
     mid_f = diag_mask(mid_heads, BLOCK, head_size)
@@ -216,7 +214,7 @@
     def conv(k, carry):
         cols = pl.ds(pl.multiple_of(k * LANES, LANES), LANES)
         bias = jnp.broadcast_to(small_ref[KERNEL : KERNEL + 1, cols], (SUB, LANES))
-        taps = lambda j: taps_s[j * SUB : (j + 1) * SUB, cols]
+        taps = lambda j: taps_ref[j * SUB : (j + 1) * SUB, cols]
         for i in range(local):
             ext = e_s[i * ROWS : (i + 1) * ROWS, cols]
             acc = [bias] * groups
@@ -270,9 +268,25 @@
         send_refs[m][...] = dot_nt(gc_s[...], wo_ref[at]).astype(BF16)
 
 
-def probs_kernel(sizes, head_size, meta_ref, q4_ref, k4_ref, p_ref, d_ref):
+def probs_kernel(sizes, tm, head_size, meta_ref, *refs):
+    q_refs, kv_refs = refs[:tm], refs[tm : 2 * tm]
+    q4_ref, v4_ref, p_ref, d_ref, k4_ref = refs[2 * tm :]
     table = Layout(meta_ref, *sizes)
-    heads = q4_ref.shape[1] // head_size
+    me = table.me()
+    local = table.blocks // tm
+    hq = q_refs[0].shape[1]
+    share = q4_ref.shape[1]
+    lead = pl.multiple_of((me % (tm // 2)) * share, share)
+    for ref in (k4_ref, v4_ref):
+        ref[: PAD * BLOCK] = jnp.zeros((PAD * BLOCK, share), BF16)
+    for m in range(tm):
+        for j in range(local):
+            at = row_at(table.block_of((me ^ m) * local + j))
+            here = slice(j * BLOCK, (j + 1) * BLOCK)
+            q4_ref[at] = q_refs[m][here, pl.ds(lead, share)]
+            k4_ref[at] = kv_refs[m][here, pl.ds(lead, share)]
+            v4_ref[at] = kv_refs[m][here, pl.ds(pl.multiple_of(hq + lead, share), share)]
+    heads = share // head_size
     mask_b = diag_mask(heads, BLOCK, head_size).astype(BF16)
     for c in range(table.blocks):
         own = slice((c + PAD) * BLOCK, (c + PAD + 1) * BLOCK)
@@ -401,6 +415,16 @@
     vmem = pl.BlockSpec(memory_space=pltpu.VMEM)
     shape = jax.ShapeDtypeStruct
 
+    taps = pl.pallas_call(
+        taps_kernel,
+        out_shape=shape((KERNEL * SUB, width), F32),
+        in_specs=[vmem],
+        out_specs=vmem,
+        compiler_params=pltpu.CompilerParams(vmem_limit_bytes=8 << 20),
+        cost_estimate=pl.CostEstimate(flops=10**6, bytes_accessed=1 << 20, transcendentals=0),
+        name="spread_taps",
+    )(small)
+
     x, normed, queries, keys_values = {}, {}, {}, {}
     made = [shape((rows, w), BF16) for w in (width, hq, kv_width, width)]
 
@@ -424,7 +448,9 @@
     if tm == 4:
         facing = swap(frames, "tm", tm, 2)
         beside = swap(frames, "tm", tm, 1)
-        later, passed, normed[0] = lax.optimization_barrier((frames, facing, normed[0]))
+        later, passed, normed[0], taps = lax.optimization_barrier(
+            (frames, facing, normed[0], taps)
+        )
         crossed = lax.ppermute(later, "tm", [(1, 2), (2, 1)])
         handed = lax.ppermute(passed, "tm", [(1, 0), (2, 3)])
         project(2, (passed,))
@@ -441,10 +467,9 @@
     results = pl.pallas_call(
         functools.partial(forward_kernel, sizes, tm, head_size),
         out_shape=[shape((rows, width), BF16)]
-        + [shape((own_rows, share), BF16)] * tm
-        + [shape((padded, share), BF16)] * 3,
-        in_specs=[smem] + [vmem] * (3 + 3 * tm),
-        out_specs=[vmem] * (tm + 4),
+        + [shape((own_rows, share), BF16)] * tm,
+        in_specs=[smem] + [vmem] * (4 + 3 * tm),
+        out_specs=[vmem] * (tm + 1),
         scratch_shapes=[
             pltpu.VMEM((padded, hq), BF16),
             pltpu.VMEM((padded, kv_width), BF16),
@@ -455,28 +480,28 @@
             pltpu.VMEM((own_rows, width), F32),
             pltpu.VMEM((own_rows, width), F32),
             pltpu.VMEM((own_rows, width), BF16),
-            pltpu.VMEM((KERNEL * SUB, width), F32),
         ],
         compiler_params=pltpu.CompilerParams(vmem_limit_bytes=32 << 20),
         name="forward_pass",
-    )(meta, out_grad, w_out, small, *by_m(x), *by_m(queries), *by_m(keys_values))
+    )(meta, out_grad, w_out, small, taps, *by_m(x), *by_m(queries), *by_m(keys_values))
     layer_out = results[0]
     sends = results[1 : 1 + tm]
-    q4, k4, v4 = results[1 + tm :]
     got = [sends[0]] + [swap(sends[m], "tm", tm, m) for m in range(1, tm)]
 
     pair_width = share // head_size * BLOCK
-    probs, slopes = pl.pallas_call(
-        functools.partial(probs_kernel, sizes, head_size),
-        out_shape=[shape((blocks, SPAN, pair_width), F32)] * 2,
-        in_specs=[smem] + [vmem] * 2,
-        out_specs=[vmem] * 2,
+    q4, v4, probs, slopes = pl.pallas_call(
+        functools.partial(probs_kernel, sizes, tm, head_size),
+        out_shape=[shape((padded, share), BF16)] * 2
+        + [shape((blocks, SPAN, pair_width), F32)] * 2,
+        in_specs=[smem] + [vmem] * (2 * tm),
+        out_specs=[vmem] * 4,
+        scratch_shapes=[pltpu.VMEM((padded, share), BF16)],
         compiler_params=pltpu.CompilerParams(vmem_limit_bytes=24 << 20),
         name="window_probs",
         cost_estimate=pl.CostEstimate(
             flops=2 * 10**9, bytes_accessed=4 * 10**6, transcendentals=800000
         ),
-    )(meta, q4, k4)
+    )(meta, *by_m(queries), *by_m(keys_values))
 
     direct = dp <= 8
     half_width = width // 2
@@ -508,6 +533,7 @@
             out_shape=[shape((share, part), BF16)] * chips,
             in_specs=[vmem] * 2,
             out_specs=[vmem] * chips,
+            compiler_params=pltpu.CompilerParams(vmem_limit_bytes=4 << 20),
             name="sum_pair",
         )(kept, arrived)
         terms = [summed[0]] + [swap(summed[q], "dp", dp, 2 * q) for q in range(1, chips)]
@@ -518,6 +544,7 @@
         out_shape=shape((width // dp, share), F32),
         in_specs=[vmem] * len(terms),
         out_specs=vmem,
+        compiler_params=pltpu.CompilerParams(vmem_limit_bytes=4 << 20),
         name="sum_groups",
     )(*terms)
     return layer_out, kv_grad

time: 66.8 us -> 61.1 us (0.915)
  Pallas kernels: 21.2 us -> 17.7 us
  local copies, waits for them, and re-layouts: 6.45 us -> 3.07 us
  other arithmetic: 0.02 us -> 0.96 us
    unnamed x26 -> x12, local copies, waits for them, and re-layouts: 5.67 us -> 2.29 us
    pallas_call x1, Pallas kernels: 1.81 us -> 0.08 us  [on_device(): pl.pallas_call(pair_kernel, out_shape=[shape((share, part), BF16)] * chip...]
    concatenate x1, other arithmetic: 0.02 us -> 0.96 us  [on_device(): jnp.concatenate([conv_kernel, conv_bias.reshape(1, -1), norm2_gain.reshap...]
    pallas_call x1, Pallas kernels: 1.7 us -> 0.76 us  [on_device(): pl.pallas_call(sum_kernel, out_shape=shape((width // dp, share), F32), in...]
    pallas_call x1 -> x2, Pallas kernels: 1.48 us -> 1.63 us  [the longest x1 1.54 us: on_device(): pl.pallas_call(functools.partial(probs_kernel, sizes, tm, head_size), out...]
  transfers between devices with their start and end apart: 11 -> 11, of which waited for: 7 -> 7; matrix products, arithmetic and copies ran while one was open for 1% -> 3% of each run, Pallas kernels for 9% -> 9%
where the time goes in v3:
time: 61.1 us; the launch traced here: 60.9 us
  waiting for transfers between devices  22.7 us (37%)
  Pallas kernels  17.7 us (29%)
  starting transfers between devices  15.7 us (26%)
  local copies, waits for them, and re-layouts  3.07 us (5%)
  other arithmetic  0.96 us (2%)
  between operations  0.82 us (1%)
    ppermute x9, waiting for transfers between devices, swap(): return lax.ppermute(value, axis, [(i, i ^ m) for i in range(size)])  17 us
    ppermute x9, starting transfers between devices, swap(): return lax.ppermute(value, axis, [(i, i ^ m) for i in range(size)])  13.7 us
    pallas_call x1, Pallas kernels, on_device(): pl.pallas_call(functools.partial(forward_kernel, sizes, tm, head_size), o...  7.55 us
    ppermute x1, waiting for transfers between devices, on_device(): handed = lax.ppermute(passed, 'tm', [(1, 0), (2, 3)])  5.75 us
    pallas_call x4, Pallas kernels, project(): pl.pallas_call(functools.partial(project_kernel, (1, 2) if two else ()),...  5.22 us
    pallas_call x1, Pallas kernels, on_device(): pl.pallas_call(functools.partial(backward_kernel, sizes, tm, width // dp,...  2.42 us
    unnamed x12, local copies, waits for them, and re-layouts  2.29 us
    pallas_call x1, Pallas kernels, on_device(): pl.pallas_call(functools.partial(probs_kernel, sizes, tm, head_size), out...  1.54 us
  transfers between devices with their start and end apart: 11, of which 7 were waited for; matrix products, arithmetic and copies ran while one was open for 3% of the time, Pallas kernels for 9%

profile of v3, /device:TPU:0, one launch (start us, length us, event | category | flops | bytes accessed | tf_op | source)
XLA Modules:
  0.0 60.9 jit_solution(12732281856627760832)
XLA Ops:
  0.6 0.0 copy-start.3
  0.6 0.0 copy-start.1
  0.7 4.1 %collective-permute-start = (bf16[128,1024]{1,0:T(8,128)(2,1)}, bf16[128,1024]{1,0:T(8,128)(2,1)S(1)}, u32[]{:S(2)}, u32[]{:S(2)}) collective-permute-start(bf16[128,1024]{1,0:T(8,128)(2,1)} %refs_5_.1), channel_id=1, source_target_pairs={{0,2},{1,3},{2,0},{3,1},{4,6},{5,7},{6,4},{7,5},{8,10},{9,11},{10,... | collective-permute-start | bytes 786440 | tf_op jit(solution)/shard_map/ppermute | solution.py:398
  4.8 1.6 %collective-permute-start.1 = (bf16[128,1024]{1,0:T(8,128)(2,1)}, bf16[128,1024]{1,0:T(8,128)(2,1)S(1)}, u32[]{:S(2)}, u32[]{:S(2)}) collective-permute-start(bf16[128,1024]{1,0:T(8,128)(2,1)} %refs_5_.1), channel_id=1, source_target_pairs={{0,1},{1,0},{2,3},{3,2},{4,5},{5,4},{6,7},{7,6},{8,9},{9,8},{10,11... | collective-permute-start | bytes 786440 | tf_op jit(solution)/shard_map/ppermute | solution.py:398
  6.3 0.8 %concatenate.6.refs_0_.meta_ref = s32[1,20]{1,0:T(1,128)S(1)} concatenate(s32[1,1]{1,0:T(1,128)} %bitcast, s32[1,1]{1,0:T(1,128)} %bitcast.1, s32[1,2]{1,0:T(1,128)} %param.21, s32[1,8]{1,0:T(1,128)} %param.22, s32[1,8]{1,0:T(1,128)} %param.23), dimensions={1} | concatenate | bytes 160 | tf_op jit(solution)/shard_map/concatenate | solution.py:400
  7.1 1.0 %pad_maximum_fusion.small_ref.refs_3_ = f32[33,1024]{1,0:T(8,128)S(1)} fusion(f32[1,1024]{1,0:T(1,128)} %bitcast.9, f32[1,1024]{1,0:T(1,128)} %bitcast.10, f32[31,1024]{1,0:T(8,128)} %param.19), kind=kLoop, calls=%fused_computation | loop fusion | flops 67584 | bytes 270336 | tf_op jit(solution)/shard_map/concatenate | solution.py:410
  8.1 0.1 spread_taps.1.refs_4_
  8.2 0.0 copy-done.3
  8.2 0.0 copy-done.1
  8.2 0.0 copy-start
  8.2 1.6 %copy-done = bf16[1024,1024]{1,0:T(8,128)(2,1)S(1)} copy-done((bf16[1024,1024]{1,0:T(8,128)(2,1)S(1)}, bf16[1024,1024]{1,0:T(8,128)(2,1)}, u32[]{:S(2)}) %copy-start) | copy-done | bytes 2097176
  9.8 0.0 copy-start.5
  9.8 0.7 %copy-done.5 = f32[1024]{0:T(1024)S(1)} copy-done((f32[1024]{0:T(1024)S(1)}, f32[1024]{0:T(1024)}, u32[]{:S(2)}) %copy-start.5) | copy-done | bytes 4120
  10.5 1.3 %project_rows_0.1 = (bf16[128,1024]{1,0:T(8,128)(2,1)S(1)}, bf16[128,512]{1,0:T(8,128)(2,1)S(1)}, bf16[128,1024]{1,0:T(8,128)(2,1)S(1)}) custom-call(s32[1,20]{1,0:T(1,128)S(1)} %concatenate.6.refs_0_.meta_ref, f32[1,1024]{1,0:T(1,128)S(1)} %bitcast.5, bf16[1024,512]{1,0:T(8,128)(2,1)S(1)} %copy-done.1, bf16[1024,1024]{1,0:T(8,128)(2,1)S(1)} %copy-done, ...), custom_call_target="tpu_custom_call" | custom-call | flops 402653184 | bytes 4194304 | tf_op jit(solution)/shard_map/project_rows_0/pallas_call | solution.py:433
  11.8 5.2 %collective-permute-done.refs_4_.refs_7_ = bf16[128,1024]{1,0:T(8,128)(2,1)S(1)} collective-permute-done((bf16[128,1024]{1,0:T(8,128)(2,1)}, bf16[128,1024]{1,0:T(8,128)(2,1)S(1)}, u32[]{:S(2)}, u32[]{:S(2)}) %collective-permute-start) | collective-permute-done | bytes 262176 | tf_op jit(solution)/shard_map/ppermute | solution.py:398
  17.0 0.7 %collective-permute-start.2 = (bf16[128,1024]{1,0:T(8,128)(2,1)S(1)}, bf16[128,1024]{1,0:T(8,128)(2,1)S(1)}, u32[]{:S(2)}, u32[]{:S(2)}) collective-permute-start(bf16[128,1024]{1,0:T(8,128)(2,1)S(1)} %copy-done.3), channel_id=1, source_target_pairs={{1,2},{2,1},{5,6},{6,5},{9,10},{10,9},{13,14},{14,13},{17,18},{18,... | collective-permute-start | bytes 786440 | tf_op jit(solution)/shard_map/ppermute | solution.py:454
  17.7 1.3 %collective-permute-start.3 = (bf16[128,1024]{1,0:T(8,128)(2,1)S(1)}, bf16[128,1024]{1,0:T(8,128)(2,1)S(1)}, u32[]{:S(2)}, u32[]{:S(2)}) collective-permute-start(bf16[128,1024]{1,0:T(8,128)(2,1)S(1)} %collective-permute-done.refs_4_.refs_7_), channel_id=1, source_target_pairs={{1,0},{2,3},{5,4},{6,7},{9,8},{10,11},{13,12},{14,15},{17,16},{18,... | collective-permute-start | bytes 786440 | tf_op jit(solution)/shard_map/ppermute | solution.py:455
  19.0 1.3 %project_rows_2.1 = (bf16[128,1024]{1,0:T(8,128)(2,1)S(1)}, bf16[128,512]{1,0:T(8,128)(2,1)S(1)}, bf16[128,1024]{1,0:T(8,128)(2,1)S(1)}) custom-call(s32[1,20]{1,0:T(1,128)S(1)} %concatenate.6.refs_0_.meta_ref, f32[1,1024]{1,0:T(1,128)S(1)} %bitcast.6, bf16[1024,512]{1,0:T(8,128)(2,1)S(1)} %copy-done.1, bf16[1024,1024]{1,0:T(8,128)(2,1)S(1)} %copy-done, ...), custom_call_target="tpu_custom_call" | custom-call | flops 402653184 | bytes 4194304 | tf_op jit(solution)/shard_map/project_rows_2/pallas_call | solution.py:433
  20.3 0.0 collective-permute-done.1.refs_4_.refs_6_
  20.3 1.3 %project_rows_1.1 = (bf16[128,1024]{1,0:T(8,128)(2,1)S(1)}, bf16[128,512]{1,0:T(8,128)(2,1)S(1)}, bf16[128,1024]{1,0:T(8,128)(2,1)S(1)}) custom-call(s32[1,20]{1,0:T(1,128)S(1)} %concatenate.6.refs_0_.meta_ref, f32[1,1024]{1,0:T(1,128)S(1)} %bitcast.7, bf16[1024,512]{1,0:T(8,128)(2,1)S(1)} %copy-done.1, bf16[1024,1024]{1,0:T(8,128)(2,1)S(1)} %copy-done, ...), custom_call_target="tpu_custom_call" | custom-call | flops 402653184 | bytes 4194304 | tf_op jit(solution)/shard_map/project_rows_1/pallas_call | solution.py:433
  21.6 0.0 copy-start.2
  21.6 0.0 copy-start.4
  21.6 0.0 collective-permute-done.2.refs_4_
  21.6 5.7 %collective-permute-done.3.refs_5_ = bf16[128,1024]{1,0:T(8,128)(2,1)S(1)} collective-permute-done((bf16[128,1024]{1,0:T(8,128)(2,1)S(1)}, bf16[128,1024]{1,0:T(8,128)(2,1)S(1)}, u32[]{:S(2)}, u32[]{:S(2)}) %collective-permute-start.3) | collective-permute-done | bytes 262176 | tf_op jit(solution)/shard_map/ppermute | solution.py:455
  27.4 1.3 %project_rows_3.1 = (bf16[128,1024]{1,0:T(8,128)(2,1)S(1)}, bf16[128,512]{1,0:T(8,128)(2,1)S(1)}, bf16[128,1024]{1,0:T(8,128)(2,1)S(1)}, bf16[128,1024]{1,0:T(8,128)(2,1)S(1)}) custom-call(s32[1,20]{1,0:T(1,128)S(1)} %concatenate.6.refs_0_.meta_ref, f32[1,1024]{1,0:T(1,128)S(1)} %bitcast.8, bf16[1024,512]{1,0:T(8,128)(2,1)S(1)} %copy-done.1, ...), custom_call_target="tpu_custom_call" | custom-call | flops 402653184 | bytes 4194304 | tf_op jit(solution)/shard_map/project_rows_3/pallas_call | solution.py:433
  28.7 0.0 copy-done.2
  28.7 0.0 copy-done.4
  28.7 7.5 %forward_pass.1 = (bf16[128,1024]{1,0:T(8,128)(2,1)}, bf16[192,256]{1,0:T(8,128)(2,1)S(1)}, bf16[192,256]{1,0:T(8,128)(2,1)S(1)}, bf16[192,256]{1,0:T(8,128)(2,1)S(1)}, bf16[192,256]{1,0:T(8,128)(2,1)S(1)}) custom-call(s32[1,20]{1,0:T(1,128)S(1)} %concatenate.6.refs_0_.meta_ref, bf16[128,1024]{1,0:T(8,128)(2,1)S(1)} %copy-done.4, ...), custom_call_target="tpu_custom_call" | custom-call | tf_op jit(solution)/shard_map/forward_pass/pallas_call | solution.py:467
  36.3 0.4 collective-permute-start.4
  36.7 4.0 %collective-permute-start.5 = (bf16[192,256]{1,0:T(8,128)(2,1)S(1)}, bf16[192,256]{1,0:T(8,128)(2,1)S(1)}, u32[]{:S(2)}, u32[]{:S(2)}) collective-permute-start(bf16[192,256]{1,0:T(8,128)(2,1)S(1)} %get-tuple-element.58), channel_id=1, source_target_pairs={{0,2},{1,3},{2,0},{3,1},{4,6},{5,7},{6,4},{7,5},{8,10},{9,11},{10,... | collective-permute-start | bytes 294920 | tf_op jit(solution)/shard_map/ppermute | solution.py:398
  40.7 0.0 collective-permute-start.6
  40.7 1.5 %window_probs.1 = (bf16[704,256]{1,0:T(8,128)(2,1)S(1)}, bf16[704,256]{1,0:T(8,128)(2,1)S(1)}, f32[8,192,256]{2,1,0:T(8,128)S(1)}, f32[8,192,256]{2,1,0:T(8,128)S(1)}) custom-call(s32[1,20]{1,0:T(1,128)S(1)} %concatenate.6.refs_0_.meta_ref, bf16[128,512]{1,0:T(8,128)(2,1)S(1)} %get-tuple-element.39.refs_9_.refs_0_, ...), custom_call_target="tpu_custom_call" | custom-call | flops 2000000000 | bytes 4000000 | tf_op jit(solution)/shard_map/window_probs/pallas_call | solution.py:492
  42.2 0.0 collective-permute-done.4.refs_10_
  42.2 5.6 %collective-permute-done.5.refs_11_ = bf16[192,256]{1,0:T(8,128)(2,1)S(1)} collective-permute-done((bf16[192,256]{1,0:T(8,128)(2,1)S(1)}, bf16[192,256]{1,0:T(8,128)(2,1)S(1)}, u32[]{:S(2)}, u32[]{:S(2)}) %collective-permute-start.5) | collective-permute-done | bytes 98336 | tf_op jit(solution)/shard_map/ppermute | solution.py:398
  47.8 0.0 collective-permute-done.6.refs_12_
  47.8 2.4 %key_value_terms.1 = (f32[256,512]{1,0:T(8,128)S(1)}, bf16[256,512]{1,0:T(8,128)(2,1)S(1)}) custom-call(s32[1,20]{1,0:T(1,128)S(1)} %concatenate.6.refs_0_.meta_ref, bf16[704,256]{1,0:T(8,128)(2,1)S(1)} %get-tuple-element.48.refs_1_, bf16[704,256]{1,0:T(8,128)(2,1)S(1)} %get-tuple-element.49.refs_2_, f32[8,192,256]{2,1,0:T(8,128)S(1)} %get-tuple-element.50.refs_3_, ...), custom_call_target="tpu_custom_call" | custom-call | tf_op jit(solution)/shard_map/key_value_terms/pallas_call | solution.py:512
  50.2 0.1 collective-permute-start.7
  50.3 1.5 %collective-permute-done.7.got_ref = bf16[256,512]{1,0:T(8,128)(2,1)S(1)} collective-permute-done((bf16[256,512]{1,0:T(8,128)(2,1)S(1)}, bf16[256,512]{1,0:T(8,128)(2,1)S(1)}, u32[]{:S(2)}, u32[]{:S(2)}) %collective-permute-start.7) | collective-permute-done | bytes 262176 | tf_op jit(solution)/shard_map/ppermute | solution.py:398
  51.8 0.1 sum_pair.1
  51.9 1.5 %collective-permute-start.8 = (bf16[256,128]{1,0:T(8,128)(2,1)S(1)}, bf16[256,128]{1,0:T(8,128)(2,1)S(1)}, u32[]{:S(2)}, u32[]{:S(2)}) collective-permute-start(bf16[256,128]{1,0:T(8,128)(2,1)S(1)} %get-tuple-element.63), channel_id=1, source_target_pairs={{0,8},{4,12},{8,0},{12,4},{16,24},{20,28},{24,16},{28,20},{1,9},{5... | collective-permute-start | bytes 196616 | tf_op jit(solution)/shard_map/ppermute | solution.py:398
  53.4 1.5 %collective-permute-start.9 = (bf16[256,128]{1,0:T(8,128)(2,1)S(1)}, bf16[256,128]{1,0:T(8,128)(2,1)S(1)}, u32[]{:S(2)}, u32[]{:S(2)}) collective-permute-start(bf16[256,128]{1,0:T(8,128)(2,1)S(1)} %get-tuple-element.64), channel_id=1, source_target_pairs={{0,16},{4,20},{8,24},{12,28},{16,0},{20,4},{24,8},{28,12},{1,17},{... | collective-permute-start | bytes 196616 | tf_op jit(solution)/shard_map/ppermute | solution.py:398
  55.0 0.5 collective-permute-start.10
  55.5 0.8 %collective-permute-done.8.refs_1_ = bf16[256,128]{1,0:T(8,128)(2,1)S(1)} collective-permute-done((bf16[256,128]{1,0:T(8,128)(2,1)S(1)}, bf16[256,128]{1,0:T(8,128)(2,1)S(1)}, u32[]{:S(2)}, u32[]{:S(2)}) %collective-permute-start.8) | collective-permute-done | bytes 65568 | tf_op jit(solution)/shard_map/ppermute | solution.py:398
  56.2 1.5 %collective-permute-done.9.refs_2_ = bf16[256,128]{1,0:T(8,128)(2,1)S(1)} collective-permute-done((bf16[256,128]{1,0:T(8,128)(2,1)S(1)}, bf16[256,128]{1,0:T(8,128)(2,1)S(1)}, u32[]{:S(2)}, u32[]{:S(2)}) %collective-permute-start.9) | collective-permute-done | bytes 65568 | tf_op jit(solution)/shard_map/ppermute | solution.py:398
  57.7 2.4 %collective-permute-done.10.refs_3_ = bf16[256,128]{1,0:T(8,128)(2,1)S(1)} collective-permute-done((bf16[256,128]{1,0:T(8,128)(2,1)S(1)}, bf16[256,128]{1,0:T(8,128)(2,1)S(1)}, u32[]{:S(2)}, u32[]{:S(2)}) %collective-permute-start.10) | collective-permute-done | bytes 65568 | tf_op jit(solution)/shard_map/ppermute | solution.py:398
  60.1 0.8 %sum_groups.1 = f32[128,256]{1,0:T(8,128)} custom-call(bf16[256,128]{1,0:T(8,128)(2,1)S(1)} %get-tuple-element.62.refs_0_, bf16[256,128]{1,0:T(8,128)(2,1)S(1)} %collective-permute-done.8.refs_1_, bf16[256,128]{1,0:T(8,128)(2,1)S(1)} %collective-permute-done.9.refs_2_, bf16[256,128]{1,0:T(8,128)(2,1)S(1)} %collective-permute-done.10.refs_3_), custom_call_target="tpu_custom_call" | custom-call | tf_op jit(solution)/shard_map/sum_groups/pallas_call | solution.py:542
Async XLA Ops:
  0.6 7.5 %copy-start.3 = (bf16[128,1024]{1,0:T(8,128)(2,1)S(1)}, bf16[128,1024]{1,0:T(8,128)(2,1)}, u32[]{:S(2)}) copy-start(bf16[128,1024]{1,0:T(8,128)(2,1)} %refs_5_.1) | copy-start | bytes 786436
  0.6 7.5 %copy-start.1 = (bf16[1024,512]{1,0:T(8,128)(2,1)S(1)}, bf16[1024,512]{1,0:T(8,128)(2,1)}, u32[]{:S(2)}) copy-start(bf16[1024,512]{1,0:T(8,128)(2,1)} %refs_2_.8) | copy-start | bytes 3145732
  0.7 16.3 %collective-permute-start = (bf16[128,1024]{1,0:T(8,128)(2,1)}, bf16[128,1024]{1,0:T(8,128)(2,1)S(1)}, u32[]{:S(2)}, u32[]{:S(2)}) collective-permute-start(bf16[128,1024]{1,0:T(8,128)(2,1)} %refs_5_.1), channel_id=1, source_target_pairs={{0,2},{1,3},{2,0},{3,1},{4,6},{5,7},{6,4},{7,5},{8,10},{9,11},{10,... | collective-permute-start | bytes 786440 | tf_op jit(solution)/shard_map/ppermute | solution.py:398
  4.8 15.5 %collective-permute-start.1 = (bf16[128,1024]{1,0:T(8,128)(2,1)}, bf16[128,1024]{1,0:T(8,128)(2,1)S(1)}, u32[]{:S(2)}, u32[]{:S(2)}) collective-permute-start(bf16[128,1024]{1,0:T(8,128)(2,1)} %refs_5_.1), channel_id=1, source_target_pairs={{0,1},{1,0},{2,3},{3,2},{4,5},{5,4},{6,7},{7,6},{8,9},{9,8},{10,11... | collective-permute-start | bytes 786440 | tf_op jit(solution)/shard_map/ppermute | solution.py:398
  8.2 1.6 %copy-start = (bf16[1024,1024]{1,0:T(8,128)(2,1)S(1)}, bf16[1024,1024]{1,0:T(8,128)(2,1)}, u32[]{:S(2)}) copy-start(bf16[1024,1024]{1,0:T(8,128)(2,1)} %refs_3_.7) | copy-start | bytes 6291460
  9.8 0.7 %copy-start.5 = (f32[1024]{0:T(1024)S(1)}, f32[1024]{0:T(1024)}, u32[]{:S(2)}) copy-start(f32[1024]{0:T(1024)} %param.14) | copy-start | bytes 12292
  17.0 4.6 %collective-permute-start.2 = (bf16[128,1024]{1,0:T(8,128)(2,1)S(1)}, bf16[128,1024]{1,0:T(8,128)(2,1)S(1)}, u32[]{:S(2)}, u32[]{:S(2)}) collective-permute-start(bf16[128,1024]{1,0:T(8,128)(2,1)S(1)} %copy-done.3), channel_id=1, source_target_pairs={{1,2},{2,1},{5,6},{6,5},{9,10},{10,9},{13,14},{14,13},{17,18},{18,... | collective-permute-start | bytes 786440 | tf_op jit(solution)/shard_map/ppermute | solution.py:454
  17.7 9.7 %collective-permute-start.3 = (bf16[128,1024]{1,0:T(8,128)(2,1)S(1)}, bf16[128,1024]{1,0:T(8,128)(2,1)S(1)}, u32[]{:S(2)}, u32[]{:S(2)}) collective-permute-start(bf16[128,1024]{1,0:T(8,128)(2,1)S(1)} %collective-permute-done.refs_4_.refs_7_), channel_id=1, source_target_pairs={{1,0},{2,3},{5,4},{6,7},{9,8},{10,11},{13,12},{14,15},{17,16},{18,... | collective-permute-start | bytes 786440 | tf_op jit(solution)/shard_map/ppermute | solution.py:455
  21.6 7.1 %copy-start.2 = (bf16[512,1024]{1,0:T(8,128)(2,1)S(1)}, bf16[512,1024]{1,0:T(8,128)(2,1)}, u32[]{:S(2)}) copy-start(bf16[512,1024]{1,0:T(8,128)(2,1)} %refs_2_.9) | copy-start | bytes 3145732
  21.6 7.1 %copy-start.4 = (bf16[128,1024]{1,0:T(8,128)(2,1)S(1)}, bf16[128,1024]{1,0:T(8,128)(2,1)}, u32[]{:S(2)}) copy-start(bf16[128,1024]{1,0:T(8,128)(2,1)} %refs_1_.1) | copy-start | bytes 786436
  36.3 5.9 %collective-permute-start.4 = (bf16[192,256]{1,0:T(8,128)(2,1)S(1)}, bf16[192,256]{1,0:T(8,128)(2,1)S(1)}, u32[]{:S(2)}, u32[]{:S(2)}) collective-permute-start(bf16[192,256]{1,0:T(8,128)(2,1)S(1)} %get-tuple-element.57), channel_id=1, source_target_pairs={{0,1},{1,0},{2,3},{3,2},{4,5},{5,4},{6,7},{7,6},{8,9},{9,8},{10,11... | collective-permute-start | bytes 294920 | tf_op jit(solution)/shard_map/ppermute | solution.py:398
  36.7 11.1 %collective-permute-start.5 = (bf16[192,256]{1,0:T(8,128)(2,1)S(1)}, bf16[192,256]{1,0:T(8,128)(2,1)S(1)}, u32[]{:S(2)}, u32[]{:S(2)}) collective-permute-start(bf16[192,256]{1,0:T(8,128)(2,1)S(1)} %get-tuple-element.58), channel_id=1, source_target_pairs={{0,2},{1,3},{2,0},{3,1},{4,6},{5,7},{6,4},{7,5},{8,10},{9,11},{10,... | collective-permute-start | bytes 294920 | tf_op jit(solution)/shard_map/ppermute | solution.py:398
  40.7 7.1 %collective-permute-start.6 = (bf16[192,256]{1,0:T(8,128)(2,1)S(1)}, bf16[192,256]{1,0:T(8,128)(2,1)S(1)}, u32[]{:S(2)}, u32[]{:S(2)}) collective-permute-start(bf16[192,256]{1,0:T(8,128)(2,1)S(1)} %get-tuple-element.59), channel_id=1, source_target_pairs={{0,3},{1,2},{2,1},{3,0},{4,7},{5,6},{6,5},{7,4},{8,11},{9,10},{10,... | collective-permute-start | bytes 294920 | tf_op jit(solution)/shard_map/ppermute | solution.py:398
  50.2 1.6 %collective-permute-start.7 = (bf16[256,512]{1,0:T(8,128)(2,1)S(1)}, bf16[256,512]{1,0:T(8,128)(2,1)S(1)}, u32[]{:S(2)}, u32[]{:S(2)}) collective-permute-start(bf16[256,512]{1,0:T(8,128)(2,1)S(1)} %get-tuple-element.61), channel_id=1, source_target_pairs={{0,4},{4,0},{8,12},{12,8},{16,20},{20,16},{24,28},{28,24},{1,5},{5... | collective-permute-start | bytes 786440 | tf_op jit(solution)/shard_map/ppermute | solution.py:398
  51.9 4.3 %collective-permute-start.8 = (bf16[256,128]{1,0:T(8,128)(2,1)S(1)}, bf16[256,128]{1,0:T(8,128)(2,1)S(1)}, u32[]{:S(2)}, u32[]{:S(2)}) collective-permute-start(bf16[256,128]{1,0:T(8,128)(2,1)S(1)} %get-tuple-element.63), channel_id=1, source_target_pairs={{0,8},{4,12},{8,0},{12,4},{16,24},{20,28},{24,16},{28,20},{1,9},{5... | collective-permute-start | bytes 196616 | tf_op jit(solution)/shard_map/ppermute | solution.py:398
  53.4 4.3 %collective-permute-start.9 = (bf16[256,128]{1,0:T(8,128)(2,1)S(1)}, bf16[256,128]{1,0:T(8,128)(2,1)S(1)}, u32[]{:S(2)}, u32[]{:S(2)}) collective-permute-start(bf16[256,128]{1,0:T(8,128)(2,1)S(1)} %get-tuple-element.64), channel_id=1, source_target_pairs={{0,16},{4,20},{8,24},{12,28},{16,0},{20,4},{24,8},{28,12},{1,17},{... | collective-permute-start | bytes 196616 | tf_op jit(solution)/shard_map/ppermute | solution.py:398
  55.0 5.2 %collective-permute-start.10 = (bf16[256,128]{1,0:T(8,128)(2,1)S(1)}, bf16[256,128]{1,0:T(8,128)(2,1)S(1)}, u32[]{:S(2)}, u32[]{:S(2)}) collective-permute-start(bf16[256,128]{1,0:T(8,128)(2,1)S(1)} %get-tuple-element.65), channel_id=1, source_target_pairs={{0,24},{4,28},{8,16},{12,20},{16,8},{20,12},{24,0},{28,4},{1,25},{... | collective-permute-start | bytes 196616 | tf_op jit(solution)/shard_map/ppermute | solution.py:398

commit v4 on v3

--- a/solution.py
+++ b/solution.py
@@ -118,17 +118,18 @@
         taps_ref[j * SUB : (j + 1) * SUB] = rows
 
 
-def project_kernel(crossed_at, *refs):
-    meta_ref, g1_ref, wq_ref, wkv_ref = refs[:4]
+def project_kernel(crossed_at, count, *refs):
+    me_ref, g1_ref, wq_ref, wkv_ref = refs[:4]
+    parts = refs[4 : 4 + count]
+    x_ref, n_ref, q_ref, kv_ref = refs[4 + count :]
     if crossed_at:
-        crossed_ref, handed_ref, n_ref, q_ref, kv_ref, x_ref = refs[4:]
-        me = meta_ref[0, 0]
+        me = me_ref[0, 0]
         middle = functools.reduce(jnp.logical_or, [me == t for t in crossed_at])
-        rows = jnp.where(middle, crossed_ref[...], handed_ref[...])
-        x_ref[...] = rows
+        handed = jnp.concatenate([ref[...] for ref in parts[1:]], axis=0)
+        rows = jnp.where(middle, parts[0][...], handed)
     else:
-        x_ref, n_ref, q_ref, kv_ref = refs[4:]
-        rows = x_ref[...]
+        rows = jnp.concatenate([ref[...] for ref in parts], axis=0)
+    x_ref[...] = rows
     unit, _ = norm_stats(rows.astype(F32))
     normed = (unit * g1_ref[...]).astype(BF16)
     n_ref[...] = normed
@@ -141,8 +142,9 @@
     x_refs, q_refs, kv_refs = (refs[5 + k * tm : 5 + (k + 1) * tm] for k in range(3))
     refs = refs[5 + 3 * tm :]
     out_ref = refs[0]
-    send_refs = refs[1 : 1 + tm]
-    q_ref, kv_ref, tail_s, ctx_s, e_s, h_s, u_s, gr_s, gc_s = refs[1 + tm :]
+    half = tm // 2
+    send_refs = refs[1 : 1 + half]
+    q_ref, kv_ref, tail_s, ctx_s, e_s, h_s, u_s, gr_s, gc_s = refs[1 + half :]
 
     table = Layout(meta_ref, *sizes)
     me = table.me()
@@ -150,7 +152,6 @@
     width = out_ref.shape[1]
     hq = q_ref.shape[1]
     share = send_refs[0].shape[1]
-    half = tm // 2
 
     for ref in (q_ref, kv_ref):
         ref[: PAD * BLOCK] = jnp.zeros((PAD * BLOCK, ref.shape[1]), BF16)
@@ -263,7 +264,7 @@
         own_grad = grad_ref[i * BLOCK : (i + 1) * BLOCK].astype(F32) + back[HALO:]
         gc_s[i * ROWS : i * ROWS + HALO] = back[:HALO].astype(BF16)
         gc_s[i * ROWS + HALO : (i + 1) * ROWS] = own_grad.astype(BF16)
-    for m in range(tm):
+    for m in range(half):
         at = pl.ds(pl.multiple_of(((me ^ m) % half) * share, share), share)
         send_refs[m][...] = dot_nt(gc_s[...], wo_ref[at]).astype(BF16)
 
@@ -397,9 +398,10 @@
     def swap(value, axis, size, m):
         return lax.ppermute(value, axis, [(i, i ^ m) for i in range(size)])
 
+    me = lax.axis_index("tm").astype(jnp.int32).reshape(1, 1)
     meta = jnp.concatenate(
         [
-            lax.axis_index("tm").astype(jnp.int32).reshape(1, 1),
+            me,
             lax.axis_index("dp").astype(jnp.int32).reshape(1, 1),
             utt_blocks,
             block_slot,
@@ -421,42 +423,45 @@
         in_specs=[vmem],
         out_specs=vmem,
         compiler_params=pltpu.CompilerParams(vmem_limit_bytes=8 << 20),
-        cost_estimate=pl.CostEstimate(flops=10**6, bytes_accessed=1 << 20, transcendentals=0),
+        cost_estimate=pl.CostEstimate(flops=1, bytes_accessed=1, transcendentals=0),
         name="spread_taps",
     )(small)
 
     x, normed, queries, keys_values = {}, {}, {}, {}
-    made = [shape((rows, w), BF16) for w in (width, hq, kv_width, width)]
-
-    def project(m, parts):
-        two = len(parts) == 2
+    made = [shape((rows, w), BF16) for w in (width, width, hq, kv_width)]
+
+    def project(m, parts, crossed_at=()):
         outs = pl.pallas_call(
-            functools.partial(project_kernel, (1, 2) if two else ()),
-            out_shape=made if two else made[:3],
+            functools.partial(project_kernel, crossed_at, len(parts)),
+            out_shape=made,
             in_specs=[smem] + [vmem] * (3 + len(parts)),
-            out_specs=[vmem] * (4 if two else 3),
+            out_specs=[vmem] * 4,
             compiler_params=pltpu.CompilerParams(vmem_limit_bytes=32 << 20),
-            cost_estimate=pl.CostEstimate(
-                flops=2 * rows * width * (hq + kv_width), bytes_accessed=4 << 20, transcendentals=0
-            ),
+            cost_estimate=pl.CostEstimate(flops=1, bytes_accessed=1, transcendentals=0),
             name=f"project_rows_{m}",
-        )(meta, norm1_gain.reshape(1, -1), w_query, w_kv, *parts)
-        normed[m], queries[m], keys_values[m] = outs[:3]
-        x[m] = outs[3] if two else parts[0]
-
-    project(0, (frames,))
+        )(me, norm1_gain.reshape(1, -1), w_query, w_kv, *parts)
+        x[m], normed[m], queries[m], keys_values[m] = outs
+
     if tm == 4:
-        facing = swap(frames, "tm", tm, 2)
-        beside = swap(frames, "tm", tm, 1)
-        later, passed, normed[0], taps = lax.optimization_barrier(
-            (frames, facing, normed[0], taps)
-        )
+        inward = [(1, 0), (2, 3)]
+        first, second = frames[: rows // 2], frames[rows // 2 :]
+        far_a = swap(first, "tm", tm, 2)
+        whole, first = lax.optimization_barrier((frames, first))
+        beside = swap(whole, "tm", tm, 1)
+        second, small = lax.optimization_barrier((second, small))
+        far_b = swap(second, "tm", tm, 2)
+        project(0, (frames,))
+        far_a, normed[0] = lax.optimization_barrier((far_a, normed[0]))
+        later, beside = lax.optimization_barrier((frames, beside))
+        handed_a = lax.ppermute(far_a, "tm", inward)
         crossed = lax.ppermute(later, "tm", [(1, 2), (2, 1)])
-        handed = lax.ppermute(passed, "tm", [(1, 0), (2, 3)])
-        project(2, (passed,))
         project(1, (beside,))
-        project(3, (crossed, handed))
+        far_b, handed_a, taps, meta = lax.optimization_barrier((far_b, handed_a, taps, meta))
+        handed_b = lax.ppermute(far_b, "tm", inward)
+        project(2, (far_a, far_b))
+        project(3, (crossed, handed_a, handed_b), (1, 2))
     else:
+        project(0, (frames,))
         for m in range(1, tm):
             project(m, (swap(frames, "tm", tm, m),))
 
@@ -467,9 +472,9 @@
     results = pl.pallas_call(
         functools.partial(forward_kernel, sizes, tm, head_size),
         out_shape=[shape((rows, width), BF16)]
-        + [shape((own_rows, share), BF16)] * tm,
+        + [shape((own_rows, share), BF16)] * (tm // 2),
         in_specs=[smem] + [vmem] * (4 + 3 * tm),
-        out_specs=[vmem] * (tm + 1),
+        out_specs=[vmem] * (tm // 2 + 1),
         scratch_shapes=[
             pltpu.VMEM((padded, hq), BF16),
             pltpu.VMEM((padded, kv_width), BF16),
@@ -485,8 +490,10 @@
         name="forward_pass",
     )(meta, out_grad, w_out, small, taps, *by_m(x), *by_m(queries), *by_m(keys_values))
     layer_out = results[0]
-    sends = results[1 : 1 + tm]
-    got = [sends[0]] + [swap(sends[m], "tm", tm, m) for m in range(1, tm)]
+    sends = results[1:]
+    got = {0: sends[0]}
+    for m in range(tm - 1, 0, -1):
+        got[m] = swap(sends[m % (tm // 2)], "tm", tm, m)
 
     pair_width = share // head_size * BLOCK
     q4, v4, probs, slopes = pl.pallas_call(
@@ -521,7 +528,7 @@
         ],
         compiler_params=pltpu.CompilerParams(vmem_limit_bytes=32 << 20),
         name="key_value_terms",
-    )(meta, q4, v4, probs, slopes, *by_m(normed), *got)
+    )(meta, q4, v4, probs, slopes, *by_m(normed), *by_m(got))
 
     if direct:
         kept, away = pieces
@@ -536,7 +543,8 @@
             compiler_params=pltpu.CompilerParams(vmem_limit_bytes=4 << 20),
             name="sum_pair",
         )(kept, arrived)
-        terms = [summed[0]] + [swap(summed[q], "dp", dp, 2 * q) for q in range(1, chips)]
+        terms = [swap(summed[q], "dp", dp, 2 * q) for q in range(chips - 1, 0, -1)]
+        terms.append(summed[0])
     else:
         terms = [lax.psum_scatter(pieces[0], "dp", scatter_dimension=1, tiled=True)]
     kv_grad = pl.pallas_call(

time: 61.1 us -> 63.2 us (1.034)
  waiting for transfers between devices: 22.7 us -> 15.7 us
  local copies, waits for them, and re-layouts: 3.07 us -> 9.03 us
  Pallas kernels: 17.7 us -> 19.1 us
  starting transfers between devices: 15.7 us -> 17.1 us
    ppermute x9 -> x10, waiting for transfers between devices: 17 us -> 10.3 us  [swap(): return lax.ppermute(value, axis, [(i, i ^ m) for i in range(size)])]
    unnamed x12 -> x42, local copies, waits for them, and re-layouts: 2.29 us -> 7.26 us
    pallas_call x4, Pallas kernels: 5.22 us -> 6.97 us  [project(): pl.pallas_call(functools.partial(project_kernel, crossed_at, len(parts)),...]
    slice x0 -> x1, local copies, waits for them, and re-layouts: none -> 1.67 us  [on_device(): first, second = (frames[:rows // 2], frames[rows // 2:])]
    ppermute x1 -> x2, starting transfers between devices: 1.29 us -> 2.56 us  [the longest x1 1.28 us: on_device(): handed_a = lax.ppermute(far_a, 'tm', inward)]
    ppermute x1, starting transfers between devices: 0.67 us -> 1.37 us  [on_device(): crossed = lax.ppermute(later, 'tm', [(1, 2), (2, 1)])]
    concatenate x1, local copies, waits for them, and re-layouts: 0.77 us -> 0.09 us  [on_device(): jnp.concatenate([me, lax.axis_index('dp').astype(jnp.int32).reshape(1, 1)...]
    ppermute x9 -> x10, starting transfers between devices: 13.7 us -> 13.1 us  [swap(): return lax.ppermute(value, axis, [(i, i ^ m) for i in range(size)])]
  transfers between devices with their start and end apart: 11 -> 13, of which waited for: 7 -> 7; matrix products, arithmetic and copies ran while one was open for 3% -> 2% of each run, Pallas kernels for 9% -> 11%
where the time goes in v4:
time: 63.2 us; the launch traced here: 62.8 us
  Pallas kernels  19.1 us (30%)
  starting transfers between devices  17.1 us (27%)
  waiting for transfers between devices  15.7 us (25%)
  local copies, waits for them, and re-layouts  9.03 us (14%)
  other arithmetic  0.95 us (2%)
  between operations  0.9 us (1%)
    ppermute x10, starting transfers between devices, swap(): return lax.ppermute(value, axis, [(i, i ^ m) for i in range(size)])  13.1 us
    ppermute x10, waiting for transfers between devices, swap(): return lax.ppermute(value, axis, [(i, i ^ m) for i in range(size)])  10.3 us
    pallas_call x1, Pallas kernels, on_device(): pl.pallas_call(functools.partial(forward_kernel, sizes, tm, head_size), o...  7.27 us
    unnamed x42, local copies, waits for them, and re-layouts  7.26 us
    pallas_call x4, Pallas kernels, project(): pl.pallas_call(functools.partial(project_kernel, crossed_at, len(parts)),...  6.97 us
    ppermute x1, waiting for transfers between devices, on_device(): handed_a = lax.ppermute(far_a, 'tm', inward)  3.34 us
    pallas_call x1, Pallas kernels, on_device(): pl.pallas_call(functools.partial(backward_kernel, sizes, tm, width // dp,...  2.42 us
    ppermute x1, waiting for transfers between devices, on_device(): handed_b = lax.ppermute(far_b, 'tm', inward)  2.08 us
  transfers between devices with their start and end apart: 13, of which 7 were waited for; matrix products, arithmetic and copies ran while one was open for 2% of the time, Pallas kernels for 11%

profile of v4, /device:TPU:0, one launch (start us, length us, event | category | flops | bytes accessed | tf_op | source)
XLA Modules:
  0.0 62.8 jit_solution(17240956268247449466)
XLA Ops:
  0.6 1.7 %fusion = (bf16[64,1024]{1,0:T(8,128)(2,1)}, bf16[64,1024]{1,0:T(8,128)(2,1)}) fusion(bf16[128,1024]{1,0:T(8,128)(2,1)} %refs_4_.1), kind=kLoop, calls=%fused_computation.1 | loop fusion | bytes 524288 | tf_op jit(solution)/shard_map/slice | solution.py:447
  2.3 3.0 %collective-permute-start.3 = (bf16[128,1024]{1,0:T(8,128)(2,1)}, bf16[128,1024]{1,0:T(8,128)(2,1)}, u32[]{:S(2)}, u32[]{:S(2)}) collective-permute-start(bf16[128,1024]{1,0:T(8,128)(2,1)} %refs_4_.1), channel_id=1, source_target_pairs={{0,1},{1,0},{2,3},{3,2},{4,5},{5,4},{6,7},{7,6},{8,9},{9,8},{10,11... | collective-permute-start | bytes 786440 | tf_op jit(solution)/shard_map/ppermute | solution.py:399
  5.3 2.6 %collective-permute-start.1 = (bf16[64,1024]{1,0:T(8,128)(2,1)}, bf16[64,1024]{1,0:T(8,128)(2,1)}, u32[]{:S(2)}, u32[]{:S(2)}) collective-permute-start(bf16[64,1024]{1,0:T(8,128)(2,1)} %get-tuple-element.82), channel_id=1, source_target_pairs={{0,2},{1,3},{2,0},{3,1},{4,6},{5,7},{6,4},{7,5},{8,10},{9,11},{10,... | collective-permute-start | bytes 393224 | tf_op jit(solution)/shard_map/ppermute | solution.py:399
  7.9 1.0 %pad_maximum_fusion.small_ref.refs_3_ = f32[33,1024]{1,0:T(8,128)S(1)} fusion(f32[1,1024]{1,0:T(1,128)} %bitcast.9, f32[1,1024]{1,0:T(1,128)} %bitcast.10, f32[31,1024]{1,0:T(8,128)} %param.19), kind=kLoop, calls=%fused_computation | loop fusion | flops 67584 | bytes 270336 | tf_op jit(solution)/shard_map/concatenate | solution.py:412
  8.9 0.4 collective-permute-start
  9.3 1.6 %copy-done = bf16[1024,1024]{1,0:T(8,128)(2,1)S(1)} copy-done((bf16[1024,1024]{1,0:T(8,128)(2,1)S(1)}, bf16[1024,1024]{1,0:T(8,128)(2,1)}, u32[]{:S(2)}) %copy-start) | copy-done | bytes 2097176
  10.9 1.2 %copy-done.2 = bf16[1024,512]{1,0:T(8,128)(2,1)S(1)} copy-done((bf16[1024,512]{1,0:T(8,128)(2,1)S(1)}, bf16[1024,512]{1,0:T(8,128)(2,1)}, u32[]{:S(2)}) %copy-start.2) | copy-done | bytes 1048600
  12.1 0.7 %copy-done.16 = f32[1024]{0:T(1024)S(1)} copy-done((f32[1024]{0:T(1024)S(1)}, f32[1024]{0:T(1024)}, u32[]{:S(2)}) %copy-start.16) | copy-done | bytes 4120
  12.8 0.0 copy-start.3
  12.8 0.0 copy-start.17
  12.8 1.9 %project_rows_0.1 = (bf16[128,1024]{1,0:T(8,128)(2,1)S(1)}, bf16[128,1024]{1,0:T(8,128)(2,1)S(1)}, bf16[128,512]{1,0:T(8,128)(2,1)S(1)}, bf16[128,1024]{1,0:T(8,128)(2,1)S(1)}) custom-call(s32[1,1]{1,0:T(1,128)} %bitcast.2.refs_0_, f32[1,1024]{1,0:T(1,128)S(1)} %bitcast.5, bf16[1024,512]{1,0:T(8,128)(2,1)S(1)} %copy-done.2, bf16[1024,1024]{1,0:T(8,128)(2,1)S(1)} %copy-done, ...), custom_call_target="tpu_custom_call" | custom-call | flops 1 | bytes 1 | tf_op jit(solution)/shard_map/project_rows_0/pallas_call | solution.py:434
  14.7 0.0 copy-start.7
  14.7 0.7 %copy-done.7 = bf16[128,1024]{1,0:T(8,128)(2,1)} copy-done((bf16[128,1024]{1,0:T(8,128)(2,1)}, bf16[128,1024]{1,0:T(8,128)(2,1)S(1)}, u32[]{:S(2)}) %copy-start.7) | copy-done | bytes 262168
  15.4 0.7 %copy-done.10 = bf16[128,1024]{1,0:T(8,128)(2,1)} copy-done((bf16[128,1024]{1,0:T(8,128)(2,1)}, bf16[128,1024]{1,0:T(8,128)(2,1)S(1)}, u32[]{:S(2)}) %copy-start.10) | copy-done | bytes 262168
  16.1 0.7 %copy-done.12 = bf16[128,1024]{1,0:T(8,128)(2,1)} copy-done((bf16[128,1024]{1,0:T(8,128)(2,1)}, bf16[128,1024]{1,0:T(8,128)(2,1)S(1)}, u32[]{:S(2)}) %copy-start.12) | copy-done | bytes 262168
  16.8 0.6 %copy-done.14 = bf16[128,512]{1,0:T(8,128)(2,1)} copy-done((bf16[128,512]{1,0:T(8,128)(2,1)}, bf16[128,512]{1,0:T(8,128)(2,1)S(1)}, u32[]{:S(2)}) %copy-start.14) | copy-done | bytes 131096
  17.4 0.0 collective-permute-done.1.refs_4_
  17.4 1.3 %collective-permute-start.2 = (bf16[64,1024]{1,0:T(8,128)(2,1)}, bf16[64,1024]{1,0:T(8,128)(2,1)}, u32[]{:S(2)}, u32[]{:S(2)}) collective-permute-start(bf16[64,1024]{1,0:T(8,128)(2,1)} %collective-permute-done.1.refs_4_), channel_id=1, source_target_pairs={{1,0},{2,3},{5,4},{6,7},{9,8},{10,11},{13,12},{14,15},{17,16},{18,... | collective-permute-start | bytes 393224 | tf_op jit(solution)/shard_map/ppermute | solution.py:456
  18.7 0.0 collective-permute-done.3.refs_4_
  18.7 1.4 %collective-permute-start.4 = (bf16[128,1024]{1,0:T(8,128)(2,1)}, bf16[128,1024]{1,0:T(8,128)(2,1)}, u32[]{:S(2)}, u32[]{:S(2)}) collective-permute-start(bf16[128,1024]{1,0:T(8,128)(2,1)} %refs_4_.1), channel_id=1, source_target_pairs={{1,2},{2,1},{5,6},{6,5},{9,10},{10,9},{13,14},{14,13},{17,18},{18,... | collective-permute-start | bytes 786440 | tf_op jit(solution)/shard_map/ppermute | solution.py:457
  20.1 0.1 spread_taps.1.refs_4_
  20.2 0.0 copy-start.4
  20.2 1.0 %copy-done.4 = f32[248,1024]{1,0:T(8,128)} copy-done((f32[248,1024]{1,0:T(8,128)}, f32[248,1024]{1,0:T(8,128)S(1)}, u32[]{:S(2)}) %copy-start.4) | copy-done | bytes 1015832
  21.2 0.0 copy-done.18
  21.2 0.0 copy-done.19
  21.2 0.0 copy-done.20
  21.2 0.1 concatenate.7.refs_0_.meta_ref
  21.3 0.0 collective-permute-done.refs_5_
  21.3 3.3 %collective-permute-done.2.refs_5_ = bf16[64,1024]{1,0:T(8,128)(2,1)} collective-permute-done((bf16[64,1024]{1,0:T(8,128)(2,1)}, bf16[64,1024]{1,0:T(8,128)(2,1)}, u32[]{:S(2)}, u32[]{:S(2)}) %collective-permute-start.2) | collective-permute-done | bytes 131104 | tf_op jit(solution)/shard_map/ppermute | solution.py:456
  24.6 1.3 %collective-permute-start.5 = (bf16[64,1024]{1,0:T(8,128)(2,1)S(1)}, bf16[64,1024]{1,0:T(8,128)(2,1)S(1)}, u32[]{:S(2)}, u32[]{:S(2)}) collective-permute-start(bf16[64,1024]{1,0:T(8,128)(2,1)S(1)} %collective-permute-done.refs_5_), channel_id=1, source_target_pairs={{1,0},{2,3},{5,4},{6,7},{9,8},{10,11},{13,12},{14,15},{17,16},{18,... | collective-permute-start | bytes 393224 | tf_op jit(solution)/shard_map/ppermute | solution.py:460
  25.9 0.0 copy-done.1
  25.9 0.0 copy-done.3
  25.9 0.0 copy-done.17
  25.9 1.7 %project_rows_2.1 = (bf16[128,1024]{1,0:T(8,128)(2,1)S(1)}, bf16[128,1024]{1,0:T(8,128)(2,1)S(1)}, bf16[128,512]{1,0:T(8,128)(2,1)S(1)}, bf16[128,1024]{1,0:T(8,128)(2,1)S(1)}) custom-call(s32[1,1]{1,0:T(1,128)} %bitcast.2.refs_0_, f32[1,1024]{1,0:T(1,128)S(1)} %bitcast.6, bf16[1024,512]{1,0:T(8,128)(2,1)S(1)} %copy-done.3, ...), custom_call_target="tpu_custom_call" | custom-call | flops 1 | bytes 1 | tf_op jit(solution)/shard_map/project_rows_2/pallas_call | solution.py:434
  27.6 1.7 %project_rows_1.1 = (bf16[128,1024]{1,0:T(8,128)(2,1)S(1)}, bf16[128,1024]{1,0:T(8,128)(2,1)S(1)}, bf16[128,512]{1,0:T(8,128)(2,1)S(1)}, bf16[128,1024]{1,0:T(8,128)(2,1)S(1)}) custom-call(s32[1,1]{1,0:T(1,128)} %bitcast.2.refs_0_, f32[1,1024]{1,0:T(1,128)S(1)} %bitcast.7, bf16[1024,512]{1,0:T(8,128)(2,1)S(1)} %copy-done.3, ...), custom_call_target="tpu_custom_call" | custom-call | flops 1 | bytes 1 | tf_op jit(solution)/shard_map/project_rows_1/pallas_call | solution.py:434
  29.3 0.0 copy-start.5
  29.3 0.0 copy-start.6
  29.3 0.0 copy-start.9
  29.3 0.0 copy-start.11
  29.3 0.0 copy-start.13
  29.4 0.0 copy-start.15
  29.4 2.1 %collective-permute-done.5.refs_6_ = bf16[64,1024]{1,0:T(8,128)(2,1)S(1)} collective-permute-done((bf16[64,1024]{1,0:T(8,128)(2,1)S(1)}, bf16[64,1024]{1,0:T(8,128)(2,1)S(1)}, u32[]{:S(2)}, u32[]{:S(2)}) %collective-permute-start.5) | collective-permute-done | bytes 131104 | tf_op jit(solution)/shard_map/ppermute | solution.py:460
  31.5 0.0 collective-permute-done.4.refs_4_
  31.5 1.7 %project_rows_3.1 = (bf16[128,1024]{1,0:T(8,128)(2,1)S(1)}, bf16[128,1024]{1,0:T(8,128)(2,1)S(1)}, bf16[128,512]{1,0:T(8,128)(2,1)S(1)}, bf16[128,1024]{1,0:T(8,128)(2,1)S(1)}) custom-call(s32[1,1]{1,0:T(1,128)} %bitcast.2.refs_0_, f32[1,1024]{1,0:T(1,128)S(1)} %bitcast.8, bf16[1024,512]{1,0:T(8,128)(2,1)S(1)} %copy-done.3, ...), custom_call_target="tpu_custom_call" | custom-call | flops 1 | bytes 1 | tf_op jit(solution)/shard_map/project_rows_3/pallas_call | solution.py:434
  33.2 0.0 copy-done.5
  33.3 7.3 %forward_pass.1 = (bf16[128,1024]{1,0:T(8,128)(2,1)}, bf16[192,256]{1,0:T(8,128)(2,1)S(1)}, bf16[192,256]{1,0:T(8,128)(2,1)S(1)}) custom-call(s32[1,20]{1,0:T(1,128)S(1)} %concatenate.7.refs_0_.meta_ref, bf16[128,1024]{1,0:T(8,128)(2,1)S(1)} %copy-done.9, bf16[512,1024]{1,0:T(8,128)(2,1)S(1)} %copy-done.6, f32[33,1024]{1,0:T(8,128)S(1)} %pad_maximum_fusion.small_ref.refs_3_, ...), custom_call_target="tpu_custom_call" | custom-call | tf_op jit(solution)/shard_map/forward_pass/pallas_call | solution.py:472
  40.5 0.7 %collective-permute-start.6 = (bf16[192,256]{1,0:T(8,128)(2,1)S(1)}, bf16[192,256]{1,0:T(8,128)(2,1)S(1)}, u32[]{:S(2)}, u32[]{:S(2)}) collective-permute-start(bf16[192,256]{1,0:T(8,128)(2,1)S(1)} %get-tuple-element.75), channel_id=1, source_target_pairs={{0,1},{1,0},{2,3},{3,2},{4,5},{5,4},{6,7},{7,6},{8,9},{9,8},{10,11... | collective-permute-start | bytes 294920 | tf_op jit(solution)/shard_map/ppermute | solution.py:399
  41.3 2.5 %collective-permute-start.8 = (bf16[192,256]{1,0:T(8,128)(2,1)S(1)}, bf16[192,256]{1,0:T(8,128)(2,1)S(1)}, u32[]{:S(2)}, u32[]{:S(2)}) collective-permute-start(bf16[192,256]{1,0:T(8,128)(2,1)S(1)} %get-tuple-element.75), channel_id=1, source_target_pairs={{0,3},{1,2},{2,1},{3,0},{4,7},{5,6},{6,5},{7,4},{8,11},{9,10},{10,... | collective-permute-start | bytes 294920 | tf_op jit(solution)/shard_map/ppermute | solution.py:399
  43.7 0.3 collective-permute-start.7
  44.0 1.5 %window_probs.1 = (bf16[704,256]{1,0:T(8,128)(2,1)S(1)}, bf16[704,256]{1,0:T(8,128)(2,1)S(1)}, f32[8,192,256]{2,1,0:T(8,128)S(1)}, f32[8,192,256]{2,1,0:T(8,128)S(1)}) custom-call(s32[1,20]{1,0:T(1,128)S(1)} %concatenate.7.refs_0_.meta_ref, bf16[128,512]{1,0:T(8,128)(2,1)S(1)} %copy-done.15, bf16[128,512]{1,0:T(8,128)(2,1)S(1)} %get-tuple-element.58.refs_10_.refs_1_, ...), custom_call_target="tpu_custom_call" | custom-call | flops 2000000000 | bytes 4000000 | tf_op jit(solution)/shard_map/window_probs/pallas_call | solution.py:499
  45.6 0.0 collective-permute-done.6.refs_10_
  45.6 5.1 %collective-permute-done.7.refs_11_ = bf16[192,256]{1,0:T(8,128)(2,1)S(1)} collective-permute-done((bf16[192,256]{1,0:T(8,128)(2,1)S(1)}, bf16[192,256]{1,0:T(8,128)(2,1)S(1)}, u32[]{:S(2)}, u32[]{:S(2)}) %collective-permute-start.7) | collective-permute-done | bytes 98336 | tf_op jit(solution)/shard_map/ppermute | solution.py:399
  50.6 0.0 collective-permute-done.8.refs_12_
  50.6 2.4 %key_value_terms.1 = (f32[256,512]{1,0:T(8,128)S(1)}, bf16[256,512]{1,0:T(8,128)(2,1)S(1)}) custom-call(s32[1,20]{1,0:T(1,128)S(1)} %concatenate.7.refs_0_.meta_ref, bf16[704,256]{1,0:T(8,128)(2,1)S(1)} %get-tuple-element.66.refs_1_, bf16[704,256]{1,0:T(8,128)(2,1)S(1)} %get-tuple-element.67.refs_2_, f32[8,192,256]{2,1,0:T(8,128)S(1)} %get-tuple-element.68.refs_3_, ...), custom_call_target="tpu_custom_call" | custom-call | tf_op jit(solution)/shard_map/key_value_terms/pallas_call | solution.py:519
  53.1 0.1 collective-permute-start.9
  53.2 1.5 %collective-permute-done.9.got_ref = bf16[256,512]{1,0:T(8,128)(2,1)S(1)} collective-permute-done((bf16[256,512]{1,0:T(8,128)(2,1)S(1)}, bf16[256,512]{1,0:T(8,128)(2,1)S(1)}, u32[]{:S(2)}, u32[]{:S(2)}) %collective-permute-start.9) | collective-permute-done | bytes 262176 | tf_op jit(solution)/shard_map/ppermute | solution.py:399
  54.7 0.1 sum_pair.1
  54.8 2.5 %collective-permute-start.10 = (bf16[256,128]{1,0:T(8,128)(2,1)S(1)}, bf16[256,128]{1,0:T(8,128)(2,1)S(1)}, u32[]{:S(2)}, u32[]{:S(2)}) collective-permute-start(bf16[256,128]{1,0:T(8,128)(2,1)S(1)} %get-tuple-element.78), channel_id=1, source_target_pairs={{0,24},{4,28},{8,16},{12,20},{16,8},{20,12},{24,0},{28,4},{1,25},{... | collective-permute-start | bytes 196616 | tf_op jit(solution)/shard_map/ppermute | solution.py:399
  57.3 0.5 collective-permute-start.11
  57.8 0.5 collective-permute-start.12
  58.3 1.7 %collective-permute-done.10.refs_0_ = bf16[256,128]{1,0:T(8,128)(2,1)S(1)} collective-permute-done((bf16[256,128]{1,0:T(8,128)(2,1)S(1)}, bf16[256,128]{1,0:T(8,128)(2,1)S(1)}, u32[]{:S(2)}, u32[]{:S(2)}) %collective-permute-start.10) | collective-permute-done | bytes 65568 | tf_op jit(solution)/shard_map/ppermute | solution.py:399
  60.0 1.5 %collective-permute-done.11.refs_1_ = bf16[256,128]{1,0:T(8,128)(2,1)S(1)} collective-permute-done((bf16[256,128]{1,0:T(8,128)(2,1)S(1)}, bf16[256,128]{1,0:T(8,128)(2,1)S(1)}, u32[]{:S(2)}, u32[]{:S(2)}) %collective-permute-start.11) | collective-permute-done | bytes 65568 | tf_op jit(solution)/shard_map/ppermute | solution.py:399
  61.5 0.5 collective-permute-done.12.refs_2_
  62.0 0.8 %sum_groups.1 = f32[128,256]{1,0:T(8,128)} custom-call(bf16[256,128]{1,0:T(8,128)(2,1)S(1)} %collective-permute-done.10.refs_0_, bf16[256,128]{1,0:T(8,128)(2,1)S(1)} %collective-permute-done.11.refs_1_, bf16[256,128]{1,0:T(8,128)(2,1)S(1)} %collective-permute-done.12.refs_2_, bf16[256,128]{1,0:T(8,128)(2,1)S(1)} %get-tuple-element.81.refs_3_), custom_call_target="tpu_custom_call" | custom-call | tf_op jit(solution)/shard_map/sum_groups/pallas_call | solution.py:550
  (17 shorter events, 0.0 us)
Async XLA Ops:
  2.3 16.4 %collective-permute-start.3 = (bf16[128,1024]{1,0:T(8,128)(2,1)}, bf16[128,1024]{1,0:T(8,128)(2,1)}, u32[]{:S(2)}, u32[]{:S(2)}) collective-permute-start(bf16[128,1024]{1,0:T(8,128)(2,1)} %refs_4_.1), channel_id=1, source_target_pairs={{0,1},{1,0},{2,3},{3,2},{4,5},{5,4},{6,7},{7,6},{8,9},{9,8},{10,11... | collective-permute-start | bytes 786440 | tf_op jit(solution)/shard_map/ppermute | solution.py:399
  5.3 12.1 %collective-permute-start.1 = (bf16[64,1024]{1,0:T(8,128)(2,1)}, bf16[64,1024]{1,0:T(8,128)(2,1)}, u32[]{:S(2)}, u32[]{:S(2)}) collective-permute-start(bf16[64,1024]{1,0:T(8,128)(2,1)} %get-tuple-element.82), channel_id=1, source_target_pairs={{0,2},{1,3},{2,0},{3,1},{4,6},{5,7},{6,4},{7,5},{8,10},{9,11},{10,... | collective-permute-start | bytes 393224 | tf_op jit(solution)/shard_map/ppermute | solution.py:399
  8.9 12.4 %collective-permute-start = (bf16[64,1024]{1,0:T(8,128)(2,1)}, bf16[64,1024]{1,0:T(8,128)(2,1)S(1)}, u32[]{:S(2)}, u32[]{:S(2)}) collective-permute-start(bf16[64,1024]{1,0:T(8,128)(2,1)} %get-tuple-element.42), channel_id=1, source_target_pairs={{0,2},{1,3},{2,0},{3,1},{4,6},{5,7},{6,4},{7,5},{8,10},{9,11},{10,... | collective-permute-start | bytes 393224 | tf_op jit(solution)/shard_map/ppermute | solution.py:399
  9.3 1.6 %copy-start = (bf16[1024,1024]{1,0:T(8,128)(2,1)S(1)}, bf16[1024,1024]{1,0:T(8,128)(2,1)}, u32[]{:S(2)}) copy-start(bf16[1024,1024]{1,0:T(8,128)(2,1)} %refs_3_.7) | copy-start | bytes 6291460
  10.9 1.2 %copy-start.2 = (bf16[1024,512]{1,0:T(8,128)(2,1)S(1)}, bf16[1024,512]{1,0:T(8,128)(2,1)}, u32[]{:S(2)}) copy-start(bf16[1024,512]{1,0:T(8,128)(2,1)} %refs_2_.8) | copy-start | bytes 3145732
  12.1 0.7 %copy-start.16 = (f32[1024]{0:T(1024)S(1)}, f32[1024]{0:T(1024)}, u32[]{:S(2)}) copy-start(f32[1024]{0:T(1024)} %param.14) | copy-start | bytes 12292
  12.8 8.4 %copy-start.18 = (s32[1,2]{1,0:T(1,128)S(1)}, s32[1,2]{1,0:T(1,128)}, u32[]{:S(2)}) copy-start(s32[1,2]{1,0:T(1,128)} %param.21) | copy-start | bytes 28
  12.8 8.4 %copy-start.19 = (s32[1,8]{1,0:T(1,128)S(1)}, s32[1,8]{1,0:T(1,128)}, u32[]{:S(2)}) copy-start(s32[1,8]{1,0:T(1,128)} %param.22) | copy-start | bytes 100
  12.8 8.4 %copy-start.20 = (s32[1,8]{1,0:T(1,128)S(1)}, s32[1,8]{1,0:T(1,128)}, u32[]{:S(2)}) copy-start(s32[1,8]{1,0:T(1,128)} %param.23) | copy-start | bytes 100
  12.8 13.1 %copy-start.1 = (bf16[1024,1024]{1,0:T(8,128)(2,1)S(1)}, bf16[1024,1024]{1,0:T(8,128)(2,1)}, u32[]{:S(2)}) copy-start(bf16[1024,1024]{1,0:T(8,128)(2,1)} %refs_3_.7) | copy-start | bytes 6291460
  12.8 13.1 %copy-start.3 = (bf16[1024,512]{1,0:T(8,128)(2,1)S(1)}, bf16[1024,512]{1,0:T(8,128)(2,1)}, u32[]{:S(2)}) copy-start(bf16[1024,512]{1,0:T(8,128)(2,1)} %refs_2_.8) | copy-start | bytes 3145732
  12.8 13.1 %copy-start.17 = (f32[1024]{0:T(1024)S(1)}, f32[1024]{0:T(1024)}, u32[]{:S(2)}) copy-start(f32[1024]{0:T(1024)} %param.14) | copy-start | bytes 12292
  14.7 0.7 %copy-start.7 = (bf16[128,1024]{1,0:T(8,128)(2,1)}, bf16[128,1024]{1,0:T(8,128)(2,1)S(1)}, u32[]{:S(2)}) copy-start(bf16[128,1024]{1,0:T(8,128)(2,1)S(1)} %get-tuple-element.70.refs_5_) | copy-start | bytes 786436
  15.4 0.7 %copy-start.10 = (bf16[128,1024]{1,0:T(8,128)(2,1)}, bf16[128,1024]{1,0:T(8,128)(2,1)S(1)}, u32[]{:S(2)}) copy-start(bf16[128,1024]{1,0:T(8,128)(2,1)S(1)} %get-tuple-element.61.refs_13_.refs_4_) | copy-start | bytes 786436
  16.1 0.7 %copy-start.12 = (bf16[128,1024]{1,0:T(8,128)(2,1)}, bf16[128,1024]{1,0:T(8,128)(2,1)S(1)}, u32[]{:S(2)}) copy-start(bf16[128,1024]{1,0:T(8,128)(2,1)S(1)} %get-tuple-element.48.refs_5_) | copy-start | bytes 786436
  16.8 0.6 %copy-start.14 = (bf16[128,512]{1,0:T(8,128)(2,1)}, bf16[128,512]{1,0:T(8,128)(2,1)S(1)}, u32[]{:S(2)}) copy-start(bf16[128,512]{1,0:T(8,128)(2,1)S(1)} %get-tuple-element.57.refs_9_.refs_0_) | copy-start | bytes 393220
  17.4 7.2 %collective-permute-start.2 = (bf16[64,1024]{1,0:T(8,128)(2,1)}, bf16[64,1024]{1,0:T(8,128)(2,1)}, u32[]{:S(2)}, u32[]{:S(2)}) collective-permute-start(bf16[64,1024]{1,0:T(8,128)(2,1)} %collective-permute-done.1.refs_4_), channel_id=1, source_target_pairs={{1,0},{2,3},{5,4},{6,7},{9,8},{10,11},{13,12},{14,15},{17,16},{18,... | collective-permute-start | bytes 393224 | tf_op jit(solution)/shard_map/ppermute | solution.py:456
  18.7 12.7 %collective-permute-start.4 = (bf16[128,1024]{1,0:T(8,128)(2,1)}, bf16[128,1024]{1,0:T(8,128)(2,1)}, u32[]{:S(2)}, u32[]{:S(2)}) collective-permute-start(bf16[128,1024]{1,0:T(8,128)(2,1)} %refs_4_.1), channel_id=1, source_target_pairs={{1,2},{2,1},{5,6},{6,5},{9,10},{10,9},{13,14},{14,13},{17,18},{18,... | collective-permute-start | bytes 786440 | tf_op jit(solution)/shard_map/ppermute | solution.py:457
  20.2 1.0 %copy-start.4 = (f32[248,1024]{1,0:T(8,128)}, f32[248,1024]{1,0:T(8,128)S(1)}, u32[]{:S(2)}) copy-start(f32[248,1024]{1,0:T(8,128)S(1)} %spread_taps.1.refs_4_) | copy-start | bytes 3047428
  24.6 6.8 %collective-permute-start.5 = (bf16[64,1024]{1,0:T(8,128)(2,1)S(1)}, bf16[64,1024]{1,0:T(8,128)(2,1)S(1)}, u32[]{:S(2)}, u32[]{:S(2)}) collective-permute-start(bf16[64,1024]{1,0:T(8,128)(2,1)S(1)} %collective-permute-done.refs_5_), channel_id=1, source_target_pairs={{1,0},{2,3},{5,4},{6,7},{9,8},{10,11},{13,12},{14,15},{17,16},{18,... | collective-permute-start | bytes 393224 | tf_op jit(solution)/shard_map/ppermute | solution.py:460
  29.3 3.9 %copy-start.5 = (f32[248,1024]{1,0:T(8,128)S(1)}, f32[248,1024]{1,0:T(8,128)}, u32[]{:S(2)}) copy-start(f32[248,1024]{1,0:T(8,128)} %copy-done.4) | copy-start | bytes 3047428
  29.3 3.9 %copy-start.6 = (bf16[512,1024]{1,0:T(8,128)(2,1)S(1)}, bf16[512,1024]{1,0:T(8,128)(2,1)}, u32[]{:S(2)}) copy-start(bf16[512,1024]{1,0:T(8,128)(2,1)} %refs_2_.9) | copy-start | bytes 3145732
  29.3 3.9 %copy-start.9 = (bf16[128,1024]{1,0:T(8,128)(2,1)S(1)}, bf16[128,1024]{1,0:T(8,128)(2,1)}, u32[]{:S(2)}) copy-start(bf16[128,1024]{1,0:T(8,128)(2,1)} %refs_1_.1) | copy-start | bytes 786436
  29.3 3.9 %copy-start.11 = (bf16[128,1024]{1,0:T(8,128)(2,1)S(1)}, bf16[128,1024]{1,0:T(8,128)(2,1)}, u32[]{:S(2)}) copy-start(bf16[128,1024]{1,0:T(8,128)(2,1)} %copy-done.10) | copy-start | bytes 786436
  29.3 3.9 %copy-start.13 = (bf16[128,1024]{1,0:T(8,128)(2,1)S(1)}, bf16[128,1024]{1,0:T(8,128)(2,1)}, u32[]{:S(2)}) copy-start(bf16[128,1024]{1,0:T(8,128)(2,1)} %copy-done.12) | copy-start | bytes 786436
  29.4 3.9 %copy-start.15 = (bf16[128,512]{1,0:T(8,128)(2,1)S(1)}, bf16[128,512]{1,0:T(8,128)(2,1)}, u32[]{:S(2)}) copy-start(bf16[128,512]{1,0:T(8,128)(2,1)} %copy-done.14) | copy-start | bytes 393220
  40.5 5.0 %collective-permute-start.6 = (bf16[192,256]{1,0:T(8,128)(2,1)S(1)}, bf16[192,256]{1,0:T(8,128)(2,1)S(1)}, u32[]{:S(2)}, u32[]{:S(2)}) collective-permute-start(bf16[192,256]{1,0:T(8,128)(2,1)S(1)} %get-tuple-element.75), channel_id=1, source_target_pairs={{0,1},{1,0},{2,3},{3,2},{4,5},{5,4},{6,7},{7,6},{8,9},{9,8},{10,11... | collective-permute-start | bytes 294920 | tf_op jit(solution)/shard_map/ppermute | solution.py:399
  41.3 9.4 %collective-permute-start.8 = (bf16[192,256]{1,0:T(8,128)(2,1)S(1)}, bf16[192,256]{1,0:T(8,128)(2,1)S(1)}, u32[]{:S(2)}, u32[]{:S(2)}) collective-permute-start(bf16[192,256]{1,0:T(8,128)(2,1)S(1)} %get-tuple-element.75), channel_id=1, source_target_pairs={{0,3},{1,2},{2,1},{3,0},{4,7},{5,6},{6,5},{7,4},{8,11},{9,10},{10,... | collective-permute-start | bytes 294920 | tf_op jit(solution)/shard_map/ppermute | solution.py:399
  43.7 6.9 %copy-start.8 = (bf16[128,1024]{1,0:T(8,128)(2,1)S(1)}, bf16[128,1024]{1,0:T(8,128)(2,1)}, u32[]{:S(2)}) copy-start(bf16[128,1024]{1,0:T(8,128)(2,1)} %copy-done.7) | copy-start | bytes 786436
  43.7 6.9 %collective-permute-start.7 = (bf16[192,256]{1,0:T(8,128)(2,1)S(1)}, bf16[192,256]{1,0:T(8,128)(2,1)S(1)}, u32[]{:S(2)}, u32[]{:S(2)}) collective-permute-start(bf16[192,256]{1,0:T(8,128)(2,1)S(1)} %get-tuple-element.74.refs_9_), channel_id=1, source_target_pairs={{0,2},{1,3},{2,0},{3,1},{4,6},{5,7},{6,4},{7,5},{8,10},{9,11},{10,... | collective-permute-start | bytes 294920 | tf_op jit(solution)/shard_map/ppermute | solution.py:399
  53.1 1.6 %collective-permute-start.9 = (bf16[256,512]{1,0:T(8,128)(2,1)S(1)}, bf16[256,512]{1,0:T(8,128)(2,1)S(1)}, u32[]{:S(2)}, u32[]{:S(2)}) collective-permute-start(bf16[256,512]{1,0:T(8,128)(2,1)S(1)} %get-tuple-element.77), channel_id=1, source_target_pairs={{0,4},{4,0},{8,12},{12,8},{16,20},{20,16},{24,28},{28,24},{1,5},{5... | collective-permute-start | bytes 786440 | tf_op jit(solution)/shard_map/ppermute | solution.py:399
  54.8 5.3 %collective-permute-start.10 = (bf16[256,128]{1,0:T(8,128)(2,1)S(1)}, bf16[256,128]{1,0:T(8,128)(2,1)S(1)}, u32[]{:S(2)}, u32[]{:S(2)}) collective-permute-start(bf16[256,128]{1,0:T(8,128)(2,1)S(1)} %get-tuple-element.78), channel_id=1, source_target_pairs={{0,24},{4,28},{8,16},{12,20},{16,8},{20,12},{24,0},{28,4},{1,25},{... | collective-permute-start | bytes 196616 | tf_op jit(solution)/shard_map/ppermute | solution.py:399
  57.3 4.3 %collective-permute-start.11 = (bf16[256,128]{1,0:T(8,128)(2,1)S(1)}, bf16[256,128]{1,0:T(8,128)(2,1)S(1)}, u32[]{:S(2)}, u32[]{:S(2)}) collective-permute-start(bf16[256,128]{1,0:T(8,128)(2,1)S(1)} %get-tuple-element.79), channel_id=1, source_target_pairs={{0,16},{4,20},{8,24},{12,28},{16,0},{20,4},{24,8},{28,12},{1,17},{... | collective-permute-start | bytes 196616 | tf_op jit(solution)/shard_map/ppermute | solution.py:399
  57.8 4.3 %collective-permute-start.12 = (bf16[256,128]{1,0:T(8,128)(2,1)S(1)}, bf16[256,128]{1,0:T(8,128)(2,1)S(1)}, u32[]{:S(2)}, u32[]{:S(2)}) collective-permute-start(bf16[256,128]{1,0:T(8,128)(2,1)S(1)} %get-tuple-element.80), channel_id=1, source_target_pairs={{0,8},{4,12},{8,0},{12,4},{16,24},{20,28},{24,16},{28,20},{1,9},{5... | collective-permute-start | bytes 196616 | tf_op jit(solution)/shard_map/ppermute | solution.py:399

commit v5 on v4

--- a/solution.py
+++ b/solution.py
@@ -118,19 +118,8 @@
         taps_ref[j * SUB : (j + 1) * SUB] = rows
 
 
-def project_kernel(crossed_at, count, *refs):
-    me_ref, g1_ref, wq_ref, wkv_ref = refs[:4]
-    parts = refs[4 : 4 + count]
-    x_ref, n_ref, q_ref, kv_ref = refs[4 + count :]
-    if crossed_at:
-        me = me_ref[0, 0]
-        middle = functools.reduce(jnp.logical_or, [me == t for t in crossed_at])
-        handed = jnp.concatenate([ref[...] for ref in parts[1:]], axis=0)
-        rows = jnp.where(middle, parts[0][...], handed)
-    else:
-        rows = jnp.concatenate([ref[...] for ref in parts], axis=0)
-    x_ref[...] = rows
-    unit, _ = norm_stats(rows.astype(F32))
+def project_kernel(x_ref, g1_ref, wq_ref, wkv_ref, n_ref, q_ref, kv_ref):
+    unit, _ = norm_stats(x_ref[...].astype(F32))
     normed = (unit * g1_ref[...]).astype(BF16)
     n_ref[...] = normed
     q_ref[...] = dot_nn(normed, wq_ref[...]).astype(BF16)
@@ -398,10 +387,9 @@
     def swap(value, axis, size, m):
         return lax.ppermute(value, axis, [(i, i ^ m) for i in range(size)])
 
-    me = lax.axis_index("tm").astype(jnp.int32).reshape(1, 1)
     meta = jnp.concatenate(
         [
-            me,
+            lax.axis_index("tm").astype(jnp.int32).reshape(1, 1),
             lax.axis_index("dp").astype(jnp.int32).reshape(1, 1),
             utt_blocks,
             block_slot,
@@ -423,47 +411,41 @@
         in_specs=[vmem],
         out_specs=vmem,
         compiler_params=pltpu.CompilerParams(vmem_limit_bytes=8 << 20),
-        cost_estimate=pl.CostEstimate(flops=1, bytes_accessed=1, transcendentals=0),
+        cost_estimate=pl.CostEstimate(flops=10**6, bytes_accessed=1 << 20, transcendentals=0),
         name="spread_taps",
     )(small)
 
     x, normed, queries, keys_values = {}, {}, {}, {}
-    made = [shape((rows, w), BF16) for w in (width, width, hq, kv_width)]
-
-    def project(m, parts, crossed_at=()):
-        outs = pl.pallas_call(
-            functools.partial(project_kernel, crossed_at, len(parts)),
+    made = [shape((rows, w), BF16) for w in (width, hq, kv_width)]
+
+    def project(m, part):
+        x[m] = part
+        normed[m], queries[m], keys_values[m] = pl.pallas_call(
+            project_kernel,
             out_shape=made,
-            in_specs=[smem] + [vmem] * (3 + len(parts)),
-            out_specs=[vmem] * 4,
-            compiler_params=pltpu.CompilerParams(vmem_limit_bytes=32 << 20),
-            cost_estimate=pl.CostEstimate(flops=1, bytes_accessed=1, transcendentals=0),
+            in_specs=[vmem] * 4,
+            out_specs=[vmem] * 3,
+            compiler_params=pltpu.CompilerParams(vmem_limit_bytes=16 << 20),
+            cost_estimate=pl.CostEstimate(
+                flops=2 * rows * width * (hq + kv_width), bytes_accessed=4 << 20, transcendentals=0
+            ),
             name=f"project_rows_{m}",
-        )(me, norm1_gain.reshape(1, -1), w_query, w_kv, *parts)
-        x[m], normed[m], queries[m], keys_values[m] = outs
-
+        )(part, norm1_gain.reshape(1, -1), w_query, w_kv)
+
+    project(0, frames)
     if tm == 4:
-        inward = [(1, 0), (2, 3)]
-        first, second = frames[: rows // 2], frames[rows // 2 :]
-        far_a = swap(first, "tm", tm, 2)
-        whole, first = lax.optimization_barrier((frames, first))
-        beside = swap(whole, "tm", tm, 1)
-        second, small = lax.optimization_barrier((second, small))
-        far_b = swap(second, "tm", tm, 2)
-        project(0, (frames,))
-        far_a, normed[0] = lax.optimization_barrier((far_a, normed[0]))
-        later, beside = lax.optimization_barrier((frames, beside))
-        handed_a = lax.ppermute(far_a, "tm", inward)
-        crossed = lax.ppermute(later, "tm", [(1, 2), (2, 1)])
-        project(1, (beside,))
-        far_b, handed_a, taps, meta = lax.optimization_barrier((far_b, handed_a, taps, meta))
-        handed_b = lax.ppermute(far_b, "tm", inward)
-        project(2, (far_a, far_b))
-        project(3, (crossed, handed_a, handed_b), (1, 2))
+        facing = swap(frames, "tm", tm, 2)
+        beside = swap(frames, "tm", tm, 1)
+        facing, normed[0], taps, meta = lax.optimization_barrier(
+            (facing, normed[0], taps, meta)
+        )
+        across = swap(facing, "tm", tm, 1)
+        project(2, facing)
+        project(1, beside)
+        project(3, across)
     else:
-        project(0, (frames,))
         for m in range(1, tm):
-            project(m, (swap(frames, "tm", tm, m),))
+            project(m, swap(frames, "tm", tm, m))
 
     def by_m(arrays):
         return [arrays[m] for m in range(tm)]

time: 63.2 us -> 58 us (0.918)
  waiting for transfers between devices: 15.7 us -> 22.9 us
  local copies, waits for them, and re-layouts: 9.03 us -> 3.07 us
  Pallas kernels: 19.1 us -> 15.2 us
  starting transfers between devices: 17.1 us -> 14.8 us
    ppermute x10, waiting for transfers between devices: 10.3 us -> 22.9 us  [swap(): return lax.ppermute(value, axis, [(i, i ^ m) for i in range(size)])]
    ppermute x3 -> x0, waiting for transfers between devices: 5.42 us -> none  [the longest x1 3.34 us: on_device(): handed_a = lax.ppermute(far_a, 'tm', inward)]
    unnamed x42 -> x14, local copies, waits for them, and re-layouts: 7.26 us -> 2.3 us
    pallas_call x4, Pallas kernels: 6.97 us -> 3.03 us  [project(): pl.pallas_call(project_kernel, out_shape=made, in_specs=[vmem] * 4, out_s...]
    ppermute x3 -> x0, starting transfers between devices: 3.93 us -> none  [the longest x1 1.37 us: on_device(): crossed = lax.ppermute(later, 'tm', [(1, 2), (2, 1)])]
    ppermute x10, starting transfers between devices: 13.1 us -> 14.8 us  [swap(): return lax.ppermute(value, axis, [(i, i ^ m) for i in range(size)])]
    slice x1 -> x0, local copies, waits for them, and re-layouts: 1.67 us -> none  [on_device(): first, second = (frames[:rows // 2], frames[rows // 2:])]
    concatenate x1, local copies, waits for them, and re-layouts: 0.09 us -> 0.77 us  [on_device(): jnp.concatenate([lax.axis_index('tm').astype(jnp.int32).reshape(1, 1), la...]
  transfers between devices with their start and end apart: 13 -> 10, of which waited for: 7 -> 7; matrix products, arithmetic and copies ran while one was open for 2% -> 3% of each run, Pallas kernels for 11% -> 7%
where the time goes in v5:
time: 58 us; the launch traced here: 57.7 us
  waiting for transfers between devices  22.9 us (39%)
  Pallas kernels  15.2 us (26%)
  starting transfers between devices  14.8 us (26%)
  local copies, waits for them, and re-layouts  3.07 us (5%)
  other arithmetic  0.96 us (2%)
  between operations  0.8 us (1%)
    ppermute x10, waiting for transfers between devices, swap(): return lax.ppermute(value, axis, [(i, i ^ m) for i in range(size)])  22.9 us
    ppermute x10, starting transfers between devices, swap(): return lax.ppermute(value, axis, [(i, i ^ m) for i in range(size)])  14.8 us
    pallas_call x1, Pallas kernels, on_device(): pl.pallas_call(functools.partial(forward_kernel, sizes, tm, head_size), o...  7.25 us
    pallas_call x4, Pallas kernels, project(): pl.pallas_call(project_kernel, out_shape=made, in_specs=[vmem] * 4, out_s...  3.03 us
    pallas_call x1, Pallas kernels, on_device(): pl.pallas_call(functools.partial(backward_kernel, sizes, tm, width // dp,...  2.43 us
    unnamed x14, local copies, waits for them, and re-layouts  2.3 us
    pallas_call x1, Pallas kernels, on_device(): pl.pallas_call(functools.partial(probs_kernel, sizes, tm, head_size), out...  1.54 us
  transfers between devices with their start and end apart: 10, of which 7 were waited for; matrix products, arithmetic and copies ran while one was open for 3% of the time, Pallas kernels for 7%

profile of v5, /device:TPU:0, one launch (start us, length us, event | category | flops | bytes accessed | tf_op | source)
XLA Modules:
  0.0 57.7 jit_solution(4421132450172934754)
XLA Ops:
  0.6 0.0 copy-start.4
  0.6 0.0 copy-start.2
  0.7 4.1 %collective-permute-start = (bf16[128,1024]{1,0:T(8,128)(2,1)}, bf16[128,1024]{1,0:T(8,128)(2,1)S(1)}, u32[]{:S(2)}, u32[]{:S(2)}) collective-permute-start(bf16[128,1024]{1,0:T(8,128)(2,1)} %refs_5_.1), channel_id=1, source_target_pairs={{0,2},{1,3},{2,0},{3,1},{4,6},{5,7},{6,4},{7,5},{8,10},{9,11},{10,... | collective-permute-start | bytes 786440 | tf_op jit(solution)/shard_map/ppermute | solution.py:388
  4.8 1.6 %collective-permute-start.1 = (bf16[128,1024]{1,0:T(8,128)(2,1)}, bf16[128,1024]{1,0:T(8,128)(2,1)S(1)}, u32[]{:S(2)}, u32[]{:S(2)}) collective-permute-start(bf16[128,1024]{1,0:T(8,128)(2,1)} %refs_5_.1), channel_id=1, source_target_pairs={{0,1},{1,0},{2,3},{3,2},{4,5},{5,4},{6,7},{7,6},{8,9},{9,8},{10,11... | collective-permute-start | bytes 786440 | tf_op jit(solution)/shard_map/ppermute | solution.py:388
  6.3 0.8 %concatenate.7.refs_0_.meta_ref = s32[1,20]{1,0:T(1,128)S(1)} concatenate(s32[1,1]{1,0:T(1,128)} %bitcast.3, s32[1,1]{1,0:T(1,128)} %bitcast.4, s32[1,2]{1,0:T(1,128)} %param.21, s32[1,8]{1,0:T(1,128)} %param.22, s32[1,8]{1,0:T(1,128)} %param.23), dimensions={1} | concatenate | bytes 160 | tf_op jit(solution)/shard_map/concatenate | solution.py:390
  7.1 1.0 %pad_maximum_fusion.small_ref.refs_3_ = f32[33,1024]{1,0:T(8,128)S(1)} fusion(f32[1,1024]{1,0:T(1,128)} %bitcast.9, f32[1,1024]{1,0:T(1,128)} %bitcast.10, f32[31,1024]{1,0:T(8,128)} %param.19), kind=kLoop, calls=%fused_computation | loop fusion | flops 67584 | bytes 270336 | tf_op jit(solution)/shard_map/concatenate | solution.py:400
  8.1 0.1 spread_taps.1.refs_4_
  8.2 0.0 copy-done.4
  8.2 0.0 copy-done.2
  8.2 0.0 copy-start
  8.2 1.6 %copy-done = bf16[1024,1024]{1,0:T(8,128)(2,1)S(1)} copy-done((bf16[1024,1024]{1,0:T(8,128)(2,1)S(1)}, bf16[1024,1024]{1,0:T(8,128)(2,1)}, u32[]{:S(2)}) %copy-start) | copy-done | bytes 2097176
  9.8 0.0 copy-start.6
  9.8 0.7 %copy-done.6 = f32[1024]{0:T(1024)S(1)} copy-done((f32[1024]{0:T(1024)S(1)}, f32[1024]{0:T(1024)}, u32[]{:S(2)}) %copy-start.6) | copy-done | bytes 4120
  10.5 0.0 copy-start.1
  10.5 0.8 %project_rows_0.1 = (bf16[128,1024]{1,0:T(8,128)(2,1)S(1)}, bf16[128,512]{1,0:T(8,128)(2,1)S(1)}, bf16[128,1024]{1,0:T(8,128)(2,1)S(1)}) custom-call(bf16[128,1024]{1,0:T(8,128)(2,1)S(1)} %copy-done.4, f32[1,1024]{1,0:T(1,128)S(1)} %bitcast.5, bf16[1024,512]{1,0:T(8,128)(2,1)S(1)} %copy-done.2, bf16[1024,1024]{1,0:T(8,128)(2,1)S(1)} %copy-done), custom_call_target="tpu_custom_call" | custom-call | flops 402653184 | bytes 4194304 | tf_op jit(solution)/shard_map/project_rows_0/pallas_call | solution.py:423
  11.2 5.8 %collective-permute-done.x_ref.refs_7_ = bf16[128,1024]{1,0:T(8,128)(2,1)S(1)} collective-permute-done((bf16[128,1024]{1,0:T(8,128)(2,1)}, bf16[128,1024]{1,0:T(8,128)(2,1)S(1)}, u32[]{:S(2)}, u32[]{:S(2)}) %collective-permute-start) | collective-permute-done | bytes 262176 | tf_op jit(solution)/shard_map/ppermute | solution.py:388
  17.0 0.7 %collective-permute-start.2 = (bf16[128,1024]{1,0:T(8,128)(2,1)S(1)}, bf16[128,1024]{1,0:T(8,128)(2,1)S(1)}, u32[]{:S(2)}, u32[]{:S(2)}) collective-permute-start(bf16[128,1024]{1,0:T(8,128)(2,1)S(1)} %collective-permute-done.x_ref.refs_7_), channel_id=1, source_target_pairs={{0,1},{1,0},{2,3},{3,2},{4,5},{5,4},{6,7},{7,6},{8,9},{9,8},{10,11... | collective-permute-start | bytes 786440 | tf_op jit(solution)/shard_map/ppermute | solution.py:388
  17.7 0.0 copy-done.1
  17.7 0.8 %project_rows_2.1 = (bf16[128,1024]{1,0:T(8,128)(2,1)S(1)}, bf16[128,512]{1,0:T(8,128)(2,1)S(1)}, bf16[128,1024]{1,0:T(8,128)(2,1)S(1)}) custom-call(bf16[128,1024]{1,0:T(8,128)(2,1)S(1)} %collective-permute-done.x_ref.refs_7_, f32[1,1024]{1,0:T(1,128)S(1)} %bitcast.6, bf16[1024,512]{1,0:T(8,128)(2,1)S(1)} %copy-done.2, bf16[1024,1024]{1,0:T(8,128)(2,1)S(1)} %copy-done.1), custom_call_target="tpu_custom_call" | custom-call | flops 402653184 | bytes 4194304 | tf_op jit(solution)/shard_map/project_rows_2/pallas_call | solution.py:423
  18.5 0.0 collective-permute-done.1.x_ref.refs_6_
  18.5 0.8 %project_rows_1.1 = (bf16[128,1024]{1,0:T(8,128)(2,1)S(1)}, bf16[128,512]{1,0:T(8,128)(2,1)S(1)}, bf16[128,1024]{1,0:T(8,128)(2,1)S(1)}) custom-call(bf16[128,1024]{1,0:T(8,128)(2,1)S(1)} %collective-permute-done.1.x_ref.refs_6_, f32[1,1024]{1,0:T(1,128)S(1)} %bitcast.7, bf16[1024,512]{1,0:T(8,128)(2,1)S(1)} %copy-done.2, bf16[1024,1024]{1,0:T(8,128)(2,1)S(1)} %copy-done.1), custom_call_target="tpu_custom_call" | custom-call | flops 402653184 | bytes 4194304 | tf_op jit(solution)/shard_map/project_rows_1/pallas_call | solution.py:423
  19.3 0.0 copy-start.3
  19.3 0.0 copy-start.5
  19.3 5.1 %collective-permute-done.2.x_ref.refs_8_ = bf16[128,1024]{1,0:T(8,128)(2,1)S(1)} collective-permute-done((bf16[128,1024]{1,0:T(8,128)(2,1)S(1)}, bf16[128,1024]{1,0:T(8,128)(2,1)S(1)}, u32[]{:S(2)}, u32[]{:S(2)}) %collective-permute-start.2) | collective-permute-done | bytes 262176 | tf_op jit(solution)/shard_map/ppermute | solution.py:388
  24.4 0.8 %project_rows_3.1 = (bf16[128,1024]{1,0:T(8,128)(2,1)S(1)}, bf16[128,512]{1,0:T(8,128)(2,1)S(1)}, bf16[128,1024]{1,0:T(8,128)(2,1)S(1)}) custom-call(bf16[128,1024]{1,0:T(8,128)(2,1)S(1)} %collective-permute-done.2.x_ref.refs_8_, f32[1,1024]{1,0:T(1,128)S(1)} %bitcast.8, bf16[1024,512]{1,0:T(8,128)(2,1)S(1)} %copy-done.2, bf16[1024,1024]{1,0:T(8,128)(2,1)S(1)} %copy-done.1), custom_call_target="tpu_custom_call" | custom-call | flops 402653184 | bytes 4194304 | tf_op jit(solution)/shard_map/project_rows_3/pallas_call | solution.py:423
  25.2 0.0 copy-done.3
  25.2 0.0 copy-done.5
  25.2 7.3 %forward_pass.1 = (bf16[128,1024]{1,0:T(8,128)(2,1)}, bf16[192,256]{1,0:T(8,128)(2,1)S(1)}, bf16[192,256]{1,0:T(8,128)(2,1)S(1)}) custom-call(s32[1,20]{1,0:T(1,128)S(1)} %concatenate.7.refs_0_.meta_ref, bf16[128,1024]{1,0:T(8,128)(2,1)S(1)} %copy-done.5, bf16[512,1024]{1,0:T(8,128)(2,1)S(1)} %copy-done.3, f32[33,1024]{1,0:T(8,128)S(1)} %pad_maximum_fusion.small_ref.refs_3_, ...), custom_call_target="tpu_custom_call" | custom-call | tf_op jit(solution)/shard_map/forward_pass/pallas_call | solution.py:454
  32.5 1.5 %collective-permute-start.3 = (bf16[192,256]{1,0:T(8,128)(2,1)S(1)}, bf16[192,256]{1,0:T(8,128)(2,1)S(1)}, u32[]{:S(2)}, u32[]{:S(2)}) collective-permute-start(bf16[192,256]{1,0:T(8,128)(2,1)S(1)} %get-tuple-element.53), channel_id=1, source_target_pairs={{0,1},{1,0},{2,3},{3,2},{4,5},{5,4},{6,7},{7,6},{8,9},{9,8},{10,11... | collective-permute-start | bytes 294920 | tf_op jit(solution)/shard_map/ppermute | solution.py:388
  34.0 3.0 %collective-permute-start.5 = (bf16[192,256]{1,0:T(8,128)(2,1)S(1)}, bf16[192,256]{1,0:T(8,128)(2,1)S(1)}, u32[]{:S(2)}, u32[]{:S(2)}) collective-permute-start(bf16[192,256]{1,0:T(8,128)(2,1)S(1)} %get-tuple-element.53), channel_id=1, source_target_pairs={{0,3},{1,2},{2,1},{3,0},{4,7},{5,6},{6,5},{7,4},{8,11},{9,10},{10,... | collective-permute-start | bytes 294920 | tf_op jit(solution)/shard_map/ppermute | solution.py:388
  37.0 0.3 collective-permute-start.4
  37.3 1.5 %window_probs.1 = (bf16[704,256]{1,0:T(8,128)(2,1)S(1)}, bf16[704,256]{1,0:T(8,128)(2,1)S(1)}, f32[8,192,256]{2,1,0:T(8,128)S(1)}, f32[8,192,256]{2,1,0:T(8,128)S(1)}) custom-call(s32[1,20]{1,0:T(1,128)S(1)} %concatenate.7.refs_0_.meta_ref, bf16[128,512]{1,0:T(8,128)(2,1)S(1)} %get-tuple-element.35.refs_9_.refs_0_, ...), custom_call_target="tpu_custom_call" | custom-call | flops 2000000000 | bytes 4000000 | tf_op jit(solution)/shard_map/window_probs/pallas_call | solution.py:481
  38.8 0.0 collective-permute-done.3.refs_10_
  38.8 6.8 %collective-permute-done.4.refs_11_ = bf16[192,256]{1,0:T(8,128)(2,1)S(1)} collective-permute-done((bf16[192,256]{1,0:T(8,128)(2,1)S(1)}, bf16[192,256]{1,0:T(8,128)(2,1)S(1)}, u32[]{:S(2)}, u32[]{:S(2)}) %collective-permute-start.4) | collective-permute-done | bytes 98336 | tf_op jit(solution)/shard_map/ppermute | solution.py:388
  45.6 0.0 collective-permute-done.5.refs_12_
  45.6 2.4 %key_value_terms.1 = (f32[256,512]{1,0:T(8,128)S(1)}, bf16[256,512]{1,0:T(8,128)(2,1)S(1)}) custom-call(s32[1,20]{1,0:T(1,128)S(1)} %concatenate.7.refs_0_.meta_ref, bf16[704,256]{1,0:T(8,128)(2,1)S(1)} %get-tuple-element.44.refs_1_, bf16[704,256]{1,0:T(8,128)(2,1)S(1)} %get-tuple-element.45.refs_2_, f32[8,192,256]{2,1,0:T(8,128)S(1)} %get-tuple-element.46.refs_3_, ...), custom_call_target="tpu_custom_call" | custom-call | tf_op jit(solution)/shard_map/key_value_terms/pallas_call | solution.py:501
  48.0 0.1 collective-permute-start.6
  48.1 1.5 %collective-permute-done.6.got_ref = bf16[256,512]{1,0:T(8,128)(2,1)S(1)} collective-permute-done((bf16[256,512]{1,0:T(8,128)(2,1)S(1)}, bf16[256,512]{1,0:T(8,128)(2,1)S(1)}, u32[]{:S(2)}, u32[]{:S(2)}) %collective-permute-start.6) | collective-permute-done | bytes 262176 | tf_op jit(solution)/shard_map/ppermute | solution.py:388
  49.6 0.1 sum_pair.1
  49.7 2.5 %collective-permute-start.7 = (bf16[256,128]{1,0:T(8,128)(2,1)S(1)}, bf16[256,128]{1,0:T(8,128)(2,1)S(1)}, u32[]{:S(2)}, u32[]{:S(2)}) collective-permute-start(bf16[256,128]{1,0:T(8,128)(2,1)S(1)} %get-tuple-element.56), channel_id=1, source_target_pairs={{0,24},{4,28},{8,16},{12,20},{16,8},{20,12},{24,0},{28,4},{1,25},{... | collective-permute-start | bytes 196616 | tf_op jit(solution)/shard_map/ppermute | solution.py:388
  52.2 0.5 collective-permute-start.8
  52.7 0.5 collective-permute-start.9
  53.3 1.7 %collective-permute-done.7.refs_0_ = bf16[256,128]{1,0:T(8,128)(2,1)S(1)} collective-permute-done((bf16[256,128]{1,0:T(8,128)(2,1)S(1)}, bf16[256,128]{1,0:T(8,128)(2,1)S(1)}, u32[]{:S(2)}, u32[]{:S(2)}) %collective-permute-start.7) | collective-permute-done | bytes 65568 | tf_op jit(solution)/shard_map/ppermute | solution.py:388
  55.0 1.5 %collective-permute-done.8.refs_1_ = bf16[256,128]{1,0:T(8,128)(2,1)S(1)} collective-permute-done((bf16[256,128]{1,0:T(8,128)(2,1)S(1)}, bf16[256,128]{1,0:T(8,128)(2,1)S(1)}, u32[]{:S(2)}, u32[]{:S(2)}) %collective-permute-start.8) | collective-permute-done | bytes 65568 | tf_op jit(solution)/shard_map/ppermute | solution.py:388
  56.5 0.5 collective-permute-done.9.refs_2_
  57.0 0.8 %sum_groups.1 = f32[128,256]{1,0:T(8,128)} custom-call(bf16[256,128]{1,0:T(8,128)(2,1)S(1)} %collective-permute-done.7.refs_0_, bf16[256,128]{1,0:T(8,128)(2,1)S(1)} %collective-permute-done.8.refs_1_, bf16[256,128]{1,0:T(8,128)(2,1)S(1)} %collective-permute-done.9.refs_2_, bf16[256,128]{1,0:T(8,128)(2,1)S(1)} %get-tuple-element.59.refs_3_), custom_call_target="tpu_custom_call" | custom-call | tf_op jit(solution)/shard_map/sum_groups/pallas_call | solution.py:532
Async XLA Ops:
  0.6 7.5 %copy-start.4 = (bf16[128,1024]{1,0:T(8,128)(2,1)S(1)}, bf16[128,1024]{1,0:T(8,128)(2,1)}, u32[]{:S(2)}) copy-start(bf16[128,1024]{1,0:T(8,128)(2,1)} %refs_5_.1) | copy-start | bytes 786436
  0.6 7.5 %copy-start.2 = (bf16[1024,512]{1,0:T(8,128)(2,1)S(1)}, bf16[1024,512]{1,0:T(8,128)(2,1)}, u32[]{:S(2)}) copy-start(bf16[1024,512]{1,0:T(8,128)(2,1)} %wq_ref.7) | copy-start | bytes 3145732
  0.7 16.3 %collective-permute-start = (bf16[128,1024]{1,0:T(8,128)(2,1)}, bf16[128,1024]{1,0:T(8,128)(2,1)S(1)}, u32[]{:S(2)}, u32[]{:S(2)}) collective-permute-start(bf16[128,1024]{1,0:T(8,128)(2,1)} %refs_5_.1), channel_id=1, source_target_pairs={{0,2},{1,3},{2,0},{3,1},{4,6},{5,7},{6,4},{7,5},{8,10},{9,11},{10,... | collective-permute-start | bytes 786440 | tf_op jit(solution)/shard_map/ppermute | solution.py:388
  4.8 13.7 %collective-permute-start.1 = (bf16[128,1024]{1,0:T(8,128)(2,1)}, bf16[128,1024]{1,0:T(8,128)(2,1)S(1)}, u32[]{:S(2)}, u32[]{:S(2)}) collective-permute-start(bf16[128,1024]{1,0:T(8,128)(2,1)} %refs_5_.1), channel_id=1, source_target_pairs={{0,1},{1,0},{2,3},{3,2},{4,5},{5,4},{6,7},{7,6},{8,9},{9,8},{10,11... | collective-permute-start | bytes 786440 | tf_op jit(solution)/shard_map/ppermute | solution.py:388
  8.2 1.6 %copy-start = (bf16[1024,1024]{1,0:T(8,128)(2,1)S(1)}, bf16[1024,1024]{1,0:T(8,128)(2,1)}, u32[]{:S(2)}) copy-start(bf16[1024,1024]{1,0:T(8,128)(2,1)} %wkv_ref.7) | copy-start | bytes 6291460
  9.8 0.7 %copy-start.6 = (f32[1024]{0:T(1024)S(1)}, f32[1024]{0:T(1024)}, u32[]{:S(2)}) copy-start(f32[1024]{0:T(1024)} %param.14) | copy-start | bytes 12292
  10.5 7.3 %copy-start.1 = (bf16[1024,1024]{1,0:T(8,128)(2,1)S(1)}, bf16[1024,1024]{1,0:T(8,128)(2,1)}, u32[]{:S(2)}) copy-start(bf16[1024,1024]{1,0:T(8,128)(2,1)} %wkv_ref.7) | copy-start | bytes 6291460
  17.0 7.4 %collective-permute-start.2 = (bf16[128,1024]{1,0:T(8,128)(2,1)S(1)}, bf16[128,1024]{1,0:T(8,128)(2,1)S(1)}, u32[]{:S(2)}, u32[]{:S(2)}) collective-permute-start(bf16[128,1024]{1,0:T(8,128)(2,1)S(1)} %collective-permute-done.x_ref.refs_7_), channel_id=1, source_target_pairs={{0,1},{1,0},{2,3},{3,2},{4,5},{5,4},{6,7},{7,6},{8,9},{9,8},{10,11... | collective-permute-start | bytes 786440 | tf_op jit(solution)/shard_map/ppermute | solution.py:388
  19.3 5.9 %copy-start.3 = (bf16[512,1024]{1,0:T(8,128)(2,1)S(1)}, bf16[512,1024]{1,0:T(8,128)(2,1)}, u32[]{:S(2)}) copy-start(bf16[512,1024]{1,0:T(8,128)(2,1)} %refs_2_.1) | copy-start | bytes 3145732
  19.3 5.9 %copy-start.5 = (bf16[128,1024]{1,0:T(8,128)(2,1)S(1)}, bf16[128,1024]{1,0:T(8,128)(2,1)}, u32[]{:S(2)}) copy-start(bf16[128,1024]{1,0:T(8,128)(2,1)} %refs_1_.1) | copy-start | bytes 786436
  32.5 6.3 %collective-permute-start.3 = (bf16[192,256]{1,0:T(8,128)(2,1)S(1)}, bf16[192,256]{1,0:T(8,128)(2,1)S(1)}, u32[]{:S(2)}, u32[]{:S(2)}) collective-permute-start(bf16[192,256]{1,0:T(8,128)(2,1)S(1)} %get-tuple-element.53), channel_id=1, source_target_pairs={{0,1},{1,0},{2,3},{3,2},{4,5},{5,4},{6,7},{7,6},{8,9},{9,8},{10,11... | collective-permute-start | bytes 294920 | tf_op jit(solution)/shard_map/ppermute | solution.py:388
  34.0 11.6 %collective-permute-start.5 = (bf16[192,256]{1,0:T(8,128)(2,1)S(1)}, bf16[192,256]{1,0:T(8,128)(2,1)S(1)}, u32[]{:S(2)}, u32[]{:S(2)}) collective-permute-start(bf16[192,256]{1,0:T(8,128)(2,1)S(1)} %get-tuple-element.53), channel_id=1, source_target_pairs={{0,3},{1,2},{2,1},{3,0},{4,7},{5,6},{6,5},{7,4},{8,11},{9,10},{10,... | collective-permute-start | bytes 294920 | tf_op jit(solution)/shard_map/ppermute | solution.py:388
  37.0 8.6 %collective-permute-start.4 = (bf16[192,256]{1,0:T(8,128)(2,1)S(1)}, bf16[192,256]{1,0:T(8,128)(2,1)S(1)}, u32[]{:S(2)}, u32[]{:S(2)}) collective-permute-start(bf16[192,256]{1,0:T(8,128)(2,1)S(1)} %get-tuple-element.52.refs_9_), channel_id=1, source_target_pairs={{0,2},{1,3},{2,0},{3,1},{4,6},{5,7},{6,4},{7,5},{8,10},{9,11},{10,... | collective-permute-start | bytes 294920 | tf_op jit(solution)/shard_map/ppermute | solution.py:388
  48.0 1.6 %collective-permute-start.6 = (bf16[256,512]{1,0:T(8,128)(2,1)S(1)}, bf16[256,512]{1,0:T(8,128)(2,1)S(1)}, u32[]{:S(2)}, u32[]{:S(2)}) collective-permute-start(bf16[256,512]{1,0:T(8,128)(2,1)S(1)} %get-tuple-element.55), channel_id=1, source_target_pairs={{0,4},{4,0},{8,12},{12,8},{16,20},{20,16},{24,28},{28,24},{1,5},{5... | collective-permute-start | bytes 786440 | tf_op jit(solution)/shard_map/ppermute | solution.py:388
  49.7 5.3 %collective-permute-start.7 = (bf16[256,128]{1,0:T(8,128)(2,1)S(1)}, bf16[256,128]{1,0:T(8,128)(2,1)S(1)}, u32[]{:S(2)}, u32[]{:S(2)}) collective-permute-start(bf16[256,128]{1,0:T(8,128)(2,1)S(1)} %get-tuple-element.56), channel_id=1, source_target_pairs={{0,24},{4,28},{8,16},{12,20},{16,8},{20,12},{24,0},{28,4},{1,25},{... | collective-permute-start | bytes 196616 | tf_op jit(solution)/shard_map/ppermute | solution.py:388
  52.2 4.3 %collective-permute-start.8 = (bf16[256,128]{1,0:T(8,128)(2,1)S(1)}, bf16[256,128]{1,0:T(8,128)(2,1)S(1)}, u32[]{:S(2)}, u32[]{:S(2)}) collective-permute-start(bf16[256,128]{1,0:T(8,128)(2,1)S(1)} %get-tuple-element.57), channel_id=1, source_target_pairs={{0,16},{4,20},{8,24},{12,28},{16,0},{20,4},{24,8},{28,12},{1,17},{... | collective-permute-start | bytes 196616 | tf_op jit(solution)/shard_map/ppermute | solution.py:388
  52.7 4.3 %collective-permute-start.9 = (bf16[256,128]{1,0:T(8,128)(2,1)S(1)}, bf16[256,128]{1,0:T(8,128)(2,1)S(1)}, u32[]{:S(2)}, u32[]{:S(2)}) collective-permute-start(bf16[256,128]{1,0:T(8,128)(2,1)S(1)} %get-tuple-element.58), channel_id=1, source_target_pairs={{0,8},{4,12},{8,0},{12,4},{16,24},{20,28},{24,16},{28,20},{1,9},{5... | collective-permute-start | bytes 196616 | tf_op jit(solution)/shard_map/ppermute | solution.py:388

commit v6 on v5

--- a/solution.py
+++ b/solution.py
@@ -119,6 +119,10 @@
 
 
 def project_kernel(x_ref, g1_ref, wq_ref, wkv_ref, n_ref, q_ref, kv_ref):
+    project(x_ref, g1_ref, wq_ref, wkv_ref, n_ref, q_ref, kv_ref)
+
+
+def project(x_ref, g1_ref, wq_ref, wkv_ref, n_ref, q_ref, kv_ref):
     unit, _ = norm_stats(x_ref[...].astype(F32))
     normed = (unit * g1_ref[...]).astype(BF16)
     n_ref[...] = normed
@@ -127,13 +131,20 @@
 
 
 def forward_kernel(sizes, tm, head_size, *refs):
-    meta_ref, grad_ref, wo_ref, small_ref, taps_ref = refs[:5]
-    x_refs, q_refs, kv_refs = (refs[5 + k * tm : 5 + (k + 1) * tm] for k in range(3))
-    refs = refs[5 + 3 * tm :]
-    out_ref = refs[0]
+    tables_ref, grad_ref, wo_ref, small_ref, taps_ref, g1_ref, wq_ref, wkv_ref = refs[:8]
+    refs = refs[8:]
+    x_refs = refs[:tm]
+    q_refs, kv_refs = (refs[tm + k * (tm - 1) : tm + (k + 1) * (tm - 1)] for k in range(2))
+    refs = refs[3 * tm - 2 :]
     half = tm // 2
-    send_refs = refs[1 : 1 + half]
-    q_ref, kv_ref, tail_s, ctx_s, e_s, h_s, u_s, gr_s, gc_s = refs[1 + half :]
+    out_ref, n_last, q_last, kv_last = refs[:4]
+    send_refs = refs[4 : 4 + tm][::-1]
+    q_ref, kv_ref, tail_s, ctx_s, e_s, h_s, u_s, gr_s, gc_s, meta_ref, sem = refs[4 + tm :]
+    fetch = pltpu.make_async_copy(tables_ref, meta_ref, sem)
+    fetch.start()
+    project(x_refs[-1], g1_ref, wq_ref, wkv_ref, n_last, q_last, kv_last)
+    q_refs, kv_refs = (*q_refs, q_last), (*kv_refs, kv_last)
+    fetch.wait()
 
     table = Layout(meta_ref, *sizes)
     me = table.me()
@@ -255,7 +266,9 @@
         gc_s[i * ROWS + HALO : (i + 1) * ROWS] = own_grad.astype(BF16)
     for m in range(half):
         at = pl.ds(pl.multiple_of(((me ^ m) % half) * share, share), share)
-        send_refs[m][...] = dot_nt(gc_s[...], wo_ref[at]).astype(BF16)
+        grad_context = dot_nt(gc_s[...], wo_ref[at]).astype(BF16)
+        send_refs[m][...] = grad_context
+        send_refs[m + half][...] = grad_context
 
 
 def probs_kernel(sizes, tm, head_size, meta_ref, *refs):
@@ -290,7 +303,7 @@
 def backward_kernel(sizes, tm, part, head_size, *refs):
     meta_ref, q4_ref, v4_ref, p_ref, d_ref = refs[:5]
     n_refs = refs[5 : 5 + tm]
-    g_refs = refs[5 + tm : 5 + 2 * tm]
+    g_refs = refs[5 + tm : 5 + 2 * tm][::-1]
     out_refs = refs[5 + 2 * tm : -3]
     gt_s, t_s, full_s = refs[-3:]
     table = Layout(meta_ref, *sizes)
@@ -418,8 +431,7 @@
     x, normed, queries, keys_values = {}, {}, {}, {}
     made = [shape((rows, w), BF16) for w in (width, hq, kv_width)]
 
-    def project(m, part):
-        x[m] = part
+    def project_shard(m, part):
         normed[m], queries[m], keys_values[m] = pl.pallas_call(
             project_kernel,
             out_shape=made,
@@ -432,31 +444,33 @@
             name=f"project_rows_{m}",
         )(part, norm1_gain.reshape(1, -1), w_query, w_kv)
 
-    project(0, frames)
+    project_shard(0, frames)
+    x[0] = frames
     if tm == 4:
-        facing = swap(frames, "tm", tm, 2)
-        beside = swap(frames, "tm", tm, 1)
-        facing, normed[0], taps, meta = lax.optimization_barrier(
-            (facing, normed[0], taps, meta)
-        )
-        across = swap(facing, "tm", tm, 1)
-        project(2, facing)
-        project(1, beside)
-        project(3, across)
+        x[2] = swap(frames, "tm", tm, 2)
+        own, small = lax.optimization_barrier((frames, small))
+        x[1] = swap(own, "tm", tm, 1)
+        facing, normed[0], taps, meta = lax.optimization_barrier((x[2], normed[0], taps, meta))
+        x[3] = swap(facing, "tm", tm, 1)
+        project_shard(2, facing)
+        project_shard(1, x[1])
     else:
         for m in range(1, tm):
-            project(m, swap(frames, "tm", tm, m))
+            x[m] = swap(frames, "tm", tm, m)
+            if m < tm - 1:
+                project_shard(m, x[m])
 
     def by_m(arrays):
-        return [arrays[m] for m in range(tm)]
+        return [arrays[m] for m in sorted(arrays)]
 
     own_rows = local * ROWS
     results = pl.pallas_call(
         functools.partial(forward_kernel, sizes, tm, head_size),
         out_shape=[shape((rows, width), BF16)]
-        + [shape((own_rows, share), BF16)] * (tm // 2),
-        in_specs=[smem] + [vmem] * (4 + 3 * tm),
-        out_specs=[vmem] * (tm // 2 + 1),
+        + made
+        + [shape((own_rows, share), BF16)] * tm,
+        in_specs=[pl.BlockSpec(memory_space=pl.ANY)] + [vmem] * (5 + 3 * tm),
+        out_specs=[vmem] * (tm + 4),
         scratch_shapes=[
             pltpu.VMEM((padded, hq), BF16),
             pltpu.VMEM((padded, kv_width), BF16),
@@ -467,15 +481,29 @@
             pltpu.VMEM((own_rows, width), F32),
             pltpu.VMEM((own_rows, width), F32),
             pltpu.VMEM((own_rows, width), BF16),
+            pltpu.SMEM(meta.shape, jnp.int32),
+            pltpu.SemaphoreType.DMA,
         ],
         compiler_params=pltpu.CompilerParams(vmem_limit_bytes=32 << 20),
         name="forward_pass",
-    )(meta, out_grad, w_out, small, taps, *by_m(x), *by_m(queries), *by_m(keys_values))
-    layer_out = results[0]
-    sends = results[1:]
+    )(
+        meta,
+        out_grad,
+        w_out,
+        small,
+        taps,
+        norm1_gain.reshape(1, -1),
+        w_query,
+        w_kv,
+        *by_m(x),
+        *by_m(queries),
+        *by_m(keys_values),
+    )
+    layer_out, normed[tm - 1], queries[tm - 1], keys_values[tm - 1] = results[:4]
+    sends = results[:3:-1]
     got = {0: sends[0]}
     for m in range(tm - 1, 0, -1):
-        got[m] = swap(sends[m % (tm // 2)], "tm", tm, m)
+        got[m] = swap(sends[m], "tm", tm, m)
 
     pair_width = share // head_size * BLOCK
     q4, v4, probs, slopes = pl.pallas_call(
@@ -510,7 +538,7 @@
         ],
         compiler_params=pltpu.CompilerParams(vmem_limit_bytes=32 << 20),
         name="key_value_terms",
-    )(meta, q4, v4, probs, slopes, *by_m(normed), *by_m(got))
+    )(meta, q4, v4, probs, slopes, *by_m(normed), *by_m(got)[::-1])
 
     if direct:
         kept, away = pieces

time: 58 us -> 56.1 us (0.967)
  waiting for transfers between devices: 22.9 us -> 21.4 us
  Pallas kernels: 15.2 us -> 14.6 us
    ppermute x10, waiting for transfers between devices: 22.9 us -> 21.4 us  [swap(): return lax.ppermute(value, axis, [(i, i ^ m) for i in range(size)])]
    pallas_call x4 -> x3, Pallas kernels: 3.03 us -> 2.27 us  [project_shard(): pl.pallas_call(project_kernel, out_shape=made, in_specs=[vmem] * 4, out_s...]
  transfers between devices with their start and end apart: 10 -> 10, of which waited for: 7 -> 8; matrix products, arithmetic and copies ran while one was open for 3% -> 3% of each run, Pallas kernels for 7% -> 7%
where the time goes in v6:
time: 56.1 us; the launch traced here: 55.9 us
  waiting for transfers between devices  21.4 us (38%)
  starting transfers between devices  15.1 us (27%)
  Pallas kernels  14.6 us (26%)
  local copies, waits for them, and re-layouts  3.07 us (5%)
  other arithmetic  0.95 us (2%)
  between operations  0.78 us (1%)
    ppermute x10, waiting for transfers between devices, swap(): return lax.ppermute(value, axis, [(i, i ^ m) for i in range(size)])  21.4 us
    ppermute x10, starting transfers between devices, swap(): return lax.ppermute(value, axis, [(i, i ^ m) for i in range(size)])  15.1 us
    pallas_call x1, Pallas kernels, on_device(): pl.pallas_call(functools.partial(forward_kernel, sizes, tm, head_size), o...  7.4 us
    pallas_call x1, Pallas kernels, on_device(): pl.pallas_call(functools.partial(backward_kernel, sizes, tm, width // dp,...  2.42 us
    unnamed x14, local copies, waits for them, and re-layouts  2.3 us
    pallas_call x3, Pallas kernels, project_shard(): pl.pallas_call(project_kernel, out_shape=made, in_specs=[vmem] * 4, out_s...  2.27 us
    pallas_call x1, Pallas kernels, on_device(): pl.pallas_call(functools.partial(probs_kernel, sizes, tm, head_size), out...  1.53 us
  transfers between devices with their start and end apart: 10, of which 8 were waited for; matrix products, arithmetic and copies ran while one was open for 3% of the time, Pallas kernels for 7%

profile of v6, /device:TPU:0, one launch (start us, length us, event | category | flops | bytes accessed | tf_op | source)
XLA Modules:
  0.0 55.9 jit_solution(14201820867519203884)
XLA Ops:
  0.6 0.0 copy-start.4
  0.6 0.0 copy-start.2
  0.7 4.1 %collective-permute-start = (bf16[128,1024]{1,0:T(8,128)(2,1)}, bf16[128,1024]{1,0:T(8,128)(2,1)S(1)}, u32[]{:S(2)}, u32[]{:S(2)}) collective-permute-start(bf16[128,1024]{1,0:T(8,128)(2,1)} %refs_8_.1), channel_id=1, source_target_pairs={{0,2},{1,3},{2,0},{3,1},{4,6},{5,7},{6,4},{7,5},{8,10},{9,11},{10,... | collective-permute-start | bytes 786440 | tf_op jit(solution)/shard_map/ppermute | solution.py:401
  4.8 1.0 %pad_maximum_fusion.small_ref.refs_3_ = f32[33,1024]{1,0:T(8,128)S(1)} fusion(f32[1,1024]{1,0:T(1,128)} %bitcast.9, f32[1,1024]{1,0:T(1,128)} %bitcast.10, f32[31,1024]{1,0:T(8,128)} %param.19), kind=kLoop, calls=%fused_computation | loop fusion | flops 67584 | bytes 270336 | tf_op jit(solution)/shard_map/concatenate | solution.py:413
  5.7 1.6 %collective-permute-start.1 = (bf16[128,1024]{1,0:T(8,128)(2,1)}, bf16[128,1024]{1,0:T(8,128)(2,1)S(1)}, u32[]{:S(2)}, u32[]{:S(2)}) collective-permute-start(bf16[128,1024]{1,0:T(8,128)(2,1)} %refs_8_.1), channel_id=1, source_target_pairs={{0,1},{1,0},{2,3},{3,2},{4,5},{5,4},{6,7},{7,6},{8,9},{9,8},{10,11... | collective-permute-start | bytes 786440 | tf_op jit(solution)/shard_map/ppermute | solution.py:401
  7.4 0.8 %concatenate.7.refs_0_.meta_ref = s32[1,20]{1,0:T(1,128)S(1)} concatenate(s32[1,1]{1,0:T(1,128)} %bitcast.3, s32[1,1]{1,0:T(1,128)} %bitcast.4, s32[1,2]{1,0:T(1,128)} %param.21, s32[1,8]{1,0:T(1,128)} %param.22, s32[1,8]{1,0:T(1,128)} %param.23), dimensions={1} | concatenate | bytes 160 | tf_op jit(solution)/shard_map/concatenate | solution.py:403
  8.1 0.1 spread_taps.1.refs_4_
  8.2 0.0 copy-done.4
  8.2 0.0 copy-done.2
  8.2 0.0 copy-start
  8.3 1.6 %copy-done = bf16[1024,1024]{1,0:T(8,128)(2,1)S(1)} copy-done((bf16[1024,1024]{1,0:T(8,128)(2,1)S(1)}, bf16[1024,1024]{1,0:T(8,128)(2,1)}, u32[]{:S(2)}) %copy-start) | copy-done | bytes 2097176
  9.8 0.0 copy-start.6
  9.8 0.7 %copy-done.6 = f32[1024]{0:T(1024)S(1)} copy-done((f32[1024]{0:T(1024)S(1)}, f32[1024]{0:T(1024)}, u32[]{:S(2)}) %copy-start.6) | copy-done | bytes 4120
  10.5 0.0 copy-start.1
  10.5 0.8 %project_rows_0.1 = (bf16[128,1024]{1,0:T(8,128)(2,1)S(1)}, bf16[128,512]{1,0:T(8,128)(2,1)S(1)}, bf16[128,1024]{1,0:T(8,128)(2,1)S(1)}) custom-call(bf16[128,1024]{1,0:T(8,128)(2,1)S(1)} %copy-done.4, f32[1,1024]{1,0:T(1,128)S(1)} %bitcast.5, bf16[1024,512]{1,0:T(8,128)(2,1)S(1)} %copy-done.2, bf16[1024,1024]{1,0:T(8,128)(2,1)S(1)} %copy-done), custom_call_target="tpu_custom_call" | custom-call | flops 402653184 | bytes 4194304 | tf_op jit(solution)/shard_map/project_rows_0/pallas_call | solution.py:435
  11.3 5.7 %collective-permute-done.x_ref.refs_10_ = bf16[128,1024]{1,0:T(8,128)(2,1)S(1)} collective-permute-done((bf16[128,1024]{1,0:T(8,128)(2,1)}, bf16[128,1024]{1,0:T(8,128)(2,1)S(1)}, u32[]{:S(2)}, u32[]{:S(2)}) %collective-permute-start) | collective-permute-done | bytes 262176 | tf_op jit(solution)/shard_map/ppermute | solution.py:401
  17.0 0.8 %collective-permute-start.2 = (bf16[128,1024]{1,0:T(8,128)(2,1)S(1)}, bf16[128,1024]{1,0:T(8,128)(2,1)S(1)}, u32[]{:S(2)}, u32[]{:S(2)}) collective-permute-start(bf16[128,1024]{1,0:T(8,128)(2,1)S(1)} %collective-permute-done.x_ref.refs_10_), channel_id=1, source_target_pairs={{0,1},{1,0},{2,3},{3,2},{4,5},{5,4},{6,7},{7,6},{8,9},{9,8},{10,11... | collective-permute-start | bytes 786440 | tf_op jit(solution)/shard_map/ppermute | solution.py:401
  17.8 0.0 copy-done.1
  17.8 0.8 %project_rows_2.1 = (bf16[128,1024]{1,0:T(8,128)(2,1)S(1)}, bf16[128,512]{1,0:T(8,128)(2,1)S(1)}, bf16[128,1024]{1,0:T(8,128)(2,1)S(1)}) custom-call(bf16[128,1024]{1,0:T(8,128)(2,1)S(1)} %collective-permute-done.x_ref.refs_10_, f32[1,1024]{1,0:T(1,128)S(1)} %bitcast.6, bf16[1024,512]{1,0:T(8,128)(2,1)S(1)} %copy-done.2, bf16[1024,1024]{1,0:T(8,128)(2,1)S(1)} %copy-done.1), custom_call_target="tpu_custom_call" | custom-call | flops 402653184 | bytes 4194304 | tf_op jit(solution)/shard_map/project_rows_2/pallas_call | solution.py:435
  18.5 0.0 copy-start.3
  18.5 0.0 copy-start.5
  18.6 0.0 collective-permute-done.1.x_ref.refs_9_
  18.6 0.8 %project_rows_1.1 = (bf16[128,1024]{1,0:T(8,128)(2,1)S(1)}, bf16[128,512]{1,0:T(8,128)(2,1)S(1)}, bf16[128,1024]{1,0:T(8,128)(2,1)S(1)}) custom-call(bf16[128,1024]{1,0:T(8,128)(2,1)S(1)} %collective-permute-done.1.x_ref.refs_9_, f32[1,1024]{1,0:T(1,128)S(1)} %bitcast.7, bf16[1024,512]{1,0:T(8,128)(2,1)S(1)} %copy-done.2, bf16[1024,1024]{1,0:T(8,128)(2,1)S(1)} %copy-done.1), custom_call_target="tpu_custom_call" | custom-call | flops 402653184 | bytes 4194304 | tf_op jit(solution)/shard_map/project_rows_1/pallas_call | solution.py:435
  19.3 5.1 %collective-permute-done.2.refs_11_ = bf16[128,1024]{1,0:T(8,128)(2,1)S(1)} collective-permute-done((bf16[128,1024]{1,0:T(8,128)(2,1)S(1)}, bf16[128,1024]{1,0:T(8,128)(2,1)S(1)}, u32[]{:S(2)}, u32[]{:S(2)}) %collective-permute-start.2) | collective-permute-done | bytes 262176 | tf_op jit(solution)/shard_map/ppermute | solution.py:401
  24.4 0.0 copy-done.3
  24.4 0.0 copy-done.5
  24.4 7.4 %forward_pass.1 = (bf16[128,1024]{1,0:T(8,128)(2,1)}, bf16[128,1024]{1,0:T(8,128)(2,1)S(1)}, bf16[128,512]{1,0:T(8,128)(2,1)S(1)}, bf16[128,1024]{1,0:T(8,128)(2...) custom-call(s32[1,20]{1,0:T(1,128)S(1)} %concatenate.7.refs_0_.meta_, ...), custom_call_target="tpu_custom_call" | custom-call | tf_op jit(solution)/shard_map/forward_pass/pallas_call | solution.py:467
  31.8 4.3 %collective-permute-start.3 = (bf16[192,256]{1,0:T(8,128)(2,1)S(1)}, bf16[192,256]{1,0:T(8,128)(2,1)S(1)}, u32[]{:S(2)}, u32[]{:S(2)}) collective-permute-start(bf16[192,256]{1,0:T(8,128)(2,1)S(1)} %get-tuple-element.58), channel_id=1, source_target_pairs={{0,3},{1,2},{2,1},{3,0},{4,7},{5,6},{6,5},{7,4},{8,11},{9,10},{10,... | collective-permute-start | bytes 294920 | tf_op jit(solution)/shard_map/ppermute | solution.py:401
  36.2 0.0 collective-permute-start.4
  36.2 0.6 %collective-permute-start.5 = (bf16[192,256]{1,0:T(8,128)(2,1)S(1)}, bf16[192,256]{1,0:T(8,128)(2,1)S(1)}, u32[]{:S(2)}, u32[]{:S(2)}) collective-permute-start(bf16[192,256]{1,0:T(8,128)(2,1)S(1)} %get-tuple-element.60), channel_id=1, source_target_pairs={{0,1},{1,0},{2,3},{3,2},{4,5},{5,4},{6,7},{7,6},{8,9},{9,8},{10,11... | collective-permute-start | bytes 294920 | tf_op jit(solution)/shard_map/ppermute | solution.py:401
  36.8 1.5 %window_probs.1 = (bf16[704,256]{1,0:T(8,128)(2,1)S(1)}, bf16[704,256]{1,0:T(8,128)(2,1)S(1)}, f32[8,192,256]{2,1,0:T(8,128)S(1)}, f32[8,192,256]{2,1,0:T(8,128)S(1)}) custom-call(s32[1,20]{1,0:T(1,128)S(1)} %concatenate.7.refs_0_.meta_ref, bf16[128,512]{1,0:T(8,128)(2,1)S(1)} %get-tuple-element.41.refs_12_.refs_0_, ...), custom_call_target="tpu_custom_call" | custom-call | flops 2000000000 | bytes 4000000 | tf_op jit(solution)/shard_map/window_probs/pallas_call | solution.py:509
  38.4 1.4 %collective-permute-done.3.refs_9_ = bf16[192,256]{1,0:T(8,128)(2,1)S(1)} collective-permute-done((bf16[192,256]{1,0:T(8,128)(2,1)S(1)}, bf16[192,256]{1,0:T(8,128)(2,1)S(1)}, u32[]{:S(2)}, u32[]{:S(2)}) %collective-permute-start.3) | collective-permute-done | bytes 98336 | tf_op jit(solution)/shard_map/ppermute | solution.py:401
  39.8 3.9 %collective-permute-done.4.refs_10_ = bf16[192,256]{1,0:T(8,128)(2,1)S(1)} collective-permute-done((bf16[192,256]{1,0:T(8,128)(2,1)S(1)}, bf16[192,256]{1,0:T(8,128)(2,1)S(1)}, u32[]{:S(2)}, u32[]{:S(2)}) %collective-permute-start.4) | collective-permute-done | bytes 98336 | tf_op jit(solution)/shard_map/ppermute | solution.py:401
  43.7 0.0 collective-permute-done.5.refs_11_
  43.7 2.4 %key_value_terms.1 = (f32[256,512]{1,0:T(8,128)S(1)}, bf16[256,512]{1,0:T(8,128)(2,1)S(1)}) custom-call(s32[1,20]{1,0:T(1,128)S(1)} %concatenate.7.refs_0_.meta_ref, bf16[704,256]{1,0:T(8,128)(2,1)S(1)} %get-tuple-element.50.refs_1_, bf16[704,256]{1,0:T(8,128)(2,1)S(1)} %get-tuple-element.51.refs_2_, f32[8,192,256]{2,1,0:T(8,128)S(1)} %get-tuple-element.52.refs_3_, ...), custom_call_target="tpu_custom_call" | custom-call | tf_op jit(solution)/shard_map/key_value_terms/pallas_call | solution.py:529
  46.1 0.1 collective-permute-start.6
  46.2 1.5 %collective-permute-done.6.got_ref = bf16[256,512]{1,0:T(8,128)(2,1)S(1)} collective-permute-done((bf16[256,512]{1,0:T(8,128)(2,1)S(1)}, bf16[256,512]{1,0:T(8,128)(2,1)S(1)}, u32[]{:S(2)}, u32[]{:S(2)}) %collective-permute-start.6) | collective-permute-done | bytes 262176 | tf_op jit(solution)/shard_map/ppermute | solution.py:401
  47.7 0.1 sum_pair.1
  47.8 2.5 %collective-permute-start.7 = (bf16[256,128]{1,0:T(8,128)(2,1)S(1)}, bf16[256,128]{1,0:T(8,128)(2,1)S(1)}, u32[]{:S(2)}, u32[]{:S(2)}) collective-permute-start(bf16[256,128]{1,0:T(8,128)(2,1)S(1)} %get-tuple-element.64), channel_id=1, source_target_pairs={{0,24},{4,28},{8,16},{12,20},{16,8},{20,12},{24,0},{28,4},{1,25},{... | collective-permute-start | bytes 196616 | tf_op jit(solution)/shard_map/ppermute | solution.py:401
  50.3 0.5 collective-permute-start.8
  50.8 0.5 collective-permute-start.9
  51.4 1.7 %collective-permute-done.7.refs_0_ = bf16[256,128]{1,0:T(8,128)(2,1)S(1)} collective-permute-done((bf16[256,128]{1,0:T(8,128)(2,1)S(1)}, bf16[256,128]{1,0:T(8,128)(2,1)S(1)}, u32[]{:S(2)}, u32[]{:S(2)}) %collective-permute-start.7) | collective-permute-done | bytes 65568 | tf_op jit(solution)/shard_map/ppermute | solution.py:401
  53.1 1.5 %collective-permute-done.8.refs_1_ = bf16[256,128]{1,0:T(8,128)(2,1)S(1)} collective-permute-done((bf16[256,128]{1,0:T(8,128)(2,1)S(1)}, bf16[256,128]{1,0:T(8,128)(2,1)S(1)}, u32[]{:S(2)}, u32[]{:S(2)}) %collective-permute-start.8) | collective-permute-done | bytes 65568 | tf_op jit(solution)/shard_map/ppermute | solution.py:401
  54.6 0.5 collective-permute-done.9.refs_2_
  55.1 0.8 %sum_groups.1 = f32[128,256]{1,0:T(8,128)} custom-call(bf16[256,128]{1,0:T(8,128)(2,1)S(1)} %collective-permute-done.7.refs_0_, bf16[256,128]{1,0:T(8,128)(2,1)S(1)} %collective-permute-done.8.refs_1_, bf16[256,128]{1,0:T(8,128)(2,1)S(1)} %collective-permute-done.9.refs_2_, bf16[256,128]{1,0:T(8,128)(2,1)S(1)} %get-tuple-element.67.refs_3_), custom_call_target="tpu_custom_call" | custom-call | tf_op jit(solution)/shard_map/sum_groups/pallas_call | solution.py:560
Async XLA Ops:
  0.6 7.6 %copy-start.4 = (bf16[128,1024]{1,0:T(8,128)(2,1)S(1)}, bf16[128,1024]{1,0:T(8,128)(2,1)}, u32[]{:S(2)}) copy-start(bf16[128,1024]{1,0:T(8,128)(2,1)} %refs_8_.1) | copy-start | bytes 786436
  0.6 7.6 %copy-start.2 = (bf16[1024,512]{1,0:T(8,128)(2,1)S(1)}, bf16[1024,512]{1,0:T(8,128)(2,1)}, u32[]{:S(2)}) copy-start(bf16[1024,512]{1,0:T(8,128)(2,1)} %refs_6_.1) | copy-start | bytes 3145732
  0.7 16.3 %collective-permute-start = (bf16[128,1024]{1,0:T(8,128)(2,1)}, bf16[128,1024]{1,0:T(8,128)(2,1)S(1)}, u32[]{:S(2)}, u32[]{:S(2)}) collective-permute-start(bf16[128,1024]{1,0:T(8,128)(2,1)} %refs_8_.1), channel_id=1, source_target_pairs={{0,2},{1,3},{2,0},{3,1},{4,6},{5,7},{6,4},{7,5},{8,10},{9,11},{10,... | collective-permute-start | bytes 786440 | tf_op jit(solution)/shard_map/ppermute | solution.py:401
  5.7 12.8 %collective-permute-start.1 = (bf16[128,1024]{1,0:T(8,128)(2,1)}, bf16[128,1024]{1,0:T(8,128)(2,1)S(1)}, u32[]{:S(2)}, u32[]{:S(2)}) collective-permute-start(bf16[128,1024]{1,0:T(8,128)(2,1)} %refs_8_.1), channel_id=1, source_target_pairs={{0,1},{1,0},{2,3},{3,2},{4,5},{5,4},{6,7},{7,6},{8,9},{9,8},{10,11... | collective-permute-start | bytes 786440 | tf_op jit(solution)/shard_map/ppermute | solution.py:401
  8.2 1.6 %copy-start = (bf16[1024,1024]{1,0:T(8,128)(2,1)S(1)}, bf16[1024,1024]{1,0:T(8,128)(2,1)}, u32[]{:S(2)}) copy-start(bf16[1024,1024]{1,0:T(8,128)(2,1)} %refs_7_.1) | copy-start | bytes 6291460
  9.8 0.7 %copy-start.6 = (f32[1024]{0:T(1024)S(1)}, f32[1024]{0:T(1024)}, u32[]{:S(2)}) copy-start(f32[1024]{0:T(1024)} %param.14) | copy-start | bytes 12292
  10.5 7.2 %copy-start.1 = (bf16[1024,1024]{1,0:T(8,128)(2,1)S(1)}, bf16[1024,1024]{1,0:T(8,128)(2,1)}, u32[]{:S(2)}) copy-start(bf16[1024,1024]{1,0:T(8,128)(2,1)} %refs_7_.1) | copy-start | bytes 6291460
  17.0 7.4 %collective-permute-start.2 = (bf16[128,1024]{1,0:T(8,128)(2,1)S(1)}, bf16[128,1024]{1,0:T(8,128)(2,1)S(1)}, u32[]{:S(2)}, u32[]{:S(2)}) collective-permute-start(bf16[128,1024]{1,0:T(8,128)(2,1)S(1)} %collective-permute-done.x_ref.refs_10_), channel_id=1, source_target_pairs={{0,1},{1,0},{2,3},{3,2},{4,5},{5,4},{6,7},{7,6},{8,9},{9,8},{10,11... | collective-permute-start | bytes 786440 | tf_op jit(solution)/shard_map/ppermute | solution.py:401
  18.5 5.9 %copy-start.3 = (bf16[512,1024]{1,0:T(8,128)(2,1)S(1)}, bf16[512,1024]{1,0:T(8,128)(2,1)}, u32[]{:S(2)}) copy-start(bf16[512,1024]{1,0:T(8,128)(2,1)} %refs_2_.1) | copy-start | bytes 3145732
  18.5 5.9 %copy-start.5 = (bf16[128,1024]{1,0:T(8,128)(2,1)S(1)}, bf16[128,1024]{1,0:T(8,128)(2,1)}, u32[]{:S(2)}) copy-start(bf16[128,1024]{1,0:T(8,128)(2,1)} %refs_1_.1) | copy-start | bytes 786436
  31.8 8.0 %collective-permute-start.3 = (bf16[192,256]{1,0:T(8,128)(2,1)S(1)}, bf16[192,256]{1,0:T(8,128)(2,1)S(1)}, u32[]{:S(2)}, u32[]{:S(2)}) collective-permute-start(bf16[192,256]{1,0:T(8,128)(2,1)S(1)} %get-tuple-element.58), channel_id=1, source_target_pairs={{0,3},{1,2},{2,1},{3,0},{4,7},{5,6},{6,5},{7,4},{8,11},{9,10},{10,... | collective-permute-start | bytes 294920 | tf_op jit(solution)/shard_map/ppermute | solution.py:401
  36.2 7.5 %collective-permute-start.4 = (bf16[192,256]{1,0:T(8,128)(2,1)S(1)}, bf16[192,256]{1,0:T(8,128)(2,1)S(1)}, u32[]{:S(2)}, u32[]{:S(2)}) collective-permute-start(bf16[192,256]{1,0:T(8,128)(2,1)S(1)} %get-tuple-element.59), channel_id=1, source_target_pairs={{0,2},{1,3},{2,0},{3,1},{4,6},{5,7},{6,4},{7,5},{8,10},{9,11},{10,... | collective-permute-start | bytes 294920 | tf_op jit(solution)/shard_map/ppermute | solution.py:401
  36.2 7.5 %collective-permute-start.5 = (bf16[192,256]{1,0:T(8,128)(2,1)S(1)}, bf16[192,256]{1,0:T(8,128)(2,1)S(1)}, u32[]{:S(2)}, u32[]{:S(2)}) collective-permute-start(bf16[192,256]{1,0:T(8,128)(2,1)S(1)} %get-tuple-element.60), channel_id=1, source_target_pairs={{0,1},{1,0},{2,3},{3,2},{4,5},{5,4},{6,7},{7,6},{8,9},{9,8},{10,11... | collective-permute-start | bytes 294920 | tf_op jit(solution)/shard_map/ppermute | solution.py:401
  46.1 1.6 %collective-permute-start.6 = (bf16[256,512]{1,0:T(8,128)(2,1)S(1)}, bf16[256,512]{1,0:T(8,128)(2,1)S(1)}, u32[]{:S(2)}, u32[]{:S(2)}) collective-permute-start(bf16[256,512]{1,0:T(8,128)(2,1)S(1)} %get-tuple-element.63), channel_id=1, source_target_pairs={{0,4},{4,0},{8,12},{12,8},{16,20},{20,16},{24,28},{28,24},{1,5},{5... | collective-permute-start | bytes 786440 | tf_op jit(solution)/shard_map/ppermute | solution.py:401
  47.8 5.3 %collective-permute-start.7 = (bf16[256,128]{1,0:T(8,128)(2,1)S(1)}, bf16[256,128]{1,0:T(8,128)(2,1)S(1)}, u32[]{:S(2)}, u32[]{:S(2)}) collective-permute-start(bf16[256,128]{1,0:T(8,128)(2,1)S(1)} %get-tuple-element.64), channel_id=1, source_target_pairs={{0,24},{4,28},{8,16},{12,20},{16,8},{20,12},{24,0},{28,4},{1,25},{... | collective-permute-start | bytes 196616 | tf_op jit(solution)/shard_map/ppermute | solution.py:401
  50.3 4.3 %collective-permute-start.8 = (bf16[256,128]{1,0:T(8,128)(2,1)S(1)}, bf16[256,128]{1,0:T(8,128)(2,1)S(1)}, u32[]{:S(2)}, u32[]{:S(2)}) collective-permute-start(bf16[256,128]{1,0:T(8,128)(2,1)S(1)} %get-tuple-element.65), channel_id=1, source_target_pairs={{0,16},{4,20},{8,24},{12,28},{16,0},{20,4},{24,8},{28,12},{1,17},{... | collective-permute-start | bytes 196616 | tf_op jit(solution)/shard_map/ppermute | solution.py:401
  50.8 4.3 %collective-permute-start.9 = (bf16[256,128]{1,0:T(8,128)(2,1)S(1)}, bf16[256,128]{1,0:T(8,128)(2,1)S(1)}, u32[]{:S(2)}, u32[]{:S(2)}) collective-permute-start(bf16[256,128]{1,0:T(8,128)(2,1)S(1)} %get-tuple-element.66), channel_id=1, source_target_pairs={{0,8},{4,12},{8,0},{12,4},{16,24},{20,28},{24,16},{28,20},{1,9},{5... | collective-permute-start | bytes 196616 | tf_op jit(solution)/shard_map/ppermute | solution.py:401

commit v7 on v6

--- a/solution.py
+++ b/solution.py
@@ -98,14 +98,11 @@
     return total
 
 
-def window_probs(diag_q, k_win, reach, head_size):
+def window_probs(diag_q, k_win, flags, head_size):
     raw = dot_nt(k_win, diag_q)
     unit = jnp.tanh(raw * (1.0 / (SOFT_CAP * math.sqrt(head_size))))
     exped = jnp.exp(SOFT_CAP * unit)
-    parts = []
-    for w in range(LC):
-        ok = jnp.where(reach >= LC - w, 1.0, 0.0).astype(F32)
-        parts.append(exped[w * BLOCK : (w + 1) * BLOCK] * ok)
+    parts = [exped[w * BLOCK : (w + 1) * BLOCK] * flags[w] for w in range(LC)]
     parts.append(exped[LC * BLOCK :])
     exped = jnp.concatenate(parts, axis=0)
     total = jnp.sum(exped, axis=0, keepdims=True)
@@ -130,16 +127,114 @@
     kv_ref[...] = dot_nn(normed, wkv_ref[...]).astype(BF16)
 
 
-def forward_kernel(sizes, tm, head_size, *refs):
+def forward_block(head_size, refs, windows, keep, scratch, out_rows):
+    q_ref, kv_ref, x_tail, x_own, grad_ref, wo_ref, small_ref, taps_ref, out_ref = refs
+    ctx_s, e_s, h_s, u_s, gr_s, gc_s = scratch
+    hq = q_ref.shape[1]
+    width = out_ref.shape[1]
+    mid_heads = 256 // BLOCK
+    mid_f = diag_mask(mid_heads, BLOCK, head_size)
+    side_f = diag_mask(HEADS, HALO, head_size)
+    for flags, first, rows, groups, mask_f in (
+        (windows[0], 0, slice(0, HALO), 1, side_f),
+        (windows[1], BLOCK, slice(HALO, ROWS), HEADS // mid_heads, mid_f),
+    ):
+        mask_b = mask_f.astype(BF16)
+        win = slice(first, first + SPAN)
+        wide = hq // groups
+        for g in range(groups):
+            cols = slice(g * wide, (g + 1) * wide)
+            vcols = slice(hq + g * wide, hq + (g + 1) * wide)
+            diag_q = spread(q_ref[rows, cols], mask_b)
+            probs, _ = window_probs(diag_q, kv_ref[win, cols], flags, head_size)
+            full = dot_tn(probs.astype(BF16), kv_ref[win, vcols])
+            ctx_s[rows, cols] = fold_heads(full, mask_f, rows.stop - rows.start).astype(BF16)
+
+    gain = small_ref[KERNEL + 1 : KERNEL + 2]
+    hidden = jnp.concatenate([x_tail[...], x_own[...]], axis=0).astype(F32)
+    hidden = hidden + dot_nn(ctx_s[...], wo_ref[...])
+    unit, inv = norm_stats(hidden)
+    conv_in = (unit * gain).astype(BF16).astype(F32)
+    e_s[:HALO] = conv_in[:HALO] * keep
+    e_s[HALO:] = conv_in[HALO:]
+    h_s[...] = hidden[HALO:]
+    u_s[...] = unit
+
+    groups = BLOCK // SUB
+    keep_lanes = keep[:, :LANES] if hasattr(keep, "shape") and keep.ndim else keep
+
+    def conv(k, carry):
+        cols = pl.ds(pl.multiple_of(k * LANES, LANES), LANES)
+        bias = jnp.broadcast_to(small_ref[KERNEL : KERNEL + 1, cols], (SUB, LANES))
+        taps = lambda j: taps_ref[j * SUB : (j + 1) * SUB, cols]
+        ext = e_s[:, cols]
+        acc = [bias] * groups
+        for s in range(SUB):
+            reps = (KERNEL - s + SUB - 1) // SUB
+            moved = ext[s + 2 : s + 2 + BLOCK + SUB * (reps - 1)]
+            for a in range(reps):
+                tap = taps(SUB * a + s)
+                for r in range(groups):
+                    piece = moved[(a + r) * SUB : (a + r + 1) * SUB]
+                    acc[r] = acc[r] + tap * piece
+        mixed = jnp.concatenate(acc, axis=0)
+        gate = 0.5 * jnp.tanh(0.5 * mixed) + 0.5
+        out_ref[out_rows, cols] = (h_s[:, cols] + mixed * gate).astype(BF16)
+        slope = gate * (1.0 + mixed * (1.0 - gate))
+        gm = grad_ref[out_rows, cols].astype(F32) * slope
+        zeros = jnp.zeros((HALO, LANES), F32)
+        padded = jnp.concatenate([zeros, gm, zeros], axis=0)
+        back = [None] * (ROWS // SUB)
+        low = HALO // SUB - 1
+        for s in range(SUB):
+            reps = (KERNEL - s + SUB - 1) // SUB
+            start = low if s else low + 1
+            moved = padded[start * SUB + s : ROWS + s]
+            for a in range(reps):
+                tap = taps(KERNEL - 1 - SUB * a - s)
+                for g in range(start, ROWS // SUB):
+                    r = g - a
+                    piece = tap * moved[(g - start) * SUB : (g - start + 1) * SUB]
+                    back[r] = piece if back[r] is None else back[r] + piece
+        for r in range(ROWS // SUB):
+            value = back[r] * keep_lanes if r < HALO // SUB else back[r]
+            gr_s[r * SUB : (r + 1) * SUB, cols] = value
+        return carry
+
+    lax.fori_loop(0, width // LANES, conv, 0)
+
+    scaled = gr_s[...] * gain
+    unit = u_s[...]
+    first = jnp.mean(scaled, axis=-1, keepdims=True)
+    second = jnp.mean(scaled * unit, axis=-1, keepdims=True)
+    back = inv * (scaled - first - unit * second)
+    own_grad = grad_ref[out_rows].astype(F32) + back[HALO:]
+    gc_s[:HALO] = back[:HALO].astype(BF16)
+    gc_s[HALO:] = own_grad.astype(BF16)
+
+
+def grad_contexts(tm, picks, gc_s, wo_ref, share):
+    half = tm // 2
+    parts = [dot_nt(gc_s[...], wo_ref[h * share : (h + 1) * share]) for h in range(half)]
+    made = []
+    for m in range(half):
+        total = parts[0] * picks[m]
+        for h in range(1, half):
+            total = total + parts[h] * picks[h ^ m]
+        made.append(total.astype(BF16))
+    return made * 2
+
+
+def first_kernel(sizes, tm, head_size, *refs):
     tables_ref, grad_ref, wo_ref, small_ref, taps_ref, g1_ref, wq_ref, wkv_ref = refs[:8]
     refs = refs[8:]
     x_refs = refs[:tm]
     q_refs, kv_refs = (refs[tm + k * (tm - 1) : tm + (k + 1) * (tm - 1)] for k in range(2))
     refs = refs[3 * tm - 2 :]
-    half = tm // 2
-    out_ref, n_last, q_last, kv_last = refs[:4]
-    send_refs = refs[4 : 4 + tm][::-1]
-    q_ref, kv_ref, tail_s, ctx_s, e_s, h_s, u_s, gr_s, gc_s, meta_ref, sem = refs[4 + tm :]
+    out_ref, n_last, q_last, kv_last, q_next, kv_next, tail_next, flags_next = refs[:8]
+    send_refs = refs[8 : 8 + tm]
+    q_ref, kv_ref, tail_s, *scratch = refs[8 + tm : -2]
+    meta_ref, sem = refs[-2:]
     fetch = pltpu.make_async_copy(tables_ref, meta_ref, sem)
     fetch.start()
     project(x_refs[-1], g1_ref, wq_ref, wkv_ref, n_last, q_last, kv_last)
@@ -150,9 +245,7 @@
     me = table.me()
     local = table.blocks // tm
     width = out_ref.shape[1]
-    hq = q_ref.shape[1]
     share = send_refs[0].shape[1]
-
     for ref in (q_ref, kv_ref):
         ref[: PAD * BLOCK] = jnp.zeros((PAD * BLOCK, ref.shape[1]), BF16)
     tail_s[:HALO] = jnp.zeros((HALO, width), BF16)
@@ -165,110 +258,77 @@
             after = pl.ds(pl.multiple_of((b + 1) * HALO, HALO), HALO)
             tail_s[after] = x_refs[m][(j + 1) * BLOCK - HALO : (j + 1) * BLOCK]
 
-    mid_heads = 256 // BLOCK
-    mid_f = diag_mask(mid_heads, BLOCK, head_size)
-    mid_b = mid_f.astype(BF16)
-    side_f = diag_mask(HEADS, HALO, head_size)
-    side_b = side_f.astype(BF16)
-
-    own = [table.block_of(me * local + i) for i in range(local)]
-    keep = [jnp.where(table.position(c) >= 1, 1.0, 0.0).astype(F32) for c in own]
-    for i, c in enumerate(own):
-        for blk, shift, count, put in ((c - 1, HALO, HALO, 0), (c, 0, BLOCK, HALO)):
-            reach = table.reach(blk)
-            win = row_at(blk - LC, SPAN)
-            at = row_at(blk, count, shift)
-            if count == BLOCK:
-                groups, mask_f, mask_b = HEADS // mid_heads, mid_f, mid_b
-            else:
-                groups, mask_f, mask_b = 1, side_f, side_b
-            wide = hq // groups
-            for g in range(groups):
-                cols = slice(g * wide, (g + 1) * wide)
-                vcols = slice(hq + g * wide, hq + (g + 1) * wide)
-                probs, _ = window_probs(
-                    spread(q_ref[at, cols], mask_b), kv_ref[win, cols], reach, head_size
-                )
-                full = dot_tn(probs.astype(BF16), kv_ref[win, vcols])
-                ctx_s[i * ROWS + put : i * ROWS + put + count, cols] = fold_heads(
-                    full, mask_f, count
-                ).astype(BF16)
-
-    gain = small_ref[KERNEL + 1 : KERNEL + 2]
-    product = dot_nn(ctx_s[...], wo_ref[...])
-    scales = []
-    for i, c in enumerate(own):
-        here = slice(i * ROWS, (i + 1) * ROWS)
-        tail = tail_s[pl.ds(pl.multiple_of(c * HALO, HALO), HALO)]
-        rows = jnp.concatenate([tail, x_refs[0][i * BLOCK : (i + 1) * BLOCK]], axis=0)
-        hidden = rows.astype(F32) + product[here]
-        unit, inv = norm_stats(hidden)
-        conv_in = (unit * gain).astype(BF16).astype(F32)
-        e_s[i * ROWS : i * ROWS + HALO] = conv_in[:HALO] * keep[i]
-        e_s[i * ROWS + HALO : (i + 1) * ROWS] = conv_in[HALO:]
-        h_s[i * BLOCK : (i + 1) * BLOCK] = hidden[HALO:]
-        u_s[here] = unit
-        scales.append(inv)
-
-    groups = BLOCK // SUB
-
-    def conv(k, carry):
-        cols = pl.ds(pl.multiple_of(k * LANES, LANES), LANES)
-        bias = jnp.broadcast_to(small_ref[KERNEL : KERNEL + 1, cols], (SUB, LANES))
-        taps = lambda j: taps_ref[j * SUB : (j + 1) * SUB, cols]
-        for i in range(local):
-            ext = e_s[i * ROWS : (i + 1) * ROWS, cols]
-            acc = [bias] * groups
-            for s in range(SUB):
-                reps = (KERNEL - s + SUB - 1) // SUB
-                moved = ext[s + 2 : s + 2 + BLOCK + SUB * (reps - 1)]
-                for a in range(reps):
-                    tap = taps(SUB * a + s)
-                    for r in range(groups):
-                        piece = moved[(a + r) * SUB : (a + r + 1) * SUB]
-                        acc[r] = acc[r] + tap * piece
-            mixed = jnp.concatenate(acc, axis=0)
-            gate = 0.5 * jnp.tanh(0.5 * mixed) + 0.5
-            rows = slice(i * BLOCK, (i + 1) * BLOCK)
-            out_ref[rows, cols] = (h_s[rows, cols] + mixed * gate).astype(BF16)
-            slope = gate * (1.0 + mixed * (1.0 - gate))
-            gm = grad_ref[rows, cols].astype(F32) * slope
-            zeros = jnp.zeros((HALO, LANES), F32)
-            padded = jnp.concatenate([zeros, gm, zeros], axis=0)
-            back = [None] * (ROWS // SUB)
-            low = HALO // SUB - 1
-            for s in range(SUB):
-                reps = (KERNEL - s + SUB - 1) // SUB
-                start = low if s else low + 1
-                moved = padded[start * SUB + s : ROWS + s]
-                for a in range(reps):
-                    tap = taps(KERNEL - 1 - SUB * a - s)
-                    for g in range(start, ROWS // SUB):
-                        r = g - a
-                        piece = tap * moved[(g - start) * SUB : (g - start + 1) * SUB]
-                        back[r] = piece if back[r] is None else back[r] + piece
-            for r in range(ROWS // SUB):
-                scale = keep[i] if r < HALO // SUB else 1.0
-                gr_s[i * ROWS + r * SUB : i * ROWS + (r + 1) * SUB, cols] = back[r] * scale
-        return carry
-
-    lax.fori_loop(0, width // LANES, conv, 0)
-
-    for i in range(local):
-        here = slice(i * ROWS, (i + 1) * ROWS)
-        scaled = gr_s[here] * gain
-        unit = u_s[here]
-        first = jnp.mean(scaled, axis=-1, keepdims=True)
-        second = jnp.mean(scaled * unit, axis=-1, keepdims=True)
-        back = scales[i] * (scaled - first - unit * second)
-        own_grad = grad_ref[i * BLOCK : (i + 1) * BLOCK].astype(F32) + back[HALO:]
-        gc_s[i * ROWS : i * ROWS + HALO] = back[:HALO].astype(BF16)
-        gc_s[i * ROWS + HALO : (i + 1) * ROWS] = own_grad.astype(BF16)
-    for m in range(half):
-        at = pl.ds(pl.multiple_of(((me ^ m) % half) * share, share), share)
-        grad_context = dot_nt(gc_s[...], wo_ref[at]).astype(BF16)
-        send_refs[m][...] = grad_context
-        send_refs[m + half][...] = grad_context
+    def one(flag):
+        return jnp.where(flag, 1.0, 0.0).astype(F32)
+
+    def places(c):
+        tail = pl.ds(pl.multiple_of(c * HALO, HALO), HALO)
+        return row_at(c, ROWS, -HALO), row_at(c - PAD, SPAN + BLOCK), tail
+
+    def flags_of(c):
+        windows = [[one(table.reach(b) >= LC - w) for w in range(LC)] for b in (c - 1, c)]
+        return windows, one(table.position(c) >= 1)
+
+    c = table.block_of(me * local + 1)
+    q_at, kv_at, tail_at = places(c)
+    q_next[...] = q_ref[q_at]
+    kv_next[...] = kv_ref[kv_at]
+    tail_next[...] = tail_s[tail_at]
+    windows, keep = flags_of(c)
+    picks = [one(me % (tm // 2) == h) for h in range(tm // 2)]
+    for k, flag in enumerate([*windows[0], *windows[1], keep, *picks]):
+        flags_next[k : k + 1] = jnp.full((1, width), 1.0, F32) * flag
+
+    c = table.block_of(me * local)
+    q_at, kv_at, tail_at = places(c)
+    windows, keep = flags_of(c)
+    block_refs = (
+        q_ref.at[q_at],
+        kv_ref.at[kv_at],
+        tail_s.at[tail_at],
+        x_refs[0].at[pl.ds(0, BLOCK)],
+        grad_ref,
+        wo_ref,
+        small_ref,
+        taps_ref,
+        out_ref,
+    )
+    forward_block(head_size, block_refs, windows, keep, scratch, slice(0, BLOCK))
+    for ref, value in zip(send_refs, grad_contexts(tm, picks, scratch[-1], wo_ref, share)):
+        ref[...] = value
+
+
+def second_kernel(tm, head_size, *refs):
+    grad_ref, wo_ref, small_ref, taps_ref, x_ref = refs[:5]
+    q_ref, kv_ref, tail_ref, flags_ref, out_first, own_first, near_first = refs[5:12]
+    out_ref = refs[12]
+    send_refs = refs[13 : 13 + tm]
+    scratch = refs[13 + tm :]
+    windows = [[flags_ref[k * LC + w : k * LC + w + 1, :256] for w in range(LC)] for k in range(2)]
+    keep = flags_ref[2 * LC : 2 * LC + 1]
+    block_refs = (
+        q_ref,
+        kv_ref,
+        tail_ref,
+        x_ref.at[pl.ds(BLOCK, BLOCK)],
+        grad_ref,
+        wo_ref,
+        small_ref,
+        taps_ref,
+        out_ref,
+    )
+    out_ref[:BLOCK] = out_first[...]
+    forward_block(head_size, block_refs, windows, keep, scratch, slice(BLOCK, 2 * BLOCK))
+    share = send_refs[0].shape[1]
+    place = 2 * LC + 1
+    picks = [flags_ref[place + h : place + h + 1, :share] for h in range(tm // 2)]
+    made = grad_contexts(tm, picks, scratch[-1], wo_ref, share)
+    for m, (ref, value) in enumerate(zip(send_refs, made)):
+        if m < 2:
+            ref[:ROWS] = (own_first, near_first)[m][...]
+            ref[ROWS:] = value
+        else:
+            ref[...] = value
 
 
 def probs_kernel(sizes, tm, head_size, meta_ref, *refs):
@@ -295,7 +355,9 @@
         own = slice((c + PAD) * BLOCK, (c + PAD + 1) * BLOCK)
         win = slice((c + PAD - LC) * BLOCK, (c + PAD + 1) * BLOCK)
         diag_q = spread(q4_ref[own], mask_b)
-        probs, unit = window_probs(diag_q, k4_ref[win], table.reach(c), head_size)
+        reach = table.reach(c)
+        flags = [jnp.where(reach >= LC - w, 1.0, 0.0).astype(F32) for w in range(LC)]
+        probs, unit = window_probs(diag_q, k4_ref[win], flags, head_size)
         p_ref[c] = probs
         d_ref[c] = (1.0 - unit * unit) * (1.0 / math.sqrt(head_size))
 
@@ -303,8 +365,11 @@
 def backward_kernel(sizes, tm, part, head_size, *refs):
     meta_ref, q4_ref, v4_ref, p_ref, d_ref = refs[:5]
     n_refs = refs[5 : 5 + tm]
-    g_refs = refs[5 + tm : 5 + 2 * tm][::-1]
-    out_refs = refs[5 + 2 * tm : -3]
+    far = 2 * (tm - 2)
+    g_far = refs[5 + tm : 5 + tm + far]
+    g_refs = [((ref, 0), (ref, ROWS)) for ref in refs[5 + tm + far : 7 + tm + far][::-1]]
+    g_refs += [((g_far[2 * k], 0), (g_far[2 * k + 1], 0)) for k in range(tm - 2)]
+    out_refs = refs[7 + tm + far : -3]
     gt_s, t_s, full_s = refs[-3:]
     table = Layout(meta_ref, *sizes)
     me = table.me()
@@ -315,11 +380,13 @@
 
     places = [(m, j, table.block_of((me ^ m) * local + j)) for m in range(tm) for j in range(local)]
     for m, j, b in places:
-        gt_s[row_at(b)] = g_refs[m][j * ROWS + HALO : (j + 1) * ROWS].astype(F32)
+        ref, top = g_refs[m][j]
+        gt_s[row_at(b)] = ref[top + HALO : top + ROWS].astype(F32)
     gt_s[(PAD - 1) * BLOCK : PAD * BLOCK] = jnp.zeros((BLOCK, share), F32)
     for m, j, b in places:
         at = row_at(b, HALO, -HALO)
-        gt_s[at] = gt_s[at] + g_refs[m][j * ROWS : j * ROWS + HALO].astype(F32)
+        ref, top = g_refs[m][j]
+        gt_s[at] = gt_s[at] + ref[top : top + HALO].astype(F32)
     t_s[...] = jnp.zeros(t_s.shape, F32)
 
     def spans(c):
@@ -448,7 +515,7 @@
     x[0] = frames
     if tm == 4:
         x[2] = swap(frames, "tm", tm, 2)
-        own, small = lax.optimization_barrier((frames, small))
+        own, normed[0] = lax.optimization_barrier((frames, normed[0]))
         x[1] = swap(own, "tm", tm, 1)
         facing, normed[0], taps, meta = lax.optimization_barrier((x[2], normed[0], taps, meta))
         x[3] = swap(facing, "tm", tm, 1)
@@ -463,29 +530,38 @@
     def by_m(arrays):
         return [arrays[m] for m in sorted(arrays)]
 
-    own_rows = local * ROWS
+    scratch = [
+        pltpu.VMEM((ROWS, hq), BF16),
+        pltpu.VMEM((ROWS, width), F32),
+        pltpu.VMEM((BLOCK, width), F32),
+        pltpu.VMEM((ROWS, width), F32),
+        pltpu.VMEM((ROWS, width), F32),
+        pltpu.VMEM((ROWS, width), BF16),
+    ]
+    sent = shape((ROWS, share), BF16)
     results = pl.pallas_call(
-        functools.partial(forward_kernel, sizes, tm, head_size),
-        out_shape=[shape((rows, width), BF16)]
+        functools.partial(first_kernel, sizes, tm, head_size),
+        out_shape=[shape((BLOCK, width), BF16)]
         + made
-        + [shape((own_rows, share), BF16)] * tm,
+        + [
+            shape((ROWS, hq), BF16),
+            shape((SPAN + BLOCK, kv_width), BF16),
+            shape((HALO, width), BF16),
+            shape((2 * SUB, width), F32),
+        ]
+        + [sent] * tm,
         in_specs=[pl.BlockSpec(memory_space=pl.ANY)] + [vmem] * (5 + 3 * tm),
-        out_specs=[vmem] * (tm + 4),
+        out_specs=[vmem] * (tm + 8),
         scratch_shapes=[
             pltpu.VMEM((padded, hq), BF16),
             pltpu.VMEM((padded, kv_width), BF16),
             pltpu.VMEM(((blocks + 1) * HALO, width), BF16),
-            pltpu.VMEM((own_rows, hq), BF16),
-            pltpu.VMEM((own_rows, width), F32),
-            pltpu.VMEM((rows, width), F32),
-            pltpu.VMEM((own_rows, width), F32),
-            pltpu.VMEM((own_rows, width), F32),
-            pltpu.VMEM((own_rows, width), BF16),
+            *scratch,
             pltpu.SMEM(meta.shape, jnp.int32),
             pltpu.SemaphoreType.DMA,
         ],
-        compiler_params=pltpu.CompilerParams(vmem_limit_bytes=32 << 20),
-        name="forward_pass",
+        compiler_params=pltpu.CompilerParams(vmem_limit_bytes=28 << 20),
+        name="first_block",
     )(
         meta,
         out_grad,
@@ -499,11 +575,26 @@
         *by_m(queries),
         *by_m(keys_values),
     )
-    layer_out, normed[tm - 1], queries[tm - 1], keys_values[tm - 1] = results[:4]
-    sends = results[:3:-1]
-    got = {0: sends[0]}
-    for m in range(tm - 1, 0, -1):
-        got[m] = swap(sends[m], "tm", tm, m)
+    out_first, normed[tm - 1], queries[tm - 1], keys_values[tm - 1] = results[:4]
+    laid_out, early = results[4:8], results[8:]
+    both = shape((local * ROWS, share), BF16)
+    results = pl.pallas_call(
+        functools.partial(second_kernel, tm, head_size),
+        out_shape=[shape((rows, width), BF16)] + [both] * 2 + [sent] * (tm - 2),
+        in_specs=[vmem] * 12,
+        out_specs=[vmem] * (tm + 1),
+        scratch_shapes=scratch,
+        compiler_params=pltpu.CompilerParams(vmem_limit_bytes=16 << 20),
+        cost_estimate=pl.CostEstimate(flops=1, bytes_accessed=1, transcendentals=0),
+        name="second_block",
+    )(out_grad, w_out, small, taps, frames, *laid_out, out_first, early[0], early[1])
+    layer_out, late = results[0], results[1:]
+    got_early = [swap(early[m], "tm", tm, m) for m in range(2, tm)]
+    *late, got_early = lax.optimization_barrier((*late, got_early))
+    got_far = []
+    for m in range(2, tm):
+        got_far += [got_early[m - 2], swap(late[m], "tm", tm, m)]
+    got_near = [swap(late[1], "tm", tm, 1), late[0]]
 
     pair_width = share // head_size * BLOCK
     q4, v4, probs, slopes = pl.pallas_call(
@@ -515,9 +606,7 @@
         scratch_shapes=[pltpu.VMEM((padded, share), BF16)],
         compiler_params=pltpu.CompilerParams(vmem_limit_bytes=24 << 20),
         name="window_probs",
-        cost_estimate=pl.CostEstimate(
-            flops=2 * 10**9, bytes_accessed=4 * 10**6, transcendentals=800000
-        ),
+        cost_estimate=pl.CostEstimate(flops=1, bytes_accessed=1, transcendentals=0),
     )(meta, *by_m(queries), *by_m(keys_values))
 
     direct = dp <= 8
@@ -529,7 +618,7 @@
     pieces = pl.pallas_call(
         functools.partial(backward_kernel, sizes, tm, width // dp, head_size),
         out_shape=piece_shapes,
-        in_specs=[smem] + [vmem] * (4 + 2 * tm),
+        in_specs=[smem] + [vmem] * (6 + tm + len(got_far)),
         out_specs=[vmem] * len(piece_shapes),
         scratch_shapes=[
             pltpu.VMEM((padded, share), F32),
@@ -538,7 +627,7 @@
         ],
         compiler_params=pltpu.CompilerParams(vmem_limit_bytes=32 << 20),
         name="key_value_terms",
-    )(meta, q4, v4, probs, slopes, *by_m(normed), *by_m(got)[::-1])
+    )(meta, q4, v4, probs, slopes, *by_m(normed), *got_far, *got_near)
 
     if direct:
         kept, away = pieces

time: 56.1 us -> 63.4 us (1.13)
  Pallas kernels: 14.6 us -> 20.9 us
  waiting for transfers between devices: 21.4 us -> 18.2 us
  starting transfers between devices: 15.1 us -> 18.1 us
  local copies, waits for them, and re-layouts: 3.07 us -> 5.04 us
  other arithmetic: 0.95 us -> 0.02 us
    pallas_call x1 -> x2, Pallas kernels: 7.4 us -> 10.7 us  [the longest x1 5.95 us: on_device(): pl.pallas_call(functools.partial(first_kernel, sizes, tm, head_size), out...]
    ppermute x10 -> x12, waiting for transfers between devices: 21.4 us -> 18.2 us  [swap(): return lax.ppermute(value, axis, [(i, i ^ m) for i in range(size)])]
    pallas_call x3, Pallas kernels: 2.27 us -> 5.33 us  [project_shard(): pl.pallas_call(project_kernel, out_shape=made, in_specs=[vmem] * 4, out_s...]
    ppermute x10 -> x12, starting transfers between devices: 15.1 us -> 18.1 us  [swap(): return lax.ppermute(value, axis, [(i, i ^ m) for i in range(size)])]
    unnamed x14 -> x36, local copies, waits for them, and re-layouts: 2.3 us -> 4.94 us
    concatenate x1, other arithmetic: 0.95 us -> 0.02 us  [on_device(): jnp.concatenate([conv_kernel, conv_bias.reshape(1, -1), norm2_gain.reshap...]
    concatenate x1, local copies, waits for them, and re-layouts: 0.77 us -> 0.09 us  [on_device(): jnp.concatenate([lax.axis_index('tm').astype(jnp.int32).reshape(1, 1), la...]
  transfers between devices with their start and end apart: 10 -> 12, of which waited for: 8 -> 9; matrix products, arithmetic and copies ran while one was open for 3% -> 0% of each run, Pallas kernels for 7% -> 19%
where the time goes in v7:
time: 63.4 us; the launch traced here: 63.1 us
  Pallas kernels  20.9 us (33%)
  waiting for transfers between devices  18.2 us (29%)
  starting transfers between devices  18.1 us (29%)
  local copies, waits for them, and re-layouts  5.04 us (8%)
  between operations  0.83 us (1%)
    ppermute x12, waiting for transfers between devices, swap(): return lax.ppermute(value, axis, [(i, i ^ m) for i in range(size)])  18.2 us
    ppermute x12, starting transfers between devices, swap(): return lax.ppermute(value, axis, [(i, i ^ m) for i in range(size)])  18.1 us
    pallas_call x1, Pallas kernels, on_device(): pl.pallas_call(functools.partial(first_kernel, sizes, tm, head_size), out...  5.95 us
    pallas_call x3, Pallas kernels, project_shard(): pl.pallas_call(project_kernel, out_shape=made, in_specs=[vmem] * 4, out_s...  5.33 us
    unnamed x36, local copies, waits for them, and re-layouts  4.94 us
    pallas_call x1, Pallas kernels, on_device(): pl.pallas_call(functools.partial(second_kernel, tm, head_size), out_shape...  4.74 us
    pallas_call x1, Pallas kernels, on_device(): pl.pallas_call(functools.partial(backward_kernel, sizes, tm, width // dp,...  2.4 us
    pallas_call x1, Pallas kernels, on_device(): pl.pallas_call(functools.partial(probs_kernel, sizes, tm, head_size), out...  1.54 us
  transfers between devices with their start and end apart: 12, of which 9 were waited for; matrix products, arithmetic and copies ran while one was open for 0% of the time, Pallas kernels for 19%

profile of v7, /device:TPU:0, one launch (start us, length us, event | category | flops | bytes accessed | tf_op | source)
XLA Modules:
  0.0 63.1 jit_solution(17711986064698092265)
XLA Ops:
  0.6 4.1 %collective-permute-start = (bf16[128,1024]{1,0:T(8,128)(2,1)}, bf16[128,1024]{1,0:T(8,128)(2,1)}, u32[]{:S(2)}, u32[]{:S(2)}) collective-permute-start(bf16[128,1024]{1,0:T(8,128)(2,1)} %refs_4_.1), channel_id=1, source_target_pairs={{0,2},{1,3},{2,0},{3,1},{4,6},{5,7},{6,4},{7,5},{8,10},{9,11},{10,... | collective-permute-start | bytes 786440 | tf_op jit(solution)/shard_map/ppermute | solution.py:468
  4.7 0.0 copy-start
  4.7 1.6 %copy-done = bf16[1024,1024]{1,0:T(8,128)(2,1)S(1)} copy-done((bf16[1024,1024]{1,0:T(8,128)(2,1)S(1)}, bf16[1024,1024]{1,0:T(8,128)(2,1)}, u32[]{:S(2)}) %copy-start) | copy-done | bytes 2097176
  6.3 0.0 copy-start.2
  6.3 1.2 %copy-done.2 = bf16[1024,512]{1,0:T(8,128)(2,1)S(1)} copy-done((bf16[1024,512]{1,0:T(8,128)(2,1)S(1)}, bf16[1024,512]{1,0:T(8,128)(2,1)}, u32[]{:S(2)}) %copy-start.2) | copy-done | bytes 1048600
  7.6 0.0 copy-start.10
  7.6 0.7 %copy-done.10 = f32[1024]{0:T(1024)S(1)} copy-done((f32[1024]{0:T(1024)S(1)}, f32[1024]{0:T(1024)}, u32[]{:S(2)}) %copy-start.10) | copy-done | bytes 4120
  8.2 0.0 copy-start.16
  8.3 0.0 copy-start.17
  8.3 0.0 copy-start.1
  8.3 0.0 copy-start.11
  8.3 1.9 %project_rows_0.1 = (bf16[128,1024]{1,0:T(8,128)(2,1)S(1)}, bf16[128,512]{1,0:T(8,128)(2,1)S(1)}, bf16[128,1024]{1,0:T(8,128)(2,1)S(1)}) custom-call(bf16[128,1024]{1,0:T(8,128)(2,1)} %refs_4_.1, f32[1,1024]{1,0:T(1,128)S(1)} %bitcast.5, bf16[1024,512]{1,0:T(8,128)(2,1)S(1)} %copy-done.2, bf16[1024,1024]{1,0:T(8,128)(2,1)S(1)} %copy-done), custom_call_target="tpu_custom_call" | custom-call | flops 402653184 | bytes 4194304 | tf_op jit(solution)/shard_map/project_rows_0/pallas_call | solution.py:502
  10.2 0.0 copy-start.6
  10.2 0.7 %copy-done.6 = bf16[128,1024]{1,0:T(8,128)(2,1)} copy-done((bf16[128,1024]{1,0:T(8,128)(2,1)}, bf16[128,1024]{1,0:T(8,128)(2,1)S(1)}, u32[]{:S(2)}) %copy-start.6) | copy-done | bytes 262168
  10.9 0.7 %copy-done.8 = bf16[128,1024]{1,0:T(8,128)(2,1)} copy-done((bf16[128,1024]{1,0:T(8,128)(2,1)}, bf16[128,1024]{1,0:T(8,128)(2,1)S(1)}, u32[]{:S(2)}) %copy-start.8) | copy-done | bytes 262168
  11.6 1.6 %collective-permute-start.1 = (bf16[128,1024]{1,0:T(8,128)(2,1)}, bf16[128,1024]{1,0:T(8,128)(2,1)}, u32[]{:S(2)}, u32[]{:S(2)}) collective-permute-start(bf16[128,1024]{1,0:T(8,128)(2,1)} %refs_4_.1), channel_id=1, source_target_pairs={{0,1},{1,0},{2,3},{3,2},{4,5},{5,4},{6,7},{7,6},{8,9},{9,8},{10,11... | collective-permute-start | bytes 786440 | tf_op jit(solution)/shard_map/ppermute | solution.py:468
  13.2 0.0 copy-done.12
  13.2 0.0 copy-done.13
  13.2 0.0 copy-done.14
  13.2 0.0 copy-done.15
  13.2 0.0 copy-done.16
  13.2 0.0 copy-done.17
  13.2 0.1 concatenate.7.refs_0_.meta_ref
  13.3 0.1 spread_taps.1.refs_4_.refs_3_
  13.4 3.7 %collective-permute-done.x_ref.refs_10_ = bf16[128,1024]{1,0:T(8,128)(2,1)} collective-permute-done((bf16[128,1024]{1,0:T(8,128)(2,1)}, bf16[128,1024]{1,0:T(8,128)(2,1)}, u32[]{:S(2)}, u32[]{:S(2)}) %collective-permute-start) | collective-permute-done | bytes 262176 | tf_op jit(solution)/shard_map/ppermute | solution.py:468
  17.1 0.7 %collective-permute-start.2 = (bf16[128,1024]{1,0:T(8,128)(2,1)}, bf16[128,1024]{1,0:T(8,128)(2,1)S(1)}, u32[]{:S(2)}, u32[]{:S(2)}) collective-permute-start(bf16[128,1024]{1,0:T(8,128)(2,1)} %collective-permute-done.x_ref.refs_10_), channel_id=1, source_target_pairs={{0,1},{1,0},{2,3},{3,2},{4,5},{5,4},{6,7},{7,6},{8,9},{9,8},{10,11... | collective-permute-start | bytes 786440 | tf_op jit(solution)/shard_map/ppermute | solution.py:468
  17.7 0.0 copy-done.1
  17.7 0.0 copy-done.11
  17.7 0.0 copy-done.3
  17.7 1.7 %project_rows_2.1 = (bf16[128,1024]{1,0:T(8,128)(2,1)S(1)}, bf16[128,512]{1,0:T(8,128)(2,1)S(1)}, bf16[128,1024]{1,0:T(8,128)(2,1)S(1)}) custom-call(bf16[128,1024]{1,0:T(8,128)(2,1)} %collective-permute-done.x_ref.refs_10_, f32[1,1024]{1,0:T(1,128)S(1)} %bitcast.6, bf16[1024,512]{1,0:T(8,128)(2,1)S(1)} %copy-done.3, bf16[1024,1024]{1,0:T(8,128)(2,1)S(1)} %copy-done.1), custom_call_target="tpu_custom_call" | custom-call | flops 402653184 | bytes 4194304 | tf_op jit(solution)/shard_map/project_rows_2/pallas_call | solution.py:502
  19.5 0.0 copy-start.4
  19.5 0.0 copy-start.5
  19.5 0.0 copy-start.7
  19.5 3.2 %collective-permute-done.1.x_ref.refs_9_ = bf16[128,1024]{1,0:T(8,128)(2,1)} collective-permute-done((bf16[128,1024]{1,0:T(8,128)(2,1)}, bf16[128,1024]{1,0:T(8,128)(2,1)}, u32[]{:S(2)}, u32[]{:S(2)}) %collective-permute-start.1) | collective-permute-done | bytes 262176 | tf_op jit(solution)/shard_map/ppermute | solution.py:468
  22.7 1.7 %project_rows_1.1 = (bf16[128,1024]{1,0:T(8,128)(2,1)S(1)}, bf16[128,512]{1,0:T(8,128)(2,1)S(1)}, bf16[128,1024]{1,0:T(8,128)(2,1)S(1)}) custom-call(bf16[128,1024]{1,0:T(8,128)(2,1)} %collective-permute-done.1.x_ref.refs_9_, f32[1,1024]{1,0:T(1,128)S(1)} %bitcast.7, bf16[1024,512]{1,0:T(8,128)(2,1)S(1)} %copy-done.3, bf16[1024,1024]{1,0:T(8,128)(2,1)S(1)} %copy-done.1), custom_call_target="tpu_custom_call" | custom-call | flops 402653184 | bytes 4194304 | tf_op jit(solution)/shard_map/project_rows_1/pallas_call | solution.py:502
  24.4 3.7 %collective-permute-done.2.refs_11_ = bf16[128,1024]{1,0:T(8,128)(2,1)S(1)} collective-permute-done((bf16[128,1024]{1,0:T(8,128)(2,1)}, bf16[128,1024]{1,0:T(8,128)(2,1)S(1)}, u32[]{:S(2)}, u32[]{:S(2)}) %collective-permute-start.2) | collective-permute-done | bytes 262176 | tf_op jit(solution)/shard_map/ppermute | solution.py:468
  28.1 0.0 copy-done.4
  28.1 0.0 copy-done.5
  28.1 0.0 copy-done.7
  28.1 6.0 %first_block.1 = (bf16[64,1024]{1,0:T(8,128)(2,1)S(1)}, bf16[128,1024]{1,0:T(8,128)(2,1)S(1)}, bf16[128,512]{1,0:T(8,128)(2,1)S(1)}, bf16[128,1024]{1,0:T(8,128)...) custom-call(s32[1,20]{1,0:T(1,128)S(1)} %concatenate.7.refs_0_.meta_, ...), custom_call_target="tpu_custom_call" | custom-call | tf_op jit(solution)/shard_map/first_block/pallas_call | solution.py:542
  34.1 1.7 %collective-permute-start.3 = (bf16[96,256]{1,0:T(8,128)(2,1)S(1)}, bf16[96,256]{1,0:T(8,128)(2,1)S(1)}, u32[]{:S(2)}, u32[]{:S(2)}) collective-permute-start(bf16[96,256]{1,0:T(8,128)(2,1)S(1)} %get-tuple-element.84), channel_id=1, source_target_pairs={{0,2},{1,3},{2,0},{3,1},{4,6},{5,7},{6,4},{7,5},{8,10},{9,11},{10,... | collective-permute-start | bytes 147464 | tf_op jit(solution)/shard_map/ppermute | solution.py:468
  35.8 1.9 %collective-permute-start.4 = (bf16[96,256]{1,0:T(8,128)(2,1)S(1)}, bf16[96,256]{1,0:T(8,128)(2,1)S(1)}, u32[]{:S(2)}, u32[]{:S(2)}) collective-permute-start(bf16[96,256]{1,0:T(8,128)(2,1)S(1)} %get-tuple-element.85), channel_id=1, source_target_pairs={{0,3},{1,2},{2,1},{3,0},{4,7},{5,6},{6,5},{7,4},{8,11},{9,10},{10,... | collective-permute-start | bytes 147464 | tf_op jit(solution)/shard_map/ppermute | solution.py:468
  37.8 4.7 %second_block.1 = (bf16[128,1024]{1,0:T(8,128)(2,1)}, bf16[192,256]{1,0:T(8,128)(2,1)S(1)}, bf16[192,256]{1,0:T(8,128)(2,1)S(1)}, bf16[96,256]{1,0:T(8,128)(2,1)S(1)}, bf16[96,256]{1,0:T(8,128)(2,1)S(1)}) custom-call(bf16[128,1024]{1,0:T(8,128)(2,1)S(1)} %copy-done.5, bf16[512,1024]{1,0:T(8,128)(2,1)S(1)} %copy-done.4, ...), custom_call_target="tpu_custom_call" | custom-call | flops 1 | bytes 1 | tf_op jit(solution)/shard_map/second_block/pallas_call | solution.py:581
  42.5 0.0 collective-permute-done.3.refs_9_
  42.5 0.0 collective-permute-done.4.refs_11_
  42.5 0.5 collective-permute-start.7
  43.1 2.0 %collective-permute-start.5 = (bf16[96,256]{1,0:T(8,128)(2,1)S(1)}, bf16[96,256]{1,0:T(8,128)(2,1)S(1)}, u32[]{:S(2)}, u32[]{:S(2)}) collective-permute-start(bf16[96,256]{1,0:T(8,128)(2,1)S(1)} %get-tuple-element.87), channel_id=1, source_target_pairs={{0,2},{1,3},{2,0},{3,1},{4,6},{5,7},{6,4},{7,5},{8,10},{9,11},{10,... | collective-permute-start | bytes 147464 | tf_op jit(solution)/shard_map/ppermute | solution.py:468
  45.0 1.9 %collective-permute-start.6 = (bf16[96,256]{1,0:T(8,128)(2,1)S(1)}, bf16[96,256]{1,0:T(8,128)(2,1)S(1)}, u32[]{:S(2)}, u32[]{:S(2)}) collective-permute-start(bf16[96,256]{1,0:T(8,128)(2,1)S(1)} %get-tuple-element.89), channel_id=1, source_target_pairs={{0,3},{1,2},{2,1},{3,0},{4,7},{5,6},{6,5},{7,4},{8,11},{9,10},{10,... | collective-permute-start | bytes 147464 | tf_op jit(solution)/shard_map/ppermute | solution.py:468
  47.0 1.5 %window_probs.1 = (bf16[704,256]{1,0:T(8,128)(2,1)S(1)}, bf16[704,256]{1,0:T(8,128)(2,1)S(1)}, f32[8,192,256]{2,1,0:T(8,128)S(1)}, f32[8,192,256]{2,1,0:T(8,128)S(1)}) custom-call(s32[1,20]{1,0:T(1,128)S(1)} %concatenate.7.refs_0_.meta_ref, bf16[128,512]{1,0:T(8,128)(2,1)S(1)} %get-tuple-element.56.refs_12_.refs_0_, ...), custom_call_target="tpu_custom_call" | custom-call | flops 1 | bytes 1 | tf_op jit(solution)/shard_map/window_probs/pallas_call | solution.py:600
  48.5 0.5 collective-permute-done.5.refs_10_
  49.0 1.9 %collective-permute-done.6.refs_12_ = bf16[96,256]{1,0:T(8,128)(2,1)S(1)} collective-permute-done((bf16[96,256]{1,0:T(8,128)(2,1)S(1)}, bf16[96,256]{1,0:T(8,128)(2,1)S(1)}, u32[]{:S(2)}, u32[]{:S(2)}) %collective-permute-start.6) | collective-permute-done | bytes 49184 | tf_op jit(solution)/shard_map/ppermute | solution.py:468
  50.9 0.0 collective-permute-done.7.refs_13_
  50.9 0.0 copy-done.9
  50.9 2.4 %key_value_terms.1 = (f32[256,512]{1,0:T(8,128)S(1)}, bf16[256,512]{1,0:T(8,128)(2,1)S(1)}) custom-call(s32[1,20]{1,0:T(1,128)S(1)} %concatenate.7.refs_0_.meta_ref, bf16[704,256]{1,0:T(8,128)(2,1)S(1)} %get-tuple-element.72.refs_1_, bf16[704,256]{1,0:T(8,128)(2,1)S(1)} %get-tuple-element.73.refs_2_, f32[8,192,256]{2,1,0:T(8,128)S(1)} %get-tuple-element.74.refs_3_, ...), custom_call_target="tpu_custom_call" | custom-call | tf_op jit(solution)/shard_map/key_value_terms/pallas_call | solution.py:618
  53.3 0.1 collective-permute-start.8
  53.4 1.5 %collective-permute-done.8.got_ref = bf16[256,512]{1,0:T(8,128)(2,1)S(1)} collective-permute-done((bf16[256,512]{1,0:T(8,128)(2,1)S(1)}, bf16[256,512]{1,0:T(8,128)(2,1)S(1)}, u32[]{:S(2)}, u32[]{:S(2)}) %collective-permute-start.8) | collective-permute-done | bytes 262176 | tf_op jit(solution)/shard_map/ppermute | solution.py:468
  54.9 0.1 sum_pair.1
  55.0 2.5 %collective-permute-start.9 = (bf16[256,128]{1,0:T(8,128)(2,1)S(1)}, bf16[256,128]{1,0:T(8,128)(2,1)S(1)}, u32[]{:S(2)}, u32[]{:S(2)}) collective-permute-start(bf16[256,128]{1,0:T(8,128)(2,1)S(1)} %get-tuple-element.94), channel_id=1, source_target_pairs={{0,24},{4,28},{8,16},{12,20},{16,8},{20,12},{24,0},{28,4},{1,25},{... | collective-permute-start | bytes 196616 | tf_op jit(solution)/shard_map/ppermute | solution.py:468
  57.5 0.5 collective-permute-start.10
  58.0 0.5 collective-permute-start.11
  58.6 1.7 %collective-permute-done.9.refs_0_ = bf16[256,128]{1,0:T(8,128)(2,1)S(1)} collective-permute-done((bf16[256,128]{1,0:T(8,128)(2,1)S(1)}, bf16[256,128]{1,0:T(8,128)(2,1)S(1)}, u32[]{:S(2)}, u32[]{:S(2)}) %collective-permute-start.9) | collective-permute-done | bytes 65568 | tf_op jit(solution)/shard_map/ppermute | solution.py:468
  60.3 1.5 %collective-permute-done.10.refs_1_ = bf16[256,128]{1,0:T(8,128)(2,1)S(1)} collective-permute-done((bf16[256,128]{1,0:T(8,128)(2,1)S(1)}, bf16[256,128]{1,0:T(8,128)(2,1)S(1)}, u32[]{:S(2)}, u32[]{:S(2)}) %collective-permute-start.10) | collective-permute-done | bytes 65568 | tf_op jit(solution)/shard_map/ppermute | solution.py:468
  61.8 0.5 collective-permute-done.11.refs_2_
  62.3 0.8 %sum_groups.1 = f32[128,256]{1,0:T(8,128)} custom-call(bf16[256,128]{1,0:T(8,128)(2,1)S(1)} %collective-permute-done.9.refs_0_, bf16[256,128]{1,0:T(8,128)(2,1)S(1)} %collective-permute-done.10.refs_1_, bf16[256,128]{1,0:T(8,128)(2,1)S(1)} %collective-permute-done.11.refs_2_, bf16[256,128]{1,0:T(8,128)(2,1)S(1)} %get-tuple-element.97.refs_3_), custom_call_target="tpu_custom_call" | custom-call | tf_op jit(solution)/shard_map/sum_groups/pallas_call | solution.py:649
  (8 shorter events, 0.0 us)
Async XLA Ops:
  0.6 16.4 %collective-permute-start = (bf16[128,1024]{1,0:T(8,128)(2,1)}, bf16[128,1024]{1,0:T(8,128)(2,1)}, u32[]{:S(2)}, u32[]{:S(2)}) collective-permute-start(bf16[128,1024]{1,0:T(8,128)(2,1)} %refs_4_.1), channel_id=1, source_target_pairs={{0,2},{1,3},{2,0},{3,1},{4,6},{5,7},{6,4},{7,5},{8,10},{9,11},{10,... | collective-permute-start | bytes 786440 | tf_op jit(solution)/shard_map/ppermute | solution.py:468
  4.7 1.6 %copy-start = (bf16[1024,1024]{1,0:T(8,128)(2,1)S(1)}, bf16[1024,1024]{1,0:T(8,128)(2,1)}, u32[]{:S(2)}) copy-start(bf16[1024,1024]{1,0:T(8,128)(2,1)} %refs_7_.1) | copy-start | bytes 6291460
  6.3 1.2 %copy-start.2 = (bf16[1024,512]{1,0:T(8,128)(2,1)S(1)}, bf16[1024,512]{1,0:T(8,128)(2,1)}, u32[]{:S(2)}) copy-start(bf16[1024,512]{1,0:T(8,128)(2,1)} %refs_6_.1) | copy-start | bytes 3145732
  7.6 0.7 %copy-start.10 = (f32[1024]{0:T(1024)S(1)}, f32[1024]{0:T(1024)}, u32[]{:S(2)}) copy-start(f32[1024]{0:T(1024)} %param.14) | copy-start | bytes 12292
  8.2 4.9 %copy-start.12 = (f32[31,1024]{1,0:T(8,128)S(1)}, f32[31,1024]{1,0:T(8,128)}, u32[]{:S(2)}) copy-start(f32[31,1024]{1,0:T(8,128)} %param.19) | copy-start | bytes 380932
  8.2 4.9 %copy-start.13 = (f32[1024]{0:T(1024)S(1)}, f32[1024]{0:T(1024)}, u32[]{:S(2)}) copy-start(f32[1024]{0:T(1024)} %param.18) | copy-start | bytes 12292
  8.2 4.9 %copy-start.14 = (f32[1024]{0:T(1024)S(1)}, f32[1024]{0:T(1024)}, u32[]{:S(2)}) copy-start(f32[1024]{0:T(1024)} %param.20) | copy-start | bytes 12292
  8.2 5.0 %copy-start.15 = (s32[1,2]{1,0:T(1,128)S(1)}, s32[1,2]{1,0:T(1,128)}, u32[]{:S(2)}) copy-start(s32[1,2]{1,0:T(1,128)} %param.21) | copy-start | bytes 28
  8.2 5.0 %copy-start.16 = (s32[1,8]{1,0:T(1,128)S(1)}, s32[1,8]{1,0:T(1,128)}, u32[]{:S(2)}) copy-start(s32[1,8]{1,0:T(1,128)} %param.22) | copy-start | bytes 100
  8.3 5.0 %copy-start.17 = (s32[1,8]{1,0:T(1,128)S(1)}, s32[1,8]{1,0:T(1,128)}, u32[]{:S(2)}) copy-start(s32[1,8]{1,0:T(1,128)} %param.23) | copy-start | bytes 100
  8.3 9.5 %copy-start.1 = (bf16[1024,1024]{1,0:T(8,128)(2,1)S(1)}, bf16[1024,1024]{1,0:T(8,128)(2,1)}, u32[]{:S(2)}) copy-start(bf16[1024,1024]{1,0:T(8,128)(2,1)} %refs_7_.1) | copy-start | bytes 6291460
  8.3 9.5 %copy-start.11 = (f32[1024]{0:T(1024)S(1)}, f32[1024]{0:T(1024)}, u32[]{:S(2)}) copy-start(f32[1024]{0:T(1024)} %param.14) | copy-start | bytes 12292
  10.2 0.7 %copy-start.6 = (bf16[128,1024]{1,0:T(8,128)(2,1)}, bf16[128,1024]{1,0:T(8,128)(2,1)S(1)}, u32[]{:S(2)}) copy-start(bf16[128,1024]{1,0:T(8,128)(2,1)S(1)} %get-tuple-element.59.refs_15_.refs_4_) | copy-start | bytes 786436
  10.9 0.7 %copy-start.8 = (bf16[128,1024]{1,0:T(8,128)(2,1)}, bf16[128,1024]{1,0:T(8,128)(2,1)S(1)}, u32[]{:S(2)}) copy-start(bf16[128,1024]{1,0:T(8,128)(2,1)S(1)} %get-tuple-element.76.refs_5_) | copy-start | bytes 786436
  11.6 6.2 %copy-start.3 = (bf16[1024,512]{1,0:T(8,128)(2,1)S(1)}, bf16[1024,512]{1,0:T(8,128)(2,1)}, u32[]{:S(2)}) copy-start(bf16[1024,512]{1,0:T(8,128)(2,1)} %refs_6_.1) | copy-start | bytes 3145732
  11.6 11.1 %collective-permute-start.1 = (bf16[128,1024]{1,0:T(8,128)(2,1)}, bf16[128,1024]{1,0:T(8,128)(2,1)}, u32[]{:S(2)}, u32[]{:S(2)}) collective-permute-start(bf16[128,1024]{1,0:T(8,128)(2,1)} %refs_4_.1), channel_id=1, source_target_pairs={{0,1},{1,0},{2,3},{3,2},{4,5},{5,4},{6,7},{7,6},{8,9},{9,8},{10,11... | collective-permute-start | bytes 786440 | tf_op jit(solution)/shard_map/ppermute | solution.py:468
  17.1 11.0 %collective-permute-start.2 = (bf16[128,1024]{1,0:T(8,128)(2,1)}, bf16[128,1024]{1,0:T(8,128)(2,1)S(1)}, u32[]{:S(2)}, u32[]{:S(2)}) collective-permute-start(bf16[128,1024]{1,0:T(8,128)(2,1)} %collective-permute-done.x_ref.refs_10_), channel_id=1, source_target_pairs={{0,1},{1,0},{2,3},{3,2},{4,5},{5,4},{6,7},{7,6},{8,9},{9,8},{10,11... | collective-permute-start | bytes 786440 | tf_op jit(solution)/shard_map/ppermute | solution.py:468
  19.5 8.6 %copy-start.4 = (bf16[512,1024]{1,0:T(8,128)(2,1)S(1)}, bf16[512,1024]{1,0:T(8,128)(2,1)}, u32[]{:S(2)}) copy-start(bf16[512,1024]{1,0:T(8,128)(2,1)} %refs_1_.3) | copy-start | bytes 3145732
  19.5 8.6 %copy-start.5 = (bf16[128,1024]{1,0:T(8,128)(2,1)S(1)}, bf16[128,1024]{1,0:T(8,128)(2,1)}, u32[]{:S(2)}) copy-start(bf16[128,1024]{1,0:T(8,128)(2,1)} %refs_0_.1) | copy-start | bytes 786436
  19.5 8.6 %copy-start.7 = (bf16[128,1024]{1,0:T(8,128)(2,1)S(1)}, bf16[128,1024]{1,0:T(8,128)(2,1)}, u32[]{:S(2)}) copy-start(bf16[128,1024]{1,0:T(8,128)(2,1)} %copy-done.6) | copy-start | bytes 786436
  34.1 8.4 %collective-permute-start.3 = (bf16[96,256]{1,0:T(8,128)(2,1)S(1)}, bf16[96,256]{1,0:T(8,128)(2,1)S(1)}, u32[]{:S(2)}, u32[]{:S(2)}) collective-permute-start(bf16[96,256]{1,0:T(8,128)(2,1)S(1)} %get-tuple-element.84), channel_id=1, source_target_pairs={{0,2},{1,3},{2,0},{3,1},{4,6},{5,7},{6,4},{7,5},{8,10},{9,11},{10,... | collective-permute-start | bytes 147464 | tf_op jit(solution)/shard_map/ppermute | solution.py:468
  35.8 6.7 %collective-permute-start.4 = (bf16[96,256]{1,0:T(8,128)(2,1)S(1)}, bf16[96,256]{1,0:T(8,128)(2,1)S(1)}, u32[]{:S(2)}, u32[]{:S(2)}) collective-permute-start(bf16[96,256]{1,0:T(8,128)(2,1)S(1)} %get-tuple-element.85), channel_id=1, source_target_pairs={{0,3},{1,2},{2,1},{3,0},{4,7},{5,6},{6,5},{7,4},{8,11},{9,10},{10,... | collective-permute-start | bytes 147464 | tf_op jit(solution)/shard_map/ppermute | solution.py:468
  42.5 8.4 %copy-start.9 = (bf16[128,1024]{1,0:T(8,128)(2,1)S(1)}, bf16[128,1024]{1,0:T(8,128)(2,1)}, u32[]{:S(2)}) copy-start(bf16[128,1024]{1,0:T(8,128)(2,1)} %copy-done.8) | copy-start | bytes 786436
  42.5 8.4 %collective-permute-start.7 = (bf16[192,256]{1,0:T(8,128)(2,1)S(1)}, bf16[192,256]{1,0:T(8,128)(2,1)S(1)}, u32[]{:S(2)}, u32[]{:S(2)}) collective-permute-start(bf16[192,256]{1,0:T(8,128)(2,1)S(1)} %get-tuple-element.90), channel_id=1, source_target_pairs={{0,1},{1,0},{2,3},{3,2},{4,5},{5,4},{6,7},{7,6},{8,9},{9,8},{10,11... | collective-permute-start | bytes 294920 | tf_op jit(solution)/shard_map/ppermute | solution.py:468
  43.1 5.9 %collective-permute-start.5 = (bf16[96,256]{1,0:T(8,128)(2,1)S(1)}, bf16[96,256]{1,0:T(8,128)(2,1)S(1)}, u32[]{:S(2)}, u32[]{:S(2)}) collective-permute-start(bf16[96,256]{1,0:T(8,128)(2,1)S(1)} %get-tuple-element.87), channel_id=1, source_target_pairs={{0,2},{1,3},{2,0},{3,1},{4,6},{5,7},{6,4},{7,5},{8,10},{9,11},{10,... | collective-permute-start | bytes 147464 | tf_op jit(solution)/shard_map/ppermute | solution.py:468
  45.0 5.9 %collective-permute-start.6 = (bf16[96,256]{1,0:T(8,128)(2,1)S(1)}, bf16[96,256]{1,0:T(8,128)(2,1)S(1)}, u32[]{:S(2)}, u32[]{:S(2)}) collective-permute-start(bf16[96,256]{1,0:T(8,128)(2,1)S(1)} %get-tuple-element.89), channel_id=1, source_target_pairs={{0,3},{1,2},{2,1},{3,0},{4,7},{5,6},{6,5},{7,4},{8,11},{9,10},{10,... | collective-permute-start | bytes 147464 | tf_op jit(solution)/shard_map/ppermute | solution.py:468
  53.3 1.6 %collective-permute-start.8 = (bf16[256,512]{1,0:T(8,128)(2,1)S(1)}, bf16[256,512]{1,0:T(8,128)(2,1)S(1)}, u32[]{:S(2)}, u32[]{:S(2)}) collective-permute-start(bf16[256,512]{1,0:T(8,128)(2,1)S(1)} %get-tuple-element.93), channel_id=1, source_target_pairs={{0,4},{4,0},{8,12},{12,8},{16,20},{20,16},{24,28},{28,24},{1,5},{5... | collective-permute-start | bytes 786440 | tf_op jit(solution)/shard_map/ppermute | solution.py:468
  55.0 5.3 %collective-permute-start.9 = (bf16[256,128]{1,0:T(8,128)(2,1)S(1)}, bf16[256,128]{1,0:T(8,128)(2,1)S(1)}, u32[]{:S(2)}, u32[]{:S(2)}) collective-permute-start(bf16[256,128]{1,0:T(8,128)(2,1)S(1)} %get-tuple-element.94), channel_id=1, source_target_pairs={{0,24},{4,28},{8,16},{12,20},{16,8},{20,12},{24,0},{28,4},{1,25},{... | collective-permute-start | bytes 196616 | tf_op jit(solution)/shard_map/ppermute | solution.py:468
  57.5 4.3 %collective-permute-start.10 = (bf16[256,128]{1,0:T(8,128)(2,1)S(1)}, bf16[256,128]{1,0:T(8,128)(2,1)S(1)}, u32[]{:S(2)}, u32[]{:S(2)}) collective-permute-start(bf16[256,128]{1,0:T(8,128)(2,1)S(1)} %get-tuple-element.95), channel_id=1, source_target_pairs={{0,16},{4,20},{8,24},{12,28},{16,0},{20,4},{24,8},{28,12},{1,17},{... | collective-permute-start | bytes 196616 | tf_op jit(solution)/shard_map/ppermute | solution.py:468
  58.0 4.3 %collective-permute-start.11 = (bf16[256,128]{1,0:T(8,128)(2,1)S(1)}, bf16[256,128]{1,0:T(8,128)(2,1)S(1)}, u32[]{:S(2)}, u32[]{:S(2)}) collective-permute-start(bf16[256,128]{1,0:T(8,128)(2,1)S(1)} %get-tuple-element.96), channel_id=1, source_target_pairs={{0,8},{4,12},{8,0},{12,4},{16,24},{20,28},{24,16},{28,20},{1,9},{5... | collective-permute-start | bytes 196616 | tf_op jit(solution)/shard_map/ppermute | solution.py:468

commit v8 on v6

--- a/solution.py
+++ b/solution.py
@@ -212,8 +212,7 @@
 
     groups = BLOCK // SUB
 
-    def conv(k, carry):
-        cols = pl.ds(pl.multiple_of(k * LANES, LANES), LANES)
+    def conv(cols):
         bias = jnp.broadcast_to(small_ref[KERNEL : KERNEL + 1, cols], (SUB, LANES))
         taps = lambda j: taps_ref[j * SUB : (j + 1) * SUB, cols]
         for i in range(local):
@@ -250,9 +249,9 @@
             for r in range(ROWS // SUB):
                 scale = keep[i] if r < HALO // SUB else 1.0
                 gr_s[i * ROWS + r * SUB : i * ROWS + (r + 1) * SUB, cols] = back[r] * scale
-        return carry
-
-    lax.fori_loop(0, width // LANES, conv, 0)
+
+    for k in range(0, width, LANES):
+        conv(slice(k, k + LANES))
 
     for i in range(local):
         here = slice(i * ROWS, (i + 1) * ROWS)
@@ -423,7 +422,7 @@
         out_shape=shape((KERNEL * SUB, width), F32),
         in_specs=[vmem],
         out_specs=vmem,
-        compiler_params=pltpu.CompilerParams(vmem_limit_bytes=8 << 20),
+        compiler_params=pltpu.CompilerParams(vmem_limit_bytes=4 << 20),
         cost_estimate=pl.CostEstimate(flops=10**6, bytes_accessed=1 << 20, transcendentals=0),
         name="spread_taps",
     )(small)
@@ -437,7 +436,7 @@
             out_shape=made,
             in_specs=[vmem] * 4,
             out_specs=[vmem] * 3,
-            compiler_params=pltpu.CompilerParams(vmem_limit_bytes=16 << 20),
+            compiler_params=pltpu.CompilerParams(vmem_limit_bytes=4 << 20),
             cost_estimate=pl.CostEstimate(
                 flops=2 * rows * width * (hq + kv_width), bytes_accessed=4 << 20, transcendentals=0
             ),
@@ -448,8 +447,7 @@
     x[0] = frames
     if tm == 4:
         x[2] = swap(frames, "tm", tm, 2)
-        own, small = lax.optimization_barrier((frames, small))
-        x[1] = swap(own, "tm", tm, 1)
+        x[1] = swap(frames, "tm", tm, 1)
         facing, normed[0], taps, meta = lax.optimization_barrier((x[2], normed[0], taps, meta))
         x[3] = swap(facing, "tm", tm, 1)
         project_shard(2, facing)
@@ -484,7 +482,7 @@
             pltpu.SMEM(meta.shape, jnp.int32),
             pltpu.SemaphoreType.DMA,
         ],
-        compiler_params=pltpu.CompilerParams(vmem_limit_bytes=32 << 20),
+        compiler_params=pltpu.CompilerParams(vmem_limit_bytes=16 << 20),
         name="forward_pass",
     )(
         meta,
@@ -513,7 +511,7 @@
         in_specs=[smem] + [vmem] * (2 * tm),
         out_specs=[vmem] * 4,
         scratch_shapes=[pltpu.VMEM((padded, share), BF16)],
-        compiler_params=pltpu.CompilerParams(vmem_limit_bytes=24 << 20),
+        compiler_params=pltpu.CompilerParams(vmem_limit_bytes=8 << 20),
         name="window_probs",
         cost_estimate=pl.CostEstimate(
             flops=2 * 10**9, bytes_accessed=4 * 10**6, transcendentals=800000
@@ -536,7 +534,7 @@
             pltpu.VMEM((padded, share), F32),
             pltpu.VMEM((share, width), F32),
         ],
-        compiler_params=pltpu.CompilerParams(vmem_limit_bytes=32 << 20),
+        compiler_params=pltpu.CompilerParams(vmem_limit_bytes=12 << 20),
         name="key_value_terms",
     )(meta, q4, v4, probs, slopes, *by_m(normed), *by_m(got)[::-1])
 

time: 56.1 us -> 56 us (level)
    unnamed x14 -> x16, local copies, waits for them, and re-layouts: 2.3 us -> 2.3 us
where the time goes in v8:
time: 56 us; the launch traced here: 55.8 us
  waiting for transfers between devices  21.6 us (39%)
  starting transfers between devices  15 us (27%)
  Pallas kernels  14.4 us (26%)
  local copies, waits for them, and re-layouts  3.07 us (5%)
  other arithmetic  0.96 us (2%)
  between operations  0.78 us (1%)
    ppermute x10, waiting for transfers between devices, swap(): return lax.ppermute(value, axis, [(i, i ^ m) for i in range(size)])  21.6 us
    ppermute x10, starting transfers between devices, swap(): return lax.ppermute(value, axis, [(i, i ^ m) for i in range(size)])  15 us
    pallas_call x1, Pallas kernels, on_device(): pl.pallas_call(functools.partial(forward_kernel, sizes, tm, head_size), o...  7.27 us
    pallas_call x1, Pallas kernels, on_device(): pl.pallas_call(functools.partial(backward_kernel, sizes, tm, width // dp,...  2.43 us
    unnamed x16, local copies, waits for them, and re-layouts  2.3 us
    pallas_call x3, Pallas kernels, project_shard(): pl.pallas_call(project_kernel, out_shape=made, in_specs=[vmem] * 4, out_s...  2.27 us
    pallas_call x1, Pallas kernels, on_device(): pl.pallas_call(functools.partial(probs_kernel, sizes, tm, head_size), out...  1.54 us
  transfers between devices with their start and end apart: 10, of which 8 were waited for; matrix products, arithmetic and copies ran while one was open for 3% of the time, Pallas kernels for 7%

profile of v8, /device:TPU:0, one launch (start us, length us, event | category | flops | bytes accessed | tf_op | source)
XLA Modules:
  0.0 55.8 jit_solution(3826102353449590685)
XLA Ops:
  0.6 0.0 copy-start.4
  0.6 0.0 copy-start.2
  0.7 4.1 %collective-permute-start = (bf16[128,1024]{1,0:T(8,128)(2,1)}, bf16[128,1024]{1,0:T(8,128)(2,1)S(1)}, u32[]{:S(2)}, u32[]{:S(2)}) collective-permute-start(bf16[128,1024]{1,0:T(8,128)(2,1)} %refs_8_.1), channel_id=1, source_target_pairs={{0,2},{1,3},{2,0},{3,1},{4,6},{5,7},{6,4},{7,5},{8,10},{9,11},{10,... | collective-permute-start | bytes 786440 | tf_op jit(solution)/shard_map/ppermute | solution.py:400
  4.8 1.6 %collective-permute-start.1 = (bf16[128,1024]{1,0:T(8,128)(2,1)}, bf16[128,1024]{1,0:T(8,128)(2,1)S(1)}, u32[]{:S(2)}, u32[]{:S(2)}) collective-permute-start(bf16[128,1024]{1,0:T(8,128)(2,1)} %refs_8_.1), channel_id=1, source_target_pairs={{0,1},{1,0},{2,3},{3,2},{4,5},{5,4},{6,7},{7,6},{8,9},{9,8},{10,11... | collective-permute-start | bytes 786440 | tf_op jit(solution)/shard_map/ppermute | solution.py:400
  6.3 0.8 %concatenate.7.refs_0_.meta_ref = s32[1,20]{1,0:T(1,128)S(1)} concatenate(s32[1,1]{1,0:T(1,128)} %bitcast.3, s32[1,1]{1,0:T(1,128)} %bitcast.4, s32[1,2]{1,0:T(1,128)} %param.21, s32[1,8]{1,0:T(1,128)} %param.22, s32[1,8]{1,0:T(1,128)} %param.23), dimensions={1} | concatenate | bytes 160 | tf_op jit(solution)/shard_map/concatenate | solution.py:402
  7.1 1.0 %pad_maximum_fusion.small_ref.refs_3_ = f32[33,1024]{1,0:T(8,128)S(1)} fusion(f32[1,1024]{1,0:T(1,128)} %bitcast.9, f32[1,1024]{1,0:T(1,128)} %bitcast.10, f32[31,1024]{1,0:T(8,128)} %param.19), kind=kLoop, calls=%fused_computation | loop fusion | flops 67584 | bytes 270336 | tf_op jit(solution)/shard_map/concatenate | solution.py:412
  8.1 0.1 spread_taps.1.refs_4_
  8.2 0.0 copy-done.4
  8.2 0.0 copy-done.2
  8.2 0.0 copy-start
  8.2 1.6 %copy-done = bf16[1024,1024]{1,0:T(8,128)(2,1)S(1)} copy-done((bf16[1024,1024]{1,0:T(8,128)(2,1)S(1)}, bf16[1024,1024]{1,0:T(8,128)(2,1)}, u32[]{:S(2)}) %copy-start) | copy-done | bytes 2097176
  9.8 0.0 copy-start.6
  9.8 0.7 %copy-done.6 = f32[1024]{0:T(1024)S(1)} copy-done((f32[1024]{0:T(1024)S(1)}, f32[1024]{0:T(1024)}, u32[]{:S(2)}) %copy-start.6) | copy-done | bytes 4120
  10.5 0.0 copy-start.1
  10.5 0.8 %project_rows_0.1 = (bf16[128,1024]{1,0:T(8,128)(2,1)S(1)}, bf16[128,512]{1,0:T(8,128)(2,1)S(1)}, bf16[128,1024]{1,0:T(8,128)(2,1)S(1)}) custom-call(bf16[128,1024]{1,0:T(8,128)(2,1)S(1)} %copy-done.4, f32[1,1024]{1,0:T(1,128)S(1)} %bitcast.5, bf16[1024,512]{1,0:T(8,128)(2,1)S(1)} %copy-done.2, bf16[1024,1024]{1,0:T(8,128)(2,1)S(1)} %copy-done), custom_call_target="tpu_custom_call" | custom-call | flops 402653184 | bytes 4194304 | tf_op jit(solution)/shard_map/project_rows_0/pallas_call | solution.py:434
  11.2 5.8 %collective-permute-done.x_ref.refs_10_ = bf16[128,1024]{1,0:T(8,128)(2,1)S(1)} collective-permute-done((bf16[128,1024]{1,0:T(8,128)(2,1)}, bf16[128,1024]{1,0:T(8,128)(2,1)S(1)}, u32[]{:S(2)}, u32[]{:S(2)}) %collective-permute-start) | collective-permute-done | bytes 262176 | tf_op jit(solution)/shard_map/ppermute | solution.py:400
  17.0 0.0 copy-start.7
  17.0 0.7 %collective-permute-start.2 = (bf16[128,1024]{1,0:T(8,128)(2,1)S(1)}, bf16[128,1024]{1,0:T(8,128)(2,1)S(1)}, u32[]{:S(2)}, u32[]{:S(2)}) collective-permute-start(bf16[128,1024]{1,0:T(8,128)(2,1)S(1)} %collective-permute-done.x_ref.refs_10_), channel_id=1, source_target_pairs={{0,1},{1,0},{2,3},{3,2},{4,5},{5,4},{6,7},{7,6},{8,9},{9,8},{10,11... | collective-permute-start | bytes 786440 | tf_op jit(solution)/shard_map/ppermute | solution.py:400
  17.7 0.0 copy-done.1
  17.7 0.8 %project_rows_2.1 = (bf16[128,1024]{1,0:T(8,128)(2,1)S(1)}, bf16[128,512]{1,0:T(8,128)(2,1)S(1)}, bf16[128,1024]{1,0:T(8,128)(2,1)S(1)}) custom-call(bf16[128,1024]{1,0:T(8,128)(2,1)S(1)} %collective-permute-done.x_ref.refs_10_, f32[1,1024]{1,0:T(1,128)S(1)} %bitcast.6, bf16[1024,512]{1,0:T(8,128)(2,1)S(1)} %copy-done.2, bf16[1024,1024]{1,0:T(8,128)(2,1)S(1)} %copy-done.1), custom_call_target="tpu_custom_call" | custom-call | flops 402653184 | bytes 4194304 | tf_op jit(solution)/shard_map/project_rows_2/pallas_call | solution.py:434
  18.5 0.0 copy-start.3
  18.5 0.0 copy-start.5
  18.5 0.0 collective-permute-done.1.x_ref.refs_9_
  18.5 0.0 copy-done.7
  18.5 0.8 %project_rows_1.1 = (bf16[128,1024]{1,0:T(8,128)(2,1)S(1)}, bf16[128,512]{1,0:T(8,128)(2,1)S(1)}, bf16[128,1024]{1,0:T(8,128)(2,1)S(1)}) custom-call(bf16[128,1024]{1,0:T(8,128)(2,1)S(1)} %collective-permute-done.1.x_ref.refs_9_, f32[1,1024]{1,0:T(1,128)S(1)} %bitcast.7, bf16[1024,512]{1,0:T(8,128)(2,1)S(1)} %copy-done.2, bf16[1024,1024]{1,0:T(8,128)(2,1)S(1)} %copy-done.1), custom_call_target="tpu_custom_call" | custom-call | flops 402653184 | bytes 4194304 | tf_op jit(solution)/shard_map/project_rows_1/pallas_call | solution.py:434
  19.3 5.1 %collective-permute-done.2.refs_11_ = bf16[128,1024]{1,0:T(8,128)(2,1)S(1)} collective-permute-done((bf16[128,1024]{1,0:T(8,128)(2,1)S(1)}, bf16[128,1024]{1,0:T(8,128)(2,1)S(1)}, u32[]{:S(2)}, u32[]{:S(2)}) %collective-permute-start.2) | collective-permute-done | bytes 262176 | tf_op jit(solution)/shard_map/ppermute | solution.py:400
  24.4 0.0 copy-done.3
  24.4 0.0 copy-done.5
  24.4 7.3 %forward_pass.1 = (bf16[128,1024]{1,0:T(8,128)(2,1)}, bf16[128,1024]{1,0:T(8,128)(2,1)S(1)}, bf16[128,512]{1,0:T(8,128)(2,1)S(1)}, bf16[128,1024]{1,0:T(8,128)(2...) custom-call(s32[1,20]{1,0:T(1,128)S(1)} %concatenate.7.refs_0_.meta_, ...), custom_call_target="tpu_custom_call" | custom-call | tf_op jit(solution)/shard_map/forward_pass/pallas_call | solution.py:465
  31.7 4.3 %collective-permute-start.3 = (bf16[192,256]{1,0:T(8,128)(2,1)S(1)}, bf16[192,256]{1,0:T(8,128)(2,1)S(1)}, u32[]{:S(2)}, u32[]{:S(2)}) collective-permute-start(bf16[192,256]{1,0:T(8,128)(2,1)S(1)} %get-tuple-element.54), channel_id=1, source_target_pairs={{0,3},{1,2},{2,1},{3,0},{4,7},{5,6},{6,5},{7,4},{8,11},{9,10},{10,... | collective-permute-start | bytes 294920 | tf_op jit(solution)/shard_map/ppermute | solution.py:400
  36.0 0.0 collective-permute-start.4
  36.0 0.6 %collective-permute-start.5 = (bf16[192,256]{1,0:T(8,128)(2,1)S(1)}, bf16[192,256]{1,0:T(8,128)(2,1)S(1)}, u32[]{:S(2)}, u32[]{:S(2)}) collective-permute-start(bf16[192,256]{1,0:T(8,128)(2,1)S(1)} %get-tuple-element.56), channel_id=1, source_target_pairs={{0,1},{1,0},{2,3},{3,2},{4,5},{5,4},{6,7},{7,6},{8,9},{9,8},{10,11... | collective-permute-start | bytes 294920 | tf_op jit(solution)/shard_map/ppermute | solution.py:400
  36.6 1.5 %window_probs.1 = (bf16[704,256]{1,0:T(8,128)(2,1)S(1)}, bf16[704,256]{1,0:T(8,128)(2,1)S(1)}, f32[8,192,256]{2,1,0:T(8,128)S(1)}, f32[8,192,256]{2,1,0:T(8,128)S(1)}) custom-call(s32[1,20]{1,0:T(1,128)S(1)} %concatenate.7.refs_0_.meta_ref, bf16[128,512]{1,0:T(8,128)(2,1)S(1)} %get-tuple-element.37.refs_12_.refs_0_, ...), custom_call_target="tpu_custom_call" | custom-call | flops 2000000000 | bytes 4000000 | tf_op jit(solution)/shard_map/window_probs/pallas_call | solution.py:507
  38.2 1.5 %collective-permute-done.3.refs_9_ = bf16[192,256]{1,0:T(8,128)(2,1)S(1)} collective-permute-done((bf16[192,256]{1,0:T(8,128)(2,1)S(1)}, bf16[192,256]{1,0:T(8,128)(2,1)S(1)}, u32[]{:S(2)}, u32[]{:S(2)}) %collective-permute-start.3) | collective-permute-done | bytes 98336 | tf_op jit(solution)/shard_map/ppermute | solution.py:400
  39.7 3.9 %collective-permute-done.4.refs_10_ = bf16[192,256]{1,0:T(8,128)(2,1)S(1)} collective-permute-done((bf16[192,256]{1,0:T(8,128)(2,1)S(1)}, bf16[192,256]{1,0:T(8,128)(2,1)S(1)}, u32[]{:S(2)}, u32[]{:S(2)}) %collective-permute-start.4) | collective-permute-done | bytes 98336 | tf_op jit(solution)/shard_map/ppermute | solution.py:400
  43.6 0.0 collective-permute-done.5.refs_11_
  43.6 2.4 %key_value_terms.1 = (f32[256,512]{1,0:T(8,128)S(1)}, bf16[256,512]{1,0:T(8,128)(2,1)S(1)}) custom-call(s32[1,20]{1,0:T(1,128)S(1)} %concatenate.7.refs_0_.meta_ref, bf16[704,256]{1,0:T(8,128)(2,1)S(1)} %get-tuple-element.46.refs_1_, bf16[704,256]{1,0:T(8,128)(2,1)S(1)} %get-tuple-element.47.refs_2_, f32[8,192,256]{2,1,0:T(8,128)S(1)} %get-tuple-element.48.refs_3_, ...), custom_call_target="tpu_custom_call" | custom-call | tf_op jit(solution)/shard_map/key_value_terms/pallas_call | solution.py:527
  46.0 0.1 collective-permute-start.6
  46.1 1.5 %collective-permute-done.6.got_ref = bf16[256,512]{1,0:T(8,128)(2,1)S(1)} collective-permute-done((bf16[256,512]{1,0:T(8,128)(2,1)S(1)}, bf16[256,512]{1,0:T(8,128)(2,1)S(1)}, u32[]{:S(2)}, u32[]{:S(2)}) %collective-permute-start.6) | collective-permute-done | bytes 262176 | tf_op jit(solution)/shard_map/ppermute | solution.py:400
  47.6 0.1 sum_pair.1
  47.7 2.5 %collective-permute-start.7 = (bf16[256,128]{1,0:T(8,128)(2,1)S(1)}, bf16[256,128]{1,0:T(8,128)(2,1)S(1)}, u32[]{:S(2)}, u32[]{:S(2)}) collective-permute-start(bf16[256,128]{1,0:T(8,128)(2,1)S(1)} %get-tuple-element.60), channel_id=1, source_target_pairs={{0,24},{4,28},{8,16},{12,20},{16,8},{20,12},{24,0},{28,4},{1,25},{... | collective-permute-start | bytes 196616 | tf_op jit(solution)/shard_map/ppermute | solution.py:400
  50.2 0.5 collective-permute-start.8
  50.7 0.5 collective-permute-start.9
  51.3 1.7 %collective-permute-done.7.refs_0_ = bf16[256,128]{1,0:T(8,128)(2,1)S(1)} collective-permute-done((bf16[256,128]{1,0:T(8,128)(2,1)S(1)}, bf16[256,128]{1,0:T(8,128)(2,1)S(1)}, u32[]{:S(2)}, u32[]{:S(2)}) %collective-permute-start.7) | collective-permute-done | bytes 65568 | tf_op jit(solution)/shard_map/ppermute | solution.py:400
  53.0 1.5 %collective-permute-done.8.refs_1_ = bf16[256,128]{1,0:T(8,128)(2,1)S(1)} collective-permute-done((bf16[256,128]{1,0:T(8,128)(2,1)S(1)}, bf16[256,128]{1,0:T(8,128)(2,1)S(1)}, u32[]{:S(2)}, u32[]{:S(2)}) %collective-permute-start.8) | collective-permute-done | bytes 65568 | tf_op jit(solution)/shard_map/ppermute | solution.py:400
  54.5 0.5 collective-permute-done.9.refs_2_
  55.0 0.8 %sum_groups.1 = f32[128,256]{1,0:T(8,128)} custom-call(bf16[256,128]{1,0:T(8,128)(2,1)S(1)} %collective-permute-done.7.refs_0_, bf16[256,128]{1,0:T(8,128)(2,1)S(1)} %collective-permute-done.8.refs_1_, bf16[256,128]{1,0:T(8,128)(2,1)S(1)} %collective-permute-done.9.refs_2_, bf16[256,128]{1,0:T(8,128)(2,1)S(1)} %get-tuple-element.63.refs_3_), custom_call_target="tpu_custom_call" | custom-call | tf_op jit(solution)/shard_map/sum_groups/pallas_call | solution.py:558
Async XLA Ops:
  0.6 7.5 %copy-start.4 = (bf16[128,1024]{1,0:T(8,128)(2,1)S(1)}, bf16[128,1024]{1,0:T(8,128)(2,1)}, u32[]{:S(2)}) copy-start(bf16[128,1024]{1,0:T(8,128)(2,1)} %refs_8_.1) | copy-start | bytes 786436
  0.6 7.5 %copy-start.2 = (bf16[1024,512]{1,0:T(8,128)(2,1)S(1)}, bf16[1024,512]{1,0:T(8,128)(2,1)}, u32[]{:S(2)}) copy-start(bf16[1024,512]{1,0:T(8,128)(2,1)} %refs_6_.1) | copy-start | bytes 3145732
  0.7 16.3 %collective-permute-start = (bf16[128,1024]{1,0:T(8,128)(2,1)}, bf16[128,1024]{1,0:T(8,128)(2,1)S(1)}, u32[]{:S(2)}, u32[]{:S(2)}) collective-permute-start(bf16[128,1024]{1,0:T(8,128)(2,1)} %refs_8_.1), channel_id=1, source_target_pairs={{0,2},{1,3},{2,0},{3,1},{4,6},{5,7},{6,4},{7,5},{8,10},{9,11},{10,... | collective-permute-start | bytes 786440 | tf_op jit(solution)/shard_map/ppermute | solution.py:400
  4.8 13.8 %collective-permute-start.1 = (bf16[128,1024]{1,0:T(8,128)(2,1)}, bf16[128,1024]{1,0:T(8,128)(2,1)S(1)}, u32[]{:S(2)}, u32[]{:S(2)}) collective-permute-start(bf16[128,1024]{1,0:T(8,128)(2,1)} %refs_8_.1), channel_id=1, source_target_pairs={{0,1},{1,0},{2,3},{3,2},{4,5},{5,4},{6,7},{7,6},{8,9},{9,8},{10,11... | collective-permute-start | bytes 786440 | tf_op jit(solution)/shard_map/ppermute | solution.py:400
  8.2 1.6 %copy-start = (bf16[1024,1024]{1,0:T(8,128)(2,1)S(1)}, bf16[1024,1024]{1,0:T(8,128)(2,1)}, u32[]{:S(2)}) copy-start(bf16[1024,1024]{1,0:T(8,128)(2,1)} %refs_7_.1) | copy-start | bytes 6291460
  9.8 0.7 %copy-start.6 = (f32[1024]{0:T(1024)S(1)}, f32[1024]{0:T(1024)}, u32[]{:S(2)}) copy-start(f32[1024]{0:T(1024)} %param.14) | copy-start | bytes 12292
  10.5 7.3 %copy-start.1 = (bf16[1024,1024]{1,0:T(8,128)(2,1)S(1)}, bf16[1024,1024]{1,0:T(8,128)(2,1)}, u32[]{:S(2)}) copy-start(bf16[1024,1024]{1,0:T(8,128)(2,1)} %refs_7_.1) | copy-start | bytes 6291460
  17.0 1.5 %copy-start.7 = (f32[1024]{0:T(1024)S(1)}, f32[1024]{0:T(1024)}, u32[]{:S(2)}) copy-start(f32[1024]{0:T(1024)} %param.14) | copy-start | bytes 12292
  17.0 7.4 %collective-permute-start.2 = (bf16[128,1024]{1,0:T(8,128)(2,1)S(1)}, bf16[128,1024]{1,0:T(8,128)(2,1)S(1)}, u32[]{:S(2)}, u32[]{:S(2)}) collective-permute-start(bf16[128,1024]{1,0:T(8,128)(2,1)S(1)} %collective-permute-done.x_ref.refs_10_), channel_id=1, source_target_pairs={{0,1},{1,0},{2,3},{3,2},{4,5},{5,4},{6,7},{7,6},{8,9},{9,8},{10,11... | collective-permute-start | bytes 786440 | tf_op jit(solution)/shard_map/ppermute | solution.py:400
  18.5 6.0 %copy-start.3 = (bf16[512,1024]{1,0:T(8,128)(2,1)S(1)}, bf16[512,1024]{1,0:T(8,128)(2,1)}, u32[]{:S(2)}) copy-start(bf16[512,1024]{1,0:T(8,128)(2,1)} %refs_2_.1) | copy-start | bytes 3145732
  18.5 5.9 %copy-start.5 = (bf16[128,1024]{1,0:T(8,128)(2,1)S(1)}, bf16[128,1024]{1,0:T(8,128)(2,1)}, u32[]{:S(2)}) copy-start(bf16[128,1024]{1,0:T(8,128)(2,1)} %refs_1_.1) | copy-start | bytes 786436
  31.7 8.0 %collective-permute-start.3 = (bf16[192,256]{1,0:T(8,128)(2,1)S(1)}, bf16[192,256]{1,0:T(8,128)(2,1)S(1)}, u32[]{:S(2)}, u32[]{:S(2)}) collective-permute-start(bf16[192,256]{1,0:T(8,128)(2,1)S(1)} %get-tuple-element.54), channel_id=1, source_target_pairs={{0,3},{1,2},{2,1},{3,0},{4,7},{5,6},{6,5},{7,4},{8,11},{9,10},{10,... | collective-permute-start | bytes 294920 | tf_op jit(solution)/shard_map/ppermute | solution.py:400
  36.0 7.6 %collective-permute-start.4 = (bf16[192,256]{1,0:T(8,128)(2,1)S(1)}, bf16[192,256]{1,0:T(8,128)(2,1)S(1)}, u32[]{:S(2)}, u32[]{:S(2)}) collective-permute-start(bf16[192,256]{1,0:T(8,128)(2,1)S(1)} %get-tuple-element.55), channel_id=1, source_target_pairs={{0,2},{1,3},{2,0},{3,1},{4,6},{5,7},{6,4},{7,5},{8,10},{9,11},{10,... | collective-permute-start | bytes 294920 | tf_op jit(solution)/shard_map/ppermute | solution.py:400
  36.0 7.6 %collective-permute-start.5 = (bf16[192,256]{1,0:T(8,128)(2,1)S(1)}, bf16[192,256]{1,0:T(8,128)(2,1)S(1)}, u32[]{:S(2)}, u32[]{:S(2)}) collective-permute-start(bf16[192,256]{1,0:T(8,128)(2,1)S(1)} %get-tuple-element.56), channel_id=1, source_target_pairs={{0,1},{1,0},{2,3},{3,2},{4,5},{5,4},{6,7},{7,6},{8,9},{9,8},{10,11... | collective-permute-start | bytes 294920 | tf_op jit(solution)/shard_map/ppermute | solution.py:400
  46.0 1.6 %collective-permute-start.6 = (bf16[256,512]{1,0:T(8,128)(2,1)S(1)}, bf16[256,512]{1,0:T(8,128)(2,1)S(1)}, u32[]{:S(2)}, u32[]{:S(2)}) collective-permute-start(bf16[256,512]{1,0:T(8,128)(2,1)S(1)} %get-tuple-element.59), channel_id=1, source_target_pairs={{0,4},{4,0},{8,12},{12,8},{16,20},{20,16},{24,28},{28,24},{1,5},{5... | collective-permute-start | bytes 786440 | tf_op jit(solution)/shard_map/ppermute | solution.py:400
  47.7 5.3 %collective-permute-start.7 = (bf16[256,128]{1,0:T(8,128)(2,1)S(1)}, bf16[256,128]{1,0:T(8,128)(2,1)S(1)}, u32[]{:S(2)}, u32[]{:S(2)}) collective-permute-start(bf16[256,128]{1,0:T(8,128)(2,1)S(1)} %get-tuple-element.60), channel_id=1, source_target_pairs={{0,24},{4,28},{8,16},{12,20},{16,8},{20,12},{24,0},{28,4},{1,25},{... | collective-permute-start | bytes 196616 | tf_op jit(solution)/shard_map/ppermute | solution.py:400
  50.2 4.3 %collective-permute-start.8 = (bf16[256,128]{1,0:T(8,128)(2,1)S(1)}, bf16[256,128]{1,0:T(8,128)(2,1)S(1)}, u32[]{:S(2)}, u32[]{:S(2)}) collective-permute-start(bf16[256,128]{1,0:T(8,128)(2,1)S(1)} %get-tuple-element.61), channel_id=1, source_target_pairs={{0,16},{4,20},{8,24},{12,28},{16,0},{20,4},{24,8},{28,12},{1,17},{... | collective-permute-start | bytes 196616 | tf_op jit(solution)/shard_map/ppermute | solution.py:400
  50.7 4.3 %collective-permute-start.9 = (bf16[256,128]{1,0:T(8,128)(2,1)S(1)}, bf16[256,128]{1,0:T(8,128)(2,1)S(1)}, u32[]{:S(2)}, u32[]{:S(2)}) collective-permute-start(bf16[256,128]{1,0:T(8,128)(2,1)S(1)} %get-tuple-element.62), channel_id=1, source_target_pairs={{0,8},{4,12},{8,0},{12,4},{16,24},{20,28},{24,16},{28,20},{1,9},{5... | collective-permute-start | bytes 196616 | tf_op jit(solution)/shard_map/ppermute | solution.py:400

commit v9 on v8

--- a/solution.py
+++ b/solution.py
@@ -112,7 +112,8 @@
     return exped * (1.0 / total), unit
 
 
-def taps_kernel(small_ref, taps_ref):
+def taps_kernel(small_ref, wo_ref, taps_ref, wot_ref):
+    wot_ref[...] = wo_ref[...].T
     for j in range(KERNEL):
         rows = jnp.broadcast_to(small_ref[j : j + 1], (SUB, small_ref.shape[1]))
         taps_ref[j * SUB : (j + 1) * SUB] = rows
@@ -131,8 +132,9 @@
 
 
 def forward_kernel(sizes, tm, head_size, *refs):
-    tables_ref, grad_ref, wo_ref, small_ref, taps_ref, g1_ref, wq_ref, wkv_ref = refs[:8]
-    refs = refs[8:]
+    tables_ref, grad_ref, wo_ref, wot_ref, small_ref, taps_ref = refs[:6]
+    g1_ref, wq_ref, wkv_ref = refs[6:9]
+    refs = refs[9:]
     x_refs = refs[:tm]
     q_refs, kv_refs = (refs[tm + k * (tm - 1) : tm + (k + 1) * (tm - 1)] for k in range(2))
     refs = refs[3 * tm - 2 :]
@@ -171,11 +173,17 @@
     side_f = diag_mask(HEADS, HALO, head_size)
     side_b = side_f.astype(BF16)
 
+    ones = jnp.ones((SPAN, LANES), BF16)
+    key_block = lax.broadcasted_iota(jnp.int32, (1, SPAN), 1) // BLOCK
     own = [table.block_of(me * local + i) for i in range(local)]
     keep = [jnp.where(table.position(c) >= 1, 1.0, 0.0).astype(F32) for c in own]
     for i, c in enumerate(own):
         for blk, shift, count, put in ((c - 1, HALO, HALO, 0), (c, 0, BLOCK, HALO)):
             reach = table.reach(blk)
+            allowed = jnp.ones((1, SPAN), F32)
+            for w in range(LC):
+                ok = jnp.where(reach >= LC - w, 1.0, 0.0).astype(F32)
+                allowed = jnp.where(key_block == w, ok, allowed)
             win = row_at(blk - LC, SPAN)
             at = row_at(blk, count, shift)
             if count == BLOCK:
@@ -186,12 +194,14 @@
             for g in range(groups):
                 cols = slice(g * wide, (g + 1) * wide)
                 vcols = slice(hq + g * wide, hq + (g + 1) * wide)
-                probs, _ = window_probs(
-                    spread(q_ref[at, cols], mask_b), kv_ref[win, cols], reach, head_size
-                )
-                full = dot_tn(probs.astype(BF16), kv_ref[win, vcols])
+                raw = dot_nt(spread(q_ref[at, cols], mask_b), kv_ref[win, cols])
+                unit = jnp.tanh(raw * (1.0 / (SOFT_CAP * math.sqrt(head_size))))
+                exped = (jnp.exp(SOFT_CAP * unit) * allowed).astype(BF16)
+                inverse = 1.0 / dot_nn(exped, ones)
+                scale = mask_f * jnp.concatenate([inverse] * (wide // LANES), axis=1)
+                full = dot_nn(exped, kv_ref[win, vcols])
                 ctx_s[i * ROWS + put : i * ROWS + put + count, cols] = fold_heads(
-                    full, mask_f, count
+                    full, scale, count
                 ).astype(BF16)
 
     gain = small_ref[KERNEL + 1 : KERNEL + 2]
@@ -265,14 +275,17 @@
         gc_s[i * ROWS + HALO : (i + 1) * ROWS] = own_grad.astype(BF16)
     for m in range(half):
         at = pl.ds(pl.multiple_of(((me ^ m) % half) * share, share), share)
-        grad_context = dot_nt(gc_s[...], wo_ref[at]).astype(BF16)
+        grad_context = dot_nn(gc_s[...], wot_ref[:, at]).astype(BF16)
         send_refs[m][...] = grad_context
         send_refs[m + half][...] = grad_context
 
 
 def probs_kernel(sizes, tm, head_size, meta_ref, *refs):
-    q_refs, kv_refs = refs[:tm], refs[tm : 2 * tm]
-    q4_ref, v4_ref, p_ref, d_ref, k4_ref = refs[2 * tm :]
+    q_refs, kv_refs, n_refs = refs[:tm], refs[tm : 2 * tm], refs[2 * tm : 3 * tm]
+    q4_ref, v4_ref, p_ref, d_ref, nt_ref, k4_ref = refs[3 * tm :]
+    for m in range(tm):
+        rows = n_refs[m].shape[0]
+        nt_ref[:, m * rows : (m + 1) * rows] = n_refs[m][...].T
     table = Layout(meta_ref, *sizes)
     me = table.me()
     local = table.blocks // tm
@@ -300,11 +313,14 @@
 
 
 def backward_kernel(sizes, tm, part, head_size, *refs):
-    meta_ref, q4_ref, v4_ref, p_ref, d_ref = refs[:5]
-    n_refs = refs[5 : 5 + tm]
-    g_refs = refs[5 + tm : 5 + 2 * tm][::-1]
-    out_refs = refs[5 + 2 * tm : -3]
-    gt_s, t_s, full_s = refs[-3:]
+    tables_ref, q4_ref, v4_ref, p_ref, d_ref, nt_ref = refs[:6]
+    g_refs = refs[6 : 6 + tm][::-1]
+    out_refs = refs[6 + tm : -5]
+    gt_s, t_s, full_s, meta_ref, sem = refs[-5:]
+    fetch = pltpu.make_async_copy(tables_ref, meta_ref, sem)
+    fetch.start()
+    t_s[...] = jnp.zeros(t_s.shape, F32)
+    fetch.wait()
     table = Layout(meta_ref, *sizes)
     me = table.me()
     blocks = table.blocks
@@ -319,7 +335,6 @@
     for m, j, b in places:
         at = row_at(b, HALO, -HALO)
         gt_s[at] = gt_s[at] + g_refs[m][j * ROWS : j * ROWS + HALO].astype(F32)
-    t_s[...] = jnp.zeros(t_s.shape, F32)
 
     def spans(c):
         own = slice((c + PAD) * BLOCK, (c + PAD + 1) * BLOCK)
@@ -343,30 +358,30 @@
             t_s[win] = t_s[win] + dot_nn(grad_raw.astype(BF16), spread(q4_ref[own], mask_b))
 
     terms = jnp.concatenate([t_s[row_at(b)].astype(BF16) for _, _, b in places], axis=0)
-    full = dot_tn(terms, jnp.concatenate([ref[...] for ref in n_refs], axis=0))
+    full = dot_nn(nt_ref[...], terms)
     if len(out_refs) == 1:
         out_refs[0][...] = full.astype(BF16)
         return
     full_s[...] = full
     chip, core = table.dp() // 2, table.dp() % 2
-    for q in range(out_refs[0].shape[1] // part):
+    for q in range(out_refs[0].shape[0] // part):
         for ref, side in zip(out_refs, (core, 1 - core)):
             at = pl.ds(pl.multiple_of(((chip ^ q) * 2 + side) * part, part), part)
-            ref[:, q * part : (q + 1) * part] = full_s[:, at].astype(ref.dtype)
+            ref[q * part : (q + 1) * part] = full_s[at].astype(ref.dtype)
 
 
 def pair_kernel(kept_ref, got_ref, *out_refs):
-    part = out_refs[0].shape[1]
+    part = out_refs[0].shape[0]
     for q, ref in enumerate(out_refs):
-        cols = slice(q * part, (q + 1) * part)
-        ref[...] = (kept_ref[:, cols] + got_ref[:, cols].astype(F32)).astype(ref.dtype)
+        rows = slice(q * part, (q + 1) * part)
+        ref[...] = (kept_ref[rows] + got_ref[rows].astype(F32)).astype(ref.dtype)
 
 
 def sum_kernel(*refs):
     total = refs[0][...].astype(F32)
     for ref in refs[1:-1]:
         total = total + ref[...].astype(F32)
-    refs[-1][...] = total.T
+    refs[-1][...] = total
 
 
 def on_device(
@@ -417,15 +432,15 @@
     vmem = pl.BlockSpec(memory_space=pltpu.VMEM)
     shape = jax.ShapeDtypeStruct
 
-    taps = pl.pallas_call(
+    taps, w_out_t = pl.pallas_call(
         taps_kernel,
-        out_shape=shape((KERNEL * SUB, width), F32),
-        in_specs=[vmem],
-        out_specs=vmem,
+        out_shape=[shape((KERNEL * SUB, width), F32), shape((width, hq), BF16)],
+        in_specs=[vmem] * 2,
+        out_specs=[vmem] * 2,
         compiler_params=pltpu.CompilerParams(vmem_limit_bytes=4 << 20),
         cost_estimate=pl.CostEstimate(flops=10**6, bytes_accessed=1 << 20, transcendentals=0),
         name="spread_taps",
-    )(small)
+    )(small, w_out)
 
     x, normed, queries, keys_values = {}, {}, {}, {}
     made = [shape((rows, w), BF16) for w in (width, hq, kv_width)]
@@ -467,7 +482,7 @@
         out_shape=[shape((rows, width), BF16)]
         + made
         + [shape((own_rows, share), BF16)] * tm,
-        in_specs=[pl.BlockSpec(memory_space=pl.ANY)] + [vmem] * (5 + 3 * tm),
+        in_specs=[pl.BlockSpec(memory_space=pl.ANY)] + [vmem] * (6 + 3 * tm),
         out_specs=[vmem] * (tm + 4),
         scratch_shapes=[
             pltpu.VMEM((padded, hq), BF16),
@@ -488,6 +503,7 @@
         meta,
         out_grad,
         w_out,
+        w_out_t,
         small,
         taps,
         norm1_gain.reshape(1, -1),
@@ -504,39 +520,42 @@
         got[m] = swap(sends[m], "tm", tm, m)
 
     pair_width = share // head_size * BLOCK
-    q4, v4, probs, slopes = pl.pallas_call(
+    q4, v4, probs, slopes, normed_t = pl.pallas_call(
         functools.partial(probs_kernel, sizes, tm, head_size),
         out_shape=[shape((padded, share), BF16)] * 2
-        + [shape((blocks, SPAN, pair_width), F32)] * 2,
-        in_specs=[smem] + [vmem] * (2 * tm),
-        out_specs=[vmem] * 4,
+        + [shape((blocks, SPAN, pair_width), F32)] * 2
+        + [shape((width, blocks * BLOCK), BF16)],
+        in_specs=[smem] + [vmem] * (3 * tm),
+        out_specs=[vmem] * 5,
         scratch_shapes=[pltpu.VMEM((padded, share), BF16)],
         compiler_params=pltpu.CompilerParams(vmem_limit_bytes=8 << 20),
         name="window_probs",
         cost_estimate=pl.CostEstimate(
             flops=2 * 10**9, bytes_accessed=4 * 10**6, transcendentals=800000
         ),
-    )(meta, *by_m(queries), *by_m(keys_values))
+    )(meta, *by_m(queries), *by_m(keys_values), *by_m(normed))
 
     direct = dp <= 8
     half_width = width // 2
     if direct:
-        piece_shapes = [shape((share, half_width), F32), shape((share, half_width), BF16)]
+        piece_shapes = [shape((half_width, share), F32), shape((half_width, share), BF16)]
     else:
-        piece_shapes = [shape((share, width), BF16)]
+        piece_shapes = [shape((width, share), BF16)]
     pieces = pl.pallas_call(
         functools.partial(backward_kernel, sizes, tm, width // dp, head_size),
         out_shape=piece_shapes,
-        in_specs=[smem] + [vmem] * (4 + 2 * tm),
+        in_specs=[pl.BlockSpec(memory_space=pl.ANY)] + [vmem] * (5 + tm),
         out_specs=[vmem] * len(piece_shapes),
         scratch_shapes=[
             pltpu.VMEM((padded, share), F32),
             pltpu.VMEM((padded, share), F32),
-            pltpu.VMEM((share, width), F32),
+            pltpu.VMEM((width, share), F32),
+            pltpu.SMEM(meta.shape, jnp.int32),
+            pltpu.SemaphoreType.DMA,
         ],
         compiler_params=pltpu.CompilerParams(vmem_limit_bytes=12 << 20),
         name="key_value_terms",
-    )(meta, q4, v4, probs, slopes, *by_m(normed), *by_m(got)[::-1])
+    )(meta, q4, v4, probs, slopes, normed_t, *by_m(got)[::-1])
 
     if direct:
         kept, away = pieces
@@ -545,7 +564,7 @@
         part = width // dp
         summed = pl.pallas_call(
             pair_kernel,
-            out_shape=[shape((share, part), BF16)] * chips,
+            out_shape=[shape((part, share), BF16)] * chips,
             in_specs=[vmem] * 2,
             out_specs=[vmem] * chips,
             compiler_params=pltpu.CompilerParams(vmem_limit_bytes=4 << 20),
@@ -554,7 +573,7 @@
         terms = [swap(summed[q], "dp", dp, 2 * q) for q in range(chips - 1, 0, -1)]
         terms.append(summed[0])
     else:
-        terms = [lax.psum_scatter(pieces[0], "dp", scatter_dimension=1, tiled=True)]
+        terms = [lax.psum_scatter(pieces[0], "dp", scatter_dimension=0, tiled=True)]
     kv_grad = pl.pallas_call(
         sum_kernel,
         out_shape=shape((width // dp, share), F32),

time: 56 us -> 56 us (level)
  waiting for transfers between devices: 21.6 us -> 19 us
  local copies, waits for them, and re-layouts: 3.07 us -> 5.25 us
    ppermute x10, waiting for transfers between devices: 21.6 us -> 19 us  [swap(): return lax.ppermute(value, axis, [(i, i ^ m) for i in range(size)])]
    unnamed x16 -> x20, local copies, waits for them, and re-layouts: 2.3 us -> 4.47 us
  transfers between devices with their start and end apart: 10 -> 10, of which waited for: 8 -> 8; matrix products, arithmetic and copies ran while one was open for 3% -> 3% of each run, Pallas kernels for 7% -> 8%
where the time goes in v9:
time: 56 us; the launch traced here: 55.7 us
  waiting for transfers between devices  19 us (34%)
  starting transfers between devices  14.9 us (27%)
  Pallas kernels  14.8 us (26%)
  local copies, waits for them, and re-layouts  5.25 us (9%)
  other arithmetic  0.96 us (2%)
  between operations  0.79 us (1%)
    ppermute x10, waiting for transfers between devices, swap(): return lax.ppermute(value, axis, [(i, i ^ m) for i in range(size)])  19 us
    ppermute x10, starting transfers between devices, swap(): return lax.ppermute(value, axis, [(i, i ^ m) for i in range(size)])  14.9 us
    pallas_call x1, Pallas kernels, on_device(): pl.pallas_call(functools.partial(forward_kernel, sizes, tm, head_size), o...  7.47 us
    unnamed x20, local copies, waits for them, and re-layouts  4.47 us
    pallas_call x1, Pallas kernels, on_device(): pl.pallas_call(functools.partial(backward_kernel, sizes, tm, width // dp,...  2.3 us
    pallas_call x3, Pallas kernels, project_shard(): pl.pallas_call(project_kernel, out_shape=made, in_specs=[vmem] * 4, out_s...  2.28 us
    pallas_call x1, Pallas kernels, on_device(): pl.pallas_call(functools.partial(probs_kernel, sizes, tm, head_size), out...  1.62 us
  transfers between devices with their start and end apart: 10, of which 8 were waited for; matrix products, arithmetic and copies ran while one was open for 3% of the time, Pallas kernels for 8%

profile of v9, /device:TPU:0, one launch (start us, length us, event | category | flops | bytes accessed | tf_op | source)
XLA Modules:
  0.0 55.7 jit_solution(188151785225557582)
XLA Ops:
  0.6 0.0 copy-start.2
  0.6 4.1 %collective-permute-start = (bf16[128,1024]{1,0:T(8,128)(2,1)}, bf16[128,1024]{1,0:T(8,128)(2,1)S(1)}, u32[]{:S(2)}, u32[]{:S(2)}) collective-permute-start(bf16[128,1024]{1,0:T(8,128)(2,1)} %refs_9_.1), channel_id=1, source_target_pairs={{0,2},{1,3},{2,0},{3,1},{4,6},{5,7},{6,4},{7,5},{8,10},{9,11},{10,... | collective-permute-start | bytes 786440 | tf_op jit(solution)/shard_map/ppermute | solution.py:415
  4.7 1.6 %collective-permute-start.1 = (bf16[128,1024]{1,0:T(8,128)(2,1)}, bf16[128,1024]{1,0:T(8,128)(2,1)S(1)}, u32[]{:S(2)}, u32[]{:S(2)}) collective-permute-start(bf16[128,1024]{1,0:T(8,128)(2,1)} %refs_9_.1), channel_id=1, source_target_pairs={{0,1},{1,0},{2,3},{3,2},{4,5},{5,4},{6,7},{7,6},{8,9},{9,8},{10,11... | collective-permute-start | bytes 786440 | tf_op jit(solution)/shard_map/ppermute | solution.py:415
  6.3 0.8 %concatenate.7.refs_0_.meta_ref = s32[1,20]{1,0:T(1,128)S(1)} concatenate(s32[1,1]{1,0:T(1,128)} %bitcast.3, s32[1,1]{1,0:T(1,128)} %bitcast.4, s32[1,2]{1,0:T(1,128)} %param.21, s32[1,8]{1,0:T(1,128)} %param.22, s32[1,8]{1,0:T(1,128)} %param.23), dimensions={1} | concatenate | bytes 160 | tf_op jit(solution)/shard_map/concatenate | solution.py:417
  7.1 1.0 %pad_maximum_fusion.small_ref.refs_4_ = f32[33,1024]{1,0:T(8,128)S(1)} fusion(f32[1,1024]{1,0:T(1,128)} %bitcast.9, f32[1,1024]{1,0:T(1,128)} %bitcast.10, f32[31,1024]{1,0:T(8,128)} %param.19), kind=kLoop, calls=%fused_computation | loop fusion | flops 67584 | bytes 270336 | tf_op jit(solution)/shard_map/concatenate | solution.py:427
  8.1 0.0 copy-start.3
  8.1 1.2 %copy-done.3 = bf16[512,1024]{1,0:T(8,128)(2,1)S(1)} copy-done((bf16[512,1024]{1,0:T(8,128)(2,1)S(1)}, bf16[512,1024]{1,0:T(8,128)(2,1)}, u32[]{:S(2)}) %copy-start.3) | copy-done | bytes 1048600
  9.3 0.4 spread_taps.1
  9.6 0.0 copy-done.2
  9.7 0.0 copy-start
  9.7 1.6 %copy-done = bf16[1024,1024]{1,0:T(8,128)(2,1)S(1)} copy-done((bf16[1024,1024]{1,0:T(8,128)(2,1)S(1)}, bf16[1024,1024]{1,0:T(8,128)(2,1)}, u32[]{:S(2)}) %copy-start) | copy-done | bytes 2097176
  11.3 0.0 copy-start.5
  11.3 0.9 %copy-done.5 = bf16[128,1024]{1,0:T(8,128)(2,1)S(1)} copy-done((bf16[128,1024]{1,0:T(8,128)(2,1)S(1)}, bf16[128,1024]{1,0:T(8,128)(2,1)}, u32[]{:S(2)}) %copy-start.5) | copy-done | bytes 262168
  12.2 0.0 copy-start.8
  12.2 0.7 %copy-done.8 = f32[1024]{0:T(1024)S(1)} copy-done((f32[1024]{0:T(1024)S(1)}, f32[1024]{0:T(1024)}, u32[]{:S(2)}) %copy-start.8) | copy-done | bytes 4120
  12.9 0.0 copy-start.1
  12.9 0.8 %project_rows_0.1 = (bf16[128,1024]{1,0:T(8,128)(2,1)S(1)}, bf16[128,512]{1,0:T(8,128)(2,1)S(1)}, bf16[128,1024]{1,0:T(8,128)(2,1)S(1)}) custom-call(bf16[128,1024]{1,0:T(8,128)(2,1)S(1)} %copy-done.5, f32[1,1024]{1,0:T(1,128)S(1)} %bitcast.5, bf16[1024,512]{1,0:T(8,128)(2,1)S(1)} %copy-done.2, bf16[1024,1024]{1,0:T(8,128)(2,1)S(1)} %copy-done), custom_call_target="tpu_custom_call" | custom-call | flops 402653184 | bytes 4194304 | tf_op jit(solution)/shard_map/project_rows_0/pallas_call | solution.py:449
  13.7 3.3 %collective-permute-done.x_ref.refs_11_ = bf16[128,1024]{1,0:T(8,128)(2,1)S(1)} collective-permute-done((bf16[128,1024]{1,0:T(8,128)(2,1)}, bf16[128,1024]{1,0:T(8,128)(2,1)S(1)}, u32[]{:S(2)}, u32[]{:S(2)}) %collective-permute-start) | collective-permute-done | bytes 262176 | tf_op jit(solution)/shard_map/ppermute | solution.py:415
  17.0 0.0 copy-start.9
  17.0 0.7 %collective-permute-start.2 = (bf16[128,1024]{1,0:T(8,128)(2,1)S(1)}, bf16[128,1024]{1,0:T(8,128)(2,1)S(1)}, u32[]{:S(2)}, u32[]{:S(2)}) collective-permute-start(bf16[128,1024]{1,0:T(8,128)(2,1)S(1)} %collective-permute-done.x_ref.refs_11_), channel_id=1, source_target_pairs={{0,1},{1,0},{2,3},{3,2},{4,5},{5,4},{6,7},{7,6},{8,9},{9,8},{10,11... | collective-permute-start | bytes 786440 | tf_op jit(solution)/shard_map/ppermute | solution.py:415
  17.7 0.0 copy-done.1
  17.7 0.8 %project_rows_2.1 = (bf16[128,1024]{1,0:T(8,128)(2,1)S(1)}, bf16[128,512]{1,0:T(8,128)(2,1)S(1)}, bf16[128,1024]{1,0:T(8,128)(2,1)S(1)}) custom-call(bf16[128,1024]{1,0:T(8,128)(2,1)S(1)} %collective-permute-done.x_ref.refs_11_, f32[1,1024]{1,0:T(1,128)S(1)} %bitcast.6, bf16[1024,512]{1,0:T(8,128)(2,1)S(1)} %copy-done.2, bf16[1024,1024]{1,0:T(8,128)(2,1)S(1)} %copy-done.1), custom_call_target="tpu_custom_call" | custom-call | flops 402653184 | bytes 4194304 | tf_op jit(solution)/shard_map/project_rows_2/pallas_call | solution.py:449
  18.5 0.0 copy-start.4
  18.5 0.0 copy-start.6
  18.5 0.0 copy-start.7
  18.5 0.0 collective-permute-done.1.x_ref.refs_10_
  18.5 0.0 copy-done.9
  18.5 0.8 %project_rows_1.1 = (bf16[128,1024]{1,0:T(8,128)(2,1)S(1)}, bf16[128,512]{1,0:T(8,128)(2,1)S(1)}, bf16[128,1024]{1,0:T(8,128)(2,1)S(1)}) custom-call(bf16[128,1024]{1,0:T(8,128)(2,1)S(1)} %collective-permute-done.1.x_ref.refs_10_, f32[1,1024]{1,0:T(1,128)S(1)} %bitcast.7, bf16[1024,512]{1,0:T(8,128)(2,1)S(1)} %copy-done.2, bf16[1024,1024]{1,0:T(8,128)(2,1)S(1)} %copy-done.1), custom_call_target="tpu_custom_call" | custom-call | flops 402653184 | bytes 4194304 | tf_op jit(solution)/shard_map/project_rows_1/pallas_call | solution.py:449
  19.3 5.1 %collective-permute-done.2.refs_12_ = bf16[128,1024]{1,0:T(8,128)(2,1)S(1)} collective-permute-done((bf16[128,1024]{1,0:T(8,128)(2,1)S(1)}, bf16[128,1024]{1,0:T(8,128)(2,1)S(1)}, u32[]{:S(2)}, u32[]{:S(2)}) %collective-permute-start.2) | collective-permute-done | bytes 262176 | tf_op jit(solution)/shard_map/ppermute | solution.py:415
  24.4 0.0 copy-done.4
  24.4 0.0 copy-done.6
  24.4 0.0 copy-done.7
  24.4 7.5 %forward_pass.1 = (bf16[128,1024]{1,0:T(8,128)(2,1)}, bf16[128,1024]{1,0:T(8,128)(2,1)S(1)}, bf16[128,512]{1,0:T(8,128)(2,1)S(1)}, bf16[128,1024]{1,0:T(8,128)(2...) custom-call(s32[1,20]{1,0:T(1,128)S(1)} %concatenate.7.refs_0_.meta_, ...), custom_call_target="tpu_custom_call" | custom-call | tf_op jit(solution)/shard_map/forward_pass/pallas_call | solution.py:480
  31.9 4.3 %collective-permute-start.3 = (bf16[192,256]{1,0:T(8,128)(2,1)S(1)}, bf16[192,256]{1,0:T(8,128)(2,1)S(1)}, u32[]{:S(2)}, u32[]{:S(2)}) collective-permute-start(bf16[192,256]{1,0:T(8,128)(2,1)S(1)} %get-tuple-element.60), channel_id=1, source_target_pairs={{0,3},{1,2},{2,1},{3,0},{4,7},{5,6},{6,5},{7,4},{8,11},{9,10},{10,... | collective-permute-start | bytes 294920 | tf_op jit(solution)/shard_map/ppermute | solution.py:415
  36.2 0.0 collective-permute-start.4
  36.2 0.6 %collective-permute-start.5 = (bf16[192,256]{1,0:T(8,128)(2,1)S(1)}, bf16[192,256]{1,0:T(8,128)(2,1)S(1)}, u32[]{:S(2)}, u32[]{:S(2)}) collective-permute-start(bf16[192,256]{1,0:T(8,128)(2,1)S(1)} %get-tuple-element.62), channel_id=1, source_target_pairs={{0,1},{1,0},{2,3},{3,2},{4,5},{5,4},{6,7},{7,6},{8,9},{9,8},{10,11... | collective-permute-start | bytes 294920 | tf_op jit(solution)/shard_map/ppermute | solution.py:415
  36.8 1.6 %window_probs.1 = (bf16[704,256]{1,0:T(8,128)(2,1)S(1)}, bf16[704,256]{1,0:T(8,128)(2,1)S(1)}, f32[8,192,256]{2,1,0:T(8,128)S(1)}, f32[8,192,256]{2,1,0:T(8,128)S(1)}, bf16[1024,512]{1,0:T(8,128)(2,1)S(1)}) custom-call(s32[1,20]{1,0:T(1,128)S(1)} %concatenate.7.refs_0_.meta_ref, bf16[128,512]{1,0:T(8,128)(2,1)S(1)} %get-tuple-element.42.refs_13_.refs_0_, ...), custom_call_target="tpu_custom_call" | custom-call | flops 2000000000 | bytes 4000000 | tf_op jit(solution)/shard_map/window_probs/pallas_call | solution.py:523
  38.5 1.4 %collective-permute-done.3.refs_6_ = bf16[192,256]{1,0:T(8,128)(2,1)S(1)} collective-permute-done((bf16[192,256]{1,0:T(8,128)(2,1)S(1)}, bf16[192,256]{1,0:T(8,128)(2,1)S(1)}, u32[]{:S(2)}, u32[]{:S(2)}) %collective-permute-start.3) | collective-permute-done | bytes 98336 | tf_op jit(solution)/shard_map/ppermute | solution.py:415
  39.9 4.0 %collective-permute-done.4.refs_7_ = bf16[192,256]{1,0:T(8,128)(2,1)S(1)} collective-permute-done((bf16[192,256]{1,0:T(8,128)(2,1)S(1)}, bf16[192,256]{1,0:T(8,128)(2,1)S(1)}, u32[]{:S(2)}, u32[]{:S(2)}) %collective-permute-start.4) | collective-permute-done | bytes 98336 | tf_op jit(solution)/shard_map/ppermute | solution.py:415
  43.8 0.0 collective-permute-done.5.refs_8_
  43.8 2.3 %key_value_terms.1 = (f32[512,256]{1,0:T(8,128)S(1)}, bf16[512,256]{1,0:T(8,128)(2,1)S(1)}) custom-call(s32[1,20]{1,0:T(1,128)S(1)} %concatenate.7.refs_0_.meta_ref, bf16[704,256]{1,0:T(8,128)(2,1)S(1)} %get-tuple-element.55.refs_1_, bf16[704,256]{1,0:T(8,128)(2,1)S(1)} %get-tuple-element.56.refs_2_, f32[8,192,256]{2,1,0:T(8,128)S(1)} %get-tuple-element.57.refs_3_, ...), custom_call_target="tpu_custom_call" | custom-call | tf_op jit(solution)/shard_map/key_value_terms/pallas_call | solution.py:544
  46.1 0.1 collective-permute-start.6
  46.2 1.5 %collective-permute-done.6.got_ref = bf16[512,256]{1,0:T(8,128)(2,1)S(1)} collective-permute-done((bf16[512,256]{1,0:T(8,128)(2,1)S(1)}, bf16[512,256]{1,0:T(8,128)(2,1)S(1)}, u32[]{:S(2)}, u32[]{:S(2)}) %collective-permute-start.6) | collective-permute-done | bytes 262176 | tf_op jit(solution)/shard_map/ppermute | solution.py:415
  47.7 0.1 sum_pair.1
  47.8 2.5 %collective-permute-start.7 = (bf16[128,256]{1,0:T(8,128)(2,1)S(1)}, bf16[128,256]{1,0:T(8,128)(2,1)S(1)}, u32[]{:S(2)}, u32[]{:S(2)}) collective-permute-start(bf16[128,256]{1,0:T(8,128)(2,1)S(1)} %get-tuple-element.66), channel_id=1, source_target_pairs={{0,24},{4,28},{8,16},{12,20},{16,8},{20,12},{24,0},{28,4},{1,25},{... | collective-permute-start | bytes 196616 | tf_op jit(solution)/shard_map/ppermute | solution.py:415
  50.3 0.5 collective-permute-start.8
  50.8 0.6 %collective-permute-start.9 = (bf16[128,256]{1,0:T(8,128)(2,1)S(1)}, bf16[128,256]{1,0:T(8,128)(2,1)S(1)}, u32[]{:S(2)}, u32[]{:S(2)}) collective-permute-start(bf16[128,256]{1,0:T(8,128)(2,1)S(1)} %get-tuple-element.68), channel_id=1, source_target_pairs={{0,8},{4,12},{8,0},{12,4},{16,24},{20,28},{24,16},{28,20},{1,9},{5... | collective-permute-start | bytes 196616 | tf_op jit(solution)/shard_map/ppermute | solution.py:415
  51.4 1.7 %collective-permute-done.7.refs_0_ = bf16[128,256]{1,0:T(8,128)(2,1)S(1)} collective-permute-done((bf16[128,256]{1,0:T(8,128)(2,1)S(1)}, bf16[128,256]{1,0:T(8,128)(2,1)S(1)}, u32[]{:S(2)}, u32[]{:S(2)}) %collective-permute-start.7) | collective-permute-done | bytes 65568 | tf_op jit(solution)/shard_map/ppermute | solution.py:415
  53.1 1.5 %collective-permute-done.8.refs_1_ = bf16[128,256]{1,0:T(8,128)(2,1)S(1)} collective-permute-done((bf16[128,256]{1,0:T(8,128)(2,1)S(1)}, bf16[128,256]{1,0:T(8,128)(2,1)S(1)}, u32[]{:S(2)}, u32[]{:S(2)}) %collective-permute-start.8) | collective-permute-done | bytes 65568 | tf_op jit(solution)/shard_map/ppermute | solution.py:415
  54.5 0.5 collective-permute-done.9.refs_2_
  55.1 0.7 %sum_groups.1 = f32[128,256]{1,0:T(8,128)} custom-call(bf16[128,256]{1,0:T(8,128)(2,1)S(1)} %collective-permute-done.7.refs_0_, bf16[128,256]{1,0:T(8,128)(2,1)S(1)} %collective-permute-done.8.refs_1_, bf16[128,256]{1,0:T(8,128)(2,1)S(1)} %collective-permute-done.9.refs_2_, bf16[128,256]{1,0:T(8,128)(2,1)S(1)} %get-tuple-element.69.refs_3_), custom_call_target="tpu_custom_call" | custom-call | tf_op jit(solution)/shard_map/sum_groups/pallas_call | solution.py:577
Async XLA Ops:
  0.6 9.0 %copy-start.2 = (bf16[1024,512]{1,0:T(8,128)(2,1)S(1)}, bf16[1024,512]{1,0:T(8,128)(2,1)}, u32[]{:S(2)}) copy-start(bf16[1024,512]{1,0:T(8,128)(2,1)} %refs_7_.1) | copy-start | bytes 3145732
  0.6 16.3 %collective-permute-start = (bf16[128,1024]{1,0:T(8,128)(2,1)}, bf16[128,1024]{1,0:T(8,128)(2,1)S(1)}, u32[]{:S(2)}, u32[]{:S(2)}) collective-permute-start(bf16[128,1024]{1,0:T(8,128)(2,1)} %refs_9_.1), channel_id=1, source_target_pairs={{0,2},{1,3},{2,0},{3,1},{4,6},{5,7},{6,4},{7,5},{8,10},{9,11},{10,... | collective-permute-start | bytes 786440 | tf_op jit(solution)/shard_map/ppermute | solution.py:415
  4.7 13.8 %collective-permute-start.1 = (bf16[128,1024]{1,0:T(8,128)(2,1)}, bf16[128,1024]{1,0:T(8,128)(2,1)S(1)}, u32[]{:S(2)}, u32[]{:S(2)}) collective-permute-start(bf16[128,1024]{1,0:T(8,128)(2,1)} %refs_9_.1), channel_id=1, source_target_pairs={{0,1},{1,0},{2,3},{3,2},{4,5},{5,4},{6,7},{7,6},{8,9},{9,8},{10,11... | collective-permute-start | bytes 786440 | tf_op jit(solution)/shard_map/ppermute | solution.py:415
  8.1 1.2 %copy-start.3 = (bf16[512,1024]{1,0:T(8,128)(2,1)S(1)}, bf16[512,1024]{1,0:T(8,128)(2,1)}, u32[]{:S(2)}) copy-start(bf16[512,1024]{1,0:T(8,128)(2,1)} %refs_2_.1) | copy-start | bytes 3145732
  9.7 1.6 %copy-start = (bf16[1024,1024]{1,0:T(8,128)(2,1)S(1)}, bf16[1024,1024]{1,0:T(8,128)(2,1)}, u32[]{:S(2)}) copy-start(bf16[1024,1024]{1,0:T(8,128)(2,1)} %refs_8_.1) | copy-start | bytes 6291460
  11.3 0.9 %copy-start.5 = (bf16[128,1024]{1,0:T(8,128)(2,1)S(1)}, bf16[128,1024]{1,0:T(8,128)(2,1)}, u32[]{:S(2)}) copy-start(bf16[128,1024]{1,0:T(8,128)(2,1)} %refs_9_.1) | copy-start | bytes 786436
  12.2 0.7 %copy-start.8 = (f32[1024]{0:T(1024)S(1)}, f32[1024]{0:T(1024)}, u32[]{:S(2)}) copy-start(f32[1024]{0:T(1024)} %param.14) | copy-start | bytes 12292
  12.9 4.8 %copy-start.1 = (bf16[1024,1024]{1,0:T(8,128)(2,1)S(1)}, bf16[1024,1024]{1,0:T(8,128)(2,1)}, u32[]{:S(2)}) copy-start(bf16[1024,1024]{1,0:T(8,128)(2,1)} %refs_8_.1) | copy-start | bytes 6291460
  17.0 1.5 %copy-start.9 = (f32[1024]{0:T(1024)S(1)}, f32[1024]{0:T(1024)}, u32[]{:S(2)}) copy-start(f32[1024]{0:T(1024)} %param.14) | copy-start | bytes 12292
  17.0 7.4 %collective-permute-start.2 = (bf16[128,1024]{1,0:T(8,128)(2,1)S(1)}, bf16[128,1024]{1,0:T(8,128)(2,1)S(1)}, u32[]{:S(2)}, u32[]{:S(2)}) collective-permute-start(bf16[128,1024]{1,0:T(8,128)(2,1)S(1)} %collective-permute-done.x_ref.refs_11_), channel_id=1, source_target_pairs={{0,1},{1,0},{2,3},{3,2},{4,5},{5,4},{6,7},{7,6},{8,9},{9,8},{10,11... | collective-permute-start | bytes 786440 | tf_op jit(solution)/shard_map/ppermute | solution.py:415
  18.5 6.0 %copy-start.4 = (bf16[512,1024]{1,0:T(8,128)(2,1)S(1)}, bf16[512,1024]{1,0:T(8,128)(2,1)}, u32[]{:S(2)}) copy-start(bf16[512,1024]{1,0:T(8,128)(2,1)} %refs_2_.1) | copy-start | bytes 3145732
  18.5 5.9 %copy-start.6 = (bf16[128,1024]{1,0:T(8,128)(2,1)S(1)}, bf16[128,1024]{1,0:T(8,128)(2,1)}, u32[]{:S(2)}) copy-start(bf16[128,1024]{1,0:T(8,128)(2,1)} %refs_9_.1) | copy-start | bytes 786436
  18.5 5.9 %copy-start.7 = (bf16[128,1024]{1,0:T(8,128)(2,1)S(1)}, bf16[128,1024]{1,0:T(8,128)(2,1)}, u32[]{:S(2)}) copy-start(bf16[128,1024]{1,0:T(8,128)(2,1)} %refs_1_.1) | copy-start | bytes 786436
  31.9 8.0 %collective-permute-start.3 = (bf16[192,256]{1,0:T(8,128)(2,1)S(1)}, bf16[192,256]{1,0:T(8,128)(2,1)S(1)}, u32[]{:S(2)}, u32[]{:S(2)}) collective-permute-start(bf16[192,256]{1,0:T(8,128)(2,1)S(1)} %get-tuple-element.60), channel_id=1, source_target_pairs={{0,3},{1,2},{2,1},{3,0},{4,7},{5,6},{6,5},{7,4},{8,11},{9,10},{10,... | collective-permute-start | bytes 294920 | tf_op jit(solution)/shard_map/ppermute | solution.py:415
  36.2 7.6 %collective-permute-start.4 = (bf16[192,256]{1,0:T(8,128)(2,1)S(1)}, bf16[192,256]{1,0:T(8,128)(2,1)S(1)}, u32[]{:S(2)}, u32[]{:S(2)}) collective-permute-start(bf16[192,256]{1,0:T(8,128)(2,1)S(1)} %get-tuple-element.61), channel_id=1, source_target_pairs={{0,2},{1,3},{2,0},{3,1},{4,6},{5,7},{6,4},{7,5},{8,10},{9,11},{10,... | collective-permute-start | bytes 294920 | tf_op jit(solution)/shard_map/ppermute | solution.py:415
  36.2 7.6 %collective-permute-start.5 = (bf16[192,256]{1,0:T(8,128)(2,1)S(1)}, bf16[192,256]{1,0:T(8,128)(2,1)S(1)}, u32[]{:S(2)}, u32[]{:S(2)}) collective-permute-start(bf16[192,256]{1,0:T(8,128)(2,1)S(1)} %get-tuple-element.62), channel_id=1, source_target_pairs={{0,1},{1,0},{2,3},{3,2},{4,5},{5,4},{6,7},{7,6},{8,9},{9,8},{10,11... | collective-permute-start | bytes 294920 | tf_op jit(solution)/shard_map/ppermute | solution.py:415
  46.1 1.6 %collective-permute-start.6 = (bf16[512,256]{1,0:T(8,128)(2,1)S(1)}, bf16[512,256]{1,0:T(8,128)(2,1)S(1)}, u32[]{:S(2)}, u32[]{:S(2)}) collective-permute-start(bf16[512,256]{1,0:T(8,128)(2,1)S(1)} %get-tuple-element.65), channel_id=1, source_target_pairs={{0,4},{4,0},{8,12},{12,8},{16,20},{20,16},{24,28},{28,24},{1,5},{5... | collective-permute-start | bytes 786440 | tf_op jit(solution)/shard_map/ppermute | solution.py:415
  47.8 5.3 %collective-permute-start.7 = (bf16[128,256]{1,0:T(8,128)(2,1)S(1)}, bf16[128,256]{1,0:T(8,128)(2,1)S(1)}, u32[]{:S(2)}, u32[]{:S(2)}) collective-permute-start(bf16[128,256]{1,0:T(8,128)(2,1)S(1)} %get-tuple-element.66), channel_id=1, source_target_pairs={{0,24},{4,28},{8,16},{12,20},{16,8},{20,12},{24,0},{28,4},{1,25},{... | collective-permute-start | bytes 196616 | tf_op jit(solution)/shard_map/ppermute | solution.py:415
  50.3 4.3 %collective-permute-start.8 = (bf16[128,256]{1,0:T(8,128)(2,1)S(1)}, bf16[128,256]{1,0:T(8,128)(2,1)S(1)}, u32[]{:S(2)}, u32[]{:S(2)}) collective-permute-start(bf16[128,256]{1,0:T(8,128)(2,1)S(1)} %get-tuple-element.67), channel_id=1, source_target_pairs={{0,16},{4,20},{8,24},{12,28},{16,0},{20,4},{24,8},{28,12},{1,17},{... | collective-permute-start | bytes 196616 | tf_op jit(solution)/shard_map/ppermute | solution.py:415
  50.8 4.3 %collective-permute-start.9 = (bf16[128,256]{1,0:T(8,128)(2,1)S(1)}, bf16[128,256]{1,0:T(8,128)(2,1)S(1)}, u32[]{:S(2)}, u32[]{:S(2)}) collective-permute-start(bf16[128,256]{1,0:T(8,128)(2,1)S(1)} %get-tuple-element.68), channel_id=1, source_target_pairs={{0,8},{4,12},{8,0},{12,4},{16,24},{20,28},{24,16},{28,20},{1,9},{5... | collective-permute-start | bytes 196616 | tf_op jit(solution)/shard_map/ppermute | solution.py:415

commit v10 on v9

--- a/solution.py
+++ b/solution.py
@@ -15,6 +15,7 @@
 SPAN = (LC + 1) * BLOCK
 HALO = 32
 ROWS = HALO + BLOCK
+KERNEL_GAP = HALO - (KERNEL - 1)
 PAD = LC + 1
 EPSILON = 1e-05
 SOFT_CAP = 4.0
@@ -129,6 +130,10 @@
     n_ref[...] = normed
     q_ref[...] = dot_nn(normed, wq_ref[...]).astype(BF16)
     kv_ref[...] = dot_nn(normed, wkv_ref[...]).astype(BF16)
+
+
+def shifted_up(values, shift):
+    return pltpu.roll(values, values.shape[0] - shift, axis=0) if shift else values
 
 
 def forward_kernel(sizes, tm, head_size, *refs):
@@ -173,17 +178,11 @@
     side_f = diag_mask(HEADS, HALO, head_size)
     side_b = side_f.astype(BF16)
 
-    ones = jnp.ones((SPAN, LANES), BF16)
-    key_block = lax.broadcasted_iota(jnp.int32, (1, SPAN), 1) // BLOCK
     own = [table.block_of(me * local + i) for i in range(local)]
     keep = [jnp.where(table.position(c) >= 1, 1.0, 0.0).astype(F32) for c in own]
     for i, c in enumerate(own):
         for blk, shift, count, put in ((c - 1, HALO, HALO, 0), (c, 0, BLOCK, HALO)):
             reach = table.reach(blk)
-            allowed = jnp.ones((1, SPAN), F32)
-            for w in range(LC):
-                ok = jnp.where(reach >= LC - w, 1.0, 0.0).astype(F32)
-                allowed = jnp.where(key_block == w, ok, allowed)
             win = row_at(blk - LC, SPAN)
             at = row_at(blk, count, shift)
             if count == BLOCK:
@@ -194,14 +193,12 @@
             for g in range(groups):
                 cols = slice(g * wide, (g + 1) * wide)
                 vcols = slice(hq + g * wide, hq + (g + 1) * wide)
-                raw = dot_nt(spread(q_ref[at, cols], mask_b), kv_ref[win, cols])
-                unit = jnp.tanh(raw * (1.0 / (SOFT_CAP * math.sqrt(head_size))))
-                exped = (jnp.exp(SOFT_CAP * unit) * allowed).astype(BF16)
-                inverse = 1.0 / dot_nn(exped, ones)
-                scale = mask_f * jnp.concatenate([inverse] * (wide // LANES), axis=1)
-                full = dot_nn(exped, kv_ref[win, vcols])
+                probs, _ = window_probs(
+                    spread(q_ref[at, cols], mask_b), kv_ref[win, cols], reach, head_size
+                )
+                full = dot_tn(probs.astype(BF16), kv_ref[win, vcols])
                 ctx_s[i * ROWS + put : i * ROWS + put + count, cols] = fold_heads(
-                    full, scale, count
+                    full, mask_f, count
                 ).astype(BF16)
 
     gain = small_ref[KERNEL + 1 : KERNEL + 2]
@@ -230,12 +227,13 @@
             acc = [bias] * groups
             for s in range(SUB):
                 reps = (KERNEL - s + SUB - 1) // SUB
-                moved = ext[s + 2 : s + 2 + BLOCK + SUB * (reps - 1)]
+                skip, shift = divmod(s + KERNEL_GAP, SUB)
+                moved = shifted_up(ext, shift)
                 for a in range(reps):
                     tap = taps(SUB * a + s)
                     for r in range(groups):
-                        piece = moved[(a + r) * SUB : (a + r + 1) * SUB]
-                        acc[r] = acc[r] + tap * piece
+                        at = (a + r + skip) * SUB
+                        acc[r] = acc[r] + tap * moved[at : at + SUB]
             mixed = jnp.concatenate(acc, axis=0)
             gate = 0.5 * jnp.tanh(0.5 * mixed) + 0.5
             rows = slice(i * BLOCK, (i + 1) * BLOCK)
@@ -243,18 +241,18 @@
             slope = gate * (1.0 + mixed * (1.0 - gate))
             gm = grad_ref[rows, cols].astype(F32) * slope
             zeros = jnp.zeros((HALO, LANES), F32)
-            padded = jnp.concatenate([zeros, gm, zeros], axis=0)
+            padded = jnp.concatenate([zeros[:SUB], gm, zeros[:SUB]], axis=0)
             back = [None] * (ROWS // SUB)
             low = HALO // SUB - 1
             for s in range(SUB):
                 reps = (KERNEL - s + SUB - 1) // SUB
                 start = low if s else low + 1
-                moved = padded[start * SUB + s : ROWS + s]
+                moved = shifted_up(padded, s)
                 for a in range(reps):
                     tap = taps(KERNEL - 1 - SUB * a - s)
                     for g in range(start, ROWS // SUB):
                         r = g - a
-                        piece = tap * moved[(g - start) * SUB : (g - start + 1) * SUB]
+                        piece = tap * moved[(g - low) * SUB : (g - low + 1) * SUB]
                         back[r] = piece if back[r] is None else back[r] + piece
             for r in range(ROWS // SUB):
                 scale = keep[i] if r < HALO // SUB else 1.0

time: 56 us -> 55.7 us (level)
  no operation moved by 1% of the time
where the time goes in v10:
time: 55.7 us; the launch traced here: 55.4 us
  waiting for transfers between devices  19 us (34%)
  starting transfers between devices  15 us (27%)
  Pallas kernels  14.5 us (26%)
  local copies, waits for them, and re-layouts  5.25 us (9%)
  other arithmetic  0.96 us (2%)
  between operations  0.79 us (1%)
    ppermute x10, waiting for transfers between devices, swap(): return lax.ppermute(value, axis, [(i, i ^ m) for i in range(size)])  19 us
    ppermute x10, starting transfers between devices, swap(): return lax.ppermute(value, axis, [(i, i ^ m) for i in range(size)])  15 us
    pallas_call x1, Pallas kernels, on_device(): pl.pallas_call(functools.partial(forward_kernel, sizes, tm, head_size), o...  7.17 us
    unnamed x20, local copies, waits for them, and re-layouts  4.47 us
    pallas_call x1, Pallas kernels, on_device(): pl.pallas_call(functools.partial(backward_kernel, sizes, tm, width // dp,...  2.3 us
    pallas_call x3, Pallas kernels, project_shard(): pl.pallas_call(project_kernel, out_shape=made, in_specs=[vmem] * 4, out_s...  2.28 us
    pallas_call x1, Pallas kernels, on_device(): pl.pallas_call(functools.partial(probs_kernel, sizes, tm, head_size), out...  1.62 us
  transfers between devices with their start and end apart: 10, of which 8 were waited for; matrix products, arithmetic and copies ran while one was open for 3% of the time, Pallas kernels for 8%

profile of v10, /device:TPU:0, one launch (start us, length us, event | category | flops | bytes accessed | tf_op | source)
XLA Modules:
  0.0 55.4 jit_solution(13592380960774746270)
XLA Ops:
  0.6 0.0 copy-start.2
  0.6 4.1 %collective-permute-start = (bf16[128,1024]{1,0:T(8,128)(2,1)}, bf16[128,1024]{1,0:T(8,128)(2,1)S(1)}, u32[]{:S(2)}, u32[]{:S(2)}) collective-permute-start(bf16[128,1024]{1,0:T(8,128)(2,1)} %refs_9_.1), channel_id=1, source_target_pairs={{0,2},{1,3},{2,0},{3,1},{4,6},{5,7},{6,4},{7,5},{8,10},{9,11},{10,... | collective-permute-start | bytes 786440 | tf_op jit(solution)/shard_map/ppermute | solution.py:413
  4.7 1.6 %collective-permute-start.1 = (bf16[128,1024]{1,0:T(8,128)(2,1)}, bf16[128,1024]{1,0:T(8,128)(2,1)S(1)}, u32[]{:S(2)}, u32[]{:S(2)}) collective-permute-start(bf16[128,1024]{1,0:T(8,128)(2,1)} %refs_9_.1), channel_id=1, source_target_pairs={{0,1},{1,0},{2,3},{3,2},{4,5},{5,4},{6,7},{7,6},{8,9},{9,8},{10,11... | collective-permute-start | bytes 786440 | tf_op jit(solution)/shard_map/ppermute | solution.py:413
  6.3 0.8 %concatenate.7.refs_0_.meta_ref = s32[1,20]{1,0:T(1,128)S(1)} concatenate(s32[1,1]{1,0:T(1,128)} %bitcast.3, s32[1,1]{1,0:T(1,128)} %bitcast.4, s32[1,2]{1,0:T(1,128)} %param.21, s32[1,8]{1,0:T(1,128)} %param.22, s32[1,8]{1,0:T(1,128)} %param.23), dimensions={1} | concatenate | bytes 160 | tf_op jit(solution)/shard_map/concatenate | solution.py:415
  7.1 1.0 %pad_maximum_fusion.small_ref.refs_4_ = f32[33,1024]{1,0:T(8,128)S(1)} fusion(f32[1,1024]{1,0:T(1,128)} %bitcast.9, f32[1,1024]{1,0:T(1,128)} %bitcast.10, f32[31,1024]{1,0:T(8,128)} %param.19), kind=kLoop, calls=%fused_computation | loop fusion | flops 67584 | bytes 270336 | tf_op jit(solution)/shard_map/concatenate | solution.py:425
  8.1 0.0 copy-start.3
  8.1 1.2 %copy-done.3 = bf16[512,1024]{1,0:T(8,128)(2,1)S(1)} copy-done((bf16[512,1024]{1,0:T(8,128)(2,1)S(1)}, bf16[512,1024]{1,0:T(8,128)(2,1)}, u32[]{:S(2)}) %copy-start.3) | copy-done | bytes 1048600
  9.3 0.4 spread_taps.1
  9.6 0.0 copy-done.2
  9.7 0.0 copy-start
  9.7 1.6 %copy-done = bf16[1024,1024]{1,0:T(8,128)(2,1)S(1)} copy-done((bf16[1024,1024]{1,0:T(8,128)(2,1)S(1)}, bf16[1024,1024]{1,0:T(8,128)(2,1)}, u32[]{:S(2)}) %copy-start) | copy-done | bytes 2097176
  11.3 0.0 copy-start.5
  11.3 0.9 %copy-done.5 = bf16[128,1024]{1,0:T(8,128)(2,1)S(1)} copy-done((bf16[128,1024]{1,0:T(8,128)(2,1)S(1)}, bf16[128,1024]{1,0:T(8,128)(2,1)}, u32[]{:S(2)}) %copy-start.5) | copy-done | bytes 262168
  12.2 0.0 copy-start.8
  12.2 0.7 %copy-done.8 = f32[1024]{0:T(1024)S(1)} copy-done((f32[1024]{0:T(1024)S(1)}, f32[1024]{0:T(1024)}, u32[]{:S(2)}) %copy-start.8) | copy-done | bytes 4120
  12.9 0.0 copy-start.1
  12.9 0.8 %project_rows_0.1 = (bf16[128,1024]{1,0:T(8,128)(2,1)S(1)}, bf16[128,512]{1,0:T(8,128)(2,1)S(1)}, bf16[128,1024]{1,0:T(8,128)(2,1)S(1)}) custom-call(bf16[128,1024]{1,0:T(8,128)(2,1)S(1)} %copy-done.5, f32[1,1024]{1,0:T(1,128)S(1)} %bitcast.5, bf16[1024,512]{1,0:T(8,128)(2,1)S(1)} %copy-done.2, bf16[1024,1024]{1,0:T(8,128)(2,1)S(1)} %copy-done), custom_call_target="tpu_custom_call" | custom-call | flops 402653184 | bytes 4194304 | tf_op jit(solution)/shard_map/project_rows_0/pallas_call | solution.py:447
  13.7 3.3 %collective-permute-done.x_ref.refs_11_ = bf16[128,1024]{1,0:T(8,128)(2,1)S(1)} collective-permute-done((bf16[128,1024]{1,0:T(8,128)(2,1)}, bf16[128,1024]{1,0:T(8,128)(2,1)S(1)}, u32[]{:S(2)}, u32[]{:S(2)}) %collective-permute-start) | collective-permute-done | bytes 262176 | tf_op jit(solution)/shard_map/ppermute | solution.py:413
  17.0 0.0 copy-start.9
  17.0 0.7 %collective-permute-start.2 = (bf16[128,1024]{1,0:T(8,128)(2,1)S(1)}, bf16[128,1024]{1,0:T(8,128)(2,1)S(1)}, u32[]{:S(2)}, u32[]{:S(2)}) collective-permute-start(bf16[128,1024]{1,0:T(8,128)(2,1)S(1)} %collective-permute-done.x_ref.refs_11_), channel_id=1, source_target_pairs={{0,1},{1,0},{2,3},{3,2},{4,5},{5,4},{6,7},{7,6},{8,9},{9,8},{10,11... | collective-permute-start | bytes 786440 | tf_op jit(solution)/shard_map/ppermute | solution.py:413
  17.7 0.0 copy-done.1
  17.7 0.8 %project_rows_2.1 = (bf16[128,1024]{1,0:T(8,128)(2,1)S(1)}, bf16[128,512]{1,0:T(8,128)(2,1)S(1)}, bf16[128,1024]{1,0:T(8,128)(2,1)S(1)}) custom-call(bf16[128,1024]{1,0:T(8,128)(2,1)S(1)} %collective-permute-done.x_ref.refs_11_, f32[1,1024]{1,0:T(1,128)S(1)} %bitcast.6, bf16[1024,512]{1,0:T(8,128)(2,1)S(1)} %copy-done.2, bf16[1024,1024]{1,0:T(8,128)(2,1)S(1)} %copy-done.1), custom_call_target="tpu_custom_call" | custom-call | flops 402653184 | bytes 4194304 | tf_op jit(solution)/shard_map/project_rows_2/pallas_call | solution.py:447
  18.5 0.0 copy-start.4
  18.5 0.0 copy-start.6
  18.5 0.0 copy-start.7
  18.5 0.0 collective-permute-done.1.x_ref.refs_10_
  18.5 0.0 copy-done.9
  18.5 0.8 %project_rows_1.1 = (bf16[128,1024]{1,0:T(8,128)(2,1)S(1)}, bf16[128,512]{1,0:T(8,128)(2,1)S(1)}, bf16[128,1024]{1,0:T(8,128)(2,1)S(1)}) custom-call(bf16[128,1024]{1,0:T(8,128)(2,1)S(1)} %collective-permute-done.1.x_ref.refs_10_, f32[1,1024]{1,0:T(1,128)S(1)} %bitcast.7, bf16[1024,512]{1,0:T(8,128)(2,1)S(1)} %copy-done.2, bf16[1024,1024]{1,0:T(8,128)(2,1)S(1)} %copy-done.1), custom_call_target="tpu_custom_call" | custom-call | flops 402653184 | bytes 4194304 | tf_op jit(solution)/shard_map/project_rows_1/pallas_call | solution.py:447
  19.3 5.1 %collective-permute-done.2.refs_12_ = bf16[128,1024]{1,0:T(8,128)(2,1)S(1)} collective-permute-done((bf16[128,1024]{1,0:T(8,128)(2,1)S(1)}, bf16[128,1024]{1,0:T(8,128)(2,1)S(1)}, u32[]{:S(2)}, u32[]{:S(2)}) %collective-permute-start.2) | collective-permute-done | bytes 262176 | tf_op jit(solution)/shard_map/ppermute | solution.py:413
  24.4 0.0 copy-done.4
  24.4 0.0 copy-done.6
  24.4 0.0 copy-done.7
  24.4 7.2 %forward_pass.1 = (bf16[128,1024]{1,0:T(8,128)(2,1)}, bf16[128,1024]{1,0:T(8,128)(2,1)S(1)}, bf16[128,512]{1,0:T(8,128)(2,1)S(1)}, bf16[128,1024]{1,0:T(8,128)(2...) custom-call(s32[1,20]{1,0:T(1,128)S(1)} %concatenate.7.refs_0_.meta_, ...), custom_call_target="tpu_custom_call" | custom-call | tf_op jit(solution)/shard_map/forward_pass/pallas_call | solution.py:478
  31.6 4.3 %collective-permute-start.3 = (bf16[192,256]{1,0:T(8,128)(2,1)S(1)}, bf16[192,256]{1,0:T(8,128)(2,1)S(1)}, u32[]{:S(2)}, u32[]{:S(2)}) collective-permute-start(bf16[192,256]{1,0:T(8,128)(2,1)S(1)} %get-tuple-element.60), channel_id=1, source_target_pairs={{0,3},{1,2},{2,1},{3,0},{4,7},{5,6},{6,5},{7,4},{8,11},{9,10},{10,... | collective-permute-start | bytes 294920 | tf_op jit(solution)/shard_map/ppermute | solution.py:413
  35.9 0.0 collective-permute-start.4
  35.9 0.6 %collective-permute-start.5 = (bf16[192,256]{1,0:T(8,128)(2,1)S(1)}, bf16[192,256]{1,0:T(8,128)(2,1)S(1)}, u32[]{:S(2)}, u32[]{:S(2)}) collective-permute-start(bf16[192,256]{1,0:T(8,128)(2,1)S(1)} %get-tuple-element.62), channel_id=1, source_target_pairs={{0,1},{1,0},{2,3},{3,2},{4,5},{5,4},{6,7},{7,6},{8,9},{9,8},{10,11... | collective-permute-start | bytes 294920 | tf_op jit(solution)/shard_map/ppermute | solution.py:413
  36.6 1.6 %window_probs.1 = (bf16[704,256]{1,0:T(8,128)(2,1)S(1)}, bf16[704,256]{1,0:T(8,128)(2,1)S(1)}, f32[8,192,256]{2,1,0:T(8,128)S(1)}, f32[8,192,256]{2,1,0:T(8,128)S(1)}, bf16[1024,512]{1,0:T(8,128)(2,1)S(1)}) custom-call(s32[1,20]{1,0:T(1,128)S(1)} %concatenate.7.refs_0_.meta_ref, bf16[128,512]{1,0:T(8,128)(2,1)S(1)} %get-tuple-element.42.refs_13_.refs_0_, ...), custom_call_target="tpu_custom_call" | custom-call | flops 2000000000 | bytes 4000000 | tf_op jit(solution)/shard_map/window_probs/pallas_call | solution.py:521
  38.2 1.5 %collective-permute-done.3.refs_6_ = bf16[192,256]{1,0:T(8,128)(2,1)S(1)} collective-permute-done((bf16[192,256]{1,0:T(8,128)(2,1)S(1)}, bf16[192,256]{1,0:T(8,128)(2,1)S(1)}, u32[]{:S(2)}, u32[]{:S(2)}) %collective-permute-start.3) | collective-permute-done | bytes 98336 | tf_op jit(solution)/shard_map/ppermute | solution.py:413
  39.7 3.8 %collective-permute-done.4.refs_7_ = bf16[192,256]{1,0:T(8,128)(2,1)S(1)} collective-permute-done((bf16[192,256]{1,0:T(8,128)(2,1)S(1)}, bf16[192,256]{1,0:T(8,128)(2,1)S(1)}, u32[]{:S(2)}, u32[]{:S(2)}) %collective-permute-start.4) | collective-permute-done | bytes 98336 | tf_op jit(solution)/shard_map/ppermute | solution.py:413
  43.5 0.0 collective-permute-done.5.refs_8_
  43.5 2.3 %key_value_terms.1 = (f32[512,256]{1,0:T(8,128)S(1)}, bf16[512,256]{1,0:T(8,128)(2,1)S(1)}) custom-call(s32[1,20]{1,0:T(1,128)S(1)} %concatenate.7.refs_0_.meta_ref, bf16[704,256]{1,0:T(8,128)(2,1)S(1)} %get-tuple-element.55.refs_1_, bf16[704,256]{1,0:T(8,128)(2,1)S(1)} %get-tuple-element.56.refs_2_, f32[8,192,256]{2,1,0:T(8,128)S(1)} %get-tuple-element.57.refs_3_, ...), custom_call_target="tpu_custom_call" | custom-call | tf_op jit(solution)/shard_map/key_value_terms/pallas_call | solution.py:542
  45.8 0.1 collective-permute-start.6
  45.9 1.5 %collective-permute-done.6.got_ref = bf16[512,256]{1,0:T(8,128)(2,1)S(1)} collective-permute-done((bf16[512,256]{1,0:T(8,128)(2,1)S(1)}, bf16[512,256]{1,0:T(8,128)(2,1)S(1)}, u32[]{:S(2)}, u32[]{:S(2)}) %collective-permute-start.6) | collective-permute-done | bytes 262176 | tf_op jit(solution)/shard_map/ppermute | solution.py:413
  47.4 0.1 sum_pair.1
  47.5 2.5 %collective-permute-start.7 = (bf16[128,256]{1,0:T(8,128)(2,1)S(1)}, bf16[128,256]{1,0:T(8,128)(2,1)S(1)}, u32[]{:S(2)}, u32[]{:S(2)}) collective-permute-start(bf16[128,256]{1,0:T(8,128)(2,1)S(1)} %get-tuple-element.66), channel_id=1, source_target_pairs={{0,24},{4,28},{8,16},{12,20},{16,8},{20,12},{24,0},{28,4},{1,25},{... | collective-permute-start | bytes 196616 | tf_op jit(solution)/shard_map/ppermute | solution.py:413
  50.0 0.5 collective-permute-start.8
  50.5 0.5 collective-permute-start.9
  51.0 1.7 %collective-permute-done.7.refs_0_ = bf16[128,256]{1,0:T(8,128)(2,1)S(1)} collective-permute-done((bf16[128,256]{1,0:T(8,128)(2,1)S(1)}, bf16[128,256]{1,0:T(8,128)(2,1)S(1)}, u32[]{:S(2)}, u32[]{:S(2)}) %collective-permute-start.7) | collective-permute-done | bytes 65568 | tf_op jit(solution)/shard_map/ppermute | solution.py:413
  52.7 1.5 %collective-permute-done.8.refs_1_ = bf16[128,256]{1,0:T(8,128)(2,1)S(1)} collective-permute-done((bf16[128,256]{1,0:T(8,128)(2,1)S(1)}, bf16[128,256]{1,0:T(8,128)(2,1)S(1)}, u32[]{:S(2)}, u32[]{:S(2)}) %collective-permute-start.8) | collective-permute-done | bytes 65568 | tf_op jit(solution)/shard_map/ppermute | solution.py:413
  54.2 0.5 collective-permute-done.9.refs_2_
  54.8 0.7 %sum_groups.1 = f32[128,256]{1,0:T(8,128)} custom-call(bf16[128,256]{1,0:T(8,128)(2,1)S(1)} %collective-permute-done.7.refs_0_, bf16[128,256]{1,0:T(8,128)(2,1)S(1)} %collective-permute-done.8.refs_1_, bf16[128,256]{1,0:T(8,128)(2,1)S(1)} %collective-permute-done.9.refs_2_, bf16[128,256]{1,0:T(8,128)(2,1)S(1)} %get-tuple-element.69.refs_3_), custom_call_target="tpu_custom_call" | custom-call | tf_op jit(solution)/shard_map/sum_groups/pallas_call | solution.py:575
Async XLA Ops:
  0.6 9.0 %copy-start.2 = (bf16[1024,512]{1,0:T(8,128)(2,1)S(1)}, bf16[1024,512]{1,0:T(8,128)(2,1)}, u32[]{:S(2)}) copy-start(bf16[1024,512]{1,0:T(8,128)(2,1)} %refs_7_.1) | copy-start | bytes 3145732
  0.6 16.3 %collective-permute-start = (bf16[128,1024]{1,0:T(8,128)(2,1)}, bf16[128,1024]{1,0:T(8,128)(2,1)S(1)}, u32[]{:S(2)}, u32[]{:S(2)}) collective-permute-start(bf16[128,1024]{1,0:T(8,128)(2,1)} %refs_9_.1), channel_id=1, source_target_pairs={{0,2},{1,3},{2,0},{3,1},{4,6},{5,7},{6,4},{7,5},{8,10},{9,11},{10,... | collective-permute-start | bytes 786440 | tf_op jit(solution)/shard_map/ppermute | solution.py:413
  4.7 13.8 %collective-permute-start.1 = (bf16[128,1024]{1,0:T(8,128)(2,1)}, bf16[128,1024]{1,0:T(8,128)(2,1)S(1)}, u32[]{:S(2)}, u32[]{:S(2)}) collective-permute-start(bf16[128,1024]{1,0:T(8,128)(2,1)} %refs_9_.1), channel_id=1, source_target_pairs={{0,1},{1,0},{2,3},{3,2},{4,5},{5,4},{6,7},{7,6},{8,9},{9,8},{10,11... | collective-permute-start | bytes 786440 | tf_op jit(solution)/shard_map/ppermute | solution.py:413
  8.1 1.2 %copy-start.3 = (bf16[512,1024]{1,0:T(8,128)(2,1)S(1)}, bf16[512,1024]{1,0:T(8,128)(2,1)}, u32[]{:S(2)}) copy-start(bf16[512,1024]{1,0:T(8,128)(2,1)} %refs_2_.1) | copy-start | bytes 3145732
  9.7 1.6 %copy-start = (bf16[1024,1024]{1,0:T(8,128)(2,1)S(1)}, bf16[1024,1024]{1,0:T(8,128)(2,1)}, u32[]{:S(2)}) copy-start(bf16[1024,1024]{1,0:T(8,128)(2,1)} %refs_8_.1) | copy-start | bytes 6291460
  11.3 0.9 %copy-start.5 = (bf16[128,1024]{1,0:T(8,128)(2,1)S(1)}, bf16[128,1024]{1,0:T(8,128)(2,1)}, u32[]{:S(2)}) copy-start(bf16[128,1024]{1,0:T(8,128)(2,1)} %refs_9_.1) | copy-start | bytes 786436
  12.2 0.7 %copy-start.8 = (f32[1024]{0:T(1024)S(1)}, f32[1024]{0:T(1024)}, u32[]{:S(2)}) copy-start(f32[1024]{0:T(1024)} %param.14) | copy-start | bytes 12292
  12.9 4.8 %copy-start.1 = (bf16[1024,1024]{1,0:T(8,128)(2,1)S(1)}, bf16[1024,1024]{1,0:T(8,128)(2,1)}, u32[]{:S(2)}) copy-start(bf16[1024,1024]{1,0:T(8,128)(2,1)} %refs_8_.1) | copy-start | bytes 6291460
  17.0 1.5 %copy-start.9 = (f32[1024]{0:T(1024)S(1)}, f32[1024]{0:T(1024)}, u32[]{:S(2)}) copy-start(f32[1024]{0:T(1024)} %param.14) | copy-start | bytes 12292
  17.0 7.4 %collective-permute-start.2 = (bf16[128,1024]{1,0:T(8,128)(2,1)S(1)}, bf16[128,1024]{1,0:T(8,128)(2,1)S(1)}, u32[]{:S(2)}, u32[]{:S(2)}) collective-permute-start(bf16[128,1024]{1,0:T(8,128)(2,1)S(1)} %collective-permute-done.x_ref.refs_11_), channel_id=1, source_target_pairs={{0,1},{1,0},{2,3},{3,2},{4,5},{5,4},{6,7},{7,6},{8,9},{9,8},{10,11... | collective-permute-start | bytes 786440 | tf_op jit(solution)/shard_map/ppermute | solution.py:413
  18.5 6.0 %copy-start.4 = (bf16[512,1024]{1,0:T(8,128)(2,1)S(1)}, bf16[512,1024]{1,0:T(8,128)(2,1)}, u32[]{:S(2)}) copy-start(bf16[512,1024]{1,0:T(8,128)(2,1)} %refs_2_.1) | copy-start | bytes 3145732
  18.5 5.9 %copy-start.6 = (bf16[128,1024]{1,0:T(8,128)(2,1)S(1)}, bf16[128,1024]{1,0:T(8,128)(2,1)}, u32[]{:S(2)}) copy-start(bf16[128,1024]{1,0:T(8,128)(2,1)} %refs_9_.1) | copy-start | bytes 786436
  18.5 5.9 %copy-start.7 = (bf16[128,1024]{1,0:T(8,128)(2,1)S(1)}, bf16[128,1024]{1,0:T(8,128)(2,1)}, u32[]{:S(2)}) copy-start(bf16[128,1024]{1,0:T(8,128)(2,1)} %refs_1_.1) | copy-start | bytes 786436
  31.6 8.1 %collective-permute-start.3 = (bf16[192,256]{1,0:T(8,128)(2,1)S(1)}, bf16[192,256]{1,0:T(8,128)(2,1)S(1)}, u32[]{:S(2)}, u32[]{:S(2)}) collective-permute-start(bf16[192,256]{1,0:T(8,128)(2,1)S(1)} %get-tuple-element.60), channel_id=1, source_target_pairs={{0,3},{1,2},{2,1},{3,0},{4,7},{5,6},{6,5},{7,4},{8,11},{9,10},{10,... | collective-permute-start | bytes 294920 | tf_op jit(solution)/shard_map/ppermute | solution.py:413
  35.9 7.6 %collective-permute-start.4 = (bf16[192,256]{1,0:T(8,128)(2,1)S(1)}, bf16[192,256]{1,0:T(8,128)(2,1)S(1)}, u32[]{:S(2)}, u32[]{:S(2)}) collective-permute-start(bf16[192,256]{1,0:T(8,128)(2,1)S(1)} %get-tuple-element.61), channel_id=1, source_target_pairs={{0,2},{1,3},{2,0},{3,1},{4,6},{5,7},{6,4},{7,5},{8,10},{9,11},{10,... | collective-permute-start | bytes 294920 | tf_op jit(solution)/shard_map/ppermute | solution.py:413
  35.9 7.6 %collective-permute-start.5 = (bf16[192,256]{1,0:T(8,128)(2,1)S(1)}, bf16[192,256]{1,0:T(8,128)(2,1)S(1)}, u32[]{:S(2)}, u32[]{:S(2)}) collective-permute-start(bf16[192,256]{1,0:T(8,128)(2,1)S(1)} %get-tuple-element.62), channel_id=1, source_target_pairs={{0,1},{1,0},{2,3},{3,2},{4,5},{5,4},{6,7},{7,6},{8,9},{9,8},{10,11... | collective-permute-start | bytes 294920 | tf_op jit(solution)/shard_map/ppermute | solution.py:413
  45.8 1.6 %collective-permute-start.6 = (bf16[512,256]{1,0:T(8,128)(2,1)S(1)}, bf16[512,256]{1,0:T(8,128)(2,1)S(1)}, u32[]{:S(2)}, u32[]{:S(2)}) collective-permute-start(bf16[512,256]{1,0:T(8,128)(2,1)S(1)} %get-tuple-element.65), channel_id=1, source_target_pairs={{0,4},{4,0},{8,12},{12,8},{16,20},{20,16},{24,28},{28,24},{1,5},{5... | collective-permute-start | bytes 786440 | tf_op jit(solution)/shard_map/ppermute | solution.py:413
  47.5 5.3 %collective-permute-start.7 = (bf16[128,256]{1,0:T(8,128)(2,1)S(1)}, bf16[128,256]{1,0:T(8,128)(2,1)S(1)}, u32[]{:S(2)}, u32[]{:S(2)}) collective-permute-start(bf16[128,256]{1,0:T(8,128)(2,1)S(1)} %get-tuple-element.66), channel_id=1, source_target_pairs={{0,24},{4,28},{8,16},{12,20},{16,8},{20,12},{24,0},{28,4},{1,25},{... | collective-permute-start | bytes 196616 | tf_op jit(solution)/shard_map/ppermute | solution.py:413
  50.0 4.3 %collective-permute-start.8 = (bf16[128,256]{1,0:T(8,128)(2,1)S(1)}, bf16[128,256]{1,0:T(8,128)(2,1)S(1)}, u32[]{:S(2)}, u32[]{:S(2)}) collective-permute-start(bf16[128,256]{1,0:T(8,128)(2,1)S(1)} %get-tuple-element.67), channel_id=1, source_target_pairs={{0,16},{4,20},{8,24},{12,28},{16,0},{20,4},{24,8},{28,12},{1,17},{... | collective-permute-start | bytes 196616 | tf_op jit(solution)/shard_map/ppermute | solution.py:413
  50.5 4.3 %collective-permute-start.9 = (bf16[128,256]{1,0:T(8,128)(2,1)S(1)}, bf16[128,256]{1,0:T(8,128)(2,1)S(1)}, u32[]{:S(2)}, u32[]{:S(2)}) collective-permute-start(bf16[128,256]{1,0:T(8,128)(2,1)S(1)} %get-tuple-element.68), channel_id=1, source_target_pairs={{0,8},{4,12},{8,0},{12,4},{16,24},{20,28},{24,16},{28,20},{1,9},{5... | collective-permute-start | bytes 196616 | tf_op jit(solution)/shard_map/ppermute | solution.py:413

commit v11 on v10

--- a/solution.py
+++ b/solution.py
@@ -45,6 +45,10 @@
     return centred * scale_inv, scale_inv
 
 
+def sending_order(tm):
+    return (*range(2, tm), 1, 0)
+
+
 class Layout:
     def __init__(self, meta_ref, utts, blocks):
         self.ref, self.utts, self.blocks = meta_ref, utts, blocks
@@ -99,18 +103,18 @@
     return total
 
 
-def window_probs(diag_q, k_win, reach, head_size):
-    raw = dot_nt(k_win, diag_q)
-    unit = jnp.tanh(raw * (1.0 / (SOFT_CAP * math.sqrt(head_size))))
-    exped = jnp.exp(SOFT_CAP * unit)
-    parts = []
+def window_probs(diag_q, k_win, reach):
+    unit = jnp.tanh(dot_nt(k_win, diag_q))
+    exped = jnp.exp2(unit * (SOFT_CAP * math.log2(math.e)))
+    parts = [exped[w * BLOCK : (w + 1) * BLOCK] for w in range(LC + 1)]
+    sums = [jnp.sum(part, axis=0, keepdims=True) for part in parts]
+    flags = [jnp.where(reach >= LC - w, 1.0, 0.0).astype(F32) for w in range(LC)]
+    total = sums[LC]
     for w in range(LC):
-        ok = jnp.where(reach >= LC - w, 1.0, 0.0).astype(F32)
-        parts.append(exped[w * BLOCK : (w + 1) * BLOCK] * ok)
-    parts.append(exped[LC * BLOCK :])
-    exped = jnp.concatenate(parts, axis=0)
-    total = jnp.sum(exped, axis=0, keepdims=True)
-    return exped * (1.0 / total), unit
+        total = total + sums[w] * flags[w]
+    inverse = 1.0 / total
+    scaled = [parts[w] * (inverse * flags[w]) for w in range(LC)] + [parts[LC] * inverse]
+    return jnp.concatenate(scaled, axis=0), unit
 
 
 def taps_kernel(small_ref, wo_ref, taps_ref, wot_ref):
@@ -174,9 +178,10 @@
 
     mid_heads = 256 // BLOCK
     mid_f = diag_mask(mid_heads, BLOCK, head_size)
-    mid_b = mid_f.astype(BF16)
+    lower = 1.0 / (SOFT_CAP * math.sqrt(head_size))
+    mid_b = (mid_f * lower).astype(BF16)
     side_f = diag_mask(HEADS, HALO, head_size)
-    side_b = side_f.astype(BF16)
+    side_b = (side_f * lower).astype(BF16)
 
     own = [table.block_of(me * local + i) for i in range(local)]
     keep = [jnp.where(table.position(c) >= 1, 1.0, 0.0).astype(F32) for c in own]
@@ -193,9 +198,7 @@
             for g in range(groups):
                 cols = slice(g * wide, (g + 1) * wide)
                 vcols = slice(hq + g * wide, hq + (g + 1) * wide)
-                probs, _ = window_probs(
-                    spread(q_ref[at, cols], mask_b), kv_ref[win, cols], reach, head_size
-                )
+                probs, _ = window_probs(spread(q_ref[at, cols], mask_b), kv_ref[win, cols], reach)
                 full = dot_tn(probs.astype(BF16), kv_ref[win, vcols])
                 ctx_s[i * ROWS + put : i * ROWS + put + count, cols] = fold_heads(
                     full, mask_f, count
@@ -300,19 +303,20 @@
             k4_ref[at] = kv_refs[m][here, pl.ds(lead, share)]
             v4_ref[at] = kv_refs[m][here, pl.ds(pl.multiple_of(hq + lead, share), share)]
     heads = share // head_size
-    mask_b = diag_mask(heads, BLOCK, head_size).astype(BF16)
+    lower = 1.0 / (SOFT_CAP * math.sqrt(head_size))
+    mask_b = (diag_mask(heads, BLOCK, head_size) * lower).astype(BF16)
     for c in range(table.blocks):
         own = slice((c + PAD) * BLOCK, (c + PAD + 1) * BLOCK)
         win = slice((c + PAD - LC) * BLOCK, (c + PAD + 1) * BLOCK)
         diag_q = spread(q4_ref[own], mask_b)
-        probs, unit = window_probs(diag_q, k4_ref[win], table.reach(c), head_size)
+        probs, unit = window_probs(diag_q, k4_ref[win], table.reach(c))
         p_ref[c] = probs
         d_ref[c] = (1.0 - unit * unit) * (1.0 / math.sqrt(head_size))
 
 
 def backward_kernel(sizes, tm, part, head_size, *refs):
     tables_ref, q4_ref, v4_ref, p_ref, d_ref, nt_ref = refs[:6]
-    g_refs = refs[6 : 6 + tm][::-1]
+    g_refs = dict(zip(sending_order(tm), refs[6 : 6 + tm]))
     out_refs = refs[6 + tm : -5]
     gt_s, t_s, full_s, meta_ref, sem = refs[-5:]
     fetch = pltpu.make_async_copy(tables_ref, meta_ref, sem)
@@ -553,7 +557,7 @@
         ],
         compiler_params=pltpu.CompilerParams(vmem_limit_bytes=12 << 20),
         name="key_value_terms",
-    )(meta, q4, v4, probs, slopes, normed_t, *by_m(got)[::-1])
+    )(meta, q4, v4, probs, slopes, normed_t, *[got[m] for m in sending_order(tm)])
 
     if direct:
         kept, away = pieces

time: 55.7 us -> 54.7 us (0.982)
  waiting for transfers between devices: 19 us -> 18.2 us
    ppermute x10, waiting for transfers between devices: 19 us -> 18.2 us  [swap(): return lax.ppermute(value, axis, [(i, i ^ m) for i in range(size)])]
where the time goes in v11:
time: 54.7 us; the launch traced here: 54.4 us
  waiting for transfers between devices  18.2 us (33%)
  starting transfers between devices  14.9 us (27%)
  Pallas kernels  14.4 us (26%)
  local copies, waits for them, and re-layouts  5.25 us (10%)
  other arithmetic  0.96 us (2%)
  between operations  0.79 us (1%)
    ppermute x10, waiting for transfers between devices, swap(): return lax.ppermute(value, axis, [(i, i ^ m) for i in range(size)])  18.2 us
    ppermute x10, starting transfers between devices, swap(): return lax.ppermute(value, axis, [(i, i ^ m) for i in range(size)])  14.9 us
    pallas_call x1, Pallas kernels, on_device(): pl.pallas_call(functools.partial(forward_kernel, sizes, tm, head_size), o...  7.18 us
    unnamed x20, local copies, waits for them, and re-layouts  4.47 us
    pallas_call x1, Pallas kernels, on_device(): pl.pallas_call(functools.partial(backward_kernel, sizes, tm, width // dp,...  2.3 us
    pallas_call x3, Pallas kernels, project_shard(): pl.pallas_call(project_kernel, out_shape=made, in_specs=[vmem] * 4, out_s...  2.28 us
    pallas_call x1, Pallas kernels, on_device(): pl.pallas_call(functools.partial(probs_kernel, sizes, tm, head_size), out...  1.51 us
  transfers between devices with their start and end apart: 10, of which 8 were waited for; matrix products, arithmetic and copies ran while one was open for 3% of the time, Pallas kernels for 8%

profile of v11, /device:TPU:0, one launch (start us, length us, event | category | flops | bytes accessed | tf_op | source)
XLA Modules:
  0.0 54.4 jit_solution(9085715850727428077)
XLA Ops:
  0.6 0.0 copy-start.2
  0.6 4.1 %collective-permute-start = (bf16[128,1024]{1,0:T(8,128)(2,1)}, bf16[128,1024]{1,0:T(8,128)(2,1)S(1)}, u32[]{:S(2)}, u32[]{:S(2)}) collective-permute-start(bf16[128,1024]{1,0:T(8,128)(2,1)} %refs_9_.1), channel_id=1, source_target_pairs={{0,2},{1,3},{2,0},{3,1},{4,6},{5,7},{6,4},{7,5},{8,10},{9,11},{10,... | collective-permute-start | bytes 786440 | tf_op jit(solution)/shard_map/ppermute | solution.py:417
  4.7 1.6 %collective-permute-start.1 = (bf16[128,1024]{1,0:T(8,128)(2,1)}, bf16[128,1024]{1,0:T(8,128)(2,1)S(1)}, u32[]{:S(2)}, u32[]{:S(2)}) collective-permute-start(bf16[128,1024]{1,0:T(8,128)(2,1)} %refs_9_.1), channel_id=1, source_target_pairs={{0,1},{1,0},{2,3},{3,2},{4,5},{5,4},{6,7},{7,6},{8,9},{9,8},{10,11... | collective-permute-start | bytes 786440 | tf_op jit(solution)/shard_map/ppermute | solution.py:417
  6.3 0.8 %concatenate.7.refs_0_.meta_ref = s32[1,20]{1,0:T(1,128)S(1)} concatenate(s32[1,1]{1,0:T(1,128)} %bitcast.3, s32[1,1]{1,0:T(1,128)} %bitcast.4, s32[1,2]{1,0:T(1,128)} %param.21, s32[1,8]{1,0:T(1,128)} %param.22, s32[1,8]{1,0:T(1,128)} %param.23), dimensions={1} | concatenate | bytes 160 | tf_op jit(solution)/shard_map/concatenate | solution.py:419
  7.1 1.0 %pad_maximum_fusion.small_ref.refs_4_ = f32[33,1024]{1,0:T(8,128)S(1)} fusion(f32[1,1024]{1,0:T(1,128)} %bitcast.9, f32[1,1024]{1,0:T(1,128)} %bitcast.10, f32[31,1024]{1,0:T(8,128)} %param.19), kind=kLoop, calls=%fused_computation | loop fusion | flops 67584 | bytes 270336 | tf_op jit(solution)/shard_map/concatenate | solution.py:429
  8.1 0.0 copy-start.3
  8.1 1.2 %copy-done.3 = bf16[512,1024]{1,0:T(8,128)(2,1)S(1)} copy-done((bf16[512,1024]{1,0:T(8,128)(2,1)S(1)}, bf16[512,1024]{1,0:T(8,128)(2,1)}, u32[]{:S(2)}) %copy-start.3) | copy-done | bytes 1048600
  9.3 0.4 spread_taps.1
  9.6 0.0 copy-done.2
  9.7 0.0 copy-start
  9.7 1.6 %copy-done = bf16[1024,1024]{1,0:T(8,128)(2,1)S(1)} copy-done((bf16[1024,1024]{1,0:T(8,128)(2,1)S(1)}, bf16[1024,1024]{1,0:T(8,128)(2,1)}, u32[]{:S(2)}) %copy-start) | copy-done | bytes 2097176
  11.3 0.0 copy-start.5
  11.3 0.9 %copy-done.5 = bf16[128,1024]{1,0:T(8,128)(2,1)S(1)} copy-done((bf16[128,1024]{1,0:T(8,128)(2,1)S(1)}, bf16[128,1024]{1,0:T(8,128)(2,1)}, u32[]{:S(2)}) %copy-start.5) | copy-done | bytes 262168
  12.2 0.0 copy-start.8
  12.2 0.7 %copy-done.8 = f32[1024]{0:T(1024)S(1)} copy-done((f32[1024]{0:T(1024)S(1)}, f32[1024]{0:T(1024)}, u32[]{:S(2)}) %copy-start.8) | copy-done | bytes 4120
  12.9 0.0 copy-start.1
  12.9 0.8 %project_rows_0.1 = (bf16[128,1024]{1,0:T(8,128)(2,1)S(1)}, bf16[128,512]{1,0:T(8,128)(2,1)S(1)}, bf16[128,1024]{1,0:T(8,128)(2,1)S(1)}) custom-call(bf16[128,1024]{1,0:T(8,128)(2,1)S(1)} %copy-done.5, f32[1,1024]{1,0:T(1,128)S(1)} %bitcast.5, bf16[1024,512]{1,0:T(8,128)(2,1)S(1)} %copy-done.2, bf16[1024,1024]{1,0:T(8,128)(2,1)S(1)} %copy-done), custom_call_target="tpu_custom_call" | custom-call | flops 402653184 | bytes 4194304 | tf_op jit(solution)/shard_map/project_rows_0/pallas_call | solution.py:451
  13.7 3.3 %collective-permute-done.x_ref.refs_11_ = bf16[128,1024]{1,0:T(8,128)(2,1)S(1)} collective-permute-done((bf16[128,1024]{1,0:T(8,128)(2,1)}, bf16[128,1024]{1,0:T(8,128)(2,1)S(1)}, u32[]{:S(2)}, u32[]{:S(2)}) %collective-permute-start) | collective-permute-done | bytes 262176 | tf_op jit(solution)/shard_map/ppermute | solution.py:417
  17.0 0.0 copy-start.9
  17.0 0.7 %collective-permute-start.2 = (bf16[128,1024]{1,0:T(8,128)(2,1)S(1)}, bf16[128,1024]{1,0:T(8,128)(2,1)S(1)}, u32[]{:S(2)}, u32[]{:S(2)}) collective-permute-start(bf16[128,1024]{1,0:T(8,128)(2,1)S(1)} %collective-permute-done.x_ref.refs_11_), channel_id=1, source_target_pairs={{0,1},{1,0},{2,3},{3,2},{4,5},{5,4},{6,7},{7,6},{8,9},{9,8},{10,11... | collective-permute-start | bytes 786440 | tf_op jit(solution)/shard_map/ppermute | solution.py:417
  17.7 0.0 copy-done.1
  17.7 0.8 %project_rows_2.1 = (bf16[128,1024]{1,0:T(8,128)(2,1)S(1)}, bf16[128,512]{1,0:T(8,128)(2,1)S(1)}, bf16[128,1024]{1,0:T(8,128)(2,1)S(1)}) custom-call(bf16[128,1024]{1,0:T(8,128)(2,1)S(1)} %collective-permute-done.x_ref.refs_11_, f32[1,1024]{1,0:T(1,128)S(1)} %bitcast.6, bf16[1024,512]{1,0:T(8,128)(2,1)S(1)} %copy-done.2, bf16[1024,1024]{1,0:T(8,128)(2,1)S(1)} %copy-done.1), custom_call_target="tpu_custom_call" | custom-call | flops 402653184 | bytes 4194304 | tf_op jit(solution)/shard_map/project_rows_2/pallas_call | solution.py:451
  18.5 0.0 copy-start.4
  18.5 0.0 copy-start.6
  18.5 0.0 copy-start.7
  18.5 0.0 collective-permute-done.1.x_ref.refs_10_
  18.5 0.0 copy-done.9
  18.5 0.8 %project_rows_1.1 = (bf16[128,1024]{1,0:T(8,128)(2,1)S(1)}, bf16[128,512]{1,0:T(8,128)(2,1)S(1)}, bf16[128,1024]{1,0:T(8,128)(2,1)S(1)}) custom-call(bf16[128,1024]{1,0:T(8,128)(2,1)S(1)} %collective-permute-done.1.x_ref.refs_10_, f32[1,1024]{1,0:T(1,128)S(1)} %bitcast.7, bf16[1024,512]{1,0:T(8,128)(2,1)S(1)} %copy-done.2, bf16[1024,1024]{1,0:T(8,128)(2,1)S(1)} %copy-done.1), custom_call_target="tpu_custom_call" | custom-call | flops 402653184 | bytes 4194304 | tf_op jit(solution)/shard_map/project_rows_1/pallas_call | solution.py:451
  19.3 5.1 %collective-permute-done.2.refs_12_ = bf16[128,1024]{1,0:T(8,128)(2,1)S(1)} collective-permute-done((bf16[128,1024]{1,0:T(8,128)(2,1)S(1)}, bf16[128,1024]{1,0:T(8,128)(2,1)S(1)}, u32[]{:S(2)}, u32[]{:S(2)}) %collective-permute-start.2) | collective-permute-done | bytes 262176 | tf_op jit(solution)/shard_map/ppermute | solution.py:417
  24.4 0.0 copy-done.4
  24.4 0.0 copy-done.6
  24.4 0.0 copy-done.7
  24.4 7.2 %forward_pass.1 = (bf16[128,1024]{1,0:T(8,128)(2,1)}, bf16[128,1024]{1,0:T(8,128)(2,1)S(1)}, bf16[128,512]{1,0:T(8,128)(2,1)S(1)}, bf16[128,1024]{1,0:T(8,128)(2...) custom-call(s32[1,20]{1,0:T(1,128)S(1)} %concatenate.7.refs_0_.meta_, ...), custom_call_target="tpu_custom_call" | custom-call | tf_op jit(solution)/shard_map/forward_pass/pallas_call | solution.py:482
  31.6 3.1 %collective-permute-start.3 = (bf16[192,256]{1,0:T(8,128)(2,1)S(1)}, bf16[192,256]{1,0:T(8,128)(2,1)S(1)}, u32[]{:S(2)}, u32[]{:S(2)}) collective-permute-start(bf16[192,256]{1,0:T(8,128)(2,1)S(1)} %get-tuple-element.60), channel_id=1, source_target_pairs={{0,2},{1,3},{2,0},{3,1},{4,6},{5,7},{6,4},{7,5},{8,10},{9,11},{10,... | collective-permute-start | bytes 294920 | tf_op jit(solution)/shard_map/ppermute | solution.py:417
  34.7 1.3 %collective-permute-start.4 = (bf16[192,256]{1,0:T(8,128)(2,1)S(1)}, bf16[192,256]{1,0:T(8,128)(2,1)S(1)}, u32[]{:S(2)}, u32[]{:S(2)}) collective-permute-start(bf16[192,256]{1,0:T(8,128)(2,1)S(1)} %get-tuple-element.61), channel_id=1, source_target_pairs={{0,3},{1,2},{2,1},{3,0},{4,7},{5,6},{6,5},{7,4},{8,11},{9,10},{10,... | collective-permute-start | bytes 294920 | tf_op jit(solution)/shard_map/ppermute | solution.py:417
  36.0 0.5 collective-permute-start.5
  36.5 1.5 %window_probs.1 = (bf16[704,256]{1,0:T(8,128)(2,1)S(1)}, bf16[704,256]{1,0:T(8,128)(2,1)S(1)}, f32[8,192,256]{2,1,0:T(8,128)S(1)}, f32[8,192,256]{2,1,0:T(8,128)S(1)}, bf16[1024,512]{1,0:T(8,128)(2,1)S(1)}) custom-call(s32[1,20]{1,0:T(1,128)S(1)} %concatenate.7.refs_0_.meta_ref, bf16[128,512]{1,0:T(8,128)(2,1)S(1)} %get-tuple-element.42.refs_13_.refs_0_, ...), custom_call_target="tpu_custom_call" | custom-call | flops 2000000000 | bytes 4000000 | tf_op jit(solution)/shard_map/window_probs/pallas_call | solution.py:525
  38.0 4.2 %collective-permute-done.3.refs_6_ = bf16[192,256]{1,0:T(8,128)(2,1)S(1)} collective-permute-done((bf16[192,256]{1,0:T(8,128)(2,1)S(1)}, bf16[192,256]{1,0:T(8,128)(2,1)S(1)}, u32[]{:S(2)}, u32[]{:S(2)}) %collective-permute-start.3) | collective-permute-done | bytes 98336 | tf_op jit(solution)/shard_map/ppermute | solution.py:417
  42.2 0.0 collective-permute-done.4.refs_7_
  42.2 0.3 collective-permute-done.5.refs_8_
  42.5 2.3 %key_value_terms.1 = (f32[512,256]{1,0:T(8,128)S(1)}, bf16[512,256]{1,0:T(8,128)(2,1)S(1)}) custom-call(s32[1,20]{1,0:T(1,128)S(1)} %concatenate.7.refs_0_.meta_ref, bf16[704,256]{1,0:T(8,128)(2,1)S(1)} %get-tuple-element.55.refs_1_, bf16[704,256]{1,0:T(8,128)(2,1)S(1)} %get-tuple-element.56.refs_2_, f32[8,192,256]{2,1,0:T(8,128)S(1)} %get-tuple-element.57.refs_3_, ...), custom_call_target="tpu_custom_call" | custom-call | tf_op jit(solution)/shard_map/key_value_terms/pallas_call | solution.py:546
  44.8 0.1 collective-permute-start.6
  44.9 1.5 %collective-permute-done.6.got_ref = bf16[512,256]{1,0:T(8,128)(2,1)S(1)} collective-permute-done((bf16[512,256]{1,0:T(8,128)(2,1)S(1)}, bf16[512,256]{1,0:T(8,128)(2,1)S(1)}, u32[]{:S(2)}, u32[]{:S(2)}) %collective-permute-start.6) | collective-permute-done | bytes 262176 | tf_op jit(solution)/shard_map/ppermute | solution.py:417
  46.4 0.1 sum_pair.1
  46.5 2.5 %collective-permute-start.7 = (bf16[128,256]{1,0:T(8,128)(2,1)S(1)}, bf16[128,256]{1,0:T(8,128)(2,1)S(1)}, u32[]{:S(2)}, u32[]{:S(2)}) collective-permute-start(bf16[128,256]{1,0:T(8,128)(2,1)S(1)} %get-tuple-element.66), channel_id=1, source_target_pairs={{0,24},{4,28},{8,16},{12,20},{16,8},{20,12},{24,0},{28,4},{1,25},{... | collective-permute-start | bytes 196616 | tf_op jit(solution)/shard_map/ppermute | solution.py:417
  49.0 0.5 collective-permute-start.8
  49.5 0.5 collective-permute-start.9
  50.0 1.7 %collective-permute-done.7.refs_0_ = bf16[128,256]{1,0:T(8,128)(2,1)S(1)} collective-permute-done((bf16[128,256]{1,0:T(8,128)(2,1)S(1)}, bf16[128,256]{1,0:T(8,128)(2,1)S(1)}, u32[]{:S(2)}, u32[]{:S(2)}) %collective-permute-start.7) | collective-permute-done | bytes 65568 | tf_op jit(solution)/shard_map/ppermute | solution.py:417
  51.7 1.5 %collective-permute-done.8.refs_1_ = bf16[128,256]{1,0:T(8,128)(2,1)S(1)} collective-permute-done((bf16[128,256]{1,0:T(8,128)(2,1)S(1)}, bf16[128,256]{1,0:T(8,128)(2,1)S(1)}, u32[]{:S(2)}, u32[]{:S(2)}) %collective-permute-start.8) | collective-permute-done | bytes 65568 | tf_op jit(solution)/shard_map/ppermute | solution.py:417
  53.2 0.5 collective-permute-done.9.refs_2_
  53.7 0.7 %sum_groups.1 = f32[128,256]{1,0:T(8,128)} custom-call(bf16[128,256]{1,0:T(8,128)(2,1)S(1)} %collective-permute-done.7.refs_0_, bf16[128,256]{1,0:T(8,128)(2,1)S(1)} %collective-permute-done.8.refs_1_, bf16[128,256]{1,0:T(8,128)(2,1)S(1)} %collective-permute-done.9.refs_2_, bf16[128,256]{1,0:T(8,128)(2,1)S(1)} %get-tuple-element.69.refs_3_), custom_call_target="tpu_custom_call" | custom-call | tf_op jit(solution)/shard_map/sum_groups/pallas_call | solution.py:579
Async XLA Ops:
  0.6 9.0 %copy-start.2 = (bf16[1024,512]{1,0:T(8,128)(2,1)S(1)}, bf16[1024,512]{1,0:T(8,128)(2,1)}, u32[]{:S(2)}) copy-start(bf16[1024,512]{1,0:T(8,128)(2,1)} %refs_7_.1) | copy-start | bytes 3145732
  0.6 16.3 %collective-permute-start = (bf16[128,1024]{1,0:T(8,128)(2,1)}, bf16[128,1024]{1,0:T(8,128)(2,1)S(1)}, u32[]{:S(2)}, u32[]{:S(2)}) collective-permute-start(bf16[128,1024]{1,0:T(8,128)(2,1)} %refs_9_.1), channel_id=1, source_target_pairs={{0,2},{1,3},{2,0},{3,1},{4,6},{5,7},{6,4},{7,5},{8,10},{9,11},{10,... | collective-permute-start | bytes 786440 | tf_op jit(solution)/shard_map/ppermute | solution.py:417
  4.7 13.8 %collective-permute-start.1 = (bf16[128,1024]{1,0:T(8,128)(2,1)}, bf16[128,1024]{1,0:T(8,128)(2,1)S(1)}, u32[]{:S(2)}, u32[]{:S(2)}) collective-permute-start(bf16[128,1024]{1,0:T(8,128)(2,1)} %refs_9_.1), channel_id=1, source_target_pairs={{0,1},{1,0},{2,3},{3,2},{4,5},{5,4},{6,7},{7,6},{8,9},{9,8},{10,11... | collective-permute-start | bytes 786440 | tf_op jit(solution)/shard_map/ppermute | solution.py:417
  8.1 1.2 %copy-start.3 = (bf16[512,1024]{1,0:T(8,128)(2,1)S(1)}, bf16[512,1024]{1,0:T(8,128)(2,1)}, u32[]{:S(2)}) copy-start(bf16[512,1024]{1,0:T(8,128)(2,1)} %refs_2_.1) | copy-start | bytes 3145732
  9.7 1.6 %copy-start = (bf16[1024,1024]{1,0:T(8,128)(2,1)S(1)}, bf16[1024,1024]{1,0:T(8,128)(2,1)}, u32[]{:S(2)}) copy-start(bf16[1024,1024]{1,0:T(8,128)(2,1)} %refs_8_.1) | copy-start | bytes 6291460
  11.3 0.9 %copy-start.5 = (bf16[128,1024]{1,0:T(8,128)(2,1)S(1)}, bf16[128,1024]{1,0:T(8,128)(2,1)}, u32[]{:S(2)}) copy-start(bf16[128,1024]{1,0:T(8,128)(2,1)} %refs_9_.1) | copy-start | bytes 786436
  12.2 0.7 %copy-start.8 = (f32[1024]{0:T(1024)S(1)}, f32[1024]{0:T(1024)}, u32[]{:S(2)}) copy-start(f32[1024]{0:T(1024)} %param.14) | copy-start | bytes 12292
  12.9 4.8 %copy-start.1 = (bf16[1024,1024]{1,0:T(8,128)(2,1)S(1)}, bf16[1024,1024]{1,0:T(8,128)(2,1)}, u32[]{:S(2)}) copy-start(bf16[1024,1024]{1,0:T(8,128)(2,1)} %refs_8_.1) | copy-start | bytes 6291460
  17.0 1.5 %copy-start.9 = (f32[1024]{0:T(1024)S(1)}, f32[1024]{0:T(1024)}, u32[]{:S(2)}) copy-start(f32[1024]{0:T(1024)} %param.14) | copy-start | bytes 12292
  17.0 7.4 %collective-permute-start.2 = (bf16[128,1024]{1,0:T(8,128)(2,1)S(1)}, bf16[128,1024]{1,0:T(8,128)(2,1)S(1)}, u32[]{:S(2)}, u32[]{:S(2)}) collective-permute-start(bf16[128,1024]{1,0:T(8,128)(2,1)S(1)} %collective-permute-done.x_ref.refs_11_), channel_id=1, source_target_pairs={{0,1},{1,0},{2,3},{3,2},{4,5},{5,4},{6,7},{7,6},{8,9},{9,8},{10,11... | collective-permute-start | bytes 786440 | tf_op jit(solution)/shard_map/ppermute | solution.py:417
  18.5 6.0 %copy-start.4 = (bf16[512,1024]{1,0:T(8,128)(2,1)S(1)}, bf16[512,1024]{1,0:T(8,128)(2,1)}, u32[]{:S(2)}) copy-start(bf16[512,1024]{1,0:T(8,128)(2,1)} %refs_2_.1) | copy-start | bytes 3145732
  18.5 5.9 %copy-start.6 = (bf16[128,1024]{1,0:T(8,128)(2,1)S(1)}, bf16[128,1024]{1,0:T(8,128)(2,1)}, u32[]{:S(2)}) copy-start(bf16[128,1024]{1,0:T(8,128)(2,1)} %refs_9_.1) | copy-start | bytes 786436
  18.5 5.9 %copy-start.7 = (bf16[128,1024]{1,0:T(8,128)(2,1)S(1)}, bf16[128,1024]{1,0:T(8,128)(2,1)}, u32[]{:S(2)}) copy-start(bf16[128,1024]{1,0:T(8,128)(2,1)} %refs_1_.1) | copy-start | bytes 786436
  31.6 10.6 %collective-permute-start.3 = (bf16[192,256]{1,0:T(8,128)(2,1)S(1)}, bf16[192,256]{1,0:T(8,128)(2,1)S(1)}, u32[]{:S(2)}, u32[]{:S(2)}) collective-permute-start(bf16[192,256]{1,0:T(8,128)(2,1)S(1)} %get-tuple-element.60), channel_id=1, source_target_pairs={{0,2},{1,3},{2,0},{3,1},{4,6},{5,7},{6,4},{7,5},{8,10},{9,11},{10,... | collective-permute-start | bytes 294920 | tf_op jit(solution)/shard_map/ppermute | solution.py:417
  34.7 7.5 %collective-permute-start.4 = (bf16[192,256]{1,0:T(8,128)(2,1)S(1)}, bf16[192,256]{1,0:T(8,128)(2,1)S(1)}, u32[]{:S(2)}, u32[]{:S(2)}) collective-permute-start(bf16[192,256]{1,0:T(8,128)(2,1)S(1)} %get-tuple-element.61), channel_id=1, source_target_pairs={{0,3},{1,2},{2,1},{3,0},{4,7},{5,6},{6,5},{7,4},{8,11},{9,10},{10,... | collective-permute-start | bytes 294920 | tf_op jit(solution)/shard_map/ppermute | solution.py:417
  36.0 6.5 %collective-permute-start.5 = (bf16[192,256]{1,0:T(8,128)(2,1)S(1)}, bf16[192,256]{1,0:T(8,128)(2,1)S(1)}, u32[]{:S(2)}, u32[]{:S(2)}) collective-permute-start(bf16[192,256]{1,0:T(8,128)(2,1)S(1)} %get-tuple-element.62), channel_id=1, source_target_pairs={{0,1},{1,0},{2,3},{3,2},{4,5},{5,4},{6,7},{7,6},{8,9},{9,8},{10,11... | collective-permute-start | bytes 294920 | tf_op jit(solution)/shard_map/ppermute | solution.py:417
  44.8 1.6 %collective-permute-start.6 = (bf16[512,256]{1,0:T(8,128)(2,1)S(1)}, bf16[512,256]{1,0:T(8,128)(2,1)S(1)}, u32[]{:S(2)}, u32[]{:S(2)}) collective-permute-start(bf16[512,256]{1,0:T(8,128)(2,1)S(1)} %get-tuple-element.65), channel_id=1, source_target_pairs={{0,4},{4,0},{8,12},{12,8},{16,20},{20,16},{24,28},{28,24},{1,5},{5... | collective-permute-start | bytes 786440 | tf_op jit(solution)/shard_map/ppermute | solution.py:417
  46.5 5.3 %collective-permute-start.7 = (bf16[128,256]{1,0:T(8,128)(2,1)S(1)}, bf16[128,256]{1,0:T(8,128)(2,1)S(1)}, u32[]{:S(2)}, u32[]{:S(2)}) collective-permute-start(bf16[128,256]{1,0:T(8,128)(2,1)S(1)} %get-tuple-element.66), channel_id=1, source_target_pairs={{0,24},{4,28},{8,16},{12,20},{16,8},{20,12},{24,0},{28,4},{1,25},{... | collective-permute-start | bytes 196616 | tf_op jit(solution)/shard_map/ppermute | solution.py:417
  49.0 4.3 %collective-permute-start.8 = (bf16[128,256]{1,0:T(8,128)(2,1)S(1)}, bf16[128,256]{1,0:T(8,128)(2,1)S(1)}, u32[]{:S(2)}, u32[]{:S(2)}) collective-permute-start(bf16[128,256]{1,0:T(8,128)(2,1)S(1)} %get-tuple-element.67), channel_id=1, source_target_pairs={{0,16},{4,20},{8,24},{12,28},{16,0},{20,4},{24,8},{28,12},{1,17},{... | collective-permute-start | bytes 196616 | tf_op jit(solution)/shard_map/ppermute | solution.py:417
  49.5 4.3 %collective-permute-start.9 = (bf16[128,256]{1,0:T(8,128)(2,1)S(1)}, bf16[128,256]{1,0:T(8,128)(2,1)S(1)}, u32[]{:S(2)}, u32[]{:S(2)}) collective-permute-start(bf16[128,256]{1,0:T(8,128)(2,1)S(1)} %get-tuple-element.68), channel_id=1, source_target_pairs={{0,8},{4,12},{8,0},{12,4},{16,24},{20,28},{24,16},{28,20},{1,9},{5... | collective-permute-start | bytes 196616 | tf_op jit(solution)/shard_map/ppermute | solution.py:417

commit v12 on v11

--- a/solution.py
+++ b/solution.py
@@ -283,7 +283,8 @@
 
 def probs_kernel(sizes, tm, head_size, meta_ref, *refs):
     q_refs, kv_refs, n_refs = refs[:tm], refs[tm : 2 * tm], refs[2 * tm : 3 * tm]
-    q4_ref, v4_ref, p_ref, d_ref, nt_ref, k4_ref = refs[3 * tm :]
+    made_ref, out_ref, q4_ref, v4_ref, p_ref, d_ref, nt_ref, k4_ref = refs[3 * tm :]
+    out_ref[...] = made_ref[...]
     for m in range(tm):
         rows = n_refs[m].shape[0]
         nt_ref[:, m * rows : (m + 1) * rows] = n_refs[m][...].T
@@ -515,27 +516,28 @@
         *by_m(queries),
         *by_m(keys_values),
     )
-    layer_out, normed[tm - 1], queries[tm - 1], keys_values[tm - 1] = results[:4]
+    made_out, normed[tm - 1], queries[tm - 1], keys_values[tm - 1] = results[:4]
     sends = results[:3:-1]
     got = {0: sends[0]}
     for m in range(tm - 1, 0, -1):
         got[m] = swap(sends[m], "tm", tm, m)
 
     pair_width = share // head_size * BLOCK
-    q4, v4, probs, slopes, normed_t = pl.pallas_call(
+    layer_out, q4, v4, probs, slopes, normed_t = pl.pallas_call(
         functools.partial(probs_kernel, sizes, tm, head_size),
-        out_shape=[shape((padded, share), BF16)] * 2
+        out_shape=[shape((rows, width), BF16)]
+        + [shape((padded, share), BF16)] * 2
         + [shape((blocks, SPAN, pair_width), F32)] * 2
         + [shape((width, blocks * BLOCK), BF16)],
-        in_specs=[smem] + [vmem] * (3 * tm),
-        out_specs=[vmem] * 5,
+        in_specs=[smem] + [vmem] * (3 * tm + 1),
+        out_specs=[vmem] * 6,
         scratch_shapes=[pltpu.VMEM((padded, share), BF16)],
         compiler_params=pltpu.CompilerParams(vmem_limit_bytes=8 << 20),
         name="window_probs",
         cost_estimate=pl.CostEstimate(
             flops=2 * 10**9, bytes_accessed=4 * 10**6, transcendentals=800000
         ),
-    )(meta, *by_m(queries), *by_m(keys_values), *by_m(normed))
+    )(meta, *by_m(queries), *by_m(keys_values), *by_m(normed), made_out)
 
     direct = dp <= 8
     half_width = width // 2

time: 54.7 us -> 54.8 us (level)
  Pallas kernels: 14.4 us -> 15.1 us
  waiting for transfers between devices: 18.2 us -> 17.6 us
    pallas_call x1, Pallas kernels: 1.51 us -> 2.15 us  [on_device(): pl.pallas_call(functools.partial(probs_kernel, sizes, tm, head_size), out...]
    ppermute x10, waiting for transfers between devices: 18.2 us -> 17.6 us  [swap(): return lax.ppermute(value, axis, [(i, i ^ m) for i in range(size)])]
  transfers between devices with their start and end apart: 10 -> 10, of which waited for: 8 -> 8; matrix products, arithmetic and copies ran while one was open for 3% -> 3% of each run, Pallas kernels for 8% -> 9%
where the time goes in v12:
time: 54.8 us; the launch traced here: 54.5 us
  waiting for transfers between devices  17.6 us (32%)
  Pallas kernels  15.1 us (28%)
  starting transfers between devices  14.9 us (27%)
  local copies, waits for them, and re-layouts  5.25 us (10%)
  other arithmetic  0.96 us (2%)
  between operations  0.79 us (1%)
    ppermute x10, waiting for transfers between devices, swap(): return lax.ppermute(value, axis, [(i, i ^ m) for i in range(size)])  17.6 us
    ppermute x10, starting transfers between devices, swap(): return lax.ppermute(value, axis, [(i, i ^ m) for i in range(size)])  14.9 us
    pallas_call x1, Pallas kernels, on_device(): pl.pallas_call(functools.partial(forward_kernel, sizes, tm, head_size), o...  7.24 us
    unnamed x20, local copies, waits for them, and re-layouts  4.48 us
    pallas_call x1, Pallas kernels, on_device(): pl.pallas_call(functools.partial(backward_kernel, sizes, tm, width // dp,...  2.3 us
    pallas_call x3, Pallas kernels, project_shard(): pl.pallas_call(project_kernel, out_shape=made, in_specs=[vmem] * 4, out_s...  2.28 us
    pallas_call x1, Pallas kernels, on_device(): pl.pallas_call(functools.partial(probs_kernel, sizes, tm, head_size), out...  2.15 us
  transfers between devices with their start and end apart: 10, of which 8 were waited for; matrix products, arithmetic and copies ran while one was open for 3% of the time, Pallas kernels for 9%

profile of v12, /device:TPU:0, one launch (start us, length us, event | category | flops | bytes accessed | tf_op | source)
XLA Modules:
  0.0 54.5 jit_solution(3626684386123330763)
XLA Ops:
  0.6 0.0 copy-start.2
  0.6 4.1 %collective-permute-start = (bf16[128,1024]{1,0:T(8,128)(2,1)}, bf16[128,1024]{1,0:T(8,128)(2,1)S(1)}, u32[]{:S(2)}, u32[]{:S(2)}) collective-permute-start(bf16[128,1024]{1,0:T(8,128)(2,1)} %refs_9_.1), channel_id=1, source_target_pairs={{0,2},{1,3},{2,0},{3,1},{4,6},{5,7},{6,4},{7,5},{8,10},{9,11},{10,... | collective-permute-start | bytes 786440 | tf_op jit(solution)/shard_map/ppermute | solution.py:418
  4.7 1.6 %collective-permute-start.1 = (bf16[128,1024]{1,0:T(8,128)(2,1)}, bf16[128,1024]{1,0:T(8,128)(2,1)S(1)}, u32[]{:S(2)}, u32[]{:S(2)}) collective-permute-start(bf16[128,1024]{1,0:T(8,128)(2,1)} %refs_9_.1), channel_id=1, source_target_pairs={{0,1},{1,0},{2,3},{3,2},{4,5},{5,4},{6,7},{7,6},{8,9},{9,8},{10,11... | collective-permute-start | bytes 786440 | tf_op jit(solution)/shard_map/ppermute | solution.py:418
  6.3 0.8 %concatenate.7.refs_0_.meta_ref = s32[1,20]{1,0:T(1,128)S(1)} concatenate(s32[1,1]{1,0:T(1,128)} %bitcast.3, s32[1,1]{1,0:T(1,128)} %bitcast.4, s32[1,2]{1,0:T(1,128)} %param.21, s32[1,8]{1,0:T(1,128)} %param.22, s32[1,8]{1,0:T(1,128)} %param.23), dimensions={1} | concatenate | bytes 160 | tf_op jit(solution)/shard_map/concatenate | solution.py:420
  7.1 1.0 %pad_maximum_fusion.small_ref.refs_4_ = f32[33,1024]{1,0:T(8,128)S(1)} fusion(f32[1,1024]{1,0:T(1,128)} %bitcast.9, f32[1,1024]{1,0:T(1,128)} %bitcast.10, f32[31,1024]{1,0:T(8,128)} %param.19), kind=kLoop, calls=%fused_computation | loop fusion | flops 67584 | bytes 270336 | tf_op jit(solution)/shard_map/concatenate | solution.py:430
  8.1 0.0 copy-start.3
  8.1 1.2 %copy-done.3 = bf16[512,1024]{1,0:T(8,128)(2,1)S(1)} copy-done((bf16[512,1024]{1,0:T(8,128)(2,1)S(1)}, bf16[512,1024]{1,0:T(8,128)(2,1)}, u32[]{:S(2)}) %copy-start.3) | copy-done | bytes 1048600
  9.3 0.4 spread_taps.1
  9.6 0.0 copy-done.2
  9.7 0.0 copy-start
  9.7 1.6 %copy-done = bf16[1024,1024]{1,0:T(8,128)(2,1)S(1)} copy-done((bf16[1024,1024]{1,0:T(8,128)(2,1)S(1)}, bf16[1024,1024]{1,0:T(8,128)(2,1)}, u32[]{:S(2)}) %copy-start) | copy-done | bytes 2097176
  11.3 0.0 copy-start.5
  11.3 0.9 %copy-done.5 = bf16[128,1024]{1,0:T(8,128)(2,1)S(1)} copy-done((bf16[128,1024]{1,0:T(8,128)(2,1)S(1)}, bf16[128,1024]{1,0:T(8,128)(2,1)}, u32[]{:S(2)}) %copy-start.5) | copy-done | bytes 262168
  12.2 0.0 copy-start.8
  12.2 0.7 %copy-done.8 = f32[1024]{0:T(1024)S(1)} copy-done((f32[1024]{0:T(1024)S(1)}, f32[1024]{0:T(1024)}, u32[]{:S(2)}) %copy-start.8) | copy-done | bytes 4120
  12.9 0.0 copy-start.1
  12.9 0.8 %project_rows_0.1 = (bf16[128,1024]{1,0:T(8,128)(2,1)S(1)}, bf16[128,512]{1,0:T(8,128)(2,1)S(1)}, bf16[128,1024]{1,0:T(8,128)(2,1)S(1)}) custom-call(bf16[128,1024]{1,0:T(8,128)(2,1)S(1)} %copy-done.5, f32[1,1024]{1,0:T(1,128)S(1)} %bitcast.5, bf16[1024,512]{1,0:T(8,128)(2,1)S(1)} %copy-done.2, bf16[1024,1024]{1,0:T(8,128)(2,1)S(1)} %copy-done), custom_call_target="tpu_custom_call" | custom-call | flops 402653184 | bytes 4194304 | tf_op jit(solution)/shard_map/project_rows_0/pallas_call | solution.py:452
  13.7 3.3 %collective-permute-done.x_ref.refs_11_ = bf16[128,1024]{1,0:T(8,128)(2,1)S(1)} collective-permute-done((bf16[128,1024]{1,0:T(8,128)(2,1)}, bf16[128,1024]{1,0:T(8,128)(2,1)S(1)}, u32[]{:S(2)}, u32[]{:S(2)}) %collective-permute-start) | collective-permute-done | bytes 262176 | tf_op jit(solution)/shard_map/ppermute | solution.py:418
  17.0 0.7 %collective-permute-start.2 = (bf16[128,1024]{1,0:T(8,128)(2,1)S(1)}, bf16[128,1024]{1,0:T(8,128)(2,1)S(1)}, u32[]{:S(2)}, u32[]{:S(2)}) collective-permute-start(bf16[128,1024]{1,0:T(8,128)(2,1)S(1)} %collective-permute-done.x_ref.refs_11_), channel_id=1, source_target_pairs={{0,1},{1,0},{2,3},{3,2},{4,5},{5,4},{6,7},{7,6},{8,9},{9,8},{10,11... | collective-permute-start | bytes 786440 | tf_op jit(solution)/shard_map/ppermute | solution.py:418
  17.7 0.0 copy-done.1
  17.7 0.8 %project_rows_2.1 = (bf16[128,1024]{1,0:T(8,128)(2,1)S(1)}, bf16[128,512]{1,0:T(8,128)(2,1)S(1)}, bf16[128,1024]{1,0:T(8,128)(2,1)S(1)}) custom-call(bf16[128,1024]{1,0:T(8,128)(2,1)S(1)} %collective-permute-done.x_ref.refs_11_, f32[1,1024]{1,0:T(1,128)S(1)} %bitcast.6, bf16[1024,512]{1,0:T(8,128)(2,1)S(1)} %copy-done.2, bf16[1024,1024]{1,0:T(8,128)(2,1)S(1)} %copy-done.1), custom_call_target="tpu_custom_call" | custom-call | flops 402653184 | bytes 4194304 | tf_op jit(solution)/shard_map/project_rows_2/pallas_call | solution.py:452
  18.5 0.0 copy-start.4
  18.5 0.0 copy-start.6
  18.5 0.0 copy-start.7
  18.5 0.0 copy-start.9
  18.5 0.0 collective-permute-done.1.x_ref.refs_10_
  18.5 0.8 %project_rows_1.1 = (bf16[128,1024]{1,0:T(8,128)(2,1)S(1)}, bf16[128,512]{1,0:T(8,128)(2,1)S(1)}, bf16[128,1024]{1,0:T(8,128)(2,1)S(1)}) custom-call(bf16[128,1024]{1,0:T(8,128)(2,1)S(1)} %collective-permute-done.1.x_ref.refs_10_, f32[1,1024]{1,0:T(1,128)S(1)} %bitcast.7, bf16[1024,512]{1,0:T(8,128)(2,1)S(1)} %copy-done.2, bf16[1024,1024]{1,0:T(8,128)(2,1)S(1)} %copy-done.1), custom_call_target="tpu_custom_call" | custom-call | flops 402653184 | bytes 4194304 | tf_op jit(solution)/shard_map/project_rows_1/pallas_call | solution.py:452
  19.3 5.1 %collective-permute-done.2.refs_12_ = bf16[128,1024]{1,0:T(8,128)(2,1)S(1)} collective-permute-done((bf16[128,1024]{1,0:T(8,128)(2,1)S(1)}, bf16[128,1024]{1,0:T(8,128)(2,1)S(1)}, u32[]{:S(2)}, u32[]{:S(2)}) %collective-permute-start.2) | collective-permute-done | bytes 262176 | tf_op jit(solution)/shard_map/ppermute | solution.py:418
  24.4 0.0 copy-done.4
  24.4 0.0 copy-done.6
  24.4 0.0 copy-done.7
  24.4 0.0 copy-done.9
  24.4 7.2 %forward_pass.1 = (bf16[128,1024]{1,0:T(8,128)(2,1)S(1)}, bf16[128,1024]{1,0:T(8,128)(2,1)S(1)}, bf16[128,512]{1,0:T(8,128)(2,1)S(1)}, bf16[128,1024]{1,0:T(8,12...) custom-call(s32[1,20]{1,0:T(1,128)S(1)} %concatenate.7.refs_0_.meta_, ...), custom_call_target="tpu_custom_call" | custom-call | tf_op jit(solution)/shard_map/forward_pass/pallas_call | solution.py:483
  31.7 3.1 %collective-permute-start.3 = (bf16[192,256]{1,0:T(8,128)(2,1)S(1)}, bf16[192,256]{1,0:T(8,128)(2,1)S(1)}, u32[]{:S(2)}, u32[]{:S(2)}) collective-permute-start(bf16[192,256]{1,0:T(8,128)(2,1)S(1)} %get-tuple-element.62), channel_id=1, source_target_pairs={{0,2},{1,3},{2,0},{3,1},{4,6},{5,7},{6,4},{7,5},{8,10},{9,11},{10,... | collective-permute-start | bytes 294920 | tf_op jit(solution)/shard_map/ppermute | solution.py:418
  34.8 1.3 %collective-permute-start.4 = (bf16[192,256]{1,0:T(8,128)(2,1)S(1)}, bf16[192,256]{1,0:T(8,128)(2,1)S(1)}, u32[]{:S(2)}, u32[]{:S(2)}) collective-permute-start(bf16[192,256]{1,0:T(8,128)(2,1)S(1)} %get-tuple-element.63), channel_id=1, source_target_pairs={{0,3},{1,2},{2,1},{3,0},{4,7},{5,6},{6,5},{7,4},{8,11},{9,10},{10,... | collective-permute-start | bytes 294920 | tf_op jit(solution)/shard_map/ppermute | solution.py:418
  36.1 0.5 collective-permute-start.5
  36.6 2.2 %window_probs.1 = (bf16[128,1024]{1,0:T(8,128)(2,1)}, bf16[704,256]{1,0:T(8,128)(2,1)S(1)}, bf16[704,256]{1,0:T(8,128)(2,1)S(1)}, f32[8,192,256]{2,1,0:T(8,128)S...) custom-call(s32[1,20]{1,0:T(1,128)S(1)} %concatenate.7.refs_0_.meta_ref, ...), custom_call_target="tpu_custom_call" | custom-call | flops 2000000000 | bytes 4000000 | tf_op jit(solution)/shard_map/window_probs/pallas_call | solution.py:526
  38.7 3.6 %collective-permute-done.3.refs_6_ = bf16[192,256]{1,0:T(8,128)(2,1)S(1)} collective-permute-done((bf16[192,256]{1,0:T(8,128)(2,1)S(1)}, bf16[192,256]{1,0:T(8,128)(2,1)S(1)}, u32[]{:S(2)}, u32[]{:S(2)}) %collective-permute-start.3) | collective-permute-done | bytes 98336 | tf_op jit(solution)/shard_map/ppermute | solution.py:418
  42.3 0.0 collective-permute-done.4.refs_7_
  42.3 0.3 collective-permute-done.5.refs_8_
  42.6 2.3 %key_value_terms.1 = (f32[512,256]{1,0:T(8,128)S(1)}, bf16[512,256]{1,0:T(8,128)(2,1)S(1)}) custom-call(s32[1,20]{1,0:T(1,128)S(1)} %concatenate.7.refs_0_.meta_ref, bf16[704,256]{1,0:T(8,128)(2,1)S(1)} %get-tuple-element.57.refs_1_, bf16[704,256]{1,0:T(8,128)(2,1)S(1)} %get-tuple-element.58.refs_2_, f32[8,192,256]{2,1,0:T(8,128)S(1)} %get-tuple-element.59.refs_3_, ...), custom_call_target="tpu_custom_call" | custom-call | tf_op jit(solution)/shard_map/key_value_terms/pallas_call | solution.py:548
  44.9 0.1 collective-permute-start.6
  45.0 1.5 %collective-permute-done.6.got_ref = bf16[512,256]{1,0:T(8,128)(2,1)S(1)} collective-permute-done((bf16[512,256]{1,0:T(8,128)(2,1)S(1)}, bf16[512,256]{1,0:T(8,128)(2,1)S(1)}, u32[]{:S(2)}, u32[]{:S(2)}) %collective-permute-start.6) | collective-permute-done | bytes 262176 | tf_op jit(solution)/shard_map/ppermute | solution.py:418
  46.5 0.1 sum_pair.1
  46.5 2.5 %collective-permute-start.7 = (bf16[128,256]{1,0:T(8,128)(2,1)S(1)}, bf16[128,256]{1,0:T(8,128)(2,1)S(1)}, u32[]{:S(2)}, u32[]{:S(2)}) collective-permute-start(bf16[128,256]{1,0:T(8,128)(2,1)S(1)} %get-tuple-element.68), channel_id=1, source_target_pairs={{0,24},{4,28},{8,16},{12,20},{16,8},{20,12},{24,0},{28,4},{1,25},{... | collective-permute-start | bytes 196616 | tf_op jit(solution)/shard_map/ppermute | solution.py:418
  49.0 0.5 collective-permute-start.8
  49.6 0.5 collective-permute-start.9
  50.1 1.7 %collective-permute-done.7.refs_0_ = bf16[128,256]{1,0:T(8,128)(2,1)S(1)} collective-permute-done((bf16[128,256]{1,0:T(8,128)(2,1)S(1)}, bf16[128,256]{1,0:T(8,128)(2,1)S(1)}, u32[]{:S(2)}, u32[]{:S(2)}) %collective-permute-start.7) | collective-permute-done | bytes 65568 | tf_op jit(solution)/shard_map/ppermute | solution.py:418
  51.8 1.5 %collective-permute-done.8.refs_1_ = bf16[128,256]{1,0:T(8,128)(2,1)S(1)} collective-permute-done((bf16[128,256]{1,0:T(8,128)(2,1)S(1)}, bf16[128,256]{1,0:T(8,128)(2,1)S(1)}, u32[]{:S(2)}, u32[]{:S(2)}) %collective-permute-start.8) | collective-permute-done | bytes 65568 | tf_op jit(solution)/shard_map/ppermute | solution.py:418
  53.3 0.5 collective-permute-done.9.refs_2_
  53.8 0.7 %sum_groups.1 = f32[128,256]{1,0:T(8,128)} custom-call(bf16[128,256]{1,0:T(8,128)(2,1)S(1)} %collective-permute-done.7.refs_0_, bf16[128,256]{1,0:T(8,128)(2,1)S(1)} %collective-permute-done.8.refs_1_, bf16[128,256]{1,0:T(8,128)(2,1)S(1)} %collective-permute-done.9.refs_2_, bf16[128,256]{1,0:T(8,128)(2,1)S(1)} %get-tuple-element.71.refs_3_), custom_call_target="tpu_custom_call" | custom-call | tf_op jit(solution)/shard_map/sum_groups/pallas_call | solution.py:581
Async XLA Ops:
  0.6 9.0 %copy-start.2 = (bf16[1024,512]{1,0:T(8,128)(2,1)S(1)}, bf16[1024,512]{1,0:T(8,128)(2,1)}, u32[]{:S(2)}) copy-start(bf16[1024,512]{1,0:T(8,128)(2,1)} %refs_7_.1) | copy-start | bytes 3145732
  0.6 16.3 %collective-permute-start = (bf16[128,1024]{1,0:T(8,128)(2,1)}, bf16[128,1024]{1,0:T(8,128)(2,1)S(1)}, u32[]{:S(2)}, u32[]{:S(2)}) collective-permute-start(bf16[128,1024]{1,0:T(8,128)(2,1)} %refs_9_.1), channel_id=1, source_target_pairs={{0,2},{1,3},{2,0},{3,1},{4,6},{5,7},{6,4},{7,5},{8,10},{9,11},{10,... | collective-permute-start | bytes 786440 | tf_op jit(solution)/shard_map/ppermute | solution.py:418
  4.7 13.8 %collective-permute-start.1 = (bf16[128,1024]{1,0:T(8,128)(2,1)}, bf16[128,1024]{1,0:T(8,128)(2,1)S(1)}, u32[]{:S(2)}, u32[]{:S(2)}) collective-permute-start(bf16[128,1024]{1,0:T(8,128)(2,1)} %refs_9_.1), channel_id=1, source_target_pairs={{0,1},{1,0},{2,3},{3,2},{4,5},{5,4},{6,7},{7,6},{8,9},{9,8},{10,11... | collective-permute-start | bytes 786440 | tf_op jit(solution)/shard_map/ppermute | solution.py:418
  8.1 1.2 %copy-start.3 = (bf16[512,1024]{1,0:T(8,128)(2,1)S(1)}, bf16[512,1024]{1,0:T(8,128)(2,1)}, u32[]{:S(2)}) copy-start(bf16[512,1024]{1,0:T(8,128)(2,1)} %refs_2_.1) | copy-start | bytes 3145732
  9.7 1.6 %copy-start = (bf16[1024,1024]{1,0:T(8,128)(2,1)S(1)}, bf16[1024,1024]{1,0:T(8,128)(2,1)}, u32[]{:S(2)}) copy-start(bf16[1024,1024]{1,0:T(8,128)(2,1)} %refs_8_.1) | copy-start | bytes 6291460
  11.3 0.9 %copy-start.5 = (bf16[128,1024]{1,0:T(8,128)(2,1)S(1)}, bf16[128,1024]{1,0:T(8,128)(2,1)}, u32[]{:S(2)}) copy-start(bf16[128,1024]{1,0:T(8,128)(2,1)} %refs_9_.1) | copy-start | bytes 786436
  12.2 0.7 %copy-start.8 = (f32[1024]{0:T(1024)S(1)}, f32[1024]{0:T(1024)}, u32[]{:S(2)}) copy-start(f32[1024]{0:T(1024)} %param.14) | copy-start | bytes 12292
  12.9 4.8 %copy-start.1 = (bf16[1024,1024]{1,0:T(8,128)(2,1)S(1)}, bf16[1024,1024]{1,0:T(8,128)(2,1)}, u32[]{:S(2)}) copy-start(bf16[1024,1024]{1,0:T(8,128)(2,1)} %refs_8_.1) | copy-start | bytes 6291460
  17.0 7.4 %collective-permute-start.2 = (bf16[128,1024]{1,0:T(8,128)(2,1)S(1)}, bf16[128,1024]{1,0:T(8,128)(2,1)S(1)}, u32[]{:S(2)}, u32[]{:S(2)}) collective-permute-start(bf16[128,1024]{1,0:T(8,128)(2,1)S(1)} %collective-permute-done.x_ref.refs_11_), channel_id=1, source_target_pairs={{0,1},{1,0},{2,3},{3,2},{4,5},{5,4},{6,7},{7,6},{8,9},{9,8},{10,11... | collective-permute-start | bytes 786440 | tf_op jit(solution)/shard_map/ppermute | solution.py:418
  18.5 5.9 %copy-start.4 = (bf16[512,1024]{1,0:T(8,128)(2,1)S(1)}, bf16[512,1024]{1,0:T(8,128)(2,1)}, u32[]{:S(2)}) copy-start(bf16[512,1024]{1,0:T(8,128)(2,1)} %refs_2_.1) | copy-start | bytes 3145732
  18.5 5.9 %copy-start.6 = (bf16[128,1024]{1,0:T(8,128)(2,1)S(1)}, bf16[128,1024]{1,0:T(8,128)(2,1)}, u32[]{:S(2)}) copy-start(bf16[128,1024]{1,0:T(8,128)(2,1)} %refs_9_.1) | copy-start | bytes 786436
  18.5 5.9 %copy-start.7 = (bf16[128,1024]{1,0:T(8,128)(2,1)S(1)}, bf16[128,1024]{1,0:T(8,128)(2,1)}, u32[]{:S(2)}) copy-start(bf16[128,1024]{1,0:T(8,128)(2,1)} %refs_1_.1) | copy-start | bytes 786436
  18.5 5.9 %copy-start.9 = (f32[1024]{0:T(1024)S(1)}, f32[1024]{0:T(1024)}, u32[]{:S(2)}) copy-start(f32[1024]{0:T(1024)} %param.14) | copy-start | bytes 12292
  31.7 10.6 %collective-permute-start.3 = (bf16[192,256]{1,0:T(8,128)(2,1)S(1)}, bf16[192,256]{1,0:T(8,128)(2,1)S(1)}, u32[]{:S(2)}, u32[]{:S(2)}) collective-permute-start(bf16[192,256]{1,0:T(8,128)(2,1)S(1)} %get-tuple-element.62), channel_id=1, source_target_pairs={{0,2},{1,3},{2,0},{3,1},{4,6},{5,7},{6,4},{7,5},{8,10},{9,11},{10,... | collective-permute-start | bytes 294920 | tf_op jit(solution)/shard_map/ppermute | solution.py:418
  34.8 7.5 %collective-permute-start.4 = (bf16[192,256]{1,0:T(8,128)(2,1)S(1)}, bf16[192,256]{1,0:T(8,128)(2,1)S(1)}, u32[]{:S(2)}, u32[]{:S(2)}) collective-permute-start(bf16[192,256]{1,0:T(8,128)(2,1)S(1)} %get-tuple-element.63), channel_id=1, source_target_pairs={{0,3},{1,2},{2,1},{3,0},{4,7},{5,6},{6,5},{7,4},{8,11},{9,10},{10,... | collective-permute-start | bytes 294920 | tf_op jit(solution)/shard_map/ppermute | solution.py:418
  36.1 6.5 %collective-permute-start.5 = (bf16[192,256]{1,0:T(8,128)(2,1)S(1)}, bf16[192,256]{1,0:T(8,128)(2,1)S(1)}, u32[]{:S(2)}, u32[]{:S(2)}) collective-permute-start(bf16[192,256]{1,0:T(8,128)(2,1)S(1)} %get-tuple-element.64), channel_id=1, source_target_pairs={{0,1},{1,0},{2,3},{3,2},{4,5},{5,4},{6,7},{7,6},{8,9},{9,8},{10,11... | collective-permute-start | bytes 294920 | tf_op jit(solution)/shard_map/ppermute | solution.py:418
  44.9 1.6 %collective-permute-start.6 = (bf16[512,256]{1,0:T(8,128)(2,1)S(1)}, bf16[512,256]{1,0:T(8,128)(2,1)S(1)}, u32[]{:S(2)}, u32[]{:S(2)}) collective-permute-start(bf16[512,256]{1,0:T(8,128)(2,1)S(1)} %get-tuple-element.67), channel_id=1, source_target_pairs={{0,4},{4,0},{8,12},{12,8},{16,20},{20,16},{24,28},{28,24},{1,5},{5... | collective-permute-start | bytes 786440 | tf_op jit(solution)/shard_map/ppermute | solution.py:418
  46.5 5.3 %collective-permute-start.7 = (bf16[128,256]{1,0:T(8,128)(2,1)S(1)}, bf16[128,256]{1,0:T(8,128)(2,1)S(1)}, u32[]{:S(2)}, u32[]{:S(2)}) collective-permute-start(bf16[128,256]{1,0:T(8,128)(2,1)S(1)} %get-tuple-element.68), channel_id=1, source_target_pairs={{0,24},{4,28},{8,16},{12,20},{16,8},{20,12},{24,0},{28,4},{1,25},{... | collective-permute-start | bytes 196616 | tf_op jit(solution)/shard_map/ppermute | solution.py:418
  49.0 4.3 %collective-permute-start.8 = (bf16[128,256]{1,0:T(8,128)(2,1)S(1)}, bf16[128,256]{1,0:T(8,128)(2,1)S(1)}, u32[]{:S(2)}, u32[]{:S(2)}) collective-permute-start(bf16[128,256]{1,0:T(8,128)(2,1)S(1)} %get-tuple-element.69), channel_id=1, source_target_pairs={{0,16},{4,20},{8,24},{12,28},{16,0},{20,4},{24,8},{28,12},{1,17},{... | collective-permute-start | bytes 196616 | tf_op jit(solution)/shard_map/ppermute | solution.py:418
  49.6 4.3 %collective-permute-start.9 = (bf16[128,256]{1,0:T(8,128)(2,1)S(1)}, bf16[128,256]{1,0:T(8,128)(2,1)S(1)}, u32[]{:S(2)}, u32[]{:S(2)}) collective-permute-start(bf16[128,256]{1,0:T(8,128)(2,1)S(1)} %get-tuple-element.70), channel_id=1, source_target_pairs={{0,8},{4,12},{8,0},{12,4},{16,24},{20,28},{24,16},{28,20},{1,9},{5... | collective-permute-start | bytes 196616 | tf_op jit(solution)/shard_map/ppermute | solution.py:418

commit v13 on v12

--- a/solution.py
+++ b/solution.py
@@ -185,86 +185,78 @@
 
     own = [table.block_of(me * local + i) for i in range(local)]
     keep = [jnp.where(table.position(c) >= 1, 1.0, 0.0).astype(F32) for c in own]
-    for i, c in enumerate(own):
-        for blk, shift, count, put in ((c - 1, HALO, HALO, 0), (c, 0, BLOCK, HALO)):
-            reach = table.reach(blk)
-            win = row_at(blk - LC, SPAN)
-            at = row_at(blk, count, shift)
-            if count == BLOCK:
-                groups, mask_f, mask_b = HEADS // mid_heads, mid_f, mid_b
-            else:
-                groups, mask_f, mask_b = 1, side_f, side_b
-            wide = hq // groups
-            for g in range(groups):
-                cols = slice(g * wide, (g + 1) * wide)
-                vcols = slice(hq + g * wide, hq + (g + 1) * wide)
-                probs, _ = window_probs(spread(q_ref[at, cols], mask_b), kv_ref[win, cols], reach)
-                full = dot_tn(probs.astype(BF16), kv_ref[win, vcols])
-                ctx_s[i * ROWS + put : i * ROWS + put + count, cols] = fold_heads(
-                    full, mask_f, count
-                ).astype(BF16)
+
+    def attend(i, unit):
+        blk, shift, count, put = ((own[i] - 1, HALO, HALO, 0), (own[i], 0, BLOCK, HALO))[unit > 0]
+        mask_f, mask_b = (mid_f, mid_b) if unit else (side_f, side_b)
+        wide = mid_heads * head_size if unit else hq
+        first = max(unit - 1, 0) * wide
+        cols = slice(first, first + wide)
+        win = row_at(blk - LC, SPAN)
+        diag_q = spread(q_ref[row_at(blk, count, shift), cols], mask_b)
+        probs, _ = window_probs(diag_q, kv_ref[win, cols], table.reach(blk))
+        full = dot_tn(probs.astype(BF16), kv_ref[win, hq + first : hq + first + wide])
+        rows = slice(i * ROWS + put, i * ROWS + put + count)
+        ctx_s[rows, cols] = fold_heads(full, mask_f, count).astype(BF16)
 
     gain = small_ref[KERNEL + 1 : KERNEL + 2]
-    product = dot_nn(ctx_s[...], wo_ref[...])
-    scales = []
-    for i, c in enumerate(own):
+    scales = {}
+
+    def settle(i):
         here = slice(i * ROWS, (i + 1) * ROWS)
-        tail = tail_s[pl.ds(pl.multiple_of(c * HALO, HALO), HALO)]
+        tail = tail_s[pl.ds(pl.multiple_of(own[i] * HALO, HALO), HALO)]
         rows = jnp.concatenate([tail, x_refs[0][i * BLOCK : (i + 1) * BLOCK]], axis=0)
-        hidden = rows.astype(F32) + product[here]
+        hidden = rows.astype(F32) + dot_nn(ctx_s[here], wo_ref[...])
         unit, inv = norm_stats(hidden)
         conv_in = (unit * gain).astype(BF16).astype(F32)
         e_s[i * ROWS : i * ROWS + HALO] = conv_in[:HALO] * keep[i]
         e_s[i * ROWS + HALO : (i + 1) * ROWS] = conv_in[HALO:]
         h_s[i * BLOCK : (i + 1) * BLOCK] = hidden[HALO:]
         u_s[here] = unit
-        scales.append(inv)
+        scales[i] = inv
 
     groups = BLOCK // SUB
 
-    def conv(cols):
+    def conv(i, k):
+        cols = slice(k * LANES, (k + 1) * LANES)
         bias = jnp.broadcast_to(small_ref[KERNEL : KERNEL + 1, cols], (SUB, LANES))
         taps = lambda j: taps_ref[j * SUB : (j + 1) * SUB, cols]
-        for i in range(local):
-            ext = e_s[i * ROWS : (i + 1) * ROWS, cols]
-            acc = [bias] * groups
-            for s in range(SUB):
-                reps = (KERNEL - s + SUB - 1) // SUB
-                skip, shift = divmod(s + KERNEL_GAP, SUB)
-                moved = shifted_up(ext, shift)
-                for a in range(reps):
-                    tap = taps(SUB * a + s)
-                    for r in range(groups):
-                        at = (a + r + skip) * SUB
-                        acc[r] = acc[r] + tap * moved[at : at + SUB]
-            mixed = jnp.concatenate(acc, axis=0)
-            gate = 0.5 * jnp.tanh(0.5 * mixed) + 0.5
-            rows = slice(i * BLOCK, (i + 1) * BLOCK)
-            out_ref[rows, cols] = (h_s[rows, cols] + mixed * gate).astype(BF16)
-            slope = gate * (1.0 + mixed * (1.0 - gate))
-            gm = grad_ref[rows, cols].astype(F32) * slope
-            zeros = jnp.zeros((HALO, LANES), F32)
-            padded = jnp.concatenate([zeros[:SUB], gm, zeros[:SUB]], axis=0)
-            back = [None] * (ROWS // SUB)
-            low = HALO // SUB - 1
-            for s in range(SUB):
-                reps = (KERNEL - s + SUB - 1) // SUB
-                start = low if s else low + 1
-                moved = shifted_up(padded, s)
-                for a in range(reps):
-                    tap = taps(KERNEL - 1 - SUB * a - s)
-                    for g in range(start, ROWS // SUB):
-                        r = g - a
-                        piece = tap * moved[(g - low) * SUB : (g - low + 1) * SUB]
-                        back[r] = piece if back[r] is None else back[r] + piece
-            for r in range(ROWS // SUB):
-                scale = keep[i] if r < HALO // SUB else 1.0
-                gr_s[i * ROWS + r * SUB : i * ROWS + (r + 1) * SUB, cols] = back[r] * scale
-
-    for k in range(0, width, LANES):
-        conv(slice(k, k + LANES))
-
-    for i in range(local):
+        ext = e_s[i * ROWS : (i + 1) * ROWS, cols]
+        acc = [bias] * groups
+        for s in range(SUB):
+            reps = (KERNEL - s + SUB - 1) // SUB
+            skip, shift = divmod(s + KERNEL_GAP, SUB)
+            moved = shifted_up(ext, shift)
+            for a in range(reps):
+                tap = taps(SUB * a + s)
+                for r in range(groups):
+                    at = (a + r + skip) * SUB
+                    acc[r] = acc[r] + tap * moved[at : at + SUB]
+        mixed = jnp.concatenate(acc, axis=0)
+        gate = 0.5 * jnp.tanh(0.5 * mixed) + 0.5
+        rows = slice(i * BLOCK, (i + 1) * BLOCK)
+        out_ref[rows, cols] = (h_s[rows, cols] + mixed * gate).astype(BF16)
+        slope = gate * (1.0 + mixed * (1.0 - gate))
+        gm = grad_ref[rows, cols].astype(F32) * slope
+        zeros = jnp.zeros((HALO, LANES), F32)
+        padded = jnp.concatenate([zeros[:SUB], gm, zeros[:SUB]], axis=0)
+        back = [None] * (ROWS // SUB)
+        low = HALO // SUB - 1
+        for s in range(SUB):
+            reps = (KERNEL - s + SUB - 1) // SUB
+            start = low if s else low + 1
+            moved = shifted_up(padded, s)
+            for a in range(reps):
+                tap = taps(KERNEL - 1 - SUB * a - s)
+                for g in range(start, ROWS // SUB):
+                    r = g - a
+                    piece = tap * moved[(g - low) * SUB : (g - low + 1) * SUB]
+                    back[r] = piece if back[r] is None else back[r] + piece
+        for r in range(ROWS // SUB):
+            scale = keep[i] if r < HALO // SUB else 1.0
+            gr_s[i * ROWS + r * SUB : i * ROWS + (r + 1) * SUB, cols] = back[r] * scale
+
+    def finish(i):
         here = slice(i * ROWS, (i + 1) * ROWS)
         scaled = gr_s[here] * gain
         unit = u_s[here]
@@ -274,11 +266,32 @@
         own_grad = grad_ref[i * BLOCK : (i + 1) * BLOCK].astype(F32) + back[HALO:]
         gc_s[i * ROWS : i * ROWS + HALO] = back[:HALO].astype(BF16)
         gc_s[i * ROWS + HALO : (i + 1) * ROWS] = own_grad.astype(BF16)
-    for m in range(half):
-        at = pl.ds(pl.multiple_of(((me ^ m) % half) * share, share), share)
-        grad_context = dot_nn(gc_s[...], wot_ref[:, at]).astype(BF16)
-        send_refs[m][...] = grad_context
-        send_refs[m + half][...] = grad_context
+        for m in range(half):
+            at = pl.ds(pl.multiple_of(((me ^ m) % half) * share, share), share)
+            grad_context = dot_nn(gc_s[here], wot_ref[:, at]).astype(BF16)
+            send_refs[m][here] = grad_context
+            send_refs[m + half][here] = grad_context
+
+    units = 1 + HEADS // mid_heads
+    chunks = width // LANES
+    for unit in range(units):
+        attend(0, unit)
+    settle(0)
+    for i in range(local):
+        done = 0
+        steps = units if i + 1 < local else 1
+        for unit in range(steps):
+            if i + 1 < local:
+                attend(i + 1, unit)
+            upto = chunks * (unit + 1) // steps
+            for k in range(done, upto):
+                conv(i, k)
+                if i > 0 and k == chunks // 2:
+                    finish(i - 1)
+            done = upto
+        if i + 1 < local:
+            settle(i + 1)
+    finish(local - 1)
 
 
 def probs_kernel(sizes, tm, head_size, meta_ref, *refs):

time: 54.8 us -> 55.7 us (1.016)
  Pallas kernels: 15.1 us -> 16 us
    pallas_call x1, Pallas kernels: 7.24 us -> 8.17 us  [on_device(): pl.pallas_call(functools.partial(forward_kernel, sizes, tm, head_size), o...]
where the time goes in v13:
time: 55.7 us; the launch traced here: 55.4 us
  waiting for transfers between devices  17.6 us (32%)
  Pallas kernels  16 us (29%)
  starting transfers between devices  14.9 us (27%)
  local copies, waits for them, and re-layouts  5.25 us (9%)
  other arithmetic  0.96 us (2%)
  between operations  0.79 us (1%)
    ppermute x10, waiting for transfers between devices, swap(): return lax.ppermute(value, axis, [(i, i ^ m) for i in range(size)])  17.6 us
    ppermute x10, starting transfers between devices, swap(): return lax.ppermute(value, axis, [(i, i ^ m) for i in range(size)])  14.9 us
    pallas_call x1, Pallas kernels, on_device(): pl.pallas_call(functools.partial(forward_kernel, sizes, tm, head_size), o...  8.17 us
    unnamed x20, local copies, waits for them, and re-layouts  4.48 us
    pallas_call x1, Pallas kernels, on_device(): pl.pallas_call(functools.partial(backward_kernel, sizes, tm, width // dp,...  2.3 us
    pallas_call x3, Pallas kernels, project_shard(): pl.pallas_call(project_kernel, out_shape=made, in_specs=[vmem] * 4, out_s...  2.28 us
    pallas_call x1, Pallas kernels, on_device(): pl.pallas_call(functools.partial(probs_kernel, sizes, tm, head_size), out...  2.15 us
  transfers between devices with their start and end apart: 10, of which 8 were waited for; matrix products, arithmetic and copies ran while one was open for 3% of the time, Pallas kernels for 9%

profile of v13, /device:TPU:0, one launch (start us, length us, event | category | flops | bytes accessed | tf_op | source)
XLA Modules:
  0.0 55.4 jit_solution(4518615657266268602)
XLA Ops:
  0.6 0.0 copy-start.2
  0.6 4.1 %collective-permute-start = (bf16[128,1024]{1,0:T(8,128)(2,1)}, bf16[128,1024]{1,0:T(8,128)(2,1)S(1)}, u32[]{:S(2)}, u32[]{:S(2)}) collective-permute-start(bf16[128,1024]{1,0:T(8,128)(2,1)} %refs_9_.1), channel_id=1, source_target_pairs={{0,2},{1,3},{2,0},{3,1},{4,6},{5,7},{6,4},{7,5},{8,10},{9,11},{10,... | collective-permute-start | bytes 786440 | tf_op jit(solution)/shard_map/ppermute | solution.py:431
  4.7 1.6 %collective-permute-start.1 = (bf16[128,1024]{1,0:T(8,128)(2,1)}, bf16[128,1024]{1,0:T(8,128)(2,1)S(1)}, u32[]{:S(2)}, u32[]{:S(2)}) collective-permute-start(bf16[128,1024]{1,0:T(8,128)(2,1)} %refs_9_.1), channel_id=1, source_target_pairs={{0,1},{1,0},{2,3},{3,2},{4,5},{5,4},{6,7},{7,6},{8,9},{9,8},{10,11... | collective-permute-start | bytes 786440 | tf_op jit(solution)/shard_map/ppermute | solution.py:431
  6.3 0.8 %concatenate.7.refs_0_.meta_ref = s32[1,20]{1,0:T(1,128)S(1)} concatenate(s32[1,1]{1,0:T(1,128)} %bitcast.3, s32[1,1]{1,0:T(1,128)} %bitcast.4, s32[1,2]{1,0:T(1,128)} %param.21, s32[1,8]{1,0:T(1,128)} %param.22, s32[1,8]{1,0:T(1,128)} %param.23), dimensions={1} | concatenate | bytes 160 | tf_op jit(solution)/shard_map/concatenate | solution.py:433
  7.1 1.0 %pad_maximum_fusion.small_ref.refs_4_ = f32[33,1024]{1,0:T(8,128)S(1)} fusion(f32[1,1024]{1,0:T(1,128)} %bitcast.9, f32[1,1024]{1,0:T(1,128)} %bitcast.10, f32[31,1024]{1,0:T(8,128)} %param.19), kind=kLoop, calls=%fused_computation | loop fusion | flops 67584 | bytes 270336 | tf_op jit(solution)/shard_map/concatenate | solution.py:443
  8.1 0.0 copy-start.3
  8.1 1.2 %copy-done.3 = bf16[512,1024]{1,0:T(8,128)(2,1)S(1)} copy-done((bf16[512,1024]{1,0:T(8,128)(2,1)S(1)}, bf16[512,1024]{1,0:T(8,128)(2,1)}, u32[]{:S(2)}) %copy-start.3) | copy-done | bytes 1048600
  9.3 0.4 spread_taps.1
  9.6 0.0 copy-done.2
  9.7 0.0 copy-start
  9.7 1.6 %copy-done = bf16[1024,1024]{1,0:T(8,128)(2,1)S(1)} copy-done((bf16[1024,1024]{1,0:T(8,128)(2,1)S(1)}, bf16[1024,1024]{1,0:T(8,128)(2,1)}, u32[]{:S(2)}) %copy-start) | copy-done | bytes 2097176
  11.3 0.0 copy-start.5
  11.3 0.9 %copy-done.5 = bf16[128,1024]{1,0:T(8,128)(2,1)S(1)} copy-done((bf16[128,1024]{1,0:T(8,128)(2,1)S(1)}, bf16[128,1024]{1,0:T(8,128)(2,1)}, u32[]{:S(2)}) %copy-start.5) | copy-done | bytes 262168
  12.2 0.0 copy-start.8
  12.2 0.7 %copy-done.8 = f32[1024]{0:T(1024)S(1)} copy-done((f32[1024]{0:T(1024)S(1)}, f32[1024]{0:T(1024)}, u32[]{:S(2)}) %copy-start.8) | copy-done | bytes 4120
  12.9 0.0 copy-start.1
  12.9 0.8 %project_rows_0.1 = (bf16[128,1024]{1,0:T(8,128)(2,1)S(1)}, bf16[128,512]{1,0:T(8,128)(2,1)S(1)}, bf16[128,1024]{1,0:T(8,128)(2,1)S(1)}) custom-call(bf16[128,1024]{1,0:T(8,128)(2,1)S(1)} %copy-done.5, f32[1,1024]{1,0:T(1,128)S(1)} %bitcast.5, bf16[1024,512]{1,0:T(8,128)(2,1)S(1)} %copy-done.2, bf16[1024,1024]{1,0:T(8,128)(2,1)S(1)} %copy-done), custom_call_target="tpu_custom_call" | custom-call | flops 402653184 | bytes 4194304 | tf_op jit(solution)/shard_map/project_rows_0/pallas_call | solution.py:465
  13.7 3.3 %collective-permute-done.x_ref.refs_11_ = bf16[128,1024]{1,0:T(8,128)(2,1)S(1)} collective-permute-done((bf16[128,1024]{1,0:T(8,128)(2,1)}, bf16[128,1024]{1,0:T(8,128)(2,1)S(1)}, u32[]{:S(2)}, u32[]{:S(2)}) %collective-permute-start) | collective-permute-done | bytes 262176 | tf_op jit(solution)/shard_map/ppermute | solution.py:431
  17.0 0.7 %collective-permute-start.2 = (bf16[128,1024]{1,0:T(8,128)(2,1)S(1)}, bf16[128,1024]{1,0:T(8,128)(2,1)S(1)}, u32[]{:S(2)}, u32[]{:S(2)}) collective-permute-start(bf16[128,1024]{1,0:T(8,128)(2,1)S(1)} %collective-permute-done.x_ref.refs_11_), channel_id=1, source_target_pairs={{0,1},{1,0},{2,3},{3,2},{4,5},{5,4},{6,7},{7,6},{8,9},{9,8},{10,11... | collective-permute-start | bytes 786440 | tf_op jit(solution)/shard_map/ppermute | solution.py:431
  17.7 0.0 copy-done.1
  17.7 0.8 %project_rows_2.1 = (bf16[128,1024]{1,0:T(8,128)(2,1)S(1)}, bf16[128,512]{1,0:T(8,128)(2,1)S(1)}, bf16[128,1024]{1,0:T(8,128)(2,1)S(1)}) custom-call(bf16[128,1024]{1,0:T(8,128)(2,1)S(1)} %collective-permute-done.x_ref.refs_11_, f32[1,1024]{1,0:T(1,128)S(1)} %bitcast.6, bf16[1024,512]{1,0:T(8,128)(2,1)S(1)} %copy-done.2, bf16[1024,1024]{1,0:T(8,128)(2,1)S(1)} %copy-done.1), custom_call_target="tpu_custom_call" | custom-call | flops 402653184 | bytes 4194304 | tf_op jit(solution)/shard_map/project_rows_2/pallas_call | solution.py:465
  18.5 0.0 copy-start.4
  18.5 0.0 copy-start.6
  18.5 0.0 copy-start.7
  18.5 0.0 copy-start.9
  18.5 0.0 collective-permute-done.1.x_ref.refs_10_
  18.5 0.8 %project_rows_1.1 = (bf16[128,1024]{1,0:T(8,128)(2,1)S(1)}, bf16[128,512]{1,0:T(8,128)(2,1)S(1)}, bf16[128,1024]{1,0:T(8,128)(2,1)S(1)}) custom-call(bf16[128,1024]{1,0:T(8,128)(2,1)S(1)} %collective-permute-done.1.x_ref.refs_10_, f32[1,1024]{1,0:T(1,128)S(1)} %bitcast.7, bf16[1024,512]{1,0:T(8,128)(2,1)S(1)} %copy-done.2, bf16[1024,1024]{1,0:T(8,128)(2,1)S(1)} %copy-done.1), custom_call_target="tpu_custom_call" | custom-call | flops 402653184 | bytes 4194304 | tf_op jit(solution)/shard_map/project_rows_1/pallas_call | solution.py:465
  19.3 5.1 %collective-permute-done.2.refs_12_ = bf16[128,1024]{1,0:T(8,128)(2,1)S(1)} collective-permute-done((bf16[128,1024]{1,0:T(8,128)(2,1)S(1)}, bf16[128,1024]{1,0:T(8,128)(2,1)S(1)}, u32[]{:S(2)}, u32[]{:S(2)}) %collective-permute-start.2) | collective-permute-done | bytes 262176 | tf_op jit(solution)/shard_map/ppermute | solution.py:431
  24.4 0.0 copy-done.4
  24.4 0.0 copy-done.6
  24.4 0.0 copy-done.7
  24.4 0.0 copy-done.9
  24.4 8.2 %forward_pass.1 = (bf16[128,1024]{1,0:T(8,128)(2,1)S(1)}, bf16[128,1024]{1,0:T(8,128)(2,1)S(1)}, bf16[128,512]{1,0:T(8,128)(2,1)S(1)}, bf16[128,1024]{1,0:T(8,12...) custom-call(s32[1,20]{1,0:T(1,128)S(1)} %concatenate.7.refs_0_.meta_, ...), custom_call_target="tpu_custom_call" | custom-call | tf_op jit(solution)/shard_map/forward_pass/pallas_call | solution.py:496
  32.6 3.1 %collective-permute-start.3 = (bf16[192,256]{1,0:T(8,128)(2,1)S(1)}, bf16[192,256]{1,0:T(8,128)(2,1)S(1)}, u32[]{:S(2)}, u32[]{:S(2)}) collective-permute-start(bf16[192,256]{1,0:T(8,128)(2,1)S(1)} %get-tuple-element.62), channel_id=1, source_target_pairs={{0,2},{1,3},{2,0},{3,1},{4,6},{5,7},{6,4},{7,5},{8,10},{9,11},{10,... | collective-permute-start | bytes 294920 | tf_op jit(solution)/shard_map/ppermute | solution.py:431
  35.7 1.3 %collective-permute-start.4 = (bf16[192,256]{1,0:T(8,128)(2,1)S(1)}, bf16[192,256]{1,0:T(8,128)(2,1)S(1)}, u32[]{:S(2)}, u32[]{:S(2)}) collective-permute-start(bf16[192,256]{1,0:T(8,128)(2,1)S(1)} %get-tuple-element.63), channel_id=1, source_target_pairs={{0,3},{1,2},{2,1},{3,0},{4,7},{5,6},{6,5},{7,4},{8,11},{9,10},{10,... | collective-permute-start | bytes 294920 | tf_op jit(solution)/shard_map/ppermute | solution.py:431
  37.0 0.5 collective-permute-start.5
  37.5 2.2 %window_probs.1 = (bf16[128,1024]{1,0:T(8,128)(2,1)}, bf16[704,256]{1,0:T(8,128)(2,1)S(1)}, bf16[704,256]{1,0:T(8,128)(2,1)S(1)}, f32[8,192,256]{2,1,0:T(8,128)S...) custom-call(s32[1,20]{1,0:T(1,128)S(1)} %concatenate.7.refs_0_.meta_ref, ...), custom_call_target="tpu_custom_call" | custom-call | flops 2000000000 | bytes 4000000 | tf_op jit(solution)/shard_map/window_probs/pallas_call | solution.py:539
  39.6 3.6 %collective-permute-done.3.refs_6_ = bf16[192,256]{1,0:T(8,128)(2,1)S(1)} collective-permute-done((bf16[192,256]{1,0:T(8,128)(2,1)S(1)}, bf16[192,256]{1,0:T(8,128)(2,1)S(1)}, u32[]{:S(2)}, u32[]{:S(2)}) %collective-permute-start.3) | collective-permute-done | bytes 98336 | tf_op jit(solution)/shard_map/ppermute | solution.py:431
  43.2 0.0 collective-permute-done.4.refs_7_
  43.2 0.3 collective-permute-done.5.refs_8_
  43.5 2.3 %key_value_terms.1 = (f32[512,256]{1,0:T(8,128)S(1)}, bf16[512,256]{1,0:T(8,128)(2,1)S(1)}) custom-call(s32[1,20]{1,0:T(1,128)S(1)} %concatenate.7.refs_0_.meta_ref, bf16[704,256]{1,0:T(8,128)(2,1)S(1)} %get-tuple-element.57.refs_1_, bf16[704,256]{1,0:T(8,128)(2,1)S(1)} %get-tuple-element.58.refs_2_, f32[8,192,256]{2,1,0:T(8,128)S(1)} %get-tuple-element.59.refs_3_, ...), custom_call_target="tpu_custom_call" | custom-call | tf_op jit(solution)/shard_map/key_value_terms/pallas_call | solution.py:561
  45.8 0.1 collective-permute-start.6
  45.9 1.5 %collective-permute-done.6.got_ref = bf16[512,256]{1,0:T(8,128)(2,1)S(1)} collective-permute-done((bf16[512,256]{1,0:T(8,128)(2,1)S(1)}, bf16[512,256]{1,0:T(8,128)(2,1)S(1)}, u32[]{:S(2)}, u32[]{:S(2)}) %collective-permute-start.6) | collective-permute-done | bytes 262176 | tf_op jit(solution)/shard_map/ppermute | solution.py:431
  47.4 0.1 sum_pair.1
  47.5 2.5 %collective-permute-start.7 = (bf16[128,256]{1,0:T(8,128)(2,1)S(1)}, bf16[128,256]{1,0:T(8,128)(2,1)S(1)}, u32[]{:S(2)}, u32[]{:S(2)}) collective-permute-start(bf16[128,256]{1,0:T(8,128)(2,1)S(1)} %get-tuple-element.68), channel_id=1, source_target_pairs={{0,24},{4,28},{8,16},{12,20},{16,8},{20,12},{24,0},{28,4},{1,25},{... | collective-permute-start | bytes 196616 | tf_op jit(solution)/shard_map/ppermute | solution.py:431
  50.0 0.5 collective-permute-start.8
  50.5 0.5 collective-permute-start.9
  51.0 1.7 %collective-permute-done.7.refs_0_ = bf16[128,256]{1,0:T(8,128)(2,1)S(1)} collective-permute-done((bf16[128,256]{1,0:T(8,128)(2,1)S(1)}, bf16[128,256]{1,0:T(8,128)(2,1)S(1)}, u32[]{:S(2)}, u32[]{:S(2)}) %collective-permute-start.7) | collective-permute-done | bytes 65568 | tf_op jit(solution)/shard_map/ppermute | solution.py:431
  52.7 1.5 %collective-permute-done.8.refs_1_ = bf16[128,256]{1,0:T(8,128)(2,1)S(1)} collective-permute-done((bf16[128,256]{1,0:T(8,128)(2,1)S(1)}, bf16[128,256]{1,0:T(8,128)(2,1)S(1)}, u32[]{:S(2)}, u32[]{:S(2)}) %collective-permute-start.8) | collective-permute-done | bytes 65568 | tf_op jit(solution)/shard_map/ppermute | solution.py:431
  54.2 0.5 collective-permute-done.9.refs_2_
  54.8 0.7 %sum_groups.1 = f32[128,256]{1,0:T(8,128)} custom-call(bf16[128,256]{1,0:T(8,128)(2,1)S(1)} %collective-permute-done.7.refs_0_, bf16[128,256]{1,0:T(8,128)(2,1)S(1)} %collective-permute-done.8.refs_1_, bf16[128,256]{1,0:T(8,128)(2,1)S(1)} %collective-permute-done.9.refs_2_, bf16[128,256]{1,0:T(8,128)(2,1)S(1)} %get-tuple-element.71.refs_3_), custom_call_target="tpu_custom_call" | custom-call | tf_op jit(solution)/shard_map/sum_groups/pallas_call | solution.py:594
Async XLA Ops:
  0.6 9.0 %copy-start.2 = (bf16[1024,512]{1,0:T(8,128)(2,1)S(1)}, bf16[1024,512]{1,0:T(8,128)(2,1)}, u32[]{:S(2)}) copy-start(bf16[1024,512]{1,0:T(8,128)(2,1)} %refs_7_.1) | copy-start | bytes 3145732
  0.6 16.3 %collective-permute-start = (bf16[128,1024]{1,0:T(8,128)(2,1)}, bf16[128,1024]{1,0:T(8,128)(2,1)S(1)}, u32[]{:S(2)}, u32[]{:S(2)}) collective-permute-start(bf16[128,1024]{1,0:T(8,128)(2,1)} %refs_9_.1), channel_id=1, source_target_pairs={{0,2},{1,3},{2,0},{3,1},{4,6},{5,7},{6,4},{7,5},{8,10},{9,11},{10,... | collective-permute-start | bytes 786440 | tf_op jit(solution)/shard_map/ppermute | solution.py:431
  4.7 13.8 %collective-permute-start.1 = (bf16[128,1024]{1,0:T(8,128)(2,1)}, bf16[128,1024]{1,0:T(8,128)(2,1)S(1)}, u32[]{:S(2)}, u32[]{:S(2)}) collective-permute-start(bf16[128,1024]{1,0:T(8,128)(2,1)} %refs_9_.1), channel_id=1, source_target_pairs={{0,1},{1,0},{2,3},{3,2},{4,5},{5,4},{6,7},{7,6},{8,9},{9,8},{10,11... | collective-permute-start | bytes 786440 | tf_op jit(solution)/shard_map/ppermute | solution.py:431
  8.1 1.2 %copy-start.3 = (bf16[512,1024]{1,0:T(8,128)(2,1)S(1)}, bf16[512,1024]{1,0:T(8,128)(2,1)}, u32[]{:S(2)}) copy-start(bf16[512,1024]{1,0:T(8,128)(2,1)} %refs_2_.1) | copy-start | bytes 3145732
  9.7 1.6 %copy-start = (bf16[1024,1024]{1,0:T(8,128)(2,1)S(1)}, bf16[1024,1024]{1,0:T(8,128)(2,1)}, u32[]{:S(2)}) copy-start(bf16[1024,1024]{1,0:T(8,128)(2,1)} %refs_8_.1) | copy-start | bytes 6291460
  11.3 0.9 %copy-start.5 = (bf16[128,1024]{1,0:T(8,128)(2,1)S(1)}, bf16[128,1024]{1,0:T(8,128)(2,1)}, u32[]{:S(2)}) copy-start(bf16[128,1024]{1,0:T(8,128)(2,1)} %refs_9_.1) | copy-start | bytes 786436
  12.2 0.7 %copy-start.8 = (f32[1024]{0:T(1024)S(1)}, f32[1024]{0:T(1024)}, u32[]{:S(2)}) copy-start(f32[1024]{0:T(1024)} %param.14) | copy-start | bytes 12292
  12.9 4.8 %copy-start.1 = (bf16[1024,1024]{1,0:T(8,128)(2,1)S(1)}, bf16[1024,1024]{1,0:T(8,128)(2,1)}, u32[]{:S(2)}) copy-start(bf16[1024,1024]{1,0:T(8,128)(2,1)} %refs_8_.1) | copy-start | bytes 6291460
  17.0 7.4 %collective-permute-start.2 = (bf16[128,1024]{1,0:T(8,128)(2,1)S(1)}, bf16[128,1024]{1,0:T(8,128)(2,1)S(1)}, u32[]{:S(2)}, u32[]{:S(2)}) collective-permute-start(bf16[128,1024]{1,0:T(8,128)(2,1)S(1)} %collective-permute-done.x_ref.refs_11_), channel_id=1, source_target_pairs={{0,1},{1,0},{2,3},{3,2},{4,5},{5,4},{6,7},{7,6},{8,9},{9,8},{10,11... | collective-permute-start | bytes 786440 | tf_op jit(solution)/shard_map/ppermute | solution.py:431
  18.5 5.9 %copy-start.4 = (bf16[512,1024]{1,0:T(8,128)(2,1)S(1)}, bf16[512,1024]{1,0:T(8,128)(2,1)}, u32[]{:S(2)}) copy-start(bf16[512,1024]{1,0:T(8,128)(2,1)} %refs_2_.1) | copy-start | bytes 3145732
  18.5 5.9 %copy-start.6 = (bf16[128,1024]{1,0:T(8,128)(2,1)S(1)}, bf16[128,1024]{1,0:T(8,128)(2,1)}, u32[]{:S(2)}) copy-start(bf16[128,1024]{1,0:T(8,128)(2,1)} %refs_9_.1) | copy-start | bytes 786436
  18.5 5.9 %copy-start.7 = (bf16[128,1024]{1,0:T(8,128)(2,1)S(1)}, bf16[128,1024]{1,0:T(8,128)(2,1)}, u32[]{:S(2)}) copy-start(bf16[128,1024]{1,0:T(8,128)(2,1)} %refs_1_.1) | copy-start | bytes 786436
  18.5 5.9 %copy-start.9 = (f32[1024]{0:T(1024)S(1)}, f32[1024]{0:T(1024)}, u32[]{:S(2)}) copy-start(f32[1024]{0:T(1024)} %param.14) | copy-start | bytes 12292
  32.6 10.6 %collective-permute-start.3 = (bf16[192,256]{1,0:T(8,128)(2,1)S(1)}, bf16[192,256]{1,0:T(8,128)(2,1)S(1)}, u32[]{:S(2)}, u32[]{:S(2)}) collective-permute-start(bf16[192,256]{1,0:T(8,128)(2,1)S(1)} %get-tuple-element.62), channel_id=1, source_target_pairs={{0,2},{1,3},{2,0},{3,1},{4,6},{5,7},{6,4},{7,5},{8,10},{9,11},{10,... | collective-permute-start | bytes 294920 | tf_op jit(solution)/shard_map/ppermute | solution.py:431
  35.7 7.5 %collective-permute-start.4 = (bf16[192,256]{1,0:T(8,128)(2,1)S(1)}, bf16[192,256]{1,0:T(8,128)(2,1)S(1)}, u32[]{:S(2)}, u32[]{:S(2)}) collective-permute-start(bf16[192,256]{1,0:T(8,128)(2,1)S(1)} %get-tuple-element.63), channel_id=1, source_target_pairs={{0,3},{1,2},{2,1},{3,0},{4,7},{5,6},{6,5},{7,4},{8,11},{9,10},{10,... | collective-permute-start | bytes 294920 | tf_op jit(solution)/shard_map/ppermute | solution.py:431
  37.0 6.5 %collective-permute-start.5 = (bf16[192,256]{1,0:T(8,128)(2,1)S(1)}, bf16[192,256]{1,0:T(8,128)(2,1)S(1)}, u32[]{:S(2)}, u32[]{:S(2)}) collective-permute-start(bf16[192,256]{1,0:T(8,128)(2,1)S(1)} %get-tuple-element.64), channel_id=1, source_target_pairs={{0,1},{1,0},{2,3},{3,2},{4,5},{5,4},{6,7},{7,6},{8,9},{9,8},{10,11... | collective-permute-start | bytes 294920 | tf_op jit(solution)/shard_map/ppermute | solution.py:431
  45.8 1.6 %collective-permute-start.6 = (bf16[512,256]{1,0:T(8,128)(2,1)S(1)}, bf16[512,256]{1,0:T(8,128)(2,1)S(1)}, u32[]{:S(2)}, u32[]{:S(2)}) collective-permute-start(bf16[512,256]{1,0:T(8,128)(2,1)S(1)} %get-tuple-element.67), channel_id=1, source_target_pairs={{0,4},{4,0},{8,12},{12,8},{16,20},{20,16},{24,28},{28,24},{1,5},{5... | collective-permute-start | bytes 786440 | tf_op jit(solution)/shard_map/ppermute | solution.py:431
  47.5 5.3 %collective-permute-start.7 = (bf16[128,256]{1,0:T(8,128)(2,1)S(1)}, bf16[128,256]{1,0:T(8,128)(2,1)S(1)}, u32[]{:S(2)}, u32[]{:S(2)}) collective-permute-start(bf16[128,256]{1,0:T(8,128)(2,1)S(1)} %get-tuple-element.68), channel_id=1, source_target_pairs={{0,24},{4,28},{8,16},{12,20},{16,8},{20,12},{24,0},{28,4},{1,25},{... | collective-permute-start | bytes 196616 | tf_op jit(solution)/shard_map/ppermute | solution.py:431
  50.0 4.3 %collective-permute-start.8 = (bf16[128,256]{1,0:T(8,128)(2,1)S(1)}, bf16[128,256]{1,0:T(8,128)(2,1)S(1)}, u32[]{:S(2)}, u32[]{:S(2)}) collective-permute-start(bf16[128,256]{1,0:T(8,128)(2,1)S(1)} %get-tuple-element.69), channel_id=1, source_target_pairs={{0,16},{4,20},{8,24},{12,28},{16,0},{20,4},{24,8},{28,12},{1,17},{... | collective-permute-start | bytes 196616 | tf_op jit(solution)/shard_map/ppermute | solution.py:431
  50.5 4.3 %collective-permute-start.9 = (bf16[128,256]{1,0:T(8,128)(2,1)S(1)}, bf16[128,256]{1,0:T(8,128)(2,1)S(1)}, u32[]{:S(2)}, u32[]{:S(2)}) collective-permute-start(bf16[128,256]{1,0:T(8,128)(2,1)S(1)} %get-tuple-element.70), channel_id=1, source_target_pairs={{0,8},{4,12},{8,0},{12,4},{16,24},{20,28},{24,16},{28,20},{1,9},{5... | collective-permute-start | bytes 196616 | tf_op jit(solution)/shard_map/ppermute | solution.py:431

commit v14 on v12

--- a/solution.py
+++ b/solution.py
@@ -281,17 +281,24 @@
         send_refs[m + half][...] = grad_context
 
 
-def probs_kernel(sizes, tm, head_size, meta_ref, *refs):
+def probs_kernel(sizes, tm, part, head_size, meta_ref, *refs):
     q_refs, kv_refs, n_refs = refs[:tm], refs[tm : 2 * tm], refs[2 * tm : 3 * tm]
-    made_ref, out_ref, q4_ref, v4_ref, p_ref, d_ref, nt_ref, k4_ref = refs[3 * tm :]
+    made_ref, out_ref, diag_ref, v4_ref, p_ref, pb_ref, d_ref, nt_ref, k4_ref, q4_ref = refs[3 * tm :]
     out_ref[...] = made_ref[...]
-    for m in range(tm):
-        rows = n_refs[m].shape[0]
-        nt_ref[:, m * rows : (m + 1) * rows] = n_refs[m][...].T
     table = Layout(meta_ref, *sizes)
     me = table.me()
     local = table.blocks // tm
     hq = q_refs[0].shape[1]
+    width = nt_ref.shape[0]
+    chip, core = table.dp() // 2, table.dp() % 2
+    for q in range(width // part):
+        at = pl.ds(q * part, part)
+        if part < width:
+            place = jnp.where(core == q % 2, 0, width // part // 2) + (chip ^ (q // 2))
+            at = pl.ds(pl.multiple_of(place * part, part), part)
+        for m in range(tm):
+            rows = n_refs[m].shape[0]
+            nt_ref[at, m * rows : (m + 1) * rows] = n_refs[m][:, q * part : (q + 1) * part].T
     share = q4_ref.shape[1]
     lead = pl.multiple_of((me % (tm // 2)) * share, share)
     for ref in (k4_ref, v4_ref):
@@ -305,21 +312,24 @@
             v4_ref[at] = kv_refs[m][here, pl.ds(pl.multiple_of(hq + lead, share), share)]
     heads = share // head_size
     lower = 1.0 / (SOFT_CAP * math.sqrt(head_size))
-    mask_b = (diag_mask(heads, BLOCK, head_size) * lower).astype(BF16)
+    mask_f = diag_mask(heads, BLOCK, head_size)
+    mask_b, low_b = mask_f.astype(BF16), (mask_f * lower).astype(BF16)
     for c in range(table.blocks):
         own = slice((c + PAD) * BLOCK, (c + PAD + 1) * BLOCK)
         win = slice((c + PAD - LC) * BLOCK, (c + PAD + 1) * BLOCK)
-        diag_q = spread(q4_ref[own], mask_b)
+        diag_ref[c] = spread(q4_ref[own], mask_b)
+        diag_q = spread(q4_ref[own], low_b)
         probs, unit = window_probs(diag_q, k4_ref[win], table.reach(c))
         p_ref[c] = probs
-        d_ref[c] = (1.0 - unit * unit) * (1.0 / math.sqrt(head_size))
-
-
-def backward_kernel(sizes, tm, part, head_size, *refs):
-    tables_ref, q4_ref, v4_ref, p_ref, d_ref, nt_ref = refs[:6]
-    g_refs = dict(zip(sending_order(tm), refs[6 : 6 + tm]))
-    out_refs = refs[6 + tm : -5]
-    gt_s, t_s, full_s, meta_ref, sem = refs[-5:]
+        pb_ref[c] = probs.astype(BF16)
+        d_ref[c] = probs * (1.0 - unit * unit) * (1.0 / math.sqrt(head_size))
+
+
+def backward_kernel(sizes, tm, head_size, *refs):
+    tables_ref, diag_ref, v4_ref, p_ref, pb_ref, d_ref, nt_ref = refs[:7]
+    g_refs = dict(zip(sending_order(tm), refs[7 : 7 + tm]))
+    out_refs = refs[7 + tm : -4]
+    gt_s, t_s, meta_ref, sem = refs[-4:]
     fetch = pltpu.make_async_copy(tables_ref, meta_ref, sem)
     fetch.start()
     t_s[...] = jnp.zeros(t_s.shape, F32)
@@ -328,7 +338,7 @@
     me = table.me()
     blocks = table.blocks
     local = blocks // tm
-    share = q4_ref.shape[1]
+    share = v4_ref.shape[1]
     mask_b = diag_mask(share // head_size, BLOCK, head_size).astype(BF16)
 
     places = [(m, j, table.block_of((me ^ m) * local + j)) for m in range(tm) for j in range(local)]
@@ -348,7 +358,7 @@
     def _():
         for c in range(blocks):
             own, win, diag_g = spans(c)
-            t_s[win] = t_s[win] + dot_nn(p_ref[c].astype(BF16), diag_g)
+            t_s[win] = t_s[win] + dot_nn(pb_ref[c], diag_g)
 
     @pl.when(me < tm // 2)
     def _():
@@ -357,20 +367,17 @@
             grad_probs = dot_nt(v4_ref[win], diag_g)
             probs = p_ref[c]
             delta = jnp.sum(probs * grad_probs, axis=0, keepdims=True)
-            grad_raw = probs * (grad_probs - delta) * d_ref[c]
-            t_s[win] = t_s[win] + dot_nn(grad_raw.astype(BF16), spread(q4_ref[own], mask_b))
+            grad_raw = (grad_probs - delta) * d_ref[c]
+            t_s[win] = t_s[win] + dot_nn(grad_raw.astype(BF16), diag_ref[c])
 
     terms = jnp.concatenate([t_s[row_at(b)].astype(BF16) for _, _, b in places], axis=0)
     full = dot_nn(nt_ref[...], terms)
     if len(out_refs) == 1:
         out_refs[0][...] = full.astype(BF16)
         return
-    full_s[...] = full
-    chip, core = table.dp() // 2, table.dp() % 2
-    for q in range(out_refs[0].shape[0] // part):
-        for ref, side in zip(out_refs, (core, 1 - core)):
-            at = pl.ds(pl.multiple_of(((chip ^ q) * 2 + side) * part, part), part)
-            ref[q * part : (q + 1) * part] = full_s[at].astype(ref.dtype)
+    kept = full.shape[0] // 2
+    out_refs[0][...] = full[:kept]
+    out_refs[1][...] = full[kept:].astype(BF16)
 
 
 def pair_kernel(kept_ref, got_ref, *out_refs):
@@ -522,16 +529,17 @@
     for m in range(tm - 1, 0, -1):
         got[m] = swap(sends[m], "tm", tm, m)
 
+    direct = dp <= 8
     pair_width = share // head_size * BLOCK
-    layer_out, q4, v4, probs, slopes, normed_t = pl.pallas_call(
-        functools.partial(probs_kernel, sizes, tm, head_size),
+    layer_out, diag_q, v4, probs, probs_b, slopes, normed_t = pl.pallas_call(
+        functools.partial(probs_kernel, sizes, tm, width // dp if direct else width, head_size),
         out_shape=[shape((rows, width), BF16)]
-        + [shape((padded, share), BF16)] * 2
-        + [shape((blocks, SPAN, pair_width), F32)] * 2
+        + [shape((blocks, pair_width, share), BF16), shape((padded, share), BF16)]
+        + [shape((blocks, SPAN, pair_width), kind) for kind in (F32, BF16, F32)]
         + [shape((width, blocks * BLOCK), BF16)],
         in_specs=[smem] + [vmem] * (3 * tm + 1),
-        out_specs=[vmem] * 6,
-        scratch_shapes=[pltpu.VMEM((padded, share), BF16)],
+        out_specs=[vmem] * 7,
+        scratch_shapes=[pltpu.VMEM((padded, share), BF16)] * 2,
         compiler_params=pltpu.CompilerParams(vmem_limit_bytes=8 << 20),
         name="window_probs",
         cost_estimate=pl.CostEstimate(
@@ -539,27 +547,25 @@
         ),
     )(meta, *by_m(queries), *by_m(keys_values), *by_m(normed), made_out)
 
-    direct = dp <= 8
     half_width = width // 2
     if direct:
         piece_shapes = [shape((half_width, share), F32), shape((half_width, share), BF16)]
     else:
         piece_shapes = [shape((width, share), BF16)]
     pieces = pl.pallas_call(
-        functools.partial(backward_kernel, sizes, tm, width // dp, head_size),
+        functools.partial(backward_kernel, sizes, tm, head_size),
         out_shape=piece_shapes,
-        in_specs=[pl.BlockSpec(memory_space=pl.ANY)] + [vmem] * (5 + tm),
+        in_specs=[pl.BlockSpec(memory_space=pl.ANY)] + [vmem] * (6 + tm),
         out_specs=[vmem] * len(piece_shapes),
         scratch_shapes=[
             pltpu.VMEM((padded, share), F32),
             pltpu.VMEM((padded, share), F32),
-            pltpu.VMEM((width, share), F32),
             pltpu.SMEM(meta.shape, jnp.int32),
             pltpu.SemaphoreType.DMA,
         ],
         compiler_params=pltpu.CompilerParams(vmem_limit_bytes=12 << 20),
         name="key_value_terms",
-    )(meta, q4, v4, probs, slopes, normed_t, *[got[m] for m in sending_order(tm)])
+    )(meta, diag_q, v4, probs, probs_b, slopes, normed_t, *[got[m] for m in sending_order(tm)])
 
     if direct:
         kept, away = pieces

time: 54.8 us -> 54.7 us (level)
  no operation moved by 1% of the time
where the time goes in v14:
time: 54.7 us; the launch traced here: 54.4 us
  waiting for transfers between devices  17.2 us (31%)
  Pallas kernels  15.3 us (28%)
  starting transfers between devices  14.9 us (27%)
  local copies, waits for them, and re-layouts  5.25 us (10%)
  other arithmetic  0.96 us (2%)
  between operations  0.79 us (1%)
    ppermute x10, waiting for transfers between devices, swap(): return lax.ppermute(value, axis, [(i, i ^ m) for i in range(size)])  17.2 us
    ppermute x10, starting transfers between devices, swap(): return lax.ppermute(value, axis, [(i, i ^ m) for i in range(size)])  14.9 us
    pallas_call x1, Pallas kernels, on_device(): pl.pallas_call(functools.partial(forward_kernel, sizes, tm, head_size), o...  7.25 us
    unnamed x20, local copies, waits for them, and re-layouts  4.48 us
    pallas_call x1, Pallas kernels, on_device(): pl.pallas_call(functools.partial(probs_kernel, sizes, tm, width // dp if...  2.47 us
    pallas_call x3, Pallas kernels, project_shard(): pl.pallas_call(project_kernel, out_shape=made, in_specs=[vmem] * 4, out_s...  2.28 us
    pallas_call x1, Pallas kernels, on_device(): pl.pallas_call(functools.partial(backward_kernel, sizes, tm, head_size),...  2.2 us
  transfers between devices with their start and end apart: 10, of which 8 were waited for; matrix products, arithmetic and copies ran while one was open for 3% of the time, Pallas kernels for 9%

profile of v14, /device:TPU:0, one launch (start us, length us, event | category | flops | bytes accessed | tf_op | source)
XLA Modules:
  0.0 54.4 jit_solution(13711588195887327153)
XLA Ops:
  0.6 0.0 copy-start.2
  0.6 4.1 %collective-permute-start = (bf16[128,1024]{1,0:T(8,128)(2,1)}, bf16[128,1024]{1,0:T(8,128)(2,1)S(1)}, u32[]{:S(2)}, u32[]{:S(2)}) collective-permute-start(bf16[128,1024]{1,0:T(8,128)(2,1)} %refs_9_.1), channel_id=1, source_target_pairs={{0,2},{1,3},{2,0},{3,1},{4,6},{5,7},{6,4},{7,5},{8,10},{9,11},{10,... | collective-permute-start | bytes 786440 | tf_op jit(solution)/shard_map/ppermute | solution.py:425
  4.7 1.6 %collective-permute-start.1 = (bf16[128,1024]{1,0:T(8,128)(2,1)}, bf16[128,1024]{1,0:T(8,128)(2,1)S(1)}, u32[]{:S(2)}, u32[]{:S(2)}) collective-permute-start(bf16[128,1024]{1,0:T(8,128)(2,1)} %refs_9_.1), channel_id=1, source_target_pairs={{0,1},{1,0},{2,3},{3,2},{4,5},{5,4},{6,7},{7,6},{8,9},{9,8},{10,11... | collective-permute-start | bytes 786440 | tf_op jit(solution)/shard_map/ppermute | solution.py:425
  6.3 0.8 %concatenate.7.refs_0_.meta_ref = s32[1,20]{1,0:T(1,128)S(1)} concatenate(s32[1,1]{1,0:T(1,128)} %bitcast.3, s32[1,1]{1,0:T(1,128)} %bitcast.4, s32[1,2]{1,0:T(1,128)} %param.21, s32[1,8]{1,0:T(1,128)} %param.22, s32[1,8]{1,0:T(1,128)} %param.23), dimensions={1} | concatenate | bytes 160 | tf_op jit(solution)/shard_map/concatenate | solution.py:427
  7.1 1.0 %pad_maximum_fusion.small_ref.refs_4_ = f32[33,1024]{1,0:T(8,128)S(1)} fusion(f32[1,1024]{1,0:T(1,128)} %bitcast.9, f32[1,1024]{1,0:T(1,128)} %bitcast.10, f32[31,1024]{1,0:T(8,128)} %param.19), kind=kLoop, calls=%fused_computation | loop fusion | flops 67584 | bytes 270336 | tf_op jit(solution)/shard_map/concatenate | solution.py:437
  8.1 0.0 copy-start.3
  8.1 1.2 %copy-done.3 = bf16[512,1024]{1,0:T(8,128)(2,1)S(1)} copy-done((bf16[512,1024]{1,0:T(8,128)(2,1)S(1)}, bf16[512,1024]{1,0:T(8,128)(2,1)}, u32[]{:S(2)}) %copy-start.3) | copy-done | bytes 1048600
  9.3 0.4 spread_taps.1
  9.6 0.0 copy-done.2
  9.7 0.0 copy-start
  9.7 1.6 %copy-done = bf16[1024,1024]{1,0:T(8,128)(2,1)S(1)} copy-done((bf16[1024,1024]{1,0:T(8,128)(2,1)S(1)}, bf16[1024,1024]{1,0:T(8,128)(2,1)}, u32[]{:S(2)}) %copy-start) | copy-done | bytes 2097176
  11.3 0.0 copy-start.5
  11.3 0.9 %copy-done.5 = bf16[128,1024]{1,0:T(8,128)(2,1)S(1)} copy-done((bf16[128,1024]{1,0:T(8,128)(2,1)S(1)}, bf16[128,1024]{1,0:T(8,128)(2,1)}, u32[]{:S(2)}) %copy-start.5) | copy-done | bytes 262168
  12.2 0.0 copy-start.8
  12.2 0.7 %copy-done.8 = f32[1024]{0:T(1024)S(1)} copy-done((f32[1024]{0:T(1024)S(1)}, f32[1024]{0:T(1024)}, u32[]{:S(2)}) %copy-start.8) | copy-done | bytes 4120
  12.9 0.0 copy-start.1
  12.9 0.8 %project_rows_0.1 = (bf16[128,1024]{1,0:T(8,128)(2,1)S(1)}, bf16[128,512]{1,0:T(8,128)(2,1)S(1)}, bf16[128,1024]{1,0:T(8,128)(2,1)S(1)}) custom-call(bf16[128,1024]{1,0:T(8,128)(2,1)S(1)} %copy-done.5, f32[1,1024]{1,0:T(1,128)S(1)} %bitcast.5, bf16[1024,512]{1,0:T(8,128)(2,1)S(1)} %copy-done.2, bf16[1024,1024]{1,0:T(8,128)(2,1)S(1)} %copy-done), custom_call_target="tpu_custom_call" | custom-call | flops 402653184 | bytes 4194304 | tf_op jit(solution)/shard_map/project_rows_0/pallas_call | solution.py:459
  13.7 3.3 %collective-permute-done.x_ref.refs_11_ = bf16[128,1024]{1,0:T(8,128)(2,1)S(1)} collective-permute-done((bf16[128,1024]{1,0:T(8,128)(2,1)}, bf16[128,1024]{1,0:T(8,128)(2,1)S(1)}, u32[]{:S(2)}, u32[]{:S(2)}) %collective-permute-start) | collective-permute-done | bytes 262176 | tf_op jit(solution)/shard_map/ppermute | solution.py:425
  17.0 0.7 %collective-permute-start.2 = (bf16[128,1024]{1,0:T(8,128)(2,1)S(1)}, bf16[128,1024]{1,0:T(8,128)(2,1)S(1)}, u32[]{:S(2)}, u32[]{:S(2)}) collective-permute-start(bf16[128,1024]{1,0:T(8,128)(2,1)S(1)} %collective-permute-done.x_ref.refs_11_), channel_id=1, source_target_pairs={{0,1},{1,0},{2,3},{3,2},{4,5},{5,4},{6,7},{7,6},{8,9},{9,8},{10,11... | collective-permute-start | bytes 786440 | tf_op jit(solution)/shard_map/ppermute | solution.py:425
  17.7 0.0 copy-done.1
  17.7 0.8 %project_rows_2.1 = (bf16[128,1024]{1,0:T(8,128)(2,1)S(1)}, bf16[128,512]{1,0:T(8,128)(2,1)S(1)}, bf16[128,1024]{1,0:T(8,128)(2,1)S(1)}) custom-call(bf16[128,1024]{1,0:T(8,128)(2,1)S(1)} %collective-permute-done.x_ref.refs_11_, f32[1,1024]{1,0:T(1,128)S(1)} %bitcast.6, bf16[1024,512]{1,0:T(8,128)(2,1)S(1)} %copy-done.2, bf16[1024,1024]{1,0:T(8,128)(2,1)S(1)} %copy-done.1), custom_call_target="tpu_custom_call" | custom-call | flops 402653184 | bytes 4194304 | tf_op jit(solution)/shard_map/project_rows_2/pallas_call | solution.py:459
  18.5 0.0 copy-start.4
  18.5 0.0 copy-start.6
  18.5 0.0 copy-start.7
  18.5 0.0 copy-start.9
  18.5 0.0 collective-permute-done.1.x_ref.refs_10_
  18.5 0.8 %project_rows_1.1 = (bf16[128,1024]{1,0:T(8,128)(2,1)S(1)}, bf16[128,512]{1,0:T(8,128)(2,1)S(1)}, bf16[128,1024]{1,0:T(8,128)(2,1)S(1)}) custom-call(bf16[128,1024]{1,0:T(8,128)(2,1)S(1)} %collective-permute-done.1.x_ref.refs_10_, f32[1,1024]{1,0:T(1,128)S(1)} %bitcast.7, bf16[1024,512]{1,0:T(8,128)(2,1)S(1)} %copy-done.2, bf16[1024,1024]{1,0:T(8,128)(2,1)S(1)} %copy-done.1), custom_call_target="tpu_custom_call" | custom-call | flops 402653184 | bytes 4194304 | tf_op jit(solution)/shard_map/project_rows_1/pallas_call | solution.py:459
  19.3 5.1 %collective-permute-done.2.refs_12_ = bf16[128,1024]{1,0:T(8,128)(2,1)S(1)} collective-permute-done((bf16[128,1024]{1,0:T(8,128)(2,1)S(1)}, bf16[128,1024]{1,0:T(8,128)(2,1)S(1)}, u32[]{:S(2)}, u32[]{:S(2)}) %collective-permute-start.2) | collective-permute-done | bytes 262176 | tf_op jit(solution)/shard_map/ppermute | solution.py:425
  24.4 0.0 copy-done.4
  24.4 0.0 copy-done.6
  24.4 0.0 copy-done.7
  24.4 0.0 copy-done.9
  24.4 7.2 %forward_pass.1 = (bf16[128,1024]{1,0:T(8,128)(2,1)S(1)}, bf16[128,1024]{1,0:T(8,128)(2,1)S(1)}, bf16[128,512]{1,0:T(8,128)(2,1)S(1)}, bf16[128,1024]{1,0:T(8,12...) custom-call(s32[1,20]{1,0:T(1,128)S(1)} %concatenate.7.refs_0_.meta_, ...), custom_call_target="tpu_custom_call" | custom-call | tf_op jit(solution)/shard_map/forward_pass/pallas_call | solution.py:490
  31.7 3.1 %collective-permute-start.3 = (bf16[192,256]{1,0:T(8,128)(2,1)S(1)}, bf16[192,256]{1,0:T(8,128)(2,1)S(1)}, u32[]{:S(2)}, u32[]{:S(2)}) collective-permute-start(bf16[192,256]{1,0:T(8,128)(2,1)S(1)} %get-tuple-element.64), channel_id=1, source_target_pairs={{0,2},{1,3},{2,0},{3,1},{4,6},{5,7},{6,4},{7,5},{8,10},{9,11},{10,... | collective-permute-start | bytes 294920 | tf_op jit(solution)/shard_map/ppermute | solution.py:425
  34.8 1.3 %collective-permute-start.4 = (bf16[192,256]{1,0:T(8,128)(2,1)S(1)}, bf16[192,256]{1,0:T(8,128)(2,1)S(1)}, u32[]{:S(2)}, u32[]{:S(2)}) collective-permute-start(bf16[192,256]{1,0:T(8,128)(2,1)S(1)} %get-tuple-element.65), channel_id=1, source_target_pairs={{0,3},{1,2},{2,1},{3,0},{4,7},{5,6},{6,5},{7,4},{8,11},{9,10},{10,... | collective-permute-start | bytes 294920 | tf_op jit(solution)/shard_map/ppermute | solution.py:425
  36.1 0.5 collective-permute-start.5
  36.6 2.5 %window_probs.1 = (bf16[128,1024]{1,0:T(8,128)(2,1)}, bf16[8,256,256]{2,1,0:T(8,128)(2,1)S(1)}, bf16[704,256]{1,0:T(8,128)(2,1)S(1)}, f32[8,192,256]{2,1,0:T(8,1...) custom-call(s32[1,20]{1,0:T(1,128)S(1)} %concatenate.7.refs_0_.meta_ref, ...), custom_call_target="tpu_custom_call" | custom-call | flops 2000000000 | bytes 4000000 | tf_op jit(solution)/shard_map/window_probs/pallas_call | solution.py:534
  39.0 3.3 %collective-permute-done.3.refs_7_ = bf16[192,256]{1,0:T(8,128)(2,1)S(1)} collective-permute-done((bf16[192,256]{1,0:T(8,128)(2,1)S(1)}, bf16[192,256]{1,0:T(8,128)(2,1)S(1)}, u32[]{:S(2)}, u32[]{:S(2)}) %collective-permute-start.3) | collective-permute-done | bytes 98336 | tf_op jit(solution)/shard_map/ppermute | solution.py:425
  42.3 0.0 collective-permute-done.4.refs_8_
  42.3 0.3 collective-permute-done.5.refs_9_
  42.6 2.2 %key_value_terms.1 = (f32[512,256]{1,0:T(8,128)S(1)}, bf16[512,256]{1,0:T(8,128)(2,1)S(1)}) custom-call(s32[1,20]{1,0:T(1,128)S(1)} %concatenate.7.refs_0_.meta_ref, bf16[8,256,256]{2,1,0:T(8,128)(2,1)S(1)} %get-tuple-element.58.refs_1_, bf16[704,256]{1,0:T(8,128)(2,1)S(1)} %get-tuple-element.59.refs_2_, f32[8,192,256]{2,1,0:T(8,128)S(1)} %get-tuple-element.60.refs_3_, ...), custom_call_target="tpu_custom_call" | custom-call | tf_op jit(solution)/shard_map/key_value_terms/pallas_call | solution.py:555
  44.8 0.1 collective-permute-start.6
  44.9 1.5 %collective-permute-done.6.got_ref = bf16[512,256]{1,0:T(8,128)(2,1)S(1)} collective-permute-done((bf16[512,256]{1,0:T(8,128)(2,1)S(1)}, bf16[512,256]{1,0:T(8,128)(2,1)S(1)}, u32[]{:S(2)}, u32[]{:S(2)}) %collective-permute-start.6) | collective-permute-done | bytes 262176 | tf_op jit(solution)/shard_map/ppermute | solution.py:425
  46.4 0.1 sum_pair.1
  46.4 2.5 %collective-permute-start.7 = (bf16[128,256]{1,0:T(8,128)(2,1)S(1)}, bf16[128,256]{1,0:T(8,128)(2,1)S(1)}, u32[]{:S(2)}, u32[]{:S(2)}) collective-permute-start(bf16[128,256]{1,0:T(8,128)(2,1)S(1)} %get-tuple-element.70), channel_id=1, source_target_pairs={{0,24},{4,28},{8,16},{12,20},{16,8},{20,12},{24,0},{28,4},{1,25},{... | collective-permute-start | bytes 196616 | tf_op jit(solution)/shard_map/ppermute | solution.py:425
  49.0 0.5 collective-permute-start.8
  49.5 0.5 %collective-permute-start.9 = (bf16[128,256]{1,0:T(8,128)(2,1)S(1)}, bf16[128,256]{1,0:T(8,128)(2,1)S(1)}, u32[]{:S(2)}, u32[]{:S(2)}) collective-permute-start(bf16[128,256]{1,0:T(8,128)(2,1)S(1)} %get-tuple-element.72), channel_id=1, source_target_pairs={{0,8},{4,12},{8,0},{12,4},{16,24},{20,28},{24,16},{28,20},{1,9},{5... | collective-permute-start | bytes 196616 | tf_op jit(solution)/shard_map/ppermute | solution.py:425
  50.0 1.7 %collective-permute-done.7.refs_0_ = bf16[128,256]{1,0:T(8,128)(2,1)S(1)} collective-permute-done((bf16[128,256]{1,0:T(8,128)(2,1)S(1)}, bf16[128,256]{1,0:T(8,128)(2,1)S(1)}, u32[]{:S(2)}, u32[]{:S(2)}) %collective-permute-start.7) | collective-permute-done | bytes 65568 | tf_op jit(solution)/shard_map/ppermute | solution.py:425
  51.7 1.5 %collective-permute-done.8.refs_1_ = bf16[128,256]{1,0:T(8,128)(2,1)S(1)} collective-permute-done((bf16[128,256]{1,0:T(8,128)(2,1)S(1)}, bf16[128,256]{1,0:T(8,128)(2,1)S(1)}, u32[]{:S(2)}, u32[]{:S(2)}) %collective-permute-start.8) | collective-permute-done | bytes 65568 | tf_op jit(solution)/shard_map/ppermute | solution.py:425
  53.2 0.5 collective-permute-done.9.refs_2_
  53.7 0.7 %sum_groups.1 = f32[128,256]{1,0:T(8,128)} custom-call(bf16[128,256]{1,0:T(8,128)(2,1)S(1)} %collective-permute-done.7.refs_0_, bf16[128,256]{1,0:T(8,128)(2,1)S(1)} %collective-permute-done.8.refs_1_, bf16[128,256]{1,0:T(8,128)(2,1)S(1)} %collective-permute-done.9.refs_2_, bf16[128,256]{1,0:T(8,128)(2,1)S(1)} %get-tuple-element.73.refs_3_), custom_call_target="tpu_custom_call" | custom-call | tf_op jit(solution)/shard_map/sum_groups/pallas_call | solution.py:587
Async XLA Ops:
  0.6 9.0 %copy-start.2 = (bf16[1024,512]{1,0:T(8,128)(2,1)S(1)}, bf16[1024,512]{1,0:T(8,128)(2,1)}, u32[]{:S(2)}) copy-start(bf16[1024,512]{1,0:T(8,128)(2,1)} %refs_7_.1) | copy-start | bytes 3145732
  0.6 16.3 %collective-permute-start = (bf16[128,1024]{1,0:T(8,128)(2,1)}, bf16[128,1024]{1,0:T(8,128)(2,1)S(1)}, u32[]{:S(2)}, u32[]{:S(2)}) collective-permute-start(bf16[128,1024]{1,0:T(8,128)(2,1)} %refs_9_.1), channel_id=1, source_target_pairs={{0,2},{1,3},{2,0},{3,1},{4,6},{5,7},{6,4},{7,5},{8,10},{9,11},{10,... | collective-permute-start | bytes 786440 | tf_op jit(solution)/shard_map/ppermute | solution.py:425
  4.7 13.8 %collective-permute-start.1 = (bf16[128,1024]{1,0:T(8,128)(2,1)}, bf16[128,1024]{1,0:T(8,128)(2,1)S(1)}, u32[]{:S(2)}, u32[]{:S(2)}) collective-permute-start(bf16[128,1024]{1,0:T(8,128)(2,1)} %refs_9_.1), channel_id=1, source_target_pairs={{0,1},{1,0},{2,3},{3,2},{4,5},{5,4},{6,7},{7,6},{8,9},{9,8},{10,11... | collective-permute-start | bytes 786440 | tf_op jit(solution)/shard_map/ppermute | solution.py:425
  8.1 1.2 %copy-start.3 = (bf16[512,1024]{1,0:T(8,128)(2,1)S(1)}, bf16[512,1024]{1,0:T(8,128)(2,1)}, u32[]{:S(2)}) copy-start(bf16[512,1024]{1,0:T(8,128)(2,1)} %refs_2_.1) | copy-start | bytes 3145732
  9.7 1.6 %copy-start = (bf16[1024,1024]{1,0:T(8,128)(2,1)S(1)}, bf16[1024,1024]{1,0:T(8,128)(2,1)}, u32[]{:S(2)}) copy-start(bf16[1024,1024]{1,0:T(8,128)(2,1)} %refs_8_.1) | copy-start | bytes 6291460
  11.3 0.9 %copy-start.5 = (bf16[128,1024]{1,0:T(8,128)(2,1)S(1)}, bf16[128,1024]{1,0:T(8,128)(2,1)}, u32[]{:S(2)}) copy-start(bf16[128,1024]{1,0:T(8,128)(2,1)} %refs_9_.1) | copy-start | bytes 786436
  12.2 0.7 %copy-start.8 = (f32[1024]{0:T(1024)S(1)}, f32[1024]{0:T(1024)}, u32[]{:S(2)}) copy-start(f32[1024]{0:T(1024)} %param.14) | copy-start | bytes 12292
  12.9 4.8 %copy-start.1 = (bf16[1024,1024]{1,0:T(8,128)(2,1)S(1)}, bf16[1024,1024]{1,0:T(8,128)(2,1)}, u32[]{:S(2)}) copy-start(bf16[1024,1024]{1,0:T(8,128)(2,1)} %refs_8_.1) | copy-start | bytes 6291460
  17.0 7.4 %collective-permute-start.2 = (bf16[128,1024]{1,0:T(8,128)(2,1)S(1)}, bf16[128,1024]{1,0:T(8,128)(2,1)S(1)}, u32[]{:S(2)}, u32[]{:S(2)}) collective-permute-start(bf16[128,1024]{1,0:T(8,128)(2,1)S(1)} %collective-permute-done.x_ref.refs_11_), channel_id=1, source_target_pairs={{0,1},{1,0},{2,3},{3,2},{4,5},{5,4},{6,7},{7,6},{8,9},{9,8},{10,11... | collective-permute-start | bytes 786440 | tf_op jit(solution)/shard_map/ppermute | solution.py:425
  18.5 5.9 %copy-start.4 = (bf16[512,1024]{1,0:T(8,128)(2,1)S(1)}, bf16[512,1024]{1,0:T(8,128)(2,1)}, u32[]{:S(2)}) copy-start(bf16[512,1024]{1,0:T(8,128)(2,1)} %refs_2_.1) | copy-start | bytes 3145732
  18.5 5.9 %copy-start.6 = (bf16[128,1024]{1,0:T(8,128)(2,1)S(1)}, bf16[128,1024]{1,0:T(8,128)(2,1)}, u32[]{:S(2)}) copy-start(bf16[128,1024]{1,0:T(8,128)(2,1)} %refs_9_.1) | copy-start | bytes 786436
  18.5 5.9 %copy-start.7 = (bf16[128,1024]{1,0:T(8,128)(2,1)S(1)}, bf16[128,1024]{1,0:T(8,128)(2,1)}, u32[]{:S(2)}) copy-start(bf16[128,1024]{1,0:T(8,128)(2,1)} %refs_1_.1) | copy-start | bytes 786436
  18.5 5.9 %copy-start.9 = (f32[1024]{0:T(1024)S(1)}, f32[1024]{0:T(1024)}, u32[]{:S(2)}) copy-start(f32[1024]{0:T(1024)} %param.14) | copy-start | bytes 12292
  31.7 10.6 %collective-permute-start.3 = (bf16[192,256]{1,0:T(8,128)(2,1)S(1)}, bf16[192,256]{1,0:T(8,128)(2,1)S(1)}, u32[]{:S(2)}, u32[]{:S(2)}) collective-permute-start(bf16[192,256]{1,0:T(8,128)(2,1)S(1)} %get-tuple-element.64), channel_id=1, source_target_pairs={{0,2},{1,3},{2,0},{3,1},{4,6},{5,7},{6,4},{7,5},{8,10},{9,11},{10,... | collective-permute-start | bytes 294920 | tf_op jit(solution)/shard_map/ppermute | solution.py:425
  34.8 7.5 %collective-permute-start.4 = (bf16[192,256]{1,0:T(8,128)(2,1)S(1)}, bf16[192,256]{1,0:T(8,128)(2,1)S(1)}, u32[]{:S(2)}, u32[]{:S(2)}) collective-permute-start(bf16[192,256]{1,0:T(8,128)(2,1)S(1)} %get-tuple-element.65), channel_id=1, source_target_pairs={{0,3},{1,2},{2,1},{3,0},{4,7},{5,6},{6,5},{7,4},{8,11},{9,10},{10,... | collective-permute-start | bytes 294920 | tf_op jit(solution)/shard_map/ppermute | solution.py:425
  36.1 6.5 %collective-permute-start.5 = (bf16[192,256]{1,0:T(8,128)(2,1)S(1)}, bf16[192,256]{1,0:T(8,128)(2,1)S(1)}, u32[]{:S(2)}, u32[]{:S(2)}) collective-permute-start(bf16[192,256]{1,0:T(8,128)(2,1)S(1)} %get-tuple-element.66), channel_id=1, source_target_pairs={{0,1},{1,0},{2,3},{3,2},{4,5},{5,4},{6,7},{7,6},{8,9},{9,8},{10,11... | collective-permute-start | bytes 294920 | tf_op jit(solution)/shard_map/ppermute | solution.py:425
  44.8 1.6 %collective-permute-start.6 = (bf16[512,256]{1,0:T(8,128)(2,1)S(1)}, bf16[512,256]{1,0:T(8,128)(2,1)S(1)}, u32[]{:S(2)}, u32[]{:S(2)}) collective-permute-start(bf16[512,256]{1,0:T(8,128)(2,1)S(1)} %get-tuple-element.69), channel_id=1, source_target_pairs={{0,4},{4,0},{8,12},{12,8},{16,20},{20,16},{24,28},{28,24},{1,5},{5... | collective-permute-start | bytes 786440 | tf_op jit(solution)/shard_map/ppermute | solution.py:425
  46.4 5.3 %collective-permute-start.7 = (bf16[128,256]{1,0:T(8,128)(2,1)S(1)}, bf16[128,256]{1,0:T(8,128)(2,1)S(1)}, u32[]{:S(2)}, u32[]{:S(2)}) collective-permute-start(bf16[128,256]{1,0:T(8,128)(2,1)S(1)} %get-tuple-element.70), channel_id=1, source_target_pairs={{0,24},{4,28},{8,16},{12,20},{16,8},{20,12},{24,0},{28,4},{1,25},{... | collective-permute-start | bytes 196616 | tf_op jit(solution)/shard_map/ppermute | solution.py:425
  49.0 4.3 %collective-permute-start.8 = (bf16[128,256]{1,0:T(8,128)(2,1)S(1)}, bf16[128,256]{1,0:T(8,128)(2,1)S(1)}, u32[]{:S(2)}, u32[]{:S(2)}) collective-permute-start(bf16[128,256]{1,0:T(8,128)(2,1)S(1)} %get-tuple-element.71), channel_id=1, source_target_pairs={{0,16},{4,20},{8,24},{12,28},{16,0},{20,4},{24,8},{28,12},{1,17},{... | collective-permute-start | bytes 196616 | tf_op jit(solution)/shard_map/ppermute | solution.py:425
  49.5 4.3 %collective-permute-start.9 = (bf16[128,256]{1,0:T(8,128)(2,1)S(1)}, bf16[128,256]{1,0:T(8,128)(2,1)S(1)}, u32[]{:S(2)}, u32[]{:S(2)}) collective-permute-start(bf16[128,256]{1,0:T(8,128)(2,1)S(1)} %get-tuple-element.72), channel_id=1, source_target_pairs={{0,8},{4,12},{8,0},{12,4},{16,24},{20,28},{24,16},{28,20},{1,9},{5... | collective-permute-start | bytes 196616 | tf_op jit(solution)/shard_map/ppermute | solution.py:425
